TPU v7x, 32 devices: a whole 2x2x4 slice. The times are simulated.
32 devices in a mesh: cfg: 2 (over core), pipe: 4 (over y, x), seq: 4 (over z).
Axes of the slice: x: 2, y: 2, z: 4, core: 2. Of those that a mesh axis runs over, the one named last changes fastest.
Arguments:
- latent: bfloat16 [4, 32, 2048], P(None, 'seq'), may hold values from -6 to 6
- modulation: float32 [4, 2, 3, 2048], P('pipe', 'cfg'), may hold values from -4 to 4
- qkv_weight: bfloat16 [4, 2048, 6144], P('pipe', None, 'seq'), may hold values from -0.125 to 0.125
- out_weight: bfloat16 [4, 2048, 2048], P('pipe', 'seq'), may hold values from -0.125 to 0.125
- norm_gain: float32 [4, 2, 128], P('pipe'), may hold values from 1.2 to 2
- stale_kv: bfloat16 [4, 2, 2, 4, 4, 4, 8, 512], P('pipe', 'cfg', None, None, 'seq'), may hold values from -2 to 2
Outputs:
- guided: bfloat16 [4, 32, 2048], P('pipe', 'seq', 'cfg')
- next_kv: bfloat16 [4, 2, 2, 4, 4, 4, 8, 512], P('pipe', 'cfg', None, None, 'seq')
All inputs are finite; a program needn't handle non-finite values.
Results may differ from a plain program's by a relative error of at most 0.033.
Values may be sent and summed in bfloat16 or wider, within the bound.
No kernel may reach another device: no remote copies, remote signals or barrier semaphores. Data moves between devices by JAX's collectives and lax.ppermute only.
A program may use at most 64 MiB of HBM per device.

v0:
```python
import math

import jax
import jax.numpy as jnp
from jax import lax
from jax.sharding import PartitionSpec as P

GUIDANCE_SCALE = 6.0
EPSILON = 1e-06


def shortened(value):
    return jax.tree.map(lambda a: a.astype(jnp.bfloat16) if a.dtype == jnp.float32 else a, value)


def swapped(value, axis, bit):
    return lax.ppermute(value, axis, [(i, i ^ 1 << bit) for i in range(lax.axis_size(axis))])


def from_behind(value, axis, steps):
    count = lax.axis_size(axis)
    initial, last = (max(0, -steps), min(count, count - steps))
    return lax.ppermute(value, axis, [(source, source + steps) for source in range(initial, last)])


def spread_2(value, axis, root):
    mine = lax.axis_index(axis) == root
    return lax.psum(jnp.where(mine, value, jnp.zeros_like(value)), axis)


def layer_norm(values):
    center = values - jnp.mean(values, axis=-1, keepdims=True)
    spread = jnp.mean(center * center, axis=-1, keepdims=True)
    return center * lax.rsqrt(spread + EPSILON)


def head_norm(values, gain_row):
    return (
        values * lax.rsqrt(jnp.mean(values * values, axis=-1, keepdims=True) + EPSILON) * gain_row
    )


def join_pair(is_upper, mine, theirs, axis_dim):
    return jnp.where(
        is_upper,
        jnp.concatenate((theirs, mine), axis_dim),
        jnp.concatenate((mine, theirs), axis_dim),
    )


def local(latent, modulation, qkv_weight, out_weight, norm_gain, stale_kv):
    seq_count = lax.axis_size("seq")
    seq_rank = lax.axis_index("seq")
    section_count = lax.axis_size("pipe")
    section_rank = lax.axis_index("pipe")
    branch_rank = lax.axis_index("cfg")
    patches, tok_dev, model_width = latent.shape
    head_dim = norm_gain.shape[2]
    slice_count = min(seq_count, 8)
    member_count = seq_count // slice_count
    member_bits = member_count.bit_length() - 1
    slice_bits = slice_count.bit_length() - 1
    own_member = seq_rank % member_count
    own_slice = seq_rank // member_count
    local_width = stale_kv.shape[7]
    local_heads = local_width // head_dim
    group_rows = slice_count * tok_dev
    divisor = math.sqrt(head_dim)
    shift_row = modulation[0, 0, 0]
    scale_row = modulation[0, 0, 1]
    gate_row = modulation[0, 0, 2]
    query_gain = norm_gain[0, 0]
    key_gain = norm_gain[0, 1]
    own_cache = stale_kv[0, 0].reshape(2, patches, group_rows, local_width)
    qkv_piece = qkv_weight[0]
    out_piece = out_weight[0]
    group_cache = own_cache[None]
    qkv_slice = qkv_piece
    out_slice = out_piece
    for level_index in range(member_bits):
        got_qkv, got_out, got_cache = (
            swapped(shortened(qkv_slice), "seq", level_index).astype(qkv_slice.dtype),
            swapped(shortened(out_slice), "seq", level_index).astype(out_slice.dtype),
            swapped(shortened(group_cache), "seq", level_index).astype(group_cache.dtype),
        )
        is_upper = own_member >> level_index & 1 == 1
        qkv_slice = join_pair(is_upper, qkv_slice, got_qkv, 1)
        out_slice = join_pair(is_upper, out_slice, got_out, 0)
        group_cache = join_pair(is_upper, group_cache, got_cache, 0)

    def tick(tick_index, carried):
        incoming, own_cache, results = carried
        patch_index = tick_index - section_rank
        is_active = jnp.logical_and(patch_index >= 0, patch_index < patches)
        patch_slot = jnp.clip(patch_index, 0, patches - 1)
        first_input = lax.dynamic_index_in_dim(latent, patch_slot, 0, keepdims=False)
        hidden_in = jnp.where(section_rank == 0, first_input, incoming)
        normed = layer_norm(hidden_in.astype(jnp.float32))
        group_features = (normed * (1.0 + scale_row) + shift_row).astype(jnp.bfloat16)
        for level_index in range(slice_bits):
            got_rows = swapped(group_features, "seq", member_bits + level_index)
            is_upper = own_slice >> level_index & 1 == 1
            group_features = join_pair(is_upper, group_features, got_rows, 0)
        mixed = jnp.dot(group_features, qkv_slice, preferred_element_type=jnp.float32)
        mixed = mixed.reshape(group_rows, local_heads, 3, head_dim)
        queries = head_norm(mixed[:, :, 0], query_gain).astype(jnp.bfloat16)
        fresh_rows = jnp.stack((head_norm(mixed[:, :, 1], key_gain), mixed[:, :, 2])).astype(
            jnp.bfloat16
        )
        updated = lax.dynamic_update_index_in_dim(
            own_cache, fresh_rows.reshape(2, group_rows, local_width), patch_slot, 1
        )

        def compute():
            view = lax.dynamic_update_index_in_dim(group_cache, updated, own_member, 0)
            key_rows = view[:, 0].reshape(-1, local_heads, head_dim)
            value_rows = view[:, 1].reshape(-1, local_heads, head_dim)
            scores = (
                jnp.einsum("qhd,khd->hqk", queries, key_rows, preferred_element_type=jnp.float32)
                / divisor
            )
            weights = jnp.exp(scores)
            weight_total = jnp.sum(weights, axis=-1)
            summed = jnp.einsum(
                "hqk,khd->qhd",
                weights.astype(jnp.bfloat16),
                value_rows,
                preferred_element_type=jnp.float32,
            )
            return (
                (summed / weight_total.T[:, :, None])
                .astype(jnp.bfloat16)
                .reshape(group_rows, local_width)
            )

        attended = lax.cond(
            is_active, compute, lambda: jnp.zeros((group_rows, local_width), jnp.bfloat16)
        )
        partial_out = jnp.dot(attended, out_slice, preferred_element_type=jnp.float32)
        for level_index in reversed(range(slice_bits)):
            half_rows = partial_out.shape[0] // 2
            is_upper = own_slice >> level_index & 1 == 1
            keep_rows = jnp.where(is_upper, partial_out[half_rows:], partial_out[:half_rows])
            send_rows = jnp.where(is_upper, partial_out[:half_rows], partial_out[half_rows:])
            partial_out = keep_rows + swapped(
                send_rows.astype(jnp.bfloat16), "seq", member_bits + level_index
            ).astype(send_rows.dtype)
        hidden_out = (hidden_in.astype(jnp.float32) + gate_row * partial_out).astype(jnp.bfloat16)
        own_cache = jnp.where(is_active, updated, own_cache)
        results = jnp.where(
            is_active, lax.dynamic_update_index_in_dim(results, hidden_out, patch_slot, 0), results
        )
        incoming = from_behind(hidden_out, "pipe", 1)
        return (incoming, own_cache, results)

    initial = (
        jnp.zeros((tok_dev, model_width), jnp.bfloat16),
        own_cache,
        jnp.zeros((patches, tok_dev, model_width), jnp.bfloat16),
    )
    incoming, own_cache, results = lax.fori_loop(0, patches + section_count - 1, tick, initial)
    half_width = model_width // 2
    partner_out = swapped(results, "cfg", 0)
    own_half = lax.dynamic_slice_in_dim(results, branch_rank * half_width, half_width, 2).astype(
        jnp.float32
    )
    partner_half = lax.dynamic_slice_in_dim(
        partner_out, branch_rank * half_width, half_width, 2
    ).astype(jnp.float32)
    conditional = jnp.where(branch_rank == 0, own_half, partner_half)
    unconditional = jnp.where(branch_rank == 0, partner_half, own_half)
    guided = (unconditional + GUIDANCE_SCALE * (conditional - unconditional)).astype(jnp.bfloat16)
    spread_all = spread_2(guided, "pipe", section_count - 1)
    per_section = patches // section_count
    guided_out = lax.dynamic_slice_in_dim(spread_all, section_rank * per_section, per_section, 0)
    next_cache = own_cache.reshape(stale_kv.shape)
    return (guided_out, next_cache)


def solution(mesh):
    placed = (
        P(None, "seq", None),
        P("pipe", "cfg", None, None),
        P("pipe", None, "seq"),
        P("pipe", "seq", None),
        P("pipe", None, None),
        P("pipe", "cfg", None, None, "seq", None, None, None),
    )
    return jax.shard_map(
        local,
        mesh=mesh,
        in_specs=placed,
        out_specs=(P("pipe", "seq", "cfg"), P("pipe", "cfg", None, None, "seq", None, None, None)),
        check_vma=False,
    )
```

profile of v0, /device:TPU:0, one launch (start us, length us, event | category | flops | bytes accessed | tf_op | source)
XLA Modules:
  0.0 295.1 jit_solution(9273950293128856161)
XLA Ops:
  9.7 231.1 %while.19 = (s32[]{:T(128)}, bf16[8,2048]{1,0:T(8,128)(2,1)S(1)}, bf16[2,4,32,512]{3,2,1,0:T(8,128)(2,1)S(1)}, bf16[4,8,2048]{2,1,0:T(8,128)(2,1)S(1)}, pred[]{:...) while((s32[]{:T(128)}, bf16[8,2048]{1,0:T(8,128)(2,1)S(1)}, ...), condition=%wide.region_8.9_spmd, body=%wide.region_0.8_spmd.sunk | while | flops 278710400 | bytes 24136480 | solution.py:161
  11.1 3.1 %collective-permute-start = (bf16[8,2048]{1,0:T(8,128)(2,1)S(1)}, bf16[8,2048]{1,0:T(8,128)(2,1)S(1)}, u32[]{:S(2)}, u32[]{:S(2)}) collective-permute-start(bf16[8,2048]{1,0:T(8,128)(2,1)S(1)} %fusion.54), channel_id=1, source_target_pairs={{0,1},{1,0},{2,3},{3,2},{4,5},{5,4},{6,7},{7,6},{8,9},{9,8},{10,11... | collective-permute-start | bytes 98312 | tf_op jit(solution)/shard_map/while/body/eval_jaxpr/ppermute | solution.py:17
  16.1 3.1 %collective-permute-start.1 = (bf16[16,2048]{1,0:T(8,128)(2,1)S(1)}, bf16[16,2048]{1,0:T(8,128)(2,1)S(1)}, u32[]{:S(2)}, u32[]{:S(2)}) collective-permute-start(bf16[16,2048]{1,0:T(8,128)(2,1)S(1)} %maximum_select_fusion.6), channel_id=1, source_target_pairs={{0,2},{1,3},{2,0},{3,1},{4,6},{5,7},{6,4},{7,5},{8,10},{9,11},{10,... | collective-permute-start | bytes 196616 | tf_op jit(solution)/shard_map/while/body/eval_jaxpr/ppermute | solution.py:17
  21.4 3.9 %fusion.55 = f32[32,1536]{1,0:T(8,128)S(1)} fusion(bf16[2048,1536]{1,0:T(8,128)(2,1)} %get-tuple-element.607, bf16[16,2048]{1,0:T(8,128)(2,1)S(1)} %maximum_select_fusion.6, bf16[16,2048]{1,0:T(8,128)(2,1)S(1)} %collective-permute-done.1, pred[]{:T(512)} %get-tuple-element.604), kind=kOutput, calls=%fused_computation.13.clone.1 | convolution fusion | flops 201916416 | bytes 6619137 | tf_op jit(solution)/shard_map/while/body/eval_jaxpr/dot_general | solution.py:104
  27.8 3.0 %collective-permute-start.2 = (bf16[16,2048]{1,0:T(8,128)(2,1)S(1)}, bf16[16,2048]{1,0:T(8,128)(2,1)S(1)}, u32[]{:S(2)}, u32[]{:S(2)}) collective-permute-start(bf16[16,2048]{1,0:T(8,128)(2,1)S(1)} %select_convert_fusion.4), channel_id=1, source_target_pairs={{0,2},{1,3},{2,0},{3,1},{4,6},{5,7},{6,4},{7,5},{8,10},{9,11},{10,... | collective-permute-start | bytes 196616 | tf_op jit(solution)/shard_map/while/body/eval_jaxpr/ppermute | solution.py:17
  30.8 2.3 collective-permute-done.2
  37.2 3.1 %collective-permute-start.4 = (bf16[8,2048]{1,0:T(8,128)(2,1)S(1)}, bf16[8,2048]{1,0:T(8,128)(2,1)S(1)}, u32[]{:S(2)}, u32[]{:S(2)}) collective-permute-start(bf16[8,2048]{1,0:T(8,128)(2,1)S(1)} %get-tuple-element.553), channel_id=1, source_target_pairs={{0,4},{4,8},{8,12},{1,5},{5,9},{9,13},{2,6},{6,10},{10,14},{3,7},{... | collective-permute-start | bytes 98312 | tf_op jit(solution)/shard_map/while/body/eval_jaxpr/ppermute | solution.py:23
  47.2 3.1 %collective-permute-start.1 = (bf16[16,2048]{1,0:T(8,128)(2,1)S(1)}, bf16[16,2048]{1,0:T(8,128)(2,1)S(1)}, u32[]{:S(2)}, u32[]{:S(2)}) collective-permute-start(bf16[16,2048]{1,0:T(8,128)(2,1)S(1)} %maximum_select_fusion.6), channel_id=1, source_target_pairs={{0,2},{1,3},{2,0},{3,1},{4,6},{5,7},{6,4},{7,5},{8,10},{9,11},{10,... | collective-permute-start | bytes 196616 | tf_op jit(solution)/shard_map/while/body/eval_jaxpr/ppermute | solution.py:17
  50.4 2.2 collective-permute-done.1
  52.6 3.9 %fusion.55 = f32[32,1536]{1,0:T(8,128)S(1)} fusion(bf16[2048,1536]{1,0:T(8,128)(2,1)} %get-tuple-element.607, bf16[16,2048]{1,0:T(8,128)(2,1)S(1)} %maximum_select_fusion.6, bf16[16,2048]{1,0:T(8,128)(2,1)S(1)} %collective-permute-done.1, pred[]{:T(512)} %get-tuple-element.604), kind=kOutput, calls=%fused_computation.13.clone.1 | convolution fusion | flops 201916416 | bytes 6619137 | tf_op jit(solution)/shard_map/while/body/eval_jaxpr/dot_general | solution.py:104
  59.0 3.0 %collective-permute-start.2 = (bf16[16,2048]{1,0:T(8,128)(2,1)S(1)}, bf16[16,2048]{1,0:T(8,128)(2,1)S(1)}, u32[]{:S(2)}, u32[]{:S(2)}) collective-permute-start(bf16[16,2048]{1,0:T(8,128)(2,1)S(1)} %select_convert_fusion.4), channel_id=1, source_target_pairs={{0,2},{1,3},{2,0},{3,1},{4,6},{5,7},{6,4},{7,5},{8,10},{9,11},{10,... | collective-permute-start | bytes 196616 | tf_op jit(solution)/shard_map/while/body/eval_jaxpr/ppermute | solution.py:17
  62.0 2.2 collective-permute-done.2
  64.2 2.2 collective-permute-start.3
  68.5 4.2 %collective-permute-start.4 = (bf16[8,2048]{1,0:T(8,128)(2,1)S(1)}, bf16[8,2048]{1,0:T(8,128)(2,1)S(1)}, u32[]{:S(2)}, u32[]{:S(2)}) collective-permute-start(bf16[8,2048]{1,0:T(8,128)(2,1)S(1)} %get-tuple-element.553), channel_id=1, source_target_pairs={{0,4},{4,8},{8,12},{1,5},{5,9},{9,13},{2,6},{6,10},{10,14},{3,7},{... | collective-permute-start | bytes 98312 | tf_op jit(solution)/shard_map/while/body/eval_jaxpr/ppermute | solution.py:23
  79.7 2.8 collective-permute-start.1
  82.6 2.5 collective-permute-done.1
  85.0 3.9 %fusion.55 = f32[32,1536]{1,0:T(8,128)S(1)} fusion(bf16[2048,1536]{1,0:T(8,128)(2,1)} %get-tuple-element.607, bf16[16,2048]{1,0:T(8,128)(2,1)S(1)} %maximum_select_fusion.6, bf16[16,2048]{1,0:T(8,128)(2,1)S(1)} %collective-permute-done.1, pred[]{:T(512)} %get-tuple-element.604), kind=kOutput, calls=%fused_computation.13.clone.1 | convolution fusion | flops 201916416 | bytes 6619137 | tf_op jit(solution)/shard_map/while/body/eval_jaxpr/dot_general | solution.py:104
  91.4 2.7 collective-permute-start.2
  94.1 2.5 collective-permute-done.2
  100.7 4.5 %collective-permute-start.4 = (bf16[8,2048]{1,0:T(8,128)(2,1)S(1)}, bf16[8,2048]{1,0:T(8,128)(2,1)S(1)}, u32[]{:S(2)}, u32[]{:S(2)}) collective-permute-start(bf16[8,2048]{1,0:T(8,128)(2,1)S(1)} %get-tuple-element.553), channel_id=1, source_target_pairs={{0,4},{4,8},{8,12},{1,5},{5,9},{9,13},{2,6},{6,10},{10,14},{3,7},{... | collective-permute-start | bytes 98312 | tf_op jit(solution)/shard_map/while/body/eval_jaxpr/ppermute | solution.py:23
  110.2 2.4 collective-permute-done
  114.8 3.0 %collective-permute-done.1 = bf16[16,2048]{1,0:T(8,128)(2,1)S(1)} collective-permute-done((bf16[16,2048]{1,0:T(8,128)(2,1)S(1)}, bf16[16,2048]{1,0:T(8,128)(2,1)S(1)}, u32[]{:S(2)}, u32[]{:S(2)}) %collective-permute-start.1) | collective-permute-done | bytes 65568 | tf_op jit(solution)/shard_map/while/body/eval_jaxpr/ppermute | solution.py:17
  117.8 3.9 %fusion.55 = f32[32,1536]{1,0:T(8,128)S(1)} fusion(bf16[2048,1536]{1,0:T(8,128)(2,1)} %get-tuple-element.607, bf16[16,2048]{1,0:T(8,128)(2,1)S(1)} %maximum_select_fusion.6, bf16[16,2048]{1,0:T(8,128)(2,1)S(1)} %collective-permute-done.1, pred[]{:T(512)} %get-tuple-element.604), kind=kOutput, calls=%fused_computation.13.clone.1 | convolution fusion | flops 201916416 | bytes 6619137 | tf_op jit(solution)/shard_map/while/body/eval_jaxpr/dot_general | solution.py:104
  126.3 4.4 %collective-permute-done.2 = bf16[16,2048]{1,0:T(8,128)(2,1)S(1)} collective-permute-done((bf16[16,2048]{1,0:T(8,128)(2,1)S(1)}, bf16[16,2048]{1,0:T(8,128)(2,1)S(1)}, u32[]{:S(2)}, u32[]{:S(2)}) %collective-permute-start.2) | collective-permute-done | bytes 65568 | tf_op jit(solution)/shard_map/while/body/eval_jaxpr/ppermute | solution.py:17
  131.1 3.7 %collective-permute-done.3 = bf16[8,2048]{1,0:T(8,128)(2,1)S(1)} collective-permute-done((bf16[8,2048]{1,0:T(8,128)(2,1)S(1)}, bf16[8,2048]{1,0:T(8,128)(2,1)S(1)}, u32[]{:S(2)}, u32[]{:S(2)}) %collective-permute-start.3) | collective-permute-done | bytes 32800 | tf_op jit(solution)/shard_map/while/body/eval_jaxpr/ppermute | solution.py:17
  134.8 3.5 %collective-permute-start.4 = (bf16[8,2048]{1,0:T(8,128)(2,1)S(1)}, bf16[8,2048]{1,0:T(8,128)(2,1)S(1)}, u32[]{:S(2)}, u32[]{:S(2)}) collective-permute-start(bf16[8,2048]{1,0:T(8,128)(2,1)S(1)} %get-tuple-element.553), channel_id=1, source_target_pairs={{0,4},{4,8},{8,12},{1,5},{5,9},{9,13},{2,6},{6,10},{10,14},{3,7},{... | collective-permute-start | bytes 98312 | tf_op jit(solution)/shard_map/while/body/eval_jaxpr/ppermute | solution.py:23
  142.8 2.4 collective-permute-done
  145.3 2.3 collective-permute-start.1
  147.6 2.9 collective-permute-done.1
  150.5 3.9 %fusion.55 = f32[32,1536]{1,0:T(8,128)S(1)} fusion(bf16[2048,1536]{1,0:T(8,128)(2,1)} %get-tuple-element.607, bf16[16,2048]{1,0:T(8,128)(2,1)S(1)} %maximum_select_fusion.6, bf16[16,2048]{1,0:T(8,128)(2,1)S(1)} %collective-permute-done.1, pred[]{:T(512)} %get-tuple-element.604), kind=kOutput, calls=%fused_computation.13.clone.1 | convolution fusion | flops 201916416 | bytes 6619137 | tf_op jit(solution)/shard_map/while/body/eval_jaxpr/dot_general | solution.py:104
  156.3 2.3 collective-permute-start.2
  158.6 2.9 collective-permute-done.2
  163.2 2.4 collective-permute-done.3
  165.6 5.3 %collective-permute-start.4 = (bf16[8,2048]{1,0:T(8,128)(2,1)S(1)}, bf16[8,2048]{1,0:T(8,128)(2,1)S(1)}, u32[]{:S(2)}, u32[]{:S(2)}) collective-permute-start(bf16[8,2048]{1,0:T(8,128)(2,1)S(1)} %get-tuple-element.553), channel_id=1, source_target_pairs={{0,4},{4,8},{8,12},{1,5},{5,9},{9,13},{2,6},{6,10},{10,14},{3,7},{... | collective-permute-start | bytes 98312 | tf_op jit(solution)/shard_map/while/body/eval_jaxpr/ppermute | solution.py:23
  177.8 3.1 %collective-permute-start.1 = (bf16[16,2048]{1,0:T(8,128)(2,1)S(1)}, bf16[16,2048]{1,0:T(8,128)(2,1)S(1)}, u32[]{:S(2)}, u32[]{:S(2)}) collective-permute-start(bf16[16,2048]{1,0:T(8,128)(2,1)S(1)} %maximum_select_fusion.6), channel_id=1, source_target_pairs={{0,2},{1,3},{2,0},{3,1},{4,6},{5,7},{6,4},{7,5},{8,10},{9,11},{10,... | collective-permute-start | bytes 196616 | tf_op jit(solution)/shard_map/while/body/eval_jaxpr/ppermute | solution.py:17
  180.9 2.9 collective-permute-done.1
  183.9 3.9 %fusion.55 = f32[32,1536]{1,0:T(8,128)S(1)} fusion(bf16[2048,1536]{1,0:T(8,128)(2,1)} %get-tuple-element.607, bf16[16,2048]{1,0:T(8,128)(2,1)S(1)} %maximum_select_fusion.6, bf16[16,2048]{1,0:T(8,128)(2,1)S(1)} %collective-permute-done.1, pred[]{:T(512)} %get-tuple-element.604), kind=kOutput, calls=%fused_computation.13.clone.1 | convolution fusion | flops 201916416 | bytes 6619137 | tf_op jit(solution)/shard_map/while/body/eval_jaxpr/dot_general | solution.py:104
  189.7 2.3 collective-permute-start.2
  191.9 4.3 %collective-permute-done.2 = bf16[16,2048]{1,0:T(8,128)(2,1)S(1)} collective-permute-done((bf16[16,2048]{1,0:T(8,128)(2,1)S(1)}, bf16[16,2048]{1,0:T(8,128)(2,1)S(1)}, u32[]{:S(2)}, u32[]{:S(2)}) %collective-permute-start.2) | collective-permute-done | bytes 65568 | tf_op jit(solution)/shard_map/while/body/eval_jaxpr/ppermute | solution.py:17
  196.6 3.6 %collective-permute-done.3 = bf16[8,2048]{1,0:T(8,128)(2,1)S(1)} collective-permute-done((bf16[8,2048]{1,0:T(8,128)(2,1)S(1)}, bf16[8,2048]{1,0:T(8,128)(2,1)S(1)}, u32[]{:S(2)}, u32[]{:S(2)}) %collective-permute-start.3) | collective-permute-done | bytes 32800 | tf_op jit(solution)/shard_map/while/body/eval_jaxpr/ppermute | solution.py:17
  200.3 6.4 %collective-permute-start.4 = (bf16[8,2048]{1,0:T(8,128)(2,1)S(1)}, bf16[8,2048]{1,0:T(8,128)(2,1)S(1)}, u32[]{:S(2)}, u32[]{:S(2)}) collective-permute-start(bf16[8,2048]{1,0:T(8,128)(2,1)S(1)} %get-tuple-element.553), channel_id=1, source_target_pairs={{0,4},{4,8},{8,12},{1,5},{5,9},{9,13},{2,6},{6,10},{10,14},{3,7},{... | collective-permute-start | bytes 98312 | tf_op jit(solution)/shard_map/while/body/eval_jaxpr/ppermute | solution.py:23
  209.7 3.9 %collective-permute-done = bf16[8,2048]{1,0:T(8,128)(2,1)S(1)} collective-permute-done((bf16[8,2048]{1,0:T(8,128)(2,1)S(1)}, bf16[8,2048]{1,0:T(8,128)(2,1)S(1)}, u32[]{:S(2)}, u32[]{:S(2)}) %collective-permute-start) | collective-permute-done | bytes 32800 | tf_op jit(solution)/shard_map/while/body/eval_jaxpr/ppermute | solution.py:17
  214.7 4.4 %collective-permute-done.1 = bf16[16,2048]{1,0:T(8,128)(2,1)S(1)} collective-permute-done((bf16[16,2048]{1,0:T(8,128)(2,1)S(1)}, bf16[16,2048]{1,0:T(8,128)(2,1)S(1)}, u32[]{:S(2)}, u32[]{:S(2)}) %collective-permute-start.1) | collective-permute-done | bytes 65568 | tf_op jit(solution)/shard_map/while/body/eval_jaxpr/ppermute | solution.py:17
  219.0 3.9 %fusion.55 = f32[32,1536]{1,0:T(8,128)S(1)} fusion(bf16[2048,1536]{1,0:T(8,128)(2,1)} %get-tuple-element.607, bf16[16,2048]{1,0:T(8,128)(2,1)S(1)} %maximum_select_fusion.6, bf16[16,2048]{1,0:T(8,128)(2,1)S(1)} %collective-permute-done.1, pred[]{:T(512)} %get-tuple-element.604), kind=kOutput, calls=%fused_computation.13.clone.1 | convolution fusion | flops 201916416 | bytes 6619137 | tf_op jit(solution)/shard_map/while/body/eval_jaxpr/dot_general | solution.py:104
  225.7 4.5 %collective-permute-done.2 = bf16[16,2048]{1,0:T(8,128)(2,1)S(1)} collective-permute-done((bf16[16,2048]{1,0:T(8,128)(2,1)S(1)}, bf16[16,2048]{1,0:T(8,128)(2,1)S(1)}, u32[]{:S(2)}, u32[]{:S(2)}) %collective-permute-start.2) | collective-permute-done | bytes 65568 | tf_op jit(solution)/shard_map/while/body/eval_jaxpr/ppermute | solution.py:17
  230.3 3.9 %collective-permute-done.3 = bf16[8,2048]{1,0:T(8,128)(2,1)S(1)} collective-permute-done((bf16[8,2048]{1,0:T(8,128)(2,1)S(1)}, bf16[8,2048]{1,0:T(8,128)(2,1)S(1)}, u32[]{:S(2)}, u32[]{:S(2)}) %collective-permute-start.3) | collective-permute-done | bytes 32800 | tf_op jit(solution)/shard_map/while/body/eval_jaxpr/ppermute | solution.py:17
  234.3 4.9 %collective-permute-start.4 = (bf16[8,2048]{1,0:T(8,128)(2,1)S(1)}, bf16[8,2048]{1,0:T(8,128)(2,1)S(1)}, u32[]{:S(2)}, u32[]{:S(2)}) collective-permute-start(bf16[8,2048]{1,0:T(8,128)(2,1)S(1)} %get-tuple-element.553), channel_id=1, source_target_pairs={{0,4},{4,8},{8,12},{1,5},{5,9},{9,13},{2,6},{6,10},{10,14},{3,7},{... | collective-permute-start | bytes 98312 | tf_op jit(solution)/shard_map/while/body/eval_jaxpr/ppermute | solution.py:23
  242.8 44.0 %all-reduce.2.cloned.1.call-done = bf16[4,8,1024]{2,1,0:T(8,128)(2,1)} async-done(((bf16[4,8,1024]{2,1,0:T(8,128)(2,1)}), bf16[4,8,1024]{2,1,0:T(8,128)(2,1)}) %all-reduce.2.cloned.1.call-update) | async-done | bytes 65552 | tf_op jit(solution)/shard_map/psum | solution.py:28
  (288 shorter events, 81.8 us)
Async XLA Ops:
  7.2 279.7 %all-reduce.2.cloned.1.call-start = ((), (), s32[]{:S(2)}) async-start(), calls=%async_computation | async-start | bytes 131072 | tf_op jit(solution)/shard_map/psum | solution.py:28
  9.7 17.6 %copy-start = (bf16[512,2048]{1,0:T(8,128)(2,1)S(1)}, bf16[512,2048]{1,0:T(8,128)(2,1)}, u32[]{:S(2)}) copy-start(bf16[512,2048]{1,0:T(8,128)(2,1)} %get-tuple-element.610) | copy-start | bytes 6291460 | tf_op jit(solution)/shard_map/while
  11.1 5.0 %collective-permute-start = (bf16[8,2048]{1,0:T(8,128)(2,1)S(1)}, bf16[8,2048]{1,0:T(8,128)(2,1)S(1)}, u32[]{:S(2)}, u32[]{:S(2)}) collective-permute-start(bf16[8,2048]{1,0:T(8,128)(2,1)S(1)} %fusion.54), channel_id=1, source_target_pairs={{0,1},{1,0},{2,3},{3,2},{4,5},{5,4},{6,7},{7,6},{8,9},{9,8},{10,11... | collective-permute-start | bytes 98312 | tf_op jit(solution)/shard_map/while/body/eval_jaxpr/ppermute | solution.py:17
  16.1 5.3 %collective-permute-start.1 = (bf16[16,2048]{1,0:T(8,128)(2,1)S(1)}, bf16[16,2048]{1,0:T(8,128)(2,1)S(1)}, u32[]{:S(2)}, u32[]{:S(2)}) collective-permute-start(bf16[16,2048]{1,0:T(8,128)(2,1)S(1)} %maximum_select_fusion.6), channel_id=1, source_target_pairs={{0,2},{1,3},{2,0},{3,1},{4,6},{5,7},{6,4},{7,5},{8,10},{9,11},{10,... | collective-permute-start | bytes 196616 | tf_op jit(solution)/shard_map/while/body/eval_jaxpr/ppermute | solution.py:17
  27.8 5.3 %collective-permute-start.2 = (bf16[16,2048]{1,0:T(8,128)(2,1)S(1)}, bf16[16,2048]{1,0:T(8,128)(2,1)S(1)}, u32[]{:S(2)}, u32[]{:S(2)}) collective-permute-start(bf16[16,2048]{1,0:T(8,128)(2,1)S(1)} %select_convert_fusion.4), channel_id=1, source_target_pairs={{0,2},{1,3},{2,0},{3,1},{4,6},{5,7},{6,4},{7,5},{8,10},{9,11},{10,... | collective-permute-start | bytes 196616 | tf_op jit(solution)/shard_map/while/body/eval_jaxpr/ppermute | solution.py:17
  33.1 4.0 %collective-permute-start.3 = (bf16[8,2048]{1,0:T(8,128)(2,1)S(1)}, bf16[8,2048]{1,0:T(8,128)(2,1)S(1)}, u32[]{:S(2)}, u32[]{:S(2)}) collective-permute-start(bf16[8,2048]{1,0:T(8,128)(2,1)S(1)} %select_convert_fusion.5), channel_id=1, source_target_pairs={{0,1},{1,0},{2,3},{3,2},{4,5},{5,4},{6,7},{7,6},{8,9},{9,8},{10,11... | collective-permute-start | bytes 98312 | tf_op jit(solution)/shard_map/while/body/eval_jaxpr/ppermute | solution.py:17
  37.2 4.7 %collective-permute-start.4 = (bf16[8,2048]{1,0:T(8,128)(2,1)S(1)}, bf16[8,2048]{1,0:T(8,128)(2,1)S(1)}, u32[]{:S(2)}, u32[]{:S(2)}) collective-permute-start(bf16[8,2048]{1,0:T(8,128)(2,1)S(1)} %get-tuple-element.553), channel_id=1, source_target_pairs={{0,4},{4,8},{8,12},{1,5},{5,9},{9,13},{2,6},{6,10},{10,14},{3,7},{... | collective-permute-start | bytes 98312 | tf_op jit(solution)/shard_map/while/body/eval_jaxpr/ppermute | solution.py:23
  41.9 16.6 %copy-start = (bf16[512,2048]{1,0:T(8,128)(2,1)S(1)}, bf16[512,2048]{1,0:T(8,128)(2,1)}, u32[]{:S(2)}) copy-start(bf16[512,2048]{1,0:T(8,128)(2,1)} %get-tuple-element.610) | copy-start | bytes 6291460 | tf_op jit(solution)/shard_map/while
  43.2 4.0 %collective-permute-start = (bf16[8,2048]{1,0:T(8,128)(2,1)S(1)}, bf16[8,2048]{1,0:T(8,128)(2,1)S(1)}, u32[]{:S(2)}, u32[]{:S(2)}) collective-permute-start(bf16[8,2048]{1,0:T(8,128)(2,1)S(1)} %fusion.54), channel_id=1, source_target_pairs={{0,1},{1,0},{2,3},{3,2},{4,5},{5,4},{6,7},{7,6},{8,9},{9,8},{10,11... | collective-permute-start | bytes 98312 | tf_op jit(solution)/shard_map/while/body/eval_jaxpr/ppermute | solution.py:17
  47.2 5.4 %collective-permute-start.1 = (bf16[16,2048]{1,0:T(8,128)(2,1)S(1)}, bf16[16,2048]{1,0:T(8,128)(2,1)S(1)}, u32[]{:S(2)}, u32[]{:S(2)}) collective-permute-start(bf16[16,2048]{1,0:T(8,128)(2,1)S(1)} %maximum_select_fusion.6), channel_id=1, source_target_pairs={{0,2},{1,3},{2,0},{3,1},{4,6},{5,7},{6,4},{7,5},{8,10},{9,11},{10,... | collective-permute-start | bytes 196616 | tf_op jit(solution)/shard_map/while/body/eval_jaxpr/ppermute | solution.py:17
  59.0 5.2 %collective-permute-start.2 = (bf16[16,2048]{1,0:T(8,128)(2,1)S(1)}, bf16[16,2048]{1,0:T(8,128)(2,1)S(1)}, u32[]{:S(2)}, u32[]{:S(2)}) collective-permute-start(bf16[16,2048]{1,0:T(8,128)(2,1)S(1)} %select_convert_fusion.4), channel_id=1, source_target_pairs={{0,2},{1,3},{2,0},{3,1},{4,6},{5,7},{6,4},{7,5},{8,10},{9,11},{10,... | collective-permute-start | bytes 196616 | tf_op jit(solution)/shard_map/while/body/eval_jaxpr/ppermute | solution.py:17
  64.2 4.3 %collective-permute-start.3 = (bf16[8,2048]{1,0:T(8,128)(2,1)S(1)}, bf16[8,2048]{1,0:T(8,128)(2,1)S(1)}, u32[]{:S(2)}, u32[]{:S(2)}) collective-permute-start(bf16[8,2048]{1,0:T(8,128)(2,1)S(1)} %select_convert_fusion.5), channel_id=1, source_target_pairs={{0,1},{1,0},{2,3},{3,2},{4,5},{5,4},{6,7},{7,6},{8,9},{9,8},{10,11... | collective-permute-start | bytes 98312 | tf_op jit(solution)/shard_map/while/body/eval_jaxpr/ppermute | solution.py:17
  68.5 5.8 %collective-permute-start.4 = (bf16[8,2048]{1,0:T(8,128)(2,1)S(1)}, bf16[8,2048]{1,0:T(8,128)(2,1)S(1)}, u32[]{:S(2)}, u32[]{:S(2)}) collective-permute-start(bf16[8,2048]{1,0:T(8,128)(2,1)S(1)} %get-tuple-element.553), channel_id=1, source_target_pairs={{0,4},{4,8},{8,12},{1,5},{5,9},{9,13},{2,6},{6,10},{10,14},{3,7},{... | collective-permute-start | bytes 98312 | tf_op jit(solution)/shard_map/while/body/eval_jaxpr/ppermute | solution.py:23
  74.3 16.6 %copy-start = (bf16[512,2048]{1,0:T(8,128)(2,1)S(1)}, bf16[512,2048]{1,0:T(8,128)(2,1)}, u32[]{:S(2)}) copy-start(bf16[512,2048]{1,0:T(8,128)(2,1)} %get-tuple-element.610) | copy-start | bytes 6291460 | tf_op jit(solution)/shard_map/while
  75.7 4.0 %collective-permute-start = (bf16[8,2048]{1,0:T(8,128)(2,1)S(1)}, bf16[8,2048]{1,0:T(8,128)(2,1)S(1)}, u32[]{:S(2)}, u32[]{:S(2)}) collective-permute-start(bf16[8,2048]{1,0:T(8,128)(2,1)S(1)} %fusion.54), channel_id=1, source_target_pairs={{0,1},{1,0},{2,3},{3,2},{4,5},{5,4},{6,7},{7,6},{8,9},{9,8},{10,11... | collective-permute-start | bytes 98312 | tf_op jit(solution)/shard_map/while/body/eval_jaxpr/ppermute | solution.py:17
  79.7 5.4 %collective-permute-start.1 = (bf16[16,2048]{1,0:T(8,128)(2,1)S(1)}, bf16[16,2048]{1,0:T(8,128)(2,1)S(1)}, u32[]{:S(2)}, u32[]{:S(2)}) collective-permute-start(bf16[16,2048]{1,0:T(8,128)(2,1)S(1)} %maximum_select_fusion.6), channel_id=1, source_target_pairs={{0,2},{1,3},{2,0},{3,1},{4,6},{5,7},{6,4},{7,5},{8,10},{9,11},{10,... | collective-permute-start | bytes 196616 | tf_op jit(solution)/shard_map/while/body/eval_jaxpr/ppermute | solution.py:17
  91.4 5.2 %collective-permute-start.2 = (bf16[16,2048]{1,0:T(8,128)(2,1)S(1)}, bf16[16,2048]{1,0:T(8,128)(2,1)S(1)}, u32[]{:S(2)}, u32[]{:S(2)}) collective-permute-start(bf16[16,2048]{1,0:T(8,128)(2,1)S(1)} %select_convert_fusion.4), channel_id=1, source_target_pairs={{0,2},{1,3},{2,0},{3,1},{4,6},{5,7},{6,4},{7,5},{8,10},{9,11},{10,... | collective-permute-start | bytes 196616 | tf_op jit(solution)/shard_map/while/body/eval_jaxpr/ppermute | solution.py:17
  96.7 4.0 %collective-permute-start.3 = (bf16[8,2048]{1,0:T(8,128)(2,1)S(1)}, bf16[8,2048]{1,0:T(8,128)(2,1)S(1)}, u32[]{:S(2)}, u32[]{:S(2)}) collective-permute-start(bf16[8,2048]{1,0:T(8,128)(2,1)S(1)} %select_convert_fusion.5), channel_id=1, source_target_pairs={{0,1},{1,0},{2,3},{3,2},{4,5},{5,4},{6,7},{7,6},{8,9},{9,8},{10,11... | collective-permute-start | bytes 98312 | tf_op jit(solution)/shard_map/while/body/eval_jaxpr/ppermute | solution.py:17
  100.7 6.1 %collective-permute-start.4 = (bf16[8,2048]{1,0:T(8,128)(2,1)S(1)}, bf16[8,2048]{1,0:T(8,128)(2,1)S(1)}, u32[]{:S(2)}, u32[]{:S(2)}) collective-permute-start(bf16[8,2048]{1,0:T(8,128)(2,1)S(1)} %get-tuple-element.553), channel_id=1, source_target_pairs={{0,4},{4,8},{8,12},{1,5},{5,9},{9,13},{2,6},{6,10},{10,14},{3,7},{... | collective-permute-start | bytes 98312 | tf_op jit(solution)/shard_map/while/body/eval_jaxpr/ppermute | solution.py:23
  106.8 16.9 %copy-start = (bf16[512,2048]{1,0:T(8,128)(2,1)S(1)}, bf16[512,2048]{1,0:T(8,128)(2,1)}, u32[]{:S(2)}) copy-start(bf16[512,2048]{1,0:T(8,128)(2,1)} %get-tuple-element.610) | copy-start | bytes 6291460 | tf_op jit(solution)/shard_map/while
  108.1 4.4 %collective-permute-start = (bf16[8,2048]{1,0:T(8,128)(2,1)S(1)}, bf16[8,2048]{1,0:T(8,128)(2,1)S(1)}, u32[]{:S(2)}, u32[]{:S(2)}) collective-permute-start(bf16[8,2048]{1,0:T(8,128)(2,1)S(1)} %fusion.54), channel_id=1, source_target_pairs={{0,1},{1,0},{2,3},{3,2},{4,5},{5,4},{6,7},{7,6},{8,9},{9,8},{10,11... | collective-permute-start | bytes 98312 | tf_op jit(solution)/shard_map/while/body/eval_jaxpr/ppermute | solution.py:17
  112.6 5.2 %collective-permute-start.1 = (bf16[16,2048]{1,0:T(8,128)(2,1)S(1)}, bf16[16,2048]{1,0:T(8,128)(2,1)S(1)}, u32[]{:S(2)}, u32[]{:S(2)}) collective-permute-start(bf16[16,2048]{1,0:T(8,128)(2,1)S(1)} %maximum_select_fusion.6), channel_id=1, source_target_pairs={{0,2},{1,3},{2,0},{3,1},{4,6},{5,7},{6,4},{7,5},{8,10},{9,11},{10,... | collective-permute-start | bytes 196616 | tf_op jit(solution)/shard_map/while/body/eval_jaxpr/ppermute | solution.py:17
  124.2 6.6 %collective-permute-start.2 = (bf16[16,2048]{1,0:T(8,128)(2,1)S(1)}, bf16[16,2048]{1,0:T(8,128)(2,1)S(1)}, u32[]{:S(2)}, u32[]{:S(2)}) collective-permute-start(bf16[16,2048]{1,0:T(8,128)(2,1)S(1)} %select_convert_fusion.4), channel_id=1, source_target_pairs={{0,2},{1,3},{2,0},{3,1},{4,6},{5,7},{6,4},{7,5},{8,10},{9,11},{10,... | collective-permute-start | bytes 196616 | tf_op jit(solution)/shard_map/while/body/eval_jaxpr/ppermute | solution.py:17
  130.8 4.0 %collective-permute-start.3 = (bf16[8,2048]{1,0:T(8,128)(2,1)S(1)}, bf16[8,2048]{1,0:T(8,128)(2,1)S(1)}, u32[]{:S(2)}, u32[]{:S(2)}) collective-permute-start(bf16[8,2048]{1,0:T(8,128)(2,1)S(1)} %select_convert_fusion.5), channel_id=1, source_target_pairs={{0,1},{1,0},{2,3},{3,2},{4,5},{5,4},{6,7},{7,6},{8,9},{9,8},{10,11... | collective-permute-start | bytes 98312 | tf_op jit(solution)/shard_map/while/body/eval_jaxpr/ppermute | solution.py:17
  134.8 5.1 %collective-permute-start.4 = (bf16[8,2048]{1,0:T(8,128)(2,1)S(1)}, bf16[8,2048]{1,0:T(8,128)(2,1)S(1)}, u32[]{:S(2)}, u32[]{:S(2)}) collective-permute-start(bf16[8,2048]{1,0:T(8,128)(2,1)S(1)} %get-tuple-element.553), channel_id=1, source_target_pairs={{0,4},{4,8},{8,12},{1,5},{5,9},{9,13},{2,6},{6,10},{10,14},{3,7},{... | collective-permute-start | bytes 98312 | tf_op jit(solution)/shard_map/while/body/eval_jaxpr/ppermute | solution.py:23
  139.9 15.9 %copy-start = (bf16[512,2048]{1,0:T(8,128)(2,1)S(1)}, bf16[512,2048]{1,0:T(8,128)(2,1)}, u32[]{:S(2)}) copy-start(bf16[512,2048]{1,0:T(8,128)(2,1)} %get-tuple-element.610) | copy-start | bytes 6291460 | tf_op jit(solution)/shard_map/while
  141.3 4.0 %collective-permute-start = (bf16[8,2048]{1,0:T(8,128)(2,1)S(1)}, bf16[8,2048]{1,0:T(8,128)(2,1)S(1)}, u32[]{:S(2)}, u32[]{:S(2)}) collective-permute-start(bf16[8,2048]{1,0:T(8,128)(2,1)S(1)} %fusion.54), channel_id=1, source_target_pairs={{0,1},{1,0},{2,3},{3,2},{4,5},{5,4},{6,7},{7,6},{8,9},{9,8},{10,11... | collective-permute-start | bytes 98312 | tf_op jit(solution)/shard_map/while/body/eval_jaxpr/ppermute | solution.py:17
  145.3 5.2 %collective-permute-start.1 = (bf16[16,2048]{1,0:T(8,128)(2,1)S(1)}, bf16[16,2048]{1,0:T(8,128)(2,1)S(1)}, u32[]{:S(2)}, u32[]{:S(2)}) collective-permute-start(bf16[16,2048]{1,0:T(8,128)(2,1)S(1)} %maximum_select_fusion.6), channel_id=1, source_target_pairs={{0,2},{1,3},{2,0},{3,1},{4,6},{5,7},{6,4},{7,5},{8,10},{9,11},{10,... | collective-permute-start | bytes 196616 | tf_op jit(solution)/shard_map/while/body/eval_jaxpr/ppermute | solution.py:17
  156.3 5.2 %collective-permute-start.2 = (bf16[16,2048]{1,0:T(8,128)(2,1)S(1)}, bf16[16,2048]{1,0:T(8,128)(2,1)S(1)}, u32[]{:S(2)}, u32[]{:S(2)}) collective-permute-start(bf16[16,2048]{1,0:T(8,128)(2,1)S(1)} %select_convert_fusion.4), channel_id=1, source_target_pairs={{0,2},{1,3},{2,0},{3,1},{4,6},{5,7},{6,4},{7,5},{8,10},{9,11},{10,... | collective-permute-start | bytes 196616 | tf_op jit(solution)/shard_map/while/body/eval_jaxpr/ppermute | solution.py:17
  161.6 4.0 %collective-permute-start.3 = (bf16[8,2048]{1,0:T(8,128)(2,1)S(1)}, bf16[8,2048]{1,0:T(8,128)(2,1)S(1)}, u32[]{:S(2)}, u32[]{:S(2)}) collective-permute-start(bf16[8,2048]{1,0:T(8,128)(2,1)S(1)} %select_convert_fusion.5), channel_id=1, source_target_pairs={{0,1},{1,0},{2,3},{3,2},{4,5},{5,4},{6,7},{7,6},{8,9},{9,8},{10,11... | collective-permute-start | bytes 98312 | tf_op jit(solution)/shard_map/while/body/eval_jaxpr/ppermute | solution.py:17
  165.6 6.9 %collective-permute-start.4 = (bf16[8,2048]{1,0:T(8,128)(2,1)S(1)}, bf16[8,2048]{1,0:T(8,128)(2,1)S(1)}, u32[]{:S(2)}, u32[]{:S(2)}) collective-permute-start(bf16[8,2048]{1,0:T(8,128)(2,1)S(1)} %get-tuple-element.553), channel_id=1, source_target_pairs={{0,4},{4,8},{8,12},{1,5},{5,9},{9,13},{2,6},{6,10},{10,14},{3,7},{... | collective-permute-start | bytes 98312 | tf_op jit(solution)/shard_map/while/body/eval_jaxpr/ppermute | solution.py:23
  172.5 16.7 %copy-start = (bf16[512,2048]{1,0:T(8,128)(2,1)S(1)}, bf16[512,2048]{1,0:T(8,128)(2,1)}, u32[]{:S(2)}) copy-start(bf16[512,2048]{1,0:T(8,128)(2,1)} %get-tuple-element.610) | copy-start | bytes 6291460 | tf_op jit(solution)/shard_map/while
  173.8 4.0 %collective-permute-start = (bf16[8,2048]{1,0:T(8,128)(2,1)S(1)}, bf16[8,2048]{1,0:T(8,128)(2,1)S(1)}, u32[]{:S(2)}, u32[]{:S(2)}) collective-permute-start(bf16[8,2048]{1,0:T(8,128)(2,1)S(1)} %fusion.54), channel_id=1, source_target_pairs={{0,1},{1,0},{2,3},{3,2},{4,5},{5,4},{6,7},{7,6},{8,9},{9,8},{10,11... | collective-permute-start | bytes 98312 | tf_op jit(solution)/shard_map/while/body/eval_jaxpr/ppermute | solution.py:17
  177.8 6.0 %collective-permute-start.1 = (bf16[16,2048]{1,0:T(8,128)(2,1)S(1)}, bf16[16,2048]{1,0:T(8,128)(2,1)S(1)}, u32[]{:S(2)}, u32[]{:S(2)}) collective-permute-start(bf16[16,2048]{1,0:T(8,128)(2,1)S(1)} %maximum_select_fusion.6), channel_id=1, source_target_pairs={{0,2},{1,3},{2,0},{3,1},{4,6},{5,7},{6,4},{7,5},{8,10},{9,11},{10,... | collective-permute-start | bytes 196616 | tf_op jit(solution)/shard_map/while/body/eval_jaxpr/ppermute | solution.py:17
  189.7 6.5 %collective-permute-start.2 = (bf16[16,2048]{1,0:T(8,128)(2,1)S(1)}, bf16[16,2048]{1,0:T(8,128)(2,1)S(1)}, u32[]{:S(2)}, u32[]{:S(2)}) collective-permute-start(bf16[16,2048]{1,0:T(8,128)(2,1)S(1)} %select_convert_fusion.4), channel_id=1, source_target_pairs={{0,2},{1,3},{2,0},{3,1},{4,6},{5,7},{6,4},{7,5},{8,10},{9,11},{10,... | collective-permute-start | bytes 196616 | tf_op jit(solution)/shard_map/while/body/eval_jaxpr/ppermute | solution.py:17
  196.3 4.0 %collective-permute-start.3 = (bf16[8,2048]{1,0:T(8,128)(2,1)S(1)}, bf16[8,2048]{1,0:T(8,128)(2,1)S(1)}, u32[]{:S(2)}, u32[]{:S(2)}) collective-permute-start(bf16[8,2048]{1,0:T(8,128)(2,1)S(1)} %select_convert_fusion.5), channel_id=1, source_target_pairs={{0,1},{1,0},{2,3},{3,2},{4,5},{5,4},{6,7},{7,6},{8,9},{9,8},{10,11... | collective-permute-start | bytes 98312 | tf_op jit(solution)/shard_map/while/body/eval_jaxpr/ppermute | solution.py:17
  200.3 8.0 %collective-permute-start.4 = (bf16[8,2048]{1,0:T(8,128)(2,1)S(1)}, bf16[8,2048]{1,0:T(8,128)(2,1)S(1)}, u32[]{:S(2)}, u32[]{:S(2)}) collective-permute-start(bf16[8,2048]{1,0:T(8,128)(2,1)S(1)} %get-tuple-element.553), channel_id=1, source_target_pairs={{0,4},{4,8},{8,12},{1,5},{5,9},{9,13},{2,6},{6,10},{10,14},{3,7},{... | collective-permute-start | bytes 98312 | tf_op jit(solution)/shard_map/while/body/eval_jaxpr/ppermute | solution.py:23
  208.3 16.1 %copy-start = (bf16[512,2048]{1,0:T(8,128)(2,1)S(1)}, bf16[512,2048]{1,0:T(8,128)(2,1)}, u32[]{:S(2)}) copy-start(bf16[512,2048]{1,0:T(8,128)(2,1)} %get-tuple-element.610) | copy-start | bytes 6291460 | tf_op jit(solution)/shard_map/while
  209.6 4.0 %collective-permute-start = (bf16[8,2048]{1,0:T(8,128)(2,1)S(1)}, bf16[8,2048]{1,0:T(8,128)(2,1)S(1)}, u32[]{:S(2)}, u32[]{:S(2)}) collective-permute-start(bf16[8,2048]{1,0:T(8,128)(2,1)S(1)} %fusion.54), channel_id=1, source_target_pairs={{0,1},{1,0},{2,3},{3,2},{4,5},{5,4},{6,7},{7,6},{8,9},{9,8},{10,11... | collective-permute-start | bytes 98312 | tf_op jit(solution)/shard_map/while/body/eval_jaxpr/ppermute | solution.py:17
  213.6 5.4 %collective-permute-start.1 = (bf16[16,2048]{1,0:T(8,128)(2,1)S(1)}, bf16[16,2048]{1,0:T(8,128)(2,1)S(1)}, u32[]{:S(2)}, u32[]{:S(2)}) collective-permute-start(bf16[16,2048]{1,0:T(8,128)(2,1)S(1)} %maximum_select_fusion.6), channel_id=1, source_target_pairs={{0,2},{1,3},{2,0},{3,1},{4,6},{5,7},{6,4},{7,5},{8,10},{9,11},{10,... | collective-permute-start | bytes 196616 | tf_op jit(solution)/shard_map/while/body/eval_jaxpr/ppermute | solution.py:17
  224.8 5.4 %collective-permute-start.2 = (bf16[16,2048]{1,0:T(8,128)(2,1)S(1)}, bf16[16,2048]{1,0:T(8,128)(2,1)S(1)}, u32[]{:S(2)}, u32[]{:S(2)}) collective-permute-start(bf16[16,2048]{1,0:T(8,128)(2,1)S(1)} %select_convert_fusion.4), channel_id=1, source_target_pairs={{0,2},{1,3},{2,0},{3,1},{4,6},{5,7},{6,4},{7,5},{8,10},{9,11},{10,... | collective-permute-start | bytes 196616 | tf_op jit(solution)/shard_map/while/body/eval_jaxpr/ppermute | solution.py:17
  230.3 4.0 %collective-permute-start.3 = (bf16[8,2048]{1,0:T(8,128)(2,1)S(1)}, bf16[8,2048]{1,0:T(8,128)(2,1)S(1)}, u32[]{:S(2)}, u32[]{:S(2)}) collective-permute-start(bf16[8,2048]{1,0:T(8,128)(2,1)S(1)} %select_convert_fusion.5), channel_id=1, source_target_pairs={{0,1},{1,0},{2,3},{3,2},{4,5},{5,4},{6,7},{7,6},{8,9},{9,8},{10,11... | collective-permute-start | bytes 98312 | tf_op jit(solution)/shard_map/while/body/eval_jaxpr/ppermute | solution.py:17
  234.3 6.5 %collective-permute-start.4 = (bf16[8,2048]{1,0:T(8,128)(2,1)S(1)}, bf16[8,2048]{1,0:T(8,128)(2,1)S(1)}, u32[]{:S(2)}, u32[]{:S(2)}) collective-permute-start(bf16[8,2048]{1,0:T(8,128)(2,1)S(1)} %get-tuple-element.553), channel_id=1, source_target_pairs={{0,4},{4,8},{8,12},{1,5},{5,9},{9,13},{2,6},{6,10},{10,14},{3,7},{... | collective-permute-start | bytes 98312 | tf_op jit(solution)/shard_map/while/body/eval_jaxpr/ppermute | solution.py:23
  240.8 47.4 %copy-start.1 = (bf16[2,4,32,512]{3,2,1,0:T(8,128)(2,1)}, bf16[2,4,32,512]{3,2,1,0:T(8,128)(2,1)S(1)}, u32[]{:S(2)}) copy-start(bf16[2,4,32,512]{3,2,1,0:T(8,128)(2,1)S(1)} %get-tuple-element.391) | copy-start | bytes 786436
  240.8 1.3 collective-permute-start.5
Sparse Core Ops, SparseCore 0:
  243.0 43.8 all-reduce.1
where the time goes:
time: 296 us; the launch traced here: 295 us
  waiting for transfers between devices  136 us (46%)
  starting transfers between devices  87 us (29%)
  matrix products  32.5 us (11%)
  other arithmetic  16.2 us (5%)
  between operations  14 us (5%)
  local copies, waits for them, and re-layouts  8.08 us (3%)
    ppermute x29, waiting for transfers between devices, swapped(): lax.ppermute(value, axis, [(i, i ^ 1 << bit) for i in range(lax.axis_size...  81 us
    ppermute x29, starting transfers between devices, swapped(): lax.ppermute(value, axis, [(i, i ^ 1 << bit) for i in range(lax.axis_size...  55 us
    psum x1, waiting for transfers between devices, spread_2(): return lax.psum(jnp.where(mine, value, jnp.zeros_like(value)), axis)  44 us
    ppermute x7, starting transfers between devices, from_behind(): lax.ppermute(value, axis, [(source, source + steps) for source in range(i...  32 us
    dot_general x7, matrix products, tick(): jnp.dot(group_features, qkv_slice, preferred_element_type=jnp.float32)  27.6 us
    ppermute x7, waiting for transfers between devices, from_behind(): lax.ppermute(value, axis, [(source, source + steps) for source in range(i...  10.5 us
    reduce_sum x7, other arithmetic, layer_norm(): center = values - jnp.mean(values, axis=-1, keepdims=True)  7.25 us
  transfers between devices with their start and end apart: 37, of which 37 were waited for; matrix products, arithmetic and copies ran while one was open for 0% of the time, Pallas kernels for 0%

commit v1 on v0

v1 whole, which is shorter than its diff:
```python
import math

import jax
import jax.numpy as jnp
from jax import lax
from jax.sharding import PartitionSpec as P

GUIDANCE_SCALE = 6.0
EPSILON = 1e-06
GROUPS = 1


def swapped(value, axis, bit):
    return lax.ppermute(value, axis, [(i, i ^ 1 << bit) for i in range(lax.axis_size(axis))])


def from_behind(value, axis, steps):
    count = lax.axis_size(axis)
    return lax.ppermute(value, axis, [(i, i + steps) for i in range(count - steps)])


def layer_norm(values):
    center = values - jnp.mean(values, axis=-1, keepdims=True)
    spread = jnp.mean(center * center, axis=-1, keepdims=True)
    return center * lax.rsqrt(spread + EPSILON)


def head_norm(values, gain_row):
    return (
        values * lax.rsqrt(jnp.mean(values * values, axis=-1, keepdims=True) + EPSILON) * gain_row
    )


def join_pair(is_upper, mine, theirs, axis_dim):
    return jnp.where(
        is_upper,
        jnp.concatenate((theirs, mine), axis_dim),
        jnp.concatenate((mine, theirs), axis_dim),
    )


def local(latent, modulation, qkv_weight, out_weight, norm_gain, stale_kv):
    seq_count = lax.axis_size("seq")
    seq_rank = lax.axis_index("seq")
    section_count = lax.axis_size("pipe")
    section_rank = lax.axis_index("pipe")
    patches, tok_dev, model_width = latent.shape
    head_dim = norm_gain.shape[2]
    slice_count = min(seq_count, 8)
    member_count = seq_count // slice_count
    member_bits = member_count.bit_length() - 1
    own_member = seq_rank % member_count
    local_width = stale_kv.shape[7]
    local_heads = local_width // head_dim
    group_rows = slice_count * tok_dev
    divisor = math.sqrt(head_dim)
    shift_row = modulation[0, 0, 0]
    scale_row = modulation[0, 0, 1]
    gate_row = modulation[0, 0, 2]
    query_gain = norm_gain[0, 0]
    key_gain = norm_gain[0, 1]
    own_cache = stale_kv[0, 0].reshape(2, patches, group_rows, local_width)
    group_cache = own_cache[None]
    qkv_slice = qkv_weight[0]
    out_slice = out_weight[0]
    for level_index in range(member_bits):
        got_qkv, got_out, got_cache = (
            swapped(qkv_slice, "seq", level_index),
            swapped(out_slice, "seq", level_index),
            swapped(group_cache, "seq", level_index),
        )
        is_upper = own_member >> level_index & 1 == 1
        qkv_slice = join_pair(is_upper, qkv_slice, got_qkv, 1)
        out_slice = join_pair(is_upper, out_slice, got_out, 0)
        group_cache = join_pair(is_upper, group_cache, got_cache, 0)
    stale_rows = group_cache.swapaxes(0, 1).reshape(2, -1, local_width)
    peers = None
    if member_count > 1:
        peers = [
            [a + member_count * b for b in range(slice_count)] for a in range(member_count)
        ]

    def exchange(value):
        return lax.all_to_all(value, "seq", 0, 0, axis_index_groups=peers)

    size = patches // GROUPS
    ticks = GROUPS + section_count - 1
    stale_patch = jnp.tile(jnp.repeat(jnp.arange(patches), group_rows), member_count)
    stale_member = jnp.repeat(jnp.arange(member_count), patches * group_rows)
    row_patch = jnp.repeat(jnp.arange(size), group_rows)
    incoming = None
    fresh_ticks = []
    result_ticks = []
    for tick in range(ticks):
        group = tick - section_rank
        if incoming is None:
            hidden_in = latent[:size]
        elif tick < GROUPS:
            hidden_in = jnp.where(
                section_rank == 0, latent[tick * size : (tick + 1) * size], incoming
            )
        else:
            hidden_in = incoming
        normed = layer_norm(hidden_in.astype(jnp.float32))
        modulated = (normed * (1.0 + scale_row) + shift_row).astype(jnp.bfloat16)
        features = exchange(jnp.broadcast_to(modulated[None], (slice_count,) + modulated.shape))
        features = features.swapaxes(0, 1).reshape(size * group_rows, model_width)
        mixed = jnp.dot(features, qkv_slice, preferred_element_type=jnp.float32)
        mixed = mixed.reshape(size * group_rows, local_heads, 3, head_dim)
        queries = head_norm(mixed[:, :, 0], query_gain).astype(jnp.bfloat16)
        fresh = jnp.stack((head_norm(mixed[:, :, 1], key_gain), mixed[:, :, 2])).astype(
            jnp.bfloat16
        )
        fresh_ticks.append(fresh)
        query_patch = group * size + row_patch
        seen = fresh_ticks[-GROUPS:]
        masks = []
        for back in range(len(seen) - 1, -1, -1):
            key_patch = (group - back) * size + row_patch
            masks.append(
                jnp.logical_and(
                    key_patch[None, :] >= 0, key_patch[None, :] <= query_patch[:, None]
                )
            )
        masks.append(
            jnp.logical_or(
                stale_patch[None, :] > query_patch[:, None], stale_member[None, :] != own_member
            )
        )
        mask = jnp.concatenate(masks, axis=1)
        tables = [f.reshape(2, size * group_rows, local_heads, head_dim) for f in seen]
        tables.append(stale_rows.reshape(2, -1, local_heads, head_dim))
        view = jnp.concatenate(tables, axis=1)
        scores = (
            jnp.einsum("qhd,khd->hqk", queries, view[0], preferred_element_type=jnp.float32)
            / divisor
        )
        weights = jnp.where(mask[None], jnp.exp(scores), 0.0)
        weight_total = jnp.sum(weights, axis=-1)
        summed = jnp.einsum(
            "hqk,khd->qhd",
            weights.astype(jnp.bfloat16),
            view[1],
            preferred_element_type=jnp.float32,
        )
        attended = (
            (summed / weight_total.T[:, :, None])
            .astype(jnp.bfloat16)
            .reshape(size * group_rows, local_width)
        )
        partial_out = jnp.dot(attended, out_slice, preferred_element_type=jnp.float32)
        partial_out = partial_out.astype(jnp.bfloat16).reshape(
            size, slice_count, tok_dev, model_width
        )
        parts = exchange(partial_out.swapaxes(0, 1))
        projected = jnp.sum(parts.astype(jnp.float32), axis=0)
        hidden_out = (hidden_in.astype(jnp.float32) + gate_row * projected).astype(jnp.bfloat16)
        result_ticks.append(hidden_out)
        if tick < ticks - 1:
            incoming = from_behind(hidden_out, "pipe", 1)

    fresh_all = jnp.stack(fresh_ticks)
    next_cache = lax.dynamic_slice_in_dim(fresh_all, section_rank, GROUPS, 0)
    next_cache = next_cache.swapaxes(0, 1).reshape(stale_kv.shape)
    results = jnp.concatenate(result_ticks[section_count - 1 :], axis=0)
    per_section = patches // section_count
    half = model_width // 2
    results = results.reshape(section_count, per_section * tok_dev, 2, half)
    results = results.transpose(2, 0, 1, 3).reshape(2 * section_count, per_section * tok_dev, half)
    got = lax.all_to_all(results, ("cfg", "pipe"), 0, 0)
    got = got.reshape(2, section_count, per_section, tok_dev, half)[:, section_count - 1]
    got = got.astype(jnp.float32)
    guided = (got[1] + GUIDANCE_SCALE * (got[0] - got[1])).astype(jnp.bfloat16)
    return (guided, next_cache)


def solution(mesh):
    placed = (
        P(None, "seq", None),
        P("pipe", "cfg", None, None),
        P("pipe", None, "seq"),
        P("pipe", "seq", None),
        P("pipe", None, None),
        P("pipe", "cfg", None, None, "seq", None, None, None),
    )
    return jax.shard_map(
        local,
        mesh=mesh,
        in_specs=placed,
        out_specs=(P("pipe", "seq", "cfg"), P("pipe", "cfg", None, None, "seq", None, None, None)),
        check_vma=False,
    )
```

time: 296 us -> 205 us (0.69)
  waiting for transfers between devices: 136 us -> 45.9 us
  blocking collectives: 0 us -> 63.6 us
  starting transfers between devices: 87 us -> 36.6 us
  between operations: 14 us -> 1.33 us
  matrix products: 32.5 us -> 20.9 us
  local copies, waits for them, and re-layouts: 8.08 us -> 19.3 us
    ppermute x36 -> x3, waiting for transfers between devices: 91.5 us -> 7.49 us  [from_behind(): lax.ppermute(value, axis, [(i, i + steps) for i in range(count - steps)])]
    ppermute x36 -> x3, starting transfers between devices: 87 us -> 11.8 us  [from_behind(): lax.ppermute(value, axis, [(i, i + steps) for i in range(count - steps)])]
    all_to_all x0 -> x4, blocking collectives: none -> 63.6 us  [exchange(): return lax.all_to_all(value, 'seq', 0, 0, axis_index_groups=peers)]
    psum x1 -> x0, waiting for transfers between devices: 44 us -> none  [spread_2(): return lax.psum(jnp.where(mine, value, jnp.zeros_like(value)), axis)]
    all_to_all x0 -> x5, waiting for transfers between devices: none -> 38.5 us  [the longest x4 35.3 us: exchange(): return lax.all_to_all(value, 'seq', 0, 0, axis_index_groups=peers)]
    all_to_all x0 -> x5, starting transfers between devices: none -> 24.8 us  [the longest x4 18.9 us: exchange(): return lax.all_to_all(value, 'seq', 0, 0, axis_index_groups=peers)]
    dot_general x22 -> x16, matrix products: 32.5 us -> 20.9 us  [the longest x4 15.7 us: local(): mixed = jnp.dot(features, qkv_slice, preferred_element_type=jnp.float32)]
    unnamed x4 -> x47, local copies, waits for them, and re-layouts: 1.69 us -> 8.79 us
  transfers between devices with their start and end apart: 37 -> 8, of which waited for: 37 -> 8; matrix products, arithmetic and copies ran while one was open for 0% -> 9% of each run, Pallas kernels for 0% -> 0%
where the time goes in v1:
time: 205 us; the launch traced here: 203 us
  blocking collectives  63.6 us (31%)
  waiting for transfers between devices  45.9 us (22%)
  starting transfers between devices  36.6 us (18%)
  matrix products  20.9 us (10%)
  local copies, waits for them, and re-layouts  19.3 us (9%)
  other arithmetic  15.7 us (8%)
    all_to_all x4, blocking collectives, exchange(): return lax.all_to_all(value, 'seq', 0, 0, axis_index_groups=peers)  63.6 us
    all_to_all x4, waiting for transfers between devices, exchange(): return lax.all_to_all(value, 'seq', 0, 0, axis_index_groups=peers)  35.3 us
    all_to_all x4, starting transfers between devices, exchange(): return lax.all_to_all(value, 'seq', 0, 0, axis_index_groups=peers)  18.9 us
    dot_general x4, matrix products, local(): mixed = jnp.dot(features, qkv_slice, preferred_element_type=jnp.float32)  15.7 us
    ppermute x3, starting transfers between devices, from_behind(): lax.ppermute(value, axis, [(i, i + steps) for i in range(count - steps)])  11.8 us
    unnamed x47, local copies, waits for them, and re-layouts  8.79 us
    ppermute x3, waiting for transfers between devices, from_behind(): lax.ppermute(value, axis, [(i, i + steps) for i in range(count - steps)])  7.49 us
    all_to_all x1, starting transfers between devices, local(): got = lax.all_to_all(results, ('cfg', 'pipe'), 0, 0)  5.91 us
  transfers between devices with their start and end apart: 8, of which 8 were waited for; matrix products, arithmetic and copies ran while one was open for 9% of the time, Pallas kernels for 0%

profile of v1, /device:TPU:0, one launch (start us, length us, event | category | flops | bytes accessed | tf_op | source)
XLA Modules:
  0.0 203.3 jit_solution(8842288129252295213)
XLA Ops:
  0.6 1.2 convert_reduce_fusion.7
  1.8 1.1 fusion.46
  2.9 0.7 fusion.94
  3.7 1.0 fusion.49
  4.7 0.9 broadcast_in_dim.54
  5.5 6.3 %all-to-all-start = ((bf16[4,4,8,2048]{3,2,1,0:T(8,128)(2,1)}), bf16[4,4,8,2048]{3,2,1,0:T(8,128)(2,1)S(1)}, u32[]{:S(2)}, u32[]{:S(2)}) async-start(bf16[4,4,8,2048]{3,2,1,0:T(8,128)(2,1)} %broadcast_in_dim.54), calls=%async_computation | async-start | bytes 1048576 | tf_op jit(solution)/shard_map/all_to_all | solution.py:84
  12.0 1.0 reshape_reshape_transpose_broadcast_in_dim_reshape_squeeze.2
  13.2 8.7 %copy.59 = bf16[1,2048,1536]{1,2,0:T(8,128)(2,1)} copy(bf16[1,2048,1536]{2,1,0:T(8,128)(2,1)} %param.8) | data formatting | bytes 12582912 | tf_op args[2]
  21.9 0.7 compare_and_fusion
  22.7 3.7 %all-to-all-done = bf16[4,4,8,2048]{3,2,1,0:T(8,128)(2,1)S(1)} async-done(((bf16[4,4,8,2048]{3,2,1,0:T(8,128)(2,1)}), bf16[4,4,8,2048]{3,2,1,0:T(8,128)(2,1)S(1)}, u32[]{:S(2)}, u32[]{:S(2)}) %all-to-all-start) | async-done | bytes 524320 | tf_op jit(solution)/shard_map/all_to_all | solution.py:84
  26.4 4.6 %fusion.99 = f32[128,4,3,128]{0,3,2,1:T(8,128)S(1)} fusion(bf16[128,2048,1,1]{1,0,3,2:T(8,128)(2,1)S(1)} %bitcast.267, bf16[4,3,128,2048]{3,2,1,0:T(8,128)(2,1)} %bitcast.251), kind=kOutput, calls=%fused_computation.217 | convolution fusion | flops 805306368 | bytes 7602176 | tf_op jit(solution)/shard_map/dot_general | solution.py:108
  32.6 16.5 %all_to_all.45 = bf16[4,4,8,2048]{3,2,1,0:T(8,128)(2,1)S(1)} all-to-all(bf16[4,4,8,2048]{3,2,1,0:T(8,128)(2,1)S(1)} %bitcast.259), channel_id=1, replica_groups=mesh['cfg'=2,'pipe'=4,'seq'=4] {'seq'}, dimensions={0} | all-to-all | bytes 1048576 | tf_op jit(solution)/shard_map/all_to_all | solution.py:84
  49.2 3.4 %collective-permute-start = (bf16[4,8,2048]{2,1,0:T(8,128)(2,1)S(1)}, bf16[4,8,2048]{2,1,0:T(8,128)(2,1)S(1)}, u32[]{:S(2)}, u32[]{:S(2)}) collective-permute-start(bf16[4,8,2048]{2,1,0:T(8,128)(2,1)S(1)} %fusion.50), channel_id=1, source_target_pairs={{0,4},{4,8},{8,12},{1,5},{5,9},{9,13},{2,6},{6,10},{10,14},{3,7},{... | collective-permute-start | bytes 393224 | tf_op jit(solution)/shard_map/ppermute | solution.py:19
  52.7 2.5 %collective-permute-done = bf16[4,8,2048]{2,1,0:T(8,128)(2,1)S(1)} collective-permute-done((bf16[4,8,2048]{2,1,0:T(8,128)(2,1)S(1)}, bf16[4,8,2048]{2,1,0:T(8,128)(2,1)S(1)}, u32[]{:S(2)}, u32[]{:S(2)}) %collective-permute-start) | collective-permute-done | bytes 131104 | tf_op jit(solution)/shard_map/ppermute | solution.py:19
  55.6 15.7 %all_to_all.46 = bf16[4,4,8,2048]{3,2,1,0:T(8,128)(2,1)S(1)} all-to-all(bf16[4,4,8,2048]{3,2,1,0:T(8,128)(2,1)S(1)} %broadcast_in_dim.58), channel_id=1, replica_groups=mesh['cfg'=2,'pipe'=4,'seq'=4] {'seq'}, dimensions={0} | all-to-all | bytes 1048576 | tf_op jit(solution)/shard_map/all_to_all | solution.py:84
  71.4 1.8 fusion.4
  74.8 15.9 %all_to_all.47 = bf16[4,4,8,2048]{3,2,1,0:T(8,128)(2,1)S(1)} all-to-all(bf16[4,4,8,2048]{3,2,1,0:T(8,128)(2,1)S(1)} %bitcast.261), channel_id=1, replica_groups=mesh['cfg'=2,'pipe'=4,'seq'=4] {'seq'}, dimensions={0} | all-to-all | bytes 1048576 | tf_op jit(solution)/shard_map/all_to_all | solution.py:84
  90.9 4.0 %collective-permute-start.1 = (bf16[4,8,2048]{2,1,0:T(8,128)(2,1)S(1)}, bf16[4,8,2048]{2,1,0:T(8,128)(2,1)S(1)}, u32[]{:S(2)}, u32[]{:S(2)}) collective-permute-start(bf16[4,8,2048]{2,1,0:T(8,128)(2,1)S(1)} %fusion.51), channel_id=1, source_target_pairs={{0,4},{4,8},{8,12},{1,5},{5,9},{9,13},{2,6},{6,10},{10,14},{3,7},{... | collective-permute-start | bytes 393224 | tf_op jit(solution)/shard_map/ppermute | solution.py:19
  94.9 2.5 %collective-permute-done.1 = bf16[4,8,2048]{2,1,0:T(8,128)(2,1)S(1)} collective-permute-done((bf16[4,8,2048]{2,1,0:T(8,128)(2,1)S(1)}, bf16[4,8,2048]{2,1,0:T(8,128)(2,1)S(1)}, u32[]{:S(2)}, u32[]{:S(2)}) %collective-permute-start.1) | collective-permute-done | bytes 131104 | tf_op jit(solution)/shard_map/ppermute | solution.py:19
  97.9 0.8 broadcast_in_dim.60
  98.7 4.1 %all-to-all-start.4 = ((bf16[4,4,8,2048]{3,2,1,0:T(8,128)(2,1)}), bf16[4,4,8,2048]{3,2,1,0:T(8,128)(2,1)}, u32[]{:S(2)}, u32[]{:S(2)}) async-start(bf16[4,4,8,2048]{3,2,1,0:T(8,128)(2,1)} %broadcast_in_dim.60), calls=%async_computation.4 | async-start | bytes 1048576 | tf_op jit(solution)/shard_map/all_to_all | solution.py:84
  102.8 1.4 pad_add_fusion.2
  104.3 11.3 %all-to-all-done.4 = bf16[4,4,8,2048]{3,2,1,0:T(8,128)(2,1)} async-done(((bf16[4,4,8,2048]{3,2,1,0:T(8,128)(2,1)}), bf16[4,4,8,2048]{3,2,1,0:T(8,128)(2,1)}, u32[]{:S(2)}, u32[]{:S(2)}) %all-to-all-start.4) | async-done | bytes 524320 | tf_op jit(solution)/shard_map/all_to_all | solution.py:84
  115.6 1.1 copy.73
  116.7 4.6 %fusion.2 = f32[128,4,3,128]{0,3,1,2:T(8,128)S(1)} fusion(bf16[128,2048,1,1]{1,0,2,3:T(8,128)(2,1)S(1)} %bitcast.270, bf16[4,3,128,2048]{3,2,1,0:T(8,128)(2,1)} %bitcast.252), kind=kOutput, calls=%fused_computation.2 | convolution fusion | flops 805306368 | bytes 7602176 | tf_op jit(solution)/shard_map/dot_general | solution.py:108
  121.4 0.8 fusion.86
  123.6 15.5 %all_to_all.48 = bf16[4,4,8,2048]{3,2,1,0:T(8,128)(2,1)S(1)} all-to-all(bf16[4,4,8,2048]{3,2,1,0:T(8,128)(2,1)S(1)} %bitcast.262), channel_id=1, replica_groups=mesh['cfg'=2,'pipe'=4,'seq'=4] {'seq'}, dimensions={0} | all-to-all | bytes 1048576 | tf_op jit(solution)/shard_map/all_to_all | solution.py:84
  139.3 4.3 %collective-permute-start.2 = (bf16[4,8,2048]{2,1,0:T(8,128)(2,1)S(1)}, bf16[4,8,2048]{2,1,0:T(8,128)(2,1)S(1)}, u32[]{:S(2)}, u32[]{:S(2)}) collective-permute-start(bf16[4,8,2048]{2,1,0:T(8,128)(2,1)S(1)} %fusion.52), channel_id=1, source_target_pairs={{0,4},{4,8},{8,12},{1,5},{5,9},{9,13},{2,6},{6,10},{10,14},{3,7},{... | collective-permute-start | bytes 393224 | tf_op jit(solution)/shard_map/ppermute | solution.py:19
  143.6 2.5 %collective-permute-done.2 = bf16[4,8,2048]{2,1,0:T(8,128)(2,1)S(1)} collective-permute-done((bf16[4,8,2048]{2,1,0:T(8,128)(2,1)S(1)}, bf16[4,8,2048]{2,1,0:T(8,128)(2,1)S(1)}, u32[]{:S(2)}, u32[]{:S(2)}) %collective-permute-start.2) | collective-permute-done | bytes 131104 | tf_op jit(solution)/shard_map/ppermute | solution.py:19
  146.5 0.9 broadcast_in_dim.62
  147.4 4.3 %all-to-all-start.6 = ((bf16[4,4,8,2048]{3,2,1,0:T(8,128)(2,1)}), bf16[4,4,8,2048]{3,2,1,0:T(8,128)(2,1)}, u32[]{:S(2)}, u32[]{:S(2)}) async-start(bf16[4,4,8,2048]{3,2,1,0:T(8,128)(2,1)} %broadcast_in_dim.62), calls=%async_computation.6 | async-start | bytes 1048576 | tf_op jit(solution)/shard_map/all_to_all | solution.py:84
  151.7 12.6 %all-to-all-done.6 = bf16[4,4,8,2048]{3,2,1,0:T(8,128)(2,1)} async-done(((bf16[4,4,8,2048]{3,2,1,0:T(8,128)(2,1)}), bf16[4,4,8,2048]{3,2,1,0:T(8,128)(2,1)}, u32[]{:S(2)}, u32[]{:S(2)}) %all-to-all-start.6) | async-done | bytes 524320 | tf_op jit(solution)/shard_map/all_to_all | solution.py:84
  164.3 1.1 copy.81
  165.4 4.6 %fusion = f32[128,4,3,128]{0,3,1,2:T(8,128)S(1)} fusion(bf16[128,2048,1,1]{1,0,2,3:T(8,128)(2,1)S(1)} %bitcast.268, bf16[4,3,128,2048]{3,2,1,0:T(8,128)(2,1)} %bitcast.253), kind=kOutput, calls=%fused_computation | convolution fusion | flops 805306368 | bytes 7602176 | tf_op jit(solution)/shard_map/dot_general | solution.py:108
  170.1 0.8 fusion.88
  171.1 1.1 fusion.98
  172.9 0.9 copy.116
  173.8 4.1 %all-to-all-start.7 = ((bf16[4,4,8,2048]{3,2,1,0:T(8,128)(2,1)}), bf16[4,4,8,2048]{3,2,1,0:T(8,128)(2,1)}, u32[]{:S(2)}, u32[]{:S(2)}) async-start(bf16[4,4,8,2048]{3,2,1,0:T(8,128)(2,1)} %bitcast.258), calls=%async_computation.7 | async-start | bytes 1048576 | tf_op jit(solution)/shard_map/all_to_all | solution.py:84
  178.0 0.7 fusion.116
  178.7 1.0 fusion.115
  179.8 1.1 fusion.114
  180.8 1.0 fusion.113
  181.9 7.7 %all-to-all-done.7 = bf16[4,4,8,2048]{3,2,1,0:T(8,128)(2,1)} async-done(((bf16[4,4,8,2048]{3,2,1,0:T(8,128)(2,1)}), bf16[4,4,8,2048]{3,2,1,0:T(8,128)(2,1)}, u32[]{:S(2)}, u32[]{:S(2)}) %all-to-all-start.7) | async-done | bytes 524320 | tf_op jit(solution)/shard_map/all_to_all | solution.py:84
  189.6 1.1 convert_reduce_fusion
  191.4 5.9 %all-to-all-start.8 = ((bf16[8,8,1024]{2,1,0:T(8,128)(2,1)}), bf16[8,8,1024]{2,1,0:T(8,128)(2,1)S(1)}, u32[]{:S(2)}, u32[]{:S(2)}) async-start(bf16[8,8,1024]{2,1,0:T(8,128)(2,1)} %bitcast.66), calls=%async_computation.8 | async-start | bytes 262144 | tf_op jit(solution)/shard_map/all_to_all | solution.py:170
  197.4 1.2 fusion.57
  198.7 0.8 reshape_transpose.3
  199.5 3.2 %all-to-all-done.8 = bf16[8,8,1024]{2,1,0:T(8,128)(2,1)S(1)} async-done(((bf16[8,8,1024]{2,1,0:T(8,128)(2,1)}), bf16[8,8,1024]{2,1,0:T(8,128)(2,1)S(1)}, u32[]{:S(2)}, u32[]{:S(2)}) %all-to-all-start.8) | async-done | bytes 131104 | tf_op jit(solution)/shard_map/all_to_all | solution.py:170
  (124 shorter events, 9.0 us)
Async XLA Ops:
  0.6 31.4 %copy-start = (bf16[1,512,2048]{2,1,0:T(8,128)(2,1)S(1)}, bf16[1,512,2048]{2,1,0:T(8,128)(2,1)}, u32[]{:S(2)}) copy-start(bf16[1,512,2048]{2,1,0:T(8,128)(2,1)} %param.9) | copy-start | bytes 6291460
  3.7 51.8 %copy-start.5 = (f32[1,1,1,2048]{3,1,2,0:T(1,128)}, f32[1,1,1,2048]{3,1,2,0:T(1,128)S(1)}, u32[]{:S(2)}) copy-start(f32[1,1,1,2048]{3,1,2,0:T(1,128)S(1)} %get-tuple-element.24) | copy-start | bytes 24580
  5.5 20.8 %all-to-all-start = ((bf16[4,4,8,2048]{3,2,1,0:T(8,128)(2,1)}), bf16[4,4,8,2048]{3,2,1,0:T(8,128)(2,1)S(1)}, u32[]{:S(2)}, u32[]{:S(2)}) async-start(bf16[4,4,8,2048]{3,2,1,0:T(8,128)(2,1)} %broadcast_in_dim.54), calls=%async_computation | async-start | bytes 1048576 | tf_op jit(solution)/shard_map/all_to_all | solution.py:84
  13.2 9.5 %copy-start.18 = (f32[1,2,128]{2,1,0:T(2,128)S(1)}, f32[1,2,128]{2,1,0:T(2,128)}, u32[]{:S(2)}) copy-start(f32[1,2,128]{2,1,0:T(2,128)} %param.10) | copy-start | bytes 3076
  22.7 50.7 %copy-start.8 = (f32[128]{0:T(128)}, f32[128]{0:T(128)S(1)}, u32[]{:S(2)}) copy-start(f32[128]{0:T(128)S(1)} %get-tuple-element.26) | copy-start | bytes 1540
  22.7 50.9 %copy-start.19 = (f32[128]{0:T(128)}, f32[128]{0:T(128)S(1)}, u32[]{:S(2)}) copy-start(f32[128]{0:T(128)S(1)} %get-tuple-element.25) | copy-start | bytes 1540
  31.0 18.2 %copy-start.1 = (bf16[4,8,2048]{2,1,0:T(8,128)(2,1)S(1)}, bf16[4,8,2048]{2,1,0:T(8,128)(2,1)}, u32[]{:S(2)}) copy-start(bf16[4,8,2048]{2,1,0:T(8,128)(2,1)} %param.6) | copy-start | bytes 393220
  31.2 40.2 %copy-start.13 = (f32[128,4]{0,1:T(4,128)}, f32[128,4]{0,1:T(4,128)S(1)}, u32[]{:S(2)}) copy-start(f32[128,4]{0,1:T(4,128)S(1)} %add_rsqrt_fusion.10) | copy-start | bytes 6148
  31.2 40.2 %slice-start = ((s8[6291456]{0:T(1024)(128)(4,1)}), s8[4194304]{0:T(1024)(128)(4,1)S(1)}, s32[]{:S(2)}) async-start(s8[6291456]{0:T(1024)(128)(4,1)} %bitcast.254), calls=%async_computation.9 | async-start | bytes 8388608
  32.0 39.3 %slice-start.1 = ((s8[6291456]{0:T(1024)(128)(4,1)}), s8[2097152]{0:T(1024)(128)(4,1)S(1)}, s32[]{:S(2)}) async-start(s8[6291456]{0:T(1024)(128)(4,1)} %bitcast.254), calls=%async_computation.10 | async-start | bytes 4194304
  49.2 5.9 %collective-permute-start = (bf16[4,8,2048]{2,1,0:T(8,128)(2,1)S(1)}, bf16[4,8,2048]{2,1,0:T(8,128)(2,1)S(1)}, u32[]{:S(2)}, u32[]{:S(2)}) collective-permute-start(bf16[4,8,2048]{2,1,0:T(8,128)(2,1)S(1)} %fusion.50), channel_id=1, source_target_pairs={{0,4},{4,8},{8,12},{1,5},{5,9},{9,13},{2,6},{6,10},{10,14},{3,7},{... | collective-permute-start | bytes 393224 | tf_op jit(solution)/shard_map/ppermute | solution.py:19
  73.2 24.2 %copy-start.2 = (f32[128,4,3,128]{0,3,1,2:T(8,128)}, f32[128,4,3,128]{0,3,1,2:T(8,128)S(1)}, u32[]{:S(2)}) copy-start(f32[128,4,3,128]{0,3,1,2:T(8,128)S(1)} %fusion.4) | copy-start | bytes 2359300
  73.2 24.5 %copy-start.6 = (f32[1,1,1,2048]{3,1,2,0:T(1,128)S(1)}, f32[1,1,1,2048]{3,1,2,0:T(1,128)}, u32[]{:S(2)}) copy-start(f32[1,1,1,2048]{3,1,2,0:T(1,128)} %copy-done.5) | copy-start | bytes 24580
  73.4 17.4 %copy-start.15 = (f32[128,4]{0,1:T(4,128)}, f32[128,4]{0,1:T(4,128)S(1)}, u32[]{:S(2)}) copy-start(f32[128,4]{0,1:T(4,128)S(1)} %add_rsqrt_fusion.7) | copy-start | bytes 6148
  90.9 6.6 %collective-permute-start.1 = (bf16[4,8,2048]{2,1,0:T(8,128)(2,1)S(1)}, bf16[4,8,2048]{2,1,0:T(8,128)(2,1)S(1)}, u32[]{:S(2)}, u32[]{:S(2)}) collective-permute-start(bf16[4,8,2048]{2,1,0:T(8,128)(2,1)S(1)} %fusion.51), channel_id=1, source_target_pairs={{0,4},{4,8},{8,12},{1,5},{5,9},{9,13},{2,6},{6,10},{10,14},{3,7},{... | collective-permute-start | bytes 393224 | tf_op jit(solution)/shard_map/ppermute | solution.py:19
  98.7 16.9 %all-to-all-start.4 = ((bf16[4,4,8,2048]{3,2,1,0:T(8,128)(2,1)}), bf16[4,4,8,2048]{3,2,1,0:T(8,128)(2,1)}, u32[]{:S(2)}, u32[]{:S(2)}) async-start(bf16[4,4,8,2048]{3,2,1,0:T(8,128)(2,1)} %broadcast_in_dim.60), calls=%async_computation.4 | async-start | bytes 1048576 | tf_op jit(solution)/shard_map/all_to_all | solution.py:84
  115.6 6.7 %copy-start.9 = (f32[128]{0:T(128)S(1)}, f32[128]{0:T(128)}, u32[]{:S(2)}) copy-start(f32[128]{0:T(128)} %copy-done.8) | copy-start | bytes 1540
  115.6 6.8 %copy-start.12 = (pred[128,256]{1,0:T(8,128)(4,1)S(1)}, pred[128,256]{1,0:T(8,128)(4,1)}, u32[]{:S(2)}) copy-start(pred[128,256]{1,0:T(8,128)(4,1)} %get-tuple-element.51) | copy-start | bytes 98308
  115.6 6.8 %copy-start.20 = (f32[128]{0:T(128)S(1)}, f32[128]{0:T(128)}, u32[]{:S(2)}) copy-start(f32[128]{0:T(128)} %copy-done.19) | copy-start | bytes 1540
  121.3 24.8 %copy-start.3 = (f32[128,4,3,128]{0,3,1,2:T(8,128)}, f32[128,4,3,128]{0,3,1,2:T(8,128)S(1)}, u32[]{:S(2)}) copy-start(f32[128,4,3,128]{0,3,1,2:T(8,128)S(1)} %fusion.2) | copy-start | bytes 2359300
  121.3 25.1 %copy-start.7 = (f32[1,1,1,2048]{3,1,2,0:T(1,128)S(1)}, f32[1,1,1,2048]{3,1,2,0:T(1,128)}, u32[]{:S(2)}) copy-start(f32[1,1,1,2048]{3,1,2,0:T(1,128)} %copy-done.5) | copy-start | bytes 24580
  122.2 24.3 %copy-start.16 = (f32[128,4]{0,1:T(4,128)}, f32[128,4]{0,1:T(4,128)S(1)}, u32[]{:S(2)}) copy-start(f32[128,4]{0,1:T(4,128)S(1)} %add_rsqrt_fusion.4) | copy-start | bytes 6148
  139.3 6.8 %collective-permute-start.2 = (bf16[4,8,2048]{2,1,0:T(8,128)(2,1)S(1)}, bf16[4,8,2048]{2,1,0:T(8,128)(2,1)S(1)}, u32[]{:S(2)}, u32[]{:S(2)}) collective-permute-start(bf16[4,8,2048]{2,1,0:T(8,128)(2,1)S(1)} %fusion.52), channel_id=1, source_target_pairs={{0,4},{4,8},{8,12},{1,5},{5,9},{9,13},{2,6},{6,10},{10,14},{3,7},{... | collective-permute-start | bytes 393224 | tf_op jit(solution)/shard_map/ppermute | solution.py:19
  146.5 24.4 %copy-start.10 = (f32[128]{0:T(128)S(1)}, f32[128]{0:T(128)}, u32[]{:S(2)}) copy-start(f32[128]{0:T(128)} %copy-done.8) | copy-start | bytes 1540
  147.4 16.9 %all-to-all-start.6 = ((bf16[4,4,8,2048]{3,2,1,0:T(8,128)(2,1)}), bf16[4,4,8,2048]{3,2,1,0:T(8,128)(2,1)}, u32[]{:S(2)}, u32[]{:S(2)}) async-start(bf16[4,4,8,2048]{3,2,1,0:T(8,128)(2,1)} %broadcast_in_dim.62), calls=%async_computation.6 | async-start | bytes 1048576 | tf_op jit(solution)/shard_map/all_to_all | solution.py:84
  164.3 6.8 %copy-start.11 = (pred[128,256]{1,0:T(8,128)(4,1)S(1)}, pred[128,256]{1,0:T(8,128)(4,1)}, u32[]{:S(2)}) copy-start(pred[128,256]{1,0:T(8,128)(4,1)} %get-tuple-element.52) | copy-start | bytes 98308
  170.0 3.8 %copy-start.4 = (f32[128,4,3,128]{0,3,1,2:T(8,128)}, f32[128,4,3,128]{0,3,1,2:T(8,128)S(1)}, u32[]{:S(2)}) copy-start(f32[128,4,3,128]{0,3,1,2:T(8,128)S(1)} %fusion) | copy-start | bytes 2359300
  170.0 7.9 %copy-start.14 = (f32[128,4]{0,1:T(4,128)S(1)}, f32[128,4]{0,1:T(4,128)}, u32[]{:S(2)}) copy-start(f32[128,4]{0,1:T(4,128)} %copy-done.13) | copy-start | bytes 6148
  170.9 2.9 %copy-start.17 = (f32[128,4]{0,1:T(4,128)}, f32[128,4]{0,1:T(4,128)S(1)}, u32[]{:S(2)}) copy-start(f32[128,4]{0,1:T(4,128)S(1)} %add_rsqrt_fusion.1) | copy-start | bytes 6148
  173.8 15.8 %all-to-all-start.7 = ((bf16[4,4,8,2048]{3,2,1,0:T(8,128)(2,1)}), bf16[4,4,8,2048]{3,2,1,0:T(8,128)(2,1)}, u32[]{:S(2)}, u32[]{:S(2)}) async-start(bf16[4,4,8,2048]{3,2,1,0:T(8,128)(2,1)} %bitcast.258), calls=%async_computation.7 | async-start | bytes 1048576 | tf_op jit(solution)/shard_map/all_to_all | solution.py:84
  191.4 11.3 %all-to-all-start.8 = ((bf16[8,8,1024]{2,1,0:T(8,128)(2,1)}), bf16[8,8,1024]{2,1,0:T(8,128)(2,1)S(1)}, u32[]{:S(2)}, u32[]{:S(2)}) async-start(bf16[8,8,1024]{2,1,0:T(8,128)(2,1)} %bitcast.66), calls=%async_computation.8 | async-start | bytes 262144 | tf_op jit(solution)/shard_map/all_to_all | solution.py:170

commit v2 on v1

--- a/solution.py
+++ b/solution.py
@@ -80,9 +80,6 @@
             [a + member_count * b for b in range(slice_count)] for a in range(member_count)
         ]
 
-    def exchange(value):
-        return lax.all_to_all(value, "seq", 0, 0, axis_index_groups=peers)
-
     size = patches // GROUPS
     ticks = GROUPS + section_count - 1
     stale_patch = jnp.tile(jnp.repeat(jnp.arange(patches), group_rows), member_count)
@@ -103,7 +100,7 @@
             hidden_in = incoming
         normed = layer_norm(hidden_in.astype(jnp.float32))
         modulated = (normed * (1.0 + scale_row) + shift_row).astype(jnp.bfloat16)
-        features = exchange(jnp.broadcast_to(modulated[None], (slice_count,) + modulated.shape))
+        features = lax.all_gather(modulated, "seq", axis_index_groups=peers)
         features = features.swapaxes(0, 1).reshape(size * group_rows, model_width)
         mixed = jnp.dot(features, qkv_slice, preferred_element_type=jnp.float32)
         mixed = mixed.reshape(size * group_rows, local_heads, 3, head_dim)
@@ -152,8 +149,9 @@
         partial_out = partial_out.astype(jnp.bfloat16).reshape(
             size, slice_count, tok_dev, model_width
         )
-        parts = exchange(partial_out.swapaxes(0, 1))
-        projected = jnp.sum(parts.astype(jnp.float32), axis=0)
+        projected = lax.psum_scatter(
+            partial_out.swapaxes(0, 1), "seq", axis_index_groups=peers
+        ).astype(jnp.float32)
         hidden_out = (hidden_in.astype(jnp.float32) + gate_row * projected).astype(jnp.bfloat16)
         result_ticks.append(hidden_out)
         if tick < ticks - 1:

time: 205 us -> 254 us (1.24)
  waiting for transfers between devices: 45.9 us -> 95.8 us
  starting transfers between devices: 36.6 us -> 13.7 us
  between operations: 1.33 us -> 14.3 us
  other arithmetic: 15.7 us -> 24.4 us
  matrix products: 20.9 us -> 24 us
    reduce_scatter x0 -> x4, waiting for transfers between devices: none -> 85.6 us  [local(): lax.psum_scatter(partial_out.swapaxes(0, 1), 'seq', axis_index_groups=peers)]
    all_to_all x4 -> x0, blocking collectives: 63.6 us -> none  [exchange(): return lax.all_to_all(value, 'seq', 0, 0, axis_index_groups=peers)]
    all_gather x0 -> x4, blocking collectives: none -> 62.5 us  [local(): features = lax.all_gather(modulated, 'seq', axis_index_groups=peers)]
    all_to_all x4 -> x0, waiting for transfers between devices: 35.3 us -> none  [exchange(): return lax.all_to_all(value, 'seq', 0, 0, axis_index_groups=peers)]
    all_to_all x4 -> x0, starting transfers between devices: 18.9 us -> none  [exchange(): return lax.all_to_all(value, 'seq', 0, 0, axis_index_groups=peers)]
    convert_element_type x4, other arithmetic: 0.17 us -> 3.78 us  [local(): (hidden_in.astype(jnp.float32) + gate_row * projected).astype(jnp.bfloat16)]
    dot_general x4, matrix products: 15.7 us -> 18.7 us  [local(): mixed = jnp.dot(features, qkv_slice, preferred_element_type=jnp.float32)]
    broadcast_in_dim x4 -> x0, local copies, waits for them, and re-layouts: 2.65 us -> none  [local(): jnp.broadcast_to(modulated[None], (slice_count,) + modulated.shape)]
  transfers between devices with their start and end apart: 8 -> 8, of which waited for: 8 -> 8; matrix products, arithmetic and copies ran while one was open for 9% -> 2% of each run, Pallas kernels for 0% -> 0%
where the time goes in v2:
time: 254 us; the launch traced here: 253 us
  waiting for transfers between devices  95.8 us (38%)
  blocking collectives  62.5 us (25%)
  other arithmetic  24.4 us (10%)
  matrix products  24 us (9%)
  local copies, waits for them, and re-layouts  18.6 us (7%)
  between operations  14.3 us (6%)
  starting transfers between devices  13.7 us (5%)
    reduce_scatter x4, waiting for transfers between devices, local(): lax.psum_scatter(partial_out.swapaxes(0, 1), 'seq', axis_index_groups=peers)  85.6 us
    all_gather x4, blocking collectives, local(): features = lax.all_gather(modulated, 'seq', axis_index_groups=peers)  62.5 us
    dot_general x4, matrix products, local(): mixed = jnp.dot(features, qkv_slice, preferred_element_type=jnp.float32)  18.7 us
    ppermute x3, starting transfers between devices, from_behind(): lax.ppermute(value, axis, [(i, i + steps) for i in range(count - steps)])  10 us
    unnamed x49, local copies, waits for them, and re-layouts  8.78 us
    ppermute x3, waiting for transfers between devices, from_behind(): lax.ppermute(value, axis, [(i, i + steps) for i in range(count - steps)])  6.09 us
  transfers between devices with their start and end apart: 8, of which 8 were waited for; matrix products, arithmetic and copies ran while one was open for 2% of the time, Pallas kernels for 0%

profile of v2, /device:TPU:0, one launch (start us, length us, event | category | flops | bytes accessed | tf_op | source)
XLA Modules:
  0.0 253.3 jit_solution(12319992401440818629)
XLA Ops:
  7.2 1.1 convert_reduce_fusion.3
  8.4 1.1 fusion.46
  9.5 0.7 fusion.94
  10.2 1.0 fusion.49
  11.3 17.4 %all-gather = bf16[16,8,2048]{2,1,0:T(8,128)(2,1)S(1)} all-gather(bf16[4,8,2048]{2,1,0:T(8,128)(2,1)S(1)} %fusion.49), channel_id=2, replica_groups=mesh['cfg'=2,'pipe'=4,'seq'=4] {'seq'}, dimensions={0}, use_global_device_ids=true | all-gather | bytes 655360 | tf_op jit(solution)/shard_map/all_gather | solution.py:103
  28.6 0.9 copy.141
  29.5 8.7 %copy.142 = bf16[1,2048,1536]{1,2,0:T(8,128)(2,1)} copy(bf16[1,2048,1536]{2,1,0:T(8,128)(2,1)} %param.8) | data formatting | bytes 12582912 | tf_op args[2]
  38.2 4.8 %fusion.99 = f32[128,4,3,128]{0,3,2,1:T(8,128)S(1)} fusion(bf16[128,2048,1,1]{1,0,3,2:T(8,128)(2,1)} %bitcast.287, bf16[4,3,128,2048]{3,2,1,0:T(8,128)(2,1)} %bitcast.271), kind=kOutput, calls=%fused_computation.217 | convolution fusion | flops 805306368 | bytes 7602176 | tf_op jit(solution)/shard_map/dot_general | solution.py:105
  44.2 0.7 fusion.82
  47.8 0.8 fusion.62
  48.6 1.0 pad_maximum_fusion.3
  50.2 1.4 compare_and_fusion
  52.2 1.1 fusion.95
  54.0 0.9 copy.203
  54.9 23.5 %reduce-scatter.5.cloned.1.call-done = bf16[1,4,8,2048]{3,2,1,0:T(8,128)(2,1)} async-done(((bf16[4,4,8,2048]{3,2,1,0:T(8,128)(2,1)}), bf16[1,4,8,2048]{3,2,1,0:T(8,128)(2,1)}) %reduce-scatter.5.cloned.1.call-update) | async-done | bytes 131088 | tf_op jit(solution)/shard_map/reduce_scatter | solution.py:152
  78.4 0.9 fusion.50
  79.4 3.3 %collective-permute-start = (bf16[4,8,2048]{2,1,0:T(8,128)(2,1)S(1)}, bf16[4,8,2048]{2,1,0:T(8,128)(2,1)S(1)}, u32[]{:S(2)}, u32[]{:S(2)}) collective-permute-start(bf16[4,8,2048]{2,1,0:T(8,128)(2,1)S(1)} %fusion.50), channel_id=1, source_target_pairs={{0,4},{4,8},{8,12},{1,5},{5,9},{9,13},{2,6},{6,10},{10,14},{3,7},{... | collective-permute-start | bytes 393224 | tf_op jit(solution)/shard_map/ppermute | solution.py:19
  82.8 2.5 collective-permute-done
  85.7 15.0 %all-gather.1 = bf16[16,8,2048]{2,1,0:T(8,128)(2,1)S(1)} all-gather(bf16[4,8,2048]{2,1,0:T(8,128)(2,1)S(1)} %fusion.45), channel_id=3, replica_groups=mesh['cfg'=2,'pipe'=4,'seq'=4] {'seq'}, dimensions={0}, use_global_device_ids=true | all-gather | bytes 655360 | tf_op jit(solution)/shard_map/all_gather | solution.py:103
  100.8 4.6 %fusion.4 = f32[128,4,3,128]{0,3,1,2:T(8,128)S(1)} fusion(bf16[128,2048,1,1]{1,0,2,3:T(8,128)(2,1)S(1)} %bitcast.289, bf16[4,3,128,2048]{3,2,1,0:T(8,128)(2,1)} %bitcast.272), kind=kOutput, calls=%fused_computation.4 | convolution fusion | flops 805306368 | bytes 7602176 | tf_op jit(solution)/shard_map/dot_general | solution.py:105
  106.9 0.8 copy.202
  107.9 21.7 %reduce-scatter.7.cloned.1.call-done = bf16[1,4,8,2048]{3,2,1,0:T(8,128)(2,1)} async-done(((bf16[4,4,8,2048]{3,2,1,0:T(8,128)(2,1)}), bf16[1,4,8,2048]{3,2,1,0:T(8,128)(2,1)}) %reduce-scatter.7.cloned.1.call-update) | async-done | bytes 131088 | tf_op jit(solution)/shard_map/reduce_scatter | solution.py:152
  129.6 0.9 fusion.51
  130.5 3.4 %collective-permute-start.1 = (bf16[4,8,2048]{2,1,0:T(8,128)(2,1)S(1)}, bf16[4,8,2048]{2,1,0:T(8,128)(2,1)S(1)}, u32[]{:S(2)}, u32[]{:S(2)}) collective-permute-start(bf16[4,8,2048]{2,1,0:T(8,128)(2,1)S(1)} %fusion.51), channel_id=1, source_target_pairs={{0,4},{4,8},{8,12},{1,5},{5,9},{9,13},{2,6},{6,10},{10,14},{3,7},{... | collective-permute-start | bytes 393224 | tf_op jit(solution)/shard_map/ppermute | solution.py:19
  133.9 1.4 pad_add_fusion.2
  135.3 1.1 collective-permute-done.1
  136.7 0.8 fusion.41
  137.5 15.0 %all-gather.2 = bf16[16,8,2048]{2,1,0:T(8,128)(2,1)S(1)} all-gather(bf16[4,8,2048]{2,1,0:T(8,128)(2,1)S(1)} %fusion.41), channel_id=4, replica_groups=mesh['cfg'=2,'pipe'=4,'seq'=4] {'seq'}, dimensions={0}, use_global_device_ids=true | all-gather | bytes 655360 | tf_op jit(solution)/shard_map/all_gather | solution.py:103
  152.5 4.6 %fusion.2 = f32[128,4,3,128]{0,3,1,2:T(8,128)S(1)} fusion(bf16[128,2048,1,1]{1,0,2,3:T(8,128)(2,1)S(1)} %bitcast.290, bf16[4,3,128,2048]{3,2,1,0:T(8,128)(2,1)} %bitcast.273), kind=kOutput, calls=%fused_computation.2 | convolution fusion | flops 805306368 | bytes 7602176 | tf_op jit(solution)/shard_map/dot_general | solution.py:105
  157.3 0.8 fusion.86
  159.4 0.9 copy.201
  160.4 21.8 %reduce-scatter.9.cloned.1.call-done = bf16[1,4,8,2048]{3,2,1,0:T(8,128)(2,1)} async-done(((bf16[4,4,8,2048]{3,2,1,0:T(8,128)(2,1)}), bf16[1,4,8,2048]{3,2,1,0:T(8,128)(2,1)}) %reduce-scatter.9.cloned.1.call-update) | async-done | bytes 131088 | tf_op jit(solution)/shard_map/reduce_scatter | solution.py:152
  182.2 0.9 fusion.52
  183.2 3.3 %collective-permute-start.2 = (bf16[4,8,2048]{2,1,0:T(8,128)(2,1)S(1)}, bf16[4,8,2048]{2,1,0:T(8,128)(2,1)S(1)}, u32[]{:S(2)}, u32[]{:S(2)}) collective-permute-start(bf16[4,8,2048]{2,1,0:T(8,128)(2,1)S(1)} %fusion.52), channel_id=1, source_target_pairs={{0,4},{4,8},{8,12},{1,5},{5,9},{9,13},{2,6},{6,10},{10,14},{3,7},{... | collective-permute-start | bytes 393224 | tf_op jit(solution)/shard_map/ppermute | solution.py:19
  186.5 2.5 collective-permute-done.2
  189.3 0.8 fusion.37
  190.1 15.2 %all-gather.3 = bf16[16,8,2048]{2,1,0:T(8,128)(2,1)S(1)} all-gather(bf16[4,8,2048]{2,1,0:T(8,128)(2,1)S(1)} %fusion.37), channel_id=5, replica_groups=mesh['cfg'=2,'pipe'=4,'seq'=4] {'seq'}, dimensions={0}, use_global_device_ids=true | all-gather | bytes 655360 | tf_op jit(solution)/shard_map/all_gather | solution.py:103
  205.3 4.6 %fusion = f32[128,4,3,128]{0,3,1,2:T(8,128)S(1)} fusion(bf16[128,2048,1,1]{1,0,2,3:T(8,128)(2,1)S(1)} %bitcast.288, bf16[4,3,128,2048]{3,2,1,0:T(8,128)(2,1)} %bitcast.274), kind=kOutput, calls=%fused_computation | convolution fusion | flops 805306368 | bytes 7602176 | tf_op jit(solution)/shard_map/dot_general | solution.py:105
  210.8 0.8 fusion.65
  212.8 0.8 copy.200
  213.8 1.0 fusion.115
  214.9 1.1 fusion.114
  215.9 1.0 fusion.113
  217.0 18.5 %reduce-scatter.11.cloned.1.call-done = bf16[1,4,8,2048]{3,2,1,0:T(8,128)(2,1)} async-done(((bf16[4,4,8,2048]{3,2,1,0:T(8,128)(2,1)}), bf16[1,4,8,2048]{3,2,1,0:T(8,128)(2,1)}) %reduce-scatter.11.cloned.1.call-update) | async-done | bytes 131088 | tf_op jit(solution)/shard_map/reduce_scatter | solution.py:152
  235.5 0.9 fusion.53
  237.2 3.6 %all-to-all-start = ((bf16[8,8,1024]{2,1,0:T(8,128)(2,1)}), bf16[8,8,1024]{2,1,0:T(8,128)(2,1)S(1)}, u32[]{:S(2)}, u32[]{:S(2)}) async-start(bf16[8,8,1024]{2,1,0:T(8,128)(2,1)} %bitcast.73), calls=%async_computation.4 | async-start | bytes 262144 | tf_op jit(solution)/shard_map/all_to_all | solution.py:168
  241.3 0.8 reshape_transpose.3
  242.1 4.0 %all-to-all-done = bf16[8,8,1024]{2,1,0:T(8,128)(2,1)S(1)} async-done(((bf16[8,8,1024]{2,1,0:T(8,128)(2,1)}), bf16[8,8,1024]{2,1,0:T(8,128)(2,1)S(1)}, u32[]{:S(2)}, u32[]{:S(2)}) %all-to-all-start) | async-done | bytes 131104 | tf_op jit(solution)/shard_map/all_to_all | solution.py:168
  (122 shorter events, 14.3 us)
Async XLA Ops:
  7.2 46.3 %copy-start = (bf16[1,512,2048]{2,1,0:T(8,128)(2,1)S(1)}, bf16[1,512,2048]{2,1,0:T(8,128)(2,1)}, u32[]{:S(2)}) copy-start(bf16[1,512,2048]{2,1,0:T(8,128)(2,1)} %param.9) | copy-start | bytes 6291460
  7.2 71.3 %reduce-scatter.5.cloned.1.call-start = ((), (), s32[]{:S(2)}) async-start(), calls=%async_computation.5 | async-start | bytes 655360 | tf_op jit(solution)/shard_map/reduce_scatter | solution.py:152
  10.2 27.9 %copy-start.8 = (f32[1,1,1,2048]{3,1,2,0:T(1,128)}, f32[1,1,1,2048]{3,1,2,0:T(1,128)S(1)}, u32[]{:S(2)}) copy-start(f32[1,1,1,2048]{3,1,2,0:T(1,128)S(1)} %get-tuple-element.28) | copy-start | bytes 24580
  38.2 6.8 %copy-start.20 = (f32[1,2,128]{2,1,0:T(2,128)S(1)}, f32[1,2,128]{2,1,0:T(2,128)}, u32[]{:S(2)}) copy-start(f32[1,2,128]{2,1,0:T(2,128)} %param.10) | copy-start | bytes 3076
  38.2 8.0 %copy-start.7 = (bf16[1,1,2,4,1,4,8,512]{7,6,5,4,3,2,1,0:T(8,128)(2,1)S(1)}, bf16[1,1,2,4,1,4,8,512]{7,6,5,4,3,2,1,0:T(8,128)(2,1)}, u32[]{:S(2)}) copy-start(bf16[1,1,2,4,1,4,8,512]{7,6,5,4,3,2,1,0:T(8,128)(2,1)} %param.11) | copy-start | bytes 786436
  43.0 35.5 %copy-start.1 = (bf16[4,8,2048]{2,1,0:T(8,128)(2,1)S(1)}, bf16[4,8,2048]{2,1,0:T(8,128)(2,1)}, u32[]{:S(2)}) copy-start(bf16[4,8,2048]{2,1,0:T(8,128)(2,1)} %param.6) | copy-start | bytes 393220
  46.4 39.2 %copy-start.9 = (f32[1,1,1,2048]{3,1,2,0:T(1,128)S(1)}, f32[1,1,1,2048]{3,1,2,0:T(1,128)}, u32[]{:S(2)}) copy-start(f32[1,1,1,2048]{3,1,2,0:T(1,128)} %copy-done.8) | copy-start | bytes 24580
  47.8 2.4 copy-start.15
  54.9 74.7 %reduce-scatter.7.cloned.1.call-start = ((), (), s32[]{:S(2)}) async-start(), calls=%async_computation.6 | async-start | bytes 655360 | tf_op jit(solution)/shard_map/reduce_scatter | solution.py:152
  78.4 27.1 %copy-start.10 = (f32[128]{0:T(128)S(1)}, f32[128]{0:T(128)}, u32[]{:S(2)}) copy-start(f32[128]{0:T(128)} %get-tuple-element.30) | copy-start | bytes 1540
  79.4 5.8 %collective-permute-start = (bf16[4,8,2048]{2,1,0:T(8,128)(2,1)S(1)}, bf16[4,8,2048]{2,1,0:T(8,128)(2,1)S(1)}, u32[]{:S(2)}, u32[]{:S(2)}) collective-permute-start(bf16[4,8,2048]{2,1,0:T(8,128)(2,1)S(1)} %fusion.50), channel_id=1, source_target_pairs={{0,4},{4,8},{8,12},{1,5},{5,9},{9,13},{2,6},{6,10},{10,14},{3,7},{... | collective-permute-start | bytes 393224 | tf_op jit(solution)/shard_map/ppermute | solution.py:19
  100.7 5.0 %copy-start.14 = (pred[128,256]{1,0:T(8,128)(4,1)S(1)}, pred[128,256]{1,0:T(8,128)(4,1)}, u32[]{:S(2)}) copy-start(pred[128,256]{1,0:T(8,128)(4,1)} %get-tuple-element.54) | copy-start | bytes 98308
  100.7 5.0 %copy-start.21 = (f32[128]{0:T(128)S(1)}, f32[128]{0:T(128)}, u32[]{:S(2)}) copy-start(f32[128]{0:T(128)} %get-tuple-element.29) | copy-start | bytes 1540
  105.4 2.4 copy-start.2
  105.5 2.2 copy-start.17
  107.8 74.4 %reduce-scatter.9.cloned.1.call-start = ((), (), s32[]{:S(2)}) async-start(), calls=%async_computation.7 | async-start | bytes 655360 | tf_op jit(solution)/shard_map/reduce_scatter | solution.py:152
  130.5 27.5 %copy-start.11 = (f32[128]{0:T(128)S(1)}, f32[128]{0:T(128)}, u32[]{:S(2)}) copy-start(f32[128]{0:T(128)} %get-tuple-element.30) | copy-start | bytes 1540
  130.5 5.9 %collective-permute-start.1 = (bf16[4,8,2048]{2,1,0:T(8,128)(2,1)S(1)}, bf16[4,8,2048]{2,1,0:T(8,128)(2,1)S(1)}, u32[]{:S(2)}, u32[]{:S(2)}) collective-permute-start(bf16[4,8,2048]{2,1,0:T(8,128)(2,1)S(1)} %fusion.51), channel_id=1, source_target_pairs={{0,4},{4,8},{8,12},{1,5},{5,9},{9,13},{2,6},{6,10},{10,14},{3,7},{... | collective-permute-start | bytes 393224 | tf_op jit(solution)/shard_map/ppermute | solution.py:19
  152.5 5.8 %copy-start.22 = (f32[128]{0:T(128)S(1)}, f32[128]{0:T(128)}, u32[]{:S(2)}) copy-start(f32[128]{0:T(128)} %get-tuple-element.29) | copy-start | bytes 1540
  157.2 3.1 %copy-start.3 = (f32[128,4,3,128]{0,3,1,2:T(8,128)}, f32[128,4,3,128]{0,3,1,2:T(8,128)S(1)}, u32[]{:S(2)}) copy-start(f32[128,4,3,128]{0,3,1,2:T(8,128)S(1)} %fusion.2) | copy-start | bytes 2359300
  158.1 2.2 copy-start.18
  160.3 75.2 %reduce-scatter.11.cloned.1.call-start = ((), (), s32[]{:S(2)}) async-start(), calls=%async_computation.8 | async-start | bytes 655360 | tf_op jit(solution)/shard_map/reduce_scatter | solution.py:152
  183.2 5.8 %collective-permute-start.2 = (bf16[4,8,2048]{2,1,0:T(8,128)(2,1)S(1)}, bf16[4,8,2048]{2,1,0:T(8,128)(2,1)S(1)}, u32[]{:S(2)}, u32[]{:S(2)}) collective-permute-start(bf16[4,8,2048]{2,1,0:T(8,128)(2,1)S(1)} %fusion.52), channel_id=1, source_target_pairs={{0,4},{4,8},{8,12},{1,5},{5,9},{9,13},{2,6},{6,10},{10,14},{3,7},{... | collective-permute-start | bytes 393224 | tf_op jit(solution)/shard_map/ppermute | solution.py:19
  205.3 6.3 %copy-start.13 = (pred[128,256]{1,0:T(8,128)(4,1)S(1)}, pred[128,256]{1,0:T(8,128)(4,1)}, u32[]{:S(2)}) copy-start(pred[128,256]{1,0:T(8,128)(4,1)} %get-tuple-element.56) | copy-start | bytes 98308
  205.3 6.3 %copy-start.23 = (f32[128]{0:T(128)S(1)}, f32[128]{0:T(128)}, u32[]{:S(2)}) copy-start(f32[128]{0:T(128)} %get-tuple-element.29) | copy-start | bytes 1540
  210.0 3.7 %copy-start.4 = (f32[128,4,3,128]{0,3,1,2:T(8,128)}, f32[128,4,3,128]{0,3,1,2:T(8,128)S(1)}, u32[]{:S(2)}) copy-start(f32[128,4,3,128]{0,3,1,2:T(8,128)S(1)} %fusion) | copy-start | bytes 2359300
  210.0 3.7 %copy-start.12 = (f32[128]{0:T(128)S(1)}, f32[128]{0:T(128)}, u32[]{:S(2)}) copy-start(f32[128]{0:T(128)} %get-tuple-element.30) | copy-start | bytes 1540
  210.0 3.7 %copy-start.16 = (f32[128,4]{0,1:T(4,128)S(1)}, f32[128,4]{0,1:T(4,128)}, u32[]{:S(2)}) copy-start(f32[128,4]{0,1:T(4,128)} %copy-done.15) | copy-start | bytes 6148
  210.0 30.8 %copy-start.5 = (bf16[1,1,128,4,128]{2,4,3,1,0:T(8,128)(2,1)S(1)}, bf16[1,1,128,4,128]{2,4,3,1,0:T(8,128)(2,1)}, u32[]{:S(2)}) copy-start(bf16[1,1,128,4,128]{2,4,3,1,0:T(8,128)(2,1)} %get-tuple-element.24) | copy-start | bytes 393220
  210.8 2.9 %copy-start.19 = (f32[128,4]{0,1:T(4,128)}, f32[128,4]{0,1:T(4,128)S(1)}, u32[]{:S(2)}) copy-start(f32[128,4]{0,1:T(4,128)S(1)} %add_rsqrt_fusion.1) | copy-start | bytes 6148
  211.6 29.2 %copy-start.6 = (bf16[1,1,128,4,128]{2,4,3,1,0:T(8,128)(2,1)S(1)}, bf16[1,1,128,4,128]{2,4,3,1,0:T(8,128)(2,1)}, u32[]{:S(2)}) copy-start(bf16[1,1,128,4,128]{2,4,3,1,0:T(8,128)(2,1)} %get-tuple-element.18) | copy-start | bytes 393220
  237.2 8.9 %all-to-all-start = ((bf16[8,8,1024]{2,1,0:T(8,128)(2,1)}), bf16[8,8,1024]{2,1,0:T(8,128)(2,1)S(1)}, u32[]{:S(2)}, u32[]{:S(2)}) async-start(bf16[8,8,1024]{2,1,0:T(8,128)(2,1)} %bitcast.73), calls=%async_computation.4 | async-start | bytes 262144 | tf_op jit(solution)/shard_map/all_to_all | solution.py:168
Sparse Core Ops, SparseCore 0:
  55.0 23.4 reduce-scatter.4
  107.9 21.6 reduce-scatter.6
  160.5 21.7 reduce-scatter.8
  213.8 21.6 reduce-scatter.10

commit v3 on v1

v3 whole, which is shorter than its diff:
```python
import math

import jax
import jax.numpy as jnp
from jax import lax
from jax.sharding import PartitionSpec as P

GUIDANCE_SCALE = 6.0
EPSILON = 1e-06


def swapped(value, axis, bit):
    return lax.ppermute(value, axis, [(i, i ^ 1 << bit) for i in range(lax.axis_size(axis))])


def layer_norm(values):
    center = values - jnp.mean(values, axis=-1, keepdims=True)
    spread = jnp.mean(center * center, axis=-1, keepdims=True)
    return center * lax.rsqrt(spread + EPSILON)


def head_norm(values, gain_row):
    return (
        values * lax.rsqrt(jnp.mean(values * values, axis=-1, keepdims=True) + EPSILON) * gain_row
    )


def join_pair(is_upper, mine, theirs, axis_dim):
    return jnp.where(
        is_upper,
        jnp.concatenate((theirs, mine), axis_dim),
        jnp.concatenate((mine, theirs), axis_dim),
    )


def local(latent, modulation, qkv_weight, out_weight, norm_gain, stale_kv):
    seq_count = lax.axis_size("seq")
    seq_rank = lax.axis_index("seq")
    section_count = lax.axis_size("pipe")
    section_rank = lax.axis_index("pipe")
    branch_rank = lax.axis_index("cfg")
    patches, tok_dev, model_width = latent.shape
    head_dim = norm_gain.shape[2]
    slice_count = min(seq_count, 8)
    member_count = seq_count // slice_count
    member_bits = member_count.bit_length() - 1
    own_member = seq_rank % member_count
    local_width = stale_kv.shape[7]
    local_heads = local_width // head_dim
    group_rows = slice_count * tok_dev
    divisor = math.sqrt(head_dim)
    shift_row = modulation[0, 0, 0]
    scale_row = modulation[0, 0, 1]
    gate_row = modulation[0, 0, 2]
    query_gain = norm_gain[0, 0]
    key_gain = norm_gain[0, 1]
    own_cache = stale_kv[0, 0].reshape(2, patches, group_rows, local_width)
    group_cache = own_cache[None]
    qkv_slice = qkv_weight[0]
    out_slice = out_weight[0]
    for level_index in range(member_bits):
        got_qkv, got_out, got_cache = (
            swapped(qkv_slice, "seq", level_index),
            swapped(out_slice, "seq", level_index),
            swapped(group_cache, "seq", level_index),
        )
        is_upper = own_member >> level_index & 1 == 1
        qkv_slice = join_pair(is_upper, qkv_slice, got_qkv, 1)
        out_slice = join_pair(is_upper, out_slice, got_out, 0)
        group_cache = join_pair(is_upper, group_cache, got_cache, 0)
    stale_rows = group_cache.swapaxes(0, 1).reshape(2, -1, local_width)
    homes = section_count * slice_count
    per_home = patches // section_count
    rows = patches * group_rows
    peers = None
    if member_count > 1:
        peers = [
            [
                q * seq_count + a + member_count * b
                for q in range(section_count)
                for b in range(slice_count)
            ]
            for a in range(member_count)
        ]

    def exchange(value):
        return lax.all_to_all(value, ("pipe", "seq"), 0, 0, axis_index_groups=peers)

    patch_of = jnp.repeat(jnp.arange(patches), group_rows)
    stale_patch = jnp.tile(patch_of, member_count)
    stale_member = jnp.repeat(jnp.arange(member_count), rows)
    mask = jnp.concatenate(
        (
            patch_of[None, :] <= patch_of[:, None],
            jnp.logical_or(
                stale_patch[None, :] > patch_of[:, None], stale_member[None, :] != own_member
            ),
        ),
        axis=1,
    )
    hidden = lax.dynamic_slice_in_dim(latent, section_rank * per_home, per_home, 0)
    next_cache = None
    for section in range(section_count):
        features = exchange(jnp.broadcast_to(hidden[None], (homes,) + hidden.shape))
        features = features.reshape(section_count, slice_count, per_home, tok_dev, model_width)
        features = features.swapaxes(1, 2).reshape(rows, model_width)
        normed = layer_norm(features.astype(jnp.float32))
        modulated = (normed * (1.0 + scale_row) + shift_row).astype(jnp.bfloat16)
        mixed = jnp.dot(modulated, qkv_slice, preferred_element_type=jnp.float32)
        mixed = mixed.reshape(rows, local_heads, 3, head_dim)
        queries = head_norm(mixed[:, :, 0], query_gain).astype(jnp.bfloat16)
        fresh = jnp.stack((head_norm(mixed[:, :, 1], key_gain), mixed[:, :, 2])).astype(
            jnp.bfloat16
        )
        next_cache = (
            fresh if next_cache is None else jnp.where(section_rank == section, fresh, next_cache)
        )
        view = jnp.concatenate(
            (fresh, stale_rows.reshape(2, -1, local_heads, head_dim)), axis=1
        )
        scores = (
            jnp.einsum("qhd,khd->hqk", queries, view[0], preferred_element_type=jnp.float32)
            / divisor
        )
        weights = jnp.where(mask[None], jnp.exp(scores), 0.0)
        weight_total = jnp.sum(weights, axis=-1)
        summed = jnp.einsum(
            "hqk,khd->qhd",
            weights.astype(jnp.bfloat16),
            view[1],
            preferred_element_type=jnp.float32,
        )
        attended = (
            (summed / weight_total.T[:, :, None]).astype(jnp.bfloat16).reshape(rows, local_width)
        )
        partial_out = jnp.dot(attended, out_slice, preferred_element_type=jnp.float32)
        partial_out = (gate_row * partial_out).astype(jnp.bfloat16)
        partial_out = partial_out.reshape(
            section_count, per_home, slice_count, tok_dev, model_width
        )
        partial_out = partial_out.swapaxes(1, 2).reshape(homes, per_home, tok_dev, model_width)
        parts = exchange(partial_out)
        parts = parts[section * slice_count : (section + 1) * slice_count].astype(jnp.float32)
        hidden = (hidden.astype(jnp.float32) + jnp.sum(parts, axis=0)).astype(jnp.bfloat16)

    next_cache = next_cache.reshape(stale_kv.shape)
    half = model_width // 2
    kept = lax.dynamic_slice_in_dim(hidden, branch_rank * half, half, 2)
    sent = lax.dynamic_slice_in_dim(hidden, (1 - branch_rank) * half, half, 2)
    got = swapped(sent, "cfg", 0)
    conditional = jnp.where(branch_rank == 0, kept, got).astype(jnp.float32)
    unconditional = jnp.where(branch_rank == 0, got, kept).astype(jnp.float32)
    guided = (unconditional + GUIDANCE_SCALE * (conditional - unconditional)).astype(jnp.bfloat16)
    return (guided, next_cache)


def solution(mesh):
    placed = (
        P(None, "seq", None),
        P("pipe", "cfg", None, None),
        P("pipe", None, "seq"),
        P("pipe", "seq", None),
        P("pipe", None, None),
        P("pipe", "cfg", None, None, "seq", None, None, None),
    )
    return jax.shard_map(
        local,
        mesh=mesh,
        in_specs=placed,
        out_specs=(P("pipe", "seq", "cfg"), P("pipe", "cfg", None, None, "seq", None, None, None)),
        check_vma=False,
    )
```

time: 205 us -> 195 us (0.951)
  waiting for transfers between devices: 45.9 us -> 16.3 us
  blocking collectives: 63.6 us -> 91.2 us
  starting transfers between devices: 36.6 us -> 17.2 us
  local copies, waits for them, and re-layouts: 19.3 us -> 34.3 us
    all_to_all x4 -> x5, blocking collectives: 63.6 us -> 91.2 us  [exchange(): return lax.all_to_all(value, ('pipe', 'seq'), 0, 0, axis_index_groups=peers)]
    all_to_all x5 -> x3, waiting for transfers between devices: 38.5 us -> 16.3 us  [exchange(): return lax.all_to_all(value, ('pipe', 'seq'), 0, 0, axis_index_groups=peers)]
    ppermute x3 -> x1, starting transfers between devices: 11.8 us -> 0.07 us  [swapped(): lax.ppermute(value, axis, [(i, i ^ 1 << bit) for i in range(lax.axis_size...]
    all_to_all x5 -> x3, starting transfers between devices: 24.8 us -> 17.1 us  [exchange(): return lax.all_to_all(value, ('pipe', 'seq'), 0, 0, axis_index_groups=peers)]
    ppermute x3 -> x1, waiting for transfers between devices: 7.49 us -> 0.01 us  [swapped(): lax.ppermute(value, axis, [(i, i ^ 1 << bit) for i in range(lax.axis_size...]
    slice x0 -> x8, local copies, waits for them, and re-layouts: none -> 6.05 us  [the longest x4 3.57 us: local(): mixed[:, :, 2]]
    mul x1 -> x6, local copies, waits for them, and re-layouts: 0.01 us -> 5.41 us  [head_norm(): values * lax.rsqrt(jnp.mean(values * values, axis=-1, keepdims=True) + EP...]
    rsqrt x0 -> x4, local copies, waits for them, and re-layouts: none -> 4.28 us  [head_norm(): lax.rsqrt(jnp.mean(values * values, axis=-1, keepdims=True) + EPSILON)]
  transfers between devices with their start and end apart: 8 -> 4, of which waited for: 8 -> 2; matrix products, arithmetic and copies ran while one was open for 9% -> 18% of each run, Pallas kernels for 0% -> 0%
where the time goes in v3:
time: 195 us; the launch traced here: 193 us
  blocking collectives  91.2 us (47%)
  local copies, waits for them, and re-layouts  34.3 us (18%)
  matrix products  19.1 us (10%)
  starting transfers between devices  17.2 us (9%)
  waiting for transfers between devices  16.3 us (8%)
  other arithmetic  13.8 us (7%)
    all_to_all x5, blocking collectives, exchange(): return lax.all_to_all(value, ('pipe', 'seq'), 0, 0, axis_index_groups=peers)  91.2 us
    all_to_all x3, starting transfers between devices, exchange(): return lax.all_to_all(value, ('pipe', 'seq'), 0, 0, axis_index_groups=peers)  17.1 us
    all_to_all x3, waiting for transfers between devices, exchange(): return lax.all_to_all(value, ('pipe', 'seq'), 0, 0, axis_index_groups=peers)  16.3 us
    dot_general x4, matrix products, local(): mixed = jnp.dot(modulated, qkv_slice, preferred_element_type=jnp.float32)  13.6 us
    unnamed x60, local copies, waits for them, and re-layouts  10.1 us
    mul x6, local copies, waits for them, and re-layouts, head_norm(): values * lax.rsqrt(jnp.mean(values * values, axis=-1, keepdims=True) + EP...  5.41 us
    rsqrt x4, local copies, waits for them, and re-layouts, head_norm(): lax.rsqrt(jnp.mean(values * values, axis=-1, keepdims=True) + EPSILON)  4.28 us
  transfers between devices with their start and end apart: 4, of which 2 were waited for; matrix products, arithmetic and copies ran while one was open for 18% of the time, Pallas kernels for 0%

profile of v3, /device:TPU:0, one launch (start us, length us, event | category | flops | bytes accessed | tf_op | source)
XLA Modules:
  0.0 193.3 jit_solution(754834847081619014)
XLA Ops:
  0.7 0.9 dynamic-slice_bitcast_fusion
  1.6 0.9 broadcast_in_dim.45
  2.4 8.3 %all-to-all-start = ((bf16[16,1,8,2048]{3,2,1,0:T(8,128)(2,1)}), bf16[16,1,8,2048]{3,2,1,0:T(8,128)(2,1)S(1)}, u32[]{:S(2)}, u32[]{:S(2)}) async-start(bf16[16,1,8,2048]{3,2,1,0:T(8,128)(2,1)} %broadcast_in_dim.45), calls=%async_computation | async-start | bytes 1048576 | tf_op jit(solution)/shard_map/all_to_all | solution.py:87
  10.8 1.0 reshape_reshape_transpose_broadcast_in_dim_reshape_squeeze.2
  12.1 8.7 %copy.236 = bf16[1,2048,1536]{1,2,0:T(8,128)(2,1)} copy(bf16[1,2048,1536]{2,1,0:T(8,128)(2,1)} %param.8) | data formatting | bytes 12582912 | tf_op args[2]
  21.0 6.0 %all-to-all-done = bf16[16,1,8,2048]{3,2,1,0:T(8,128)(2,1)S(1)} async-done(((bf16[16,1,8,2048]{3,2,1,0:T(8,128)(2,1)}), bf16[16,1,8,2048]{3,2,1,0:T(8,128)(2,1)S(1)}, u32[]{:S(2)}, u32[]{:S(2)}) %all-to-all-start) | async-done | bytes 524320 | tf_op jit(solution)/shard_map/all_to_all | solution.py:87
  27.4 4.9 %fusion.59 = f32[128,4,3,128]{0,3,2,1:T(8,128)S(1)} fusion(bf16[4,3,128,2048]{3,2,1,0:T(8,128)(2,1)} %bitcast.261, bf16[16,1,8,2048]{3,2,1,0:T(8,128)(2,1)S(1)} %all-to-all-done, f32[2048]{0:T(1024)S(1)} %bitcast.285, f32[2048]{0:T(1024)S(1)} %bitcast.289, f32[16,8]{1,0:T(8,128)S(1)} %add_rsqrt_fusion.3, f32[16,8]{1,0:T(8,128)S(1)} %broadcast_multiply_fusion.3), kind=kOutput, calls=%fused_computation.83 | convolution fusion | flops 806879232 | bytes 7619584 | tf_op jit(solution)/shard_map/dot_general | solution.py:109
  34.4 18.4 %all_to_all.40 = bf16[16,1,8,2048]{3,2,1,0:T(8,128)(2,1)S(1)} all-to-all(bf16[16,1,8,2048]{3,2,1,0:T(8,128)(2,1)S(1)} %fusion.13), channel_id=1, replica_groups=mesh['cfg'=2,'pipe'=4,'seq'=4] {'pipe','seq'}, dimensions={0} | all-to-all | bytes 1048576 | tf_op jit(solution)/shard_map/all_to_all | solution.py:87
  52.8 0.8 fusion.107
  53.6 18.3 %all_to_all.41 = bf16[16,1,8,2048]{3,2,1,0:T(8,128)(2,1)S(1)} all-to-all(bf16[16,1,8,2048]{3,2,1,0:T(8,128)(2,1)S(1)} %broadcast_in_dim.50), channel_id=1, replica_groups=mesh['cfg'=2,'pipe'=4,'seq'=4] {'pipe','seq'}, dimensions={0} | all-to-all | bytes 1048576 | tf_op jit(solution)/shard_map/all_to_all | solution.py:87
  72.4 1.9 fusion.4
  75.9 18.2 %all_to_all.42 = bf16[16,1,8,2048]{3,2,1,0:T(8,128)(2,1)S(1)} all-to-all(bf16[16,1,8,2048]{3,2,1,0:T(8,128)(2,1)S(1)} %fusion.12), channel_id=1, replica_groups=mesh['cfg'=2,'pipe'=4,'seq'=4] {'pipe','seq'}, dimensions={0} | all-to-all | bytes 1048576 | tf_op jit(solution)/shard_map/all_to_all | solution.py:87
  94.2 18.1 %all_to_all.43 = bf16[16,1,8,2048]{3,2,1,0:T(8,128)(2,1)S(1)} all-to-all(bf16[16,1,8,2048]{3,2,1,0:T(8,128)(2,1)S(1)} %broadcast_in_dim.52), channel_id=1, replica_groups=mesh['cfg'=2,'pipe'=4,'seq'=4] {'pipe','seq'}, dimensions={0} | all-to-all | bytes 1048576 | tf_op jit(solution)/shard_map/all_to_all | solution.py:87
  112.9 1.9 fusion.2
  114.9 0.7 fusion.112
  117.0 18.1 %all_to_all.44 = bf16[16,1,8,2048]{3,2,1,0:T(8,128)(2,1)S(1)} all-to-all(bf16[16,1,8,2048]{3,2,1,0:T(8,128)(2,1)S(1)} %fusion.11), channel_id=1, replica_groups=mesh['cfg'=2,'pipe'=4,'seq'=4] {'pipe','seq'}, dimensions={0} | all-to-all | bytes 1048576 | tf_op jit(solution)/shard_map/all_to_all | solution.py:87
  135.7 0.9 broadcast_in_dim.100
  136.6 4.4 %all-to-all-start.6 = ((bf16[16,1,8,2048]{3,2,1,0:T(8,128)(2,1)}), bf16[16,1,8,2048]{3,2,1,0:T(8,128)(2,1)}, u32[]{:S(2)}, u32[]{:S(2)}) async-start(bf16[16,1,8,2048]{3,2,1,0:T(8,128)(2,1)} %broadcast_in_dim.100), calls=%async_computation.6 | async-start | bytes 1048576 | tf_op jit(solution)/shard_map/all_to_all | solution.py:87
  141.1 1.3 broadcast_bitcast_fusion
  142.3 1.4 copy.273
  144.4 1.0 copy.274
  145.4 0.7 stack.58
  146.1 10.3 %all-to-all-done.6 = bf16[16,1,8,2048]{3,2,1,0:T(8,128)(2,1)} async-done(((bf16[16,1,8,2048]{3,2,1,0:T(8,128)(2,1)}), bf16[16,1,8,2048]{3,2,1,0:T(8,128)(2,1)}, u32[]{:S(2)}, u32[]{:S(2)}) %all-to-all-start.6) | async-done | bytes 524320 | tf_op jit(solution)/shard_map/all_to_all | solution.py:87
  156.4 1.2 convert_reduce_fusion
  157.6 1.3 fusion.42
  159.0 4.9 %fusion = f32[128,4,3,128]{0,3,1,2:T(8,128)S(1)} fusion(bf16[4,3,128,2048]{3,2,1,0:T(8,128)(2,1)} %bitcast.262, bf16[16,1,8,2048]{3,2,1,0:T(8,128)(2,1)} %all-to-all-done.6, f32[16,8]{1,0:T(8,128)S(1)} %add_rsqrt_fusion, f32[16,8]{1,0:T(8,128)S(1)} %broadcast_multiply_fusion, f32[2048]{0:T(1024)S(1)} %bitcast.288, f32[2048]{0:T(1024)} %bitcast.292), kind=kOutput, calls=%fused_computation | convolution fusion | flops 806879232 | bytes 7619584 | tf_op jit(solution)/shard_map/dot_general | solution.py:109
  164.0 0.8 fusion.113
  165.7 1.3 fusion.10
  167.1 4.4 %all-to-all-start.7 = ((bf16[16,1,8,2048]{3,2,1,0:T(8,128)(2,1)}), bf16[16,1,8,2048]{3,2,1,0:T(8,128)(2,1)}, u32[]{:S(2)}, u32[]{:S(2)}) async-start(bf16[16,1,8,2048]{3,2,1,0:T(8,128)(2,1)} %fusion.10), calls=%async_computation.7 | async-start | bytes 1048576 | tf_op jit(solution)/shard_map/all_to_all | solution.py:87
  171.6 1.0 slice.203
  172.6 0.7 copy.270
  173.5 0.7 stack.55
  174.3 1.0 slice.202
  175.3 0.7 copy.267
  176.2 0.7 stack.52
  176.9 1.1 copy.266
  178.0 1.0 slice.201
  179.0 1.4 copy.264
  180.5 0.7 stack.49
  181.3 1.1 copy.263
  182.4 1.0 mul.522
  183.4 1.0 mul.518
  184.4 1.0 mul.514
  185.5 1.0 mul.507
  186.5 2.4 %multiply_convert_fusion = (bf16[1,4,4,8,512]{4,0,3,2,1:T(2,128)(2,1)S(1)}, bf16[1,4,4,8,512]{4,0,3,2,1:T(2,128)(2,1)S(1)}, bf16[1,4,4,8,512]{4,0,3,2,1:T(2,128)(2,1)S(1)}, bf16[1,4,4,8,512]{4,0,3,2,1:T(2,128)(2,1)S(1)}) fusion(f32[1,4,4,8,512]{4,0,3,2,1:T(1,128)S(1)} %bitcast.271, f32[1,4,4,8,512]{4,0,3,2,1:T(1,128)S(1)} %bitcast.267, ...), kind=kLoop, calls=%fused_computation.135 | loop fusion | flops 786432 | bytes 2623488 | tf_op jit(solution)/shard_map/convert.3
  189.0 0.9 convert_reduce_fusion.4
  189.9 0.8 fusion.104
  190.8 1.8 fusion.83
  (136 shorter events, 10.6 us)
Async XLA Ops:
  0.6 33.3 %copy-start = (bf16[1,512,2048]{2,1,0:T(8,128)(2,1)S(1)}, bf16[1,512,2048]{2,1,0:T(8,128)(2,1)}, u32[]{:S(2)}) copy-start(bf16[1,512,2048]{2,1,0:T(8,128)(2,1)} %param.9) | copy-start | bytes 6291460
  2.4 24.5 %all-to-all-start = ((bf16[16,1,8,2048]{3,2,1,0:T(8,128)(2,1)}), bf16[16,1,8,2048]{3,2,1,0:T(8,128)(2,1)S(1)}, u32[]{:S(2)}, u32[]{:S(2)}) async-start(bf16[16,1,8,2048]{3,2,1,0:T(8,128)(2,1)} %broadcast_in_dim.45), calls=%async_computation | async-start | bytes 1048576 | tf_op jit(solution)/shard_map/all_to_all | solution.py:87
  12.1 8.8 %copy-start.22 = (f32[1,2,128]{2,1,0:T(2,128)S(1)}, f32[1,2,128]{2,1,0:T(2,128)}, u32[]{:S(2)}) copy-start(f32[1,2,128]{2,1,0:T(2,128)} %param.10) | copy-start | bytes 3076
  12.1 8.9 %copy-start.12 = (f32[1,1,3,2048]{3,1,2,0:T(1,128)S(1)}, f32[1,1,3,2048]{3,1,2,0:T(1,128)}, u32[]{:S(2)}) copy-start(f32[1,1,3,2048]{3,1,2,0:T(1,128)} %param.7) | copy-start | bytes 73732
  20.9 53.8 %copy-start.8 = (pred[128,256]{1,0:T(8,128)(4,1)}, pred[128,256]{1,0:T(8,128)(4,1)S(1)}, u32[]{:S(2)}) copy-start(pred[128,256]{1,0:T(8,128)(4,1)S(1)} %pad_add_fusion) | copy-start | bytes 98308
  20.9 53.6 %copy-start.13 = (f32[128]{0:T(128)}, f32[128]{0:T(128)S(1)}, u32[]{:S(2)}) copy-start(f32[128]{0:T(128)S(1)} %get-tuple-element.28) | copy-start | bytes 1540
  20.9 53.8 %copy-start.23 = (f32[128]{0:T(128)}, f32[128]{0:T(128)S(1)}, u32[]{:S(2)}) copy-start(f32[128]{0:T(128)S(1)} %get-tuple-element.27) | copy-start | bytes 1540
  21.0 91.9 %copy-start.11 = (f32[1,1,1,2048]{3,1,2,0:T(1,128)}, f32[1,1,1,2048]{3,1,2,0:T(1,128)S(1)}, u32[]{:S(2)}) copy-start(f32[1,1,1,2048]{3,1,2,0:T(1,128)S(1)} %get-tuple-element.22) | copy-start | bytes 24580
  27.4 45.0 %slice-start = ((s8[6291456]{0:T(1024)(128)(4,1)}), s8[4194304]{0:T(1024)(128)(4,1)S(1)}, s32[]{:S(2)}) async-start(s8[6291456]{0:T(1024)(128)(4,1)} %bitcast.263), calls=%async_computation.8 | async-start | bytes 8388608
  32.3 0.9 copy-start.1
  32.4 42.0 %copy-start.18 = (f32[128,4]{0,1:T(4,128)}, f32[128,4]{0,1:T(4,128)S(1)}, u32[]{:S(2)}) copy-start(f32[128,4]{0,1:T(4,128)S(1)} %add_rsqrt_fusion.11) | copy-start | bytes 6148
  32.5 39.9 %slice-start.1 = ((s8[6291456]{0:T(1024)(128)(4,1)}), s8[2097152]{0:T(1024)(128)(4,1)S(1)}, s32[]{:S(2)}) async-start(s8[6291456]{0:T(1024)(128)(4,1)} %bitcast.263), calls=%async_computation.9 | async-start | bytes 4194304
  74.4 40.4 %copy-start.3 = (f32[128,4,3,128]{0,3,1,2:T(8,128)}, f32[128,4,3,128]{0,3,1,2:T(8,128)S(1)}, u32[]{:S(2)}) copy-start(f32[128,4,3,128]{0,3,1,2:T(8,128)S(1)} %fusion.4) | copy-start | bytes 2359300
  74.5 0.7 copy-start.16
  112.4 3.2 %copy-start.14 = (f32[128]{0:T(128)S(1)}, f32[128]{0:T(128)}, u32[]{:S(2)}) copy-start(f32[128]{0:T(128)} %copy-done.13) | copy-start | bytes 1540
  112.8 3.0 %copy-start.9 = (pred[128,256]{1,0:T(8,128)(4,1)S(1)}, pred[128,256]{1,0:T(8,128)(4,1)}, u32[]{:S(2)}) copy-start(pred[128,256]{1,0:T(8,128)(4,1)} %copy-done.8) | copy-start | bytes 98308
  112.8 3.0 %copy-start.24 = (f32[128]{0:T(128)S(1)}, f32[128]{0:T(128)}, u32[]{:S(2)}) copy-start(f32[128]{0:T(128)} %copy-done.23) | copy-start | bytes 1540
  114.8 20.3 %copy-start.4 = (f32[128,4,3,128]{0,3,1,2:T(8,128)}, f32[128,4,3,128]{0,3,1,2:T(8,128)S(1)}, u32[]{:S(2)}) copy-start(f32[128,4,3,128]{0,3,1,2:T(8,128)S(1)} %fusion.2) | copy-start | bytes 2359300
  114.8 28.9 %copy-start.2 = (f32[128,4,3,128]{0,3,2,1:T(8,128)S(1)}, f32[128,4,3,128]{0,3,2,1:T(8,128)}, u32[]{:S(2)}) copy-start(f32[128,4,3,128]{0,3,2,1:T(8,128)} %copy-done.1) | copy-start | bytes 2359300
  115.6 0.7 copy-start.19
  135.1 0.6 copy-start.7
  136.6 19.8 %all-to-all-start.6 = ((bf16[16,1,8,2048]{3,2,1,0:T(8,128)(2,1)}), bf16[16,1,8,2048]{3,2,1,0:T(8,128)(2,1)}, u32[]{:S(2)}, u32[]{:S(2)}) async-start(bf16[16,1,8,2048]{3,2,1,0:T(8,128)(2,1)} %broadcast_in_dim.100), calls=%async_computation.6 | async-start | bytes 1048576 | tf_op jit(solution)/shard_map/all_to_all | solution.py:87
  146.1 18.7 %copy-start.15 = (f32[128]{0:T(128)S(1)}, f32[128]{0:T(128)}, u32[]{:S(2)}) copy-start(f32[128]{0:T(128)} %copy-done.13) | copy-start | bytes 1540
  159.0 6.1 %copy-start.10 = (pred[128,256]{1,0:T(8,128)(4,1)S(1)}, pred[128,256]{1,0:T(8,128)(4,1)}, u32[]{:S(2)}) copy-start(pred[128,256]{1,0:T(8,128)(4,1)} %copy-done.8) | copy-start | bytes 98308
  159.0 6.1 %copy-start.25 = (f32[128]{0:T(128)S(1)}, f32[128]{0:T(128)}, u32[]{:S(2)}) copy-start(f32[128]{0:T(128)} %copy-done.23) | copy-start | bytes 1540
  163.9 1.1 copy-start.5
  163.9 8.7 %copy-start.17 = (f32[128,4]{0,1:T(4,128)S(1)}, f32[128,4]{0,1:T(4,128)}, u32[]{:S(2)}) copy-start(f32[128,4]{0,1:T(4,128)} %copy-done.16) | copy-start | bytes 6148
  163.9 11.4 %copy-start.20 = (f32[128,4]{0,1:T(4,128)S(1)}, f32[128,4]{0,1:T(4,128)}, u32[]{:S(2)}) copy-start(f32[128,4]{0,1:T(4,128)} %copy-done.19) | copy-start | bytes 6148
  164.8 0.7 copy-start.21
  167.1 23.8 %copy-start.6 = (bf16[1,1,1,4,1,4,8,512]{7,6,5,3,4,2,1,0:T(8,128)(2,1)S(1)}, bf16[1,1,1,4,1,4,8,512]{7,6,5,3,4,2,1,0:T(8,128)(2,1)}, u32[]{:S(2)}) copy-start(bf16[1,1,1,4,1,4,8,512]{7,6,5,3,4,2,1,0:T(8,128)(2,1)} %stack.58) | copy-start | bytes 393220
  167.1 22.0 %all-to-all-start.7 = ((bf16[16,1,8,2048]{3,2,1,0:T(8,128)(2,1)}), bf16[16,1,8,2048]{3,2,1,0:T(8,128)(2,1)}, u32[]{:S(2)}, u32[]{:S(2)}) async-start(bf16[16,1,8,2048]{3,2,1,0:T(8,128)(2,1)} %fusion.10), calls=%async_computation.7 | async-start | bytes 1048576 | tf_op jit(solution)/shard_map/all_to_all | solution.py:87
  190.7 1.9 collective-permute-start

commit v4 on v3

v4 whole, which is shorter than its diff:
```python
import functools
import math

import jax
import jax.numpy as jnp
from jax import lax
from jax.experimental import pallas as pl
from jax.experimental.pallas import tpu as pltpu
from jax.sharding import PartitionSpec as P

GUIDANCE_SCALE = 6.0
EPSILON = 1e-06
GROUPS = 2


def swapped(value, axis, bit):
    return lax.ppermute(value, axis, [(i, i ^ 1 << bit) for i in range(lax.axis_size(axis))])


def head_norm(values, gain_row):
    return (
        values * lax.rsqrt(jnp.mean(values * values, axis=-1, keepdims=True) + EPSILON) * gain_row
    )


def join_pair(is_upper, mine, theirs, axis_dim):
    return jnp.where(
        is_upper,
        jnp.concatenate((theirs, mine), axis_dim),
        jnp.concatenate((mine, theirs), axis_dim),
    )


def section_kernel(sizes, where_ref, rows_ref, mod_ref, qkv_ref, out_ref, gain_ref, stale_ref, *refs):
    *prev_refs, partial_ref, fresh_ref = refs
    patches, tok_dev, group_rows, head_dim = sizes
    blocks, slices, block_rows, block_cols = rows_ref.shape
    rows = slices * block_rows
    width = blocks * block_cols
    in_group = block_rows // tok_dev
    heads = stale_ref.shape[2] // head_dim
    group, own_member = where_ref[0], where_ref[1]
    parts = [rows_ref[q].reshape(rows, block_cols).astype(jnp.float32) for q in range(blocks)]
    mean = sum(jnp.sum(x, axis=-1, keepdims=True) for x in parts) / width
    parts = [x - mean for x in parts]
    spread = sum(jnp.sum(x * x, axis=-1, keepdims=True) for x in parts) / width
    inverse = lax.rsqrt(spread + EPSILON)
    modulated = []
    for q, x in enumerate(parts):
        at = pl.ds(q * block_cols, block_cols)
        modulated.append(
            (x * inverse * (1.0 + mod_ref[1:2, at]) + mod_ref[0:1, at]).astype(jnp.bfloat16)
        )
    modulated = jnp.concatenate(modulated, axis=1)
    mixed = jnp.dot(modulated, qkv_ref[...], preferred_element_type=jnp.float32)

    def patch_in_group(shape, axis):
        return lax.broadcasted_iota(jnp.int32, shape, axis) // tok_dev % in_group

    square = (rows, rows)
    masks = []
    for back in range(len(prev_refs), 0, -1):
        masks.append(jnp.broadcast_to(group >= back, square))
    masks.append(patch_in_group(square, 1) <= patch_in_group(square, 0))
    wide = (rows, stale_ref.shape[1])
    key_at = lax.broadcasted_iota(jnp.int32, wide, 1)
    masks.append(
        jnp.logical_or(
            key_at // group_rows % patches > group * in_group + patch_in_group(wide, 0),
            key_at // (group_rows * patches) != own_member,
        )
    )
    attended = []
    for head in range(heads):
        at = slice(head * head_dim, (head + 1) * head_dim)
        query, key, value = (
            mixed[:, (3 * head + j) * head_dim : (3 * head + j + 1) * head_dim] for j in range(3)
        )
        query = head_norm(query, gain_ref[0:1, :]).astype(jnp.bfloat16)
        key = head_norm(key, gain_ref[1:2, :]).astype(jnp.bfloat16)
        value = value.astype(jnp.bfloat16)
        fresh_ref[0, :, at] = key
        fresh_ref[1, :, at] = value
        keys = [ref[0, :, at] for ref in prev_refs] + [key, stale_ref[0, :, at]]
        values = [ref[1, :, at] for ref in prev_refs] + [value, stale_ref[1, :, at]]
        total = 0.0
        summed = 0.0
        for mask, key_rows, value_rows in zip(masks, keys, values):
            scores = lax.dot_general(
                query, key_rows, (((1,), (1,)), ((), ())), preferred_element_type=jnp.float32
            )
            weights = jnp.where(mask, jnp.exp(scores / math.sqrt(head_dim)), 0.0)
            total = total + jnp.sum(weights, axis=-1, keepdims=True)
            summed = summed + jnp.dot(
                weights.astype(jnp.bfloat16), value_rows, preferred_element_type=jnp.float32
            )
        attended.append((summed / total).astype(jnp.bfloat16))
    attended = jnp.concatenate(attended, axis=1)
    projected = jnp.dot(attended, out_ref[...], preferred_element_type=jnp.float32)
    projected = (mod_ref[2:3, :] * projected).astype(jnp.bfloat16)
    for q in range(blocks):
        partial_ref[q] = projected[:, q * block_cols : (q + 1) * block_cols].reshape(
            slices, block_rows, block_cols
        )


def local(latent, modulation, qkv_weight, out_weight, norm_gain, stale_kv):
    seq_count = lax.axis_size("seq")
    seq_rank = lax.axis_index("seq")
    section_count = lax.axis_size("pipe")
    section_rank = lax.axis_index("pipe")
    branch_rank = lax.axis_index("cfg")
    patches, tok_dev, model_width = latent.shape
    head_dim = norm_gain.shape[2]
    slice_count = min(seq_count, 8)
    member_count = seq_count // slice_count
    member_bits = member_count.bit_length() - 1
    own_member = seq_rank % member_count
    local_width = stale_kv.shape[7]
    group_rows = slice_count * tok_dev
    own_cache = stale_kv[0, 0].reshape(2, patches, group_rows, local_width)
    group_cache = own_cache[None]
    qkv_slice = qkv_weight[0]
    out_slice = out_weight[0]
    for level_index in range(member_bits):
        got_qkv, got_out, got_cache = (
            swapped(qkv_slice, "seq", level_index),
            swapped(out_slice, "seq", level_index),
            swapped(group_cache, "seq", level_index),
        )
        is_upper = own_member >> level_index & 1 == 1
        qkv_slice = join_pair(is_upper, qkv_slice, got_qkv, 1)
        out_slice = join_pair(is_upper, out_slice, got_out, 0)
        group_cache = join_pair(is_upper, group_cache, got_cache, 0)
    stale_rows = group_cache.swapaxes(0, 1).reshape(2, -1, local_width)
    homes = section_count * slice_count
    in_group = patches // GROUPS
    block_rows = in_group * tok_dev
    block_cols = model_width // section_count
    rows = slice_count * block_rows
    peers = None
    if member_count > 1:
        peers = [
            [
                q * seq_count + a + member_count * b
                for q in range(section_count)
                for b in range(slice_count)
            ]
            for a in range(member_count)
        ]

    def exchange(value):
        value = value.reshape(homes, block_rows, block_cols)
        value = lax.all_to_all(value, ("pipe", "seq"), 0, 0, axis_index_groups=peers)
        return value.reshape(section_count, slice_count, block_rows, block_cols)

    in_vmem = functools.partial(pltpu.with_memory_space_constraint, memory_space=pltpu.VMEM)
    qkv_slice, out_slice = in_vmem(qkv_slice), in_vmem(out_slice)

    def attend(group, features, prev):
        vmem = pl.BlockSpec(memory_space=pltpu.VMEM)
        return pl.pallas_call(
            functools.partial(section_kernel, (patches, tok_dev, group_rows, head_dim)),
            out_shape=(
                jax.ShapeDtypeStruct(features.shape, jnp.bfloat16),
                jax.ShapeDtypeStruct((2, rows, local_width), jnp.bfloat16),
            ),
            in_specs=[pl.BlockSpec(memory_space=pltpu.SMEM)] + [vmem] * (6 + len(prev)),
            out_specs=(vmem, vmem),
            compiler_params=pltpu.CompilerParams(vmem_limit_bytes=24 * 1024 * 1024),
        )(
            jnp.stack((group, own_member)).astype(jnp.int32),
            features,
            modulation[0, 0],
            qkv_slice,
            out_slice,
            norm_gain[0],
            stale_rows,
            *prev,
        )

    sources = lax.dynamic_slice_in_dim(
        latent.reshape(GROUPS, block_rows, model_width), section_rank * block_cols, block_cols, 2
    )
    zeros = jnp.zeros_like(sources[0])
    streams = jnp.stack([sources[0]] + [zeros] * (section_count - 1))
    fresh_ticks = []
    finals = []
    for tick in range(GROUPS + section_count - 1):
        features = exchange(
            jnp.broadcast_to(
                streams[:, None], (section_count, slice_count, block_rows, block_cols)
            )
        )
        prev = fresh_ticks[-(GROUPS - 1) :] if GROUPS > 1 else []
        partial_out, fresh = attend(tick - section_rank, features, prev)
        fresh_ticks.append(fresh)
        parts = exchange(partial_out).astype(jnp.float32)
        results = (streams.astype(jnp.float32) + jnp.sum(parts, axis=1)).astype(jnp.bfloat16)
        finals.append(results[-1])
        entering = sources[tick + 1] if tick + 1 < GROUPS else zeros
        streams = jnp.concatenate((entering[None], results[:-1]))

    next_cache = lax.dynamic_slice_in_dim(jnp.stack(fresh_ticks), section_rank, GROUPS, 0)
    next_cache = next_cache.reshape(GROUPS, 2, slice_count, in_group, tok_dev, local_width)
    next_cache = next_cache.transpose(1, 0, 3, 2, 4, 5).reshape(stale_kv.shape)
    per_home = patches // section_count
    finals = jnp.stack(finals[section_count - 1 :])
    finals = finals.reshape(1, section_count, per_home, tok_dev, block_cols)
    finals = jnp.broadcast_to(finals, (2,) + finals.shape[1:])
    got = lax.all_to_all(
        finals.reshape((-1,) + finals.shape[2:]), ("cfg", "pipe"), 0, 0
    ).reshape(finals.shape)
    half = section_count // 2
    got = lax.dynamic_slice_in_dim(got, branch_rank * half, half, 1).astype(jnp.float32)
    guided = (got[1] + GUIDANCE_SCALE * (got[0] - got[1])).astype(jnp.bfloat16)
    guided = guided.transpose(1, 2, 0, 3).reshape(per_home, tok_dev, half * block_cols)
    return (guided, next_cache)


def solution(mesh):
    placed = (
        P(None, "seq", None),
        P("pipe", "cfg", None, None),
        P("pipe", None, "seq"),
        P("pipe", "seq", None),
        P("pipe", None, None),
        P("pipe", "cfg", None, None, "seq", None, None, None),
    )
    return jax.shard_map(
        local,
        mesh=mesh,
        in_specs=placed,
        out_specs=(P("pipe", "seq", "cfg"), P("pipe", "cfg", None, None, "seq", None, None, None)),
        check_vma=False,
    )
```

time: 195 us -> 179 us (0.918)
  blocking collectives: 91.2 us -> 35.9 us
  waiting for transfers between devices: 16.3 us -> 62.5 us
  matrix products: 19.1 us -> 0 us
  Pallas kernels: 0 us -> 16.6 us
  starting transfers between devices: 17.2 us -> 32.9 us
  other arithmetic: 13.8 us -> 1.34 us
  local copies, waits for them, and re-layouts: 34.3 us -> 28.1 us
    all_to_all x5 -> x3, blocking collectives: 91.2 us -> 35.9 us  [exchange(): lax.all_to_all(value, ('pipe', 'seq'), 0, 0, axis_index_groups=peers)]
    all_to_all x3 -> x8, waiting for transfers between devices: 16.3 us -> 62.5 us  [the longest x7 59.3 us: exchange(): lax.all_to_all(value, ('pipe', 'seq'), 0, 0, axis_index_groups=peers)]
    dot_general x16 -> x0, matrix products: 19.1 us -> none  [the longest x4 13.6 us: local(): mixed = jnp.dot(modulated, qkv_slice, preferred_element_type=jnp.float32)]
    pallas_call x0 -> x5, Pallas kernels: none -> 16.6 us  [attend(): pl.pallas_call(functools.partial(section_kernel, (patches, tok_dev, group...]
    all_to_all x3 -> x8, starting transfers between devices: 17.1 us -> 32.9 us  [the longest x7 29.5 us: exchange(): lax.all_to_all(value, ('pipe', 'seq'), 0, 0, axis_index_groups=peers)]
    unnamed x60 -> x27, local copies, waits for them, and re-layouts: 10.1 us -> 20.5 us
    mul x6 -> x0, local copies, waits for them, and re-layouts: 5.41 us -> none  [head_norm(): values * lax.rsqrt(jnp.mean(values * values, axis=-1, keepdims=True) + EP...]
    slice x8 -> x3, local copies, waits for them, and re-layouts: 6.05 us -> 0.75 us  [the longest x1 0.74 us: local(): streams = jnp.stack([sources[0]] + [zeros] * (section_count - 1))]
  transfers between devices with their start and end apart: 4 -> 8, of which waited for: 2 -> 8; matrix products, arithmetic and copies ran while one was open for 18% -> 3% of each run, Pallas kernels for 0% -> 0%
where the time goes in v4:
time: 179 us; the launch traced here: 178 us
  waiting for transfers between devices  62.5 us (35%)
  blocking collectives  35.9 us (20%)
  starting transfers between devices  32.9 us (18%)
  local copies, waits for them, and re-layouts  28.1 us (16%)
  Pallas kernels  16.6 us (9%)
    all_to_all x7, waiting for transfers between devices, exchange(): lax.all_to_all(value, ('pipe', 'seq'), 0, 0, axis_index_groups=peers)  59.3 us
    all_to_all x3, blocking collectives, exchange(): lax.all_to_all(value, ('pipe', 'seq'), 0, 0, axis_index_groups=peers)  35.9 us
    all_to_all x7, starting transfers between devices, exchange(): lax.all_to_all(value, ('pipe', 'seq'), 0, 0, axis_index_groups=peers)  29.5 us
    unnamed x27, local copies, waits for them, and re-layouts  20.5 us
    pallas_call x5, Pallas kernels, attend(): pl.pallas_call(functools.partial(section_kernel, (patches, tok_dev, group...  16.6 us
    broadcast_in_dim x5, local copies, waits for them, and re-layouts, local(): jnp.broadcast_to(streams[:, None], (section_count, slice_count, block_row...  3.65 us
  transfers between devices with their start and end apart: 8, of which 8 were waited for; matrix products, arithmetic and copies ran while one was open for 3% of the time, Pallas kernels for 0%

profile of v4, /device:TPU:0, one launch (start us, length us, event | category | flops | bytes accessed | tf_op | source)
XLA Modules:
  0.0 178.1 jit_solution(14044439265183257197)
XLA Ops:
  0.8 0.7 constant_dynamic-slice_fusion.2
  1.6 0.7 broadcast_in_dim.16
  2.4 8.3 %all-to-all-start = ((bf16[16,16,512]{2,1,0:T(8,128)(2,1)}), bf16[16,16,512]{2,1,0:T(8,128)(2,1)S(1)}, u32[]{:S(2)}, u32[]{:S(2)}) async-start(bf16[16,16,512]{2,1,0:T(8,128)(2,1)} %bitcast.2), calls=%async_computation | async-start | bytes 524288 | tf_op jit(solution)/shard_map/all_to_all | solution.py:154
  10.7 0.8 copy.15
  11.5 9.7 %all-to-all-done = bf16[16,16,512]{2,1,0:T(8,128)(2,1)S(1)} async-done(((bf16[16,16,512]{2,1,0:T(8,128)(2,1)}), bf16[16,16,512]{2,1,0:T(8,128)(2,1)S(1)}, u32[]{:S(2)}, u32[]{:S(2)}) %all-to-all-start) | async-done | bytes 262176 | tf_op jit(solution)/shard_map/all_to_all | solution.py:154
  21.3 2.8 %copy-done = bf16[1,2048,1536]{2,1,0:T(8,128)(2,1)S(1)} copy-done((bf16[1,2048,1536]{2,1,0:T(8,128)(2,1)S(1)}, bf16[1,2048,1536]{2,1,0:T(8,128)(2,1)}, u32[]{:S(2)}) %copy-start) | copy-done | bytes 6291480
  24.1 1.6 copy-done.5
  25.6 0.9 copy-done.7
  26.6 0.7 copy-done.9
  27.3 3.1 %shard_map.77 = (bf16[4,4,16,512]{3,2,1,0:T(8,128)(2,1)S(1)}, bf16[2,64,512]{2,1,0:T(8,128)(2,1)S(1)}) custom-call(s32[2]{0:T(128)S(1)} %pad_add_fusion.4.where_ref, bf16[4,4,16,512]{3,2,1,0:T(8,128)(2,1)S(1)} %bitcast.105, f32[3,2048]{1,0:T(4,128)S(1)} %bitcast.97, bf16[2048,1536]{1,0:T(8,128)(2,1)S(1)} %bitcast.82, bf16[512,2048]{1,0:T(8,128)(2,1)S(1)} %bitcast.87, ...), custom_call_target="tpu_custom_call" | custom-call | tf_op jit(solution)/shard_map/pallas_call | solution.py:162
  30.3 12.6 %all_to_all.55 = bf16[16,16,512]{2,1,0:T(8,128)(2,1)S(1)} all-to-all(bf16[16,16,512]{2,1,0:T(8,128)(2,1)S(1)} %bitcast.107), channel_id=1, replica_groups=mesh['cfg'=2,'pipe'=4,'seq'=4] {'pipe','seq'}, dimensions={0} | all-to-all | bytes 524288 | tf_op jit(solution)/shard_map/all_to_all | solution.py:154
  43.0 0.7 broadcast_in_dim.17
  43.8 3.5 %all-to-all-start.2 = ((bf16[16,16,512]{2,1,0:T(8,128)(2,1)}), bf16[16,16,512]{2,1,0:T(8,128)(2,1)S(1)}, u32[]{:S(2)}, u32[]{:S(2)}) async-start(bf16[16,16,512]{2,1,0:T(8,128)(2,1)} %bitcast.11), calls=%async_computation.2 | async-start | bytes 524288 | tf_op jit(solution)/shard_map/all_to_all | solution.py:154
  47.4 9.1 %all-to-all-done.2 = bf16[16,16,512]{2,1,0:T(8,128)(2,1)S(1)} async-done(((bf16[16,16,512]{2,1,0:T(8,128)(2,1)}), bf16[16,16,512]{2,1,0:T(8,128)(2,1)S(1)}, u32[]{:S(2)}, u32[]{:S(2)}) %all-to-all-start.2) | async-done | bytes 262176 | tf_op jit(solution)/shard_map/all_to_all | solution.py:154
  56.5 2.8 %copy-done.1 = bf16[1,2048,1536]{2,1,0:T(8,128)(2,1)S(1)} copy-done((bf16[1,2048,1536]{2,1,0:T(8,128)(2,1)S(1)}, bf16[1,2048,1536]{2,1,0:T(8,128)(2,1)}, u32[]{:S(2)}) %copy-start.1) | copy-done | bytes 6291480
  59.2 3.0 %shard_map.78 = (bf16[4,4,16,512]{3,2,1,0:T(8,128)(2,1)S(1)}, bf16[2,64,512]{2,1,0:T(8,128)(2,1)S(1)}) custom-call(s32[2]{0:T(128)S(1)} %pad_add_fusion.3.where_ref, bf16[4,4,16,512]{3,2,1,0:T(8,128)(2,1)S(1)} %bitcast.103, f32[3,2048]{1,0:T(4,128)S(1)} %bitcast.98, bf16[2048,1536]{1,0:T(8,128)(2,1)S(1)} %bitcast.83, bf16[512,2048]{1,0:T(8,128)(2,1)S(1)} %bitcast.88, ...), custom_call_target="tpu_custom_call" | custom-call | tf_op jit(solution)/shard_map/pallas_call | solution.py:162
  62.3 11.5 %all_to_all.56 = bf16[16,16,512]{2,1,0:T(8,128)(2,1)S(1)} all-to-all(bf16[16,16,512]{2,1,0:T(8,128)(2,1)S(1)} %bitcast.108), channel_id=1, replica_groups=mesh['cfg'=2,'pipe'=4,'seq'=4] {'pipe','seq'}, dimensions={0} | all-to-all | bytes 524288 | tf_op jit(solution)/shard_map/all_to_all | solution.py:154
  73.8 0.7 broadcast_in_dim.18
  74.6 3.5 %all-to-all-start.4 = ((bf16[16,16,512]{2,1,0:T(8,128)(2,1)}), bf16[16,16,512]{2,1,0:T(8,128)(2,1)S(1)}, u32[]{:S(2)}, u32[]{:S(2)}) async-start(bf16[16,16,512]{2,1,0:T(8,128)(2,1)} %bitcast.16), calls=%async_computation.4 | async-start | bytes 524288 | tf_op jit(solution)/shard_map/all_to_all | solution.py:154
  78.2 8.7 %all-to-all-done.4 = bf16[16,16,512]{2,1,0:T(8,128)(2,1)S(1)} async-done(((bf16[16,16,512]{2,1,0:T(8,128)(2,1)}), bf16[16,16,512]{2,1,0:T(8,128)(2,1)S(1)}, u32[]{:S(2)}, u32[]{:S(2)}) %all-to-all-start.4) | async-done | bytes 262176 | tf_op jit(solution)/shard_map/all_to_all | solution.py:154
  86.9 2.8 %copy-done.2 = bf16[1,2048,1536]{2,1,0:T(8,128)(2,1)S(1)} copy-done((bf16[1,2048,1536]{2,1,0:T(8,128)(2,1)S(1)}, bf16[1,2048,1536]{2,1,0:T(8,128)(2,1)}, u32[]{:S(2)}) %copy-start.2) | copy-done | bytes 6291480
  89.7 3.0 %shard_map.79 = (bf16[4,4,16,512]{3,2,1,0:T(8,128)(2,1)S(1)}, bf16[2,64,512]{2,1,0:T(8,128)(2,1)S(1)}) custom-call(s32[2]{0:T(128)S(1)} %pad_add_fusion.2.where_ref, bf16[4,4,16,512]{3,2,1,0:T(8,128)(2,1)S(1)} %bitcast.106, f32[3,2048]{1,0:T(4,128)S(1)} %bitcast.99, bf16[2048,1536]{1,0:T(8,128)(2,1)S(1)} %bitcast.84, bf16[512,2048]{1,0:T(8,128)(2,1)S(1)} %bitcast.89, ...), custom_call_target="tpu_custom_call" | custom-call | tf_op jit(solution)/shard_map/pallas_call | solution.py:162
  92.7 11.8 %all_to_all.57 = bf16[16,16,512]{2,1,0:T(8,128)(2,1)S(1)} all-to-all(bf16[16,16,512]{2,1,0:T(8,128)(2,1)S(1)} %bitcast.109), channel_id=1, replica_groups=mesh['cfg'=2,'pipe'=4,'seq'=4] {'pipe','seq'}, dimensions={0} | all-to-all | bytes 524288 | tf_op jit(solution)/shard_map/all_to_all | solution.py:154
  104.6 0.7 broadcast_in_dim.19
  105.3 3.5 %all-to-all-start.6 = ((bf16[16,16,512]{2,1,0:T(8,128)(2,1)}), bf16[16,16,512]{2,1,0:T(8,128)(2,1)S(1)}, u32[]{:S(2)}, u32[]{:S(2)}) async-start(bf16[16,16,512]{2,1,0:T(8,128)(2,1)} %bitcast.21), calls=%async_computation.6 | async-start | bytes 524288 | tf_op jit(solution)/shard_map/all_to_all | solution.py:154
  108.9 8.7 %all-to-all-done.6 = bf16[16,16,512]{2,1,0:T(8,128)(2,1)S(1)} async-done(((bf16[16,16,512]{2,1,0:T(8,128)(2,1)}), bf16[16,16,512]{2,1,0:T(8,128)(2,1)S(1)}, u32[]{:S(2)}, u32[]{:S(2)}) %all-to-all-start.6) | async-done | bytes 262176 | tf_op jit(solution)/shard_map/all_to_all | solution.py:154
  117.7 2.8 %copy-done.3 = bf16[1,2048,1536]{2,1,0:T(8,128)(2,1)S(1)} copy-done((bf16[1,2048,1536]{2,1,0:T(8,128)(2,1)S(1)}, bf16[1,2048,1536]{2,1,0:T(8,128)(2,1)}, u32[]{:S(2)}) %copy-start.3) | copy-done | bytes 6291480
  120.4 3.7 %shard_map.80 = (bf16[4,4,16,512]{3,2,1,0:T(8,128)(2,1)}, bf16[2,64,512]{2,1,0:T(8,128)(2,1)S(1)}) custom-call(s32[2]{0:T(128)S(1)} %pad_add_fusion.1.where_ref, bf16[4,4,16,512]{3,2,1,0:T(8,128)(2,1)S(1)} %bitcast.104, f32[3,2048]{1,0:T(4,128)S(1)} %bitcast.100, bf16[2048,1536]{1,0:T(8,128)(2,1)S(1)} %bitcast.85, bf16[512,2048]{1,0:T(8,128)(2,1)S(1)} %bitcast.90, ...), custom_call_target="tpu_custom_call" | custom-call | tf_op jit(solution)/shard_map/pallas_call | solution.py:162
  124.2 3.5 %all-to-all-start.7 = ((bf16[16,16,512]{2,1,0:T(8,128)(2,1)}), bf16[16,16,512]{2,1,0:T(8,128)(2,1)S(1)}, u32[]{:S(2)}, u32[]{:S(2)}) async-start(bf16[16,16,512]{2,1,0:T(8,128)(2,1)} %bitcast.23), calls=%async_computation.7 | async-start | bytes 524288 | tf_op jit(solution)/shard_map/all_to_all | solution.py:154
  127.7 8.9 %all-to-all-done.7 = bf16[16,16,512]{2,1,0:T(8,128)(2,1)S(1)} async-done(((bf16[16,16,512]{2,1,0:T(8,128)(2,1)}), bf16[16,16,512]{2,1,0:T(8,128)(2,1)S(1)}, u32[]{:S(2)}, u32[]{:S(2)}) %all-to-all-start.7) | async-done | bytes 262176 | tf_op jit(solution)/shard_map/all_to_all | solution.py:154
  136.7 0.7 broadcast_in_dim.20
  137.4 3.5 %all-to-all-start.8 = ((bf16[16,16,512]{2,1,0:T(8,128)(2,1)}), bf16[16,16,512]{2,1,0:T(8,128)(2,1)S(1)}, u32[]{:S(2)}, u32[]{:S(2)}) async-start(bf16[16,16,512]{2,1,0:T(8,128)(2,1)} %bitcast.26), calls=%async_computation.8 | async-start | bytes 524288 | tf_op jit(solution)/shard_map/all_to_all | solution.py:154
  141.0 0.7 bitcast_dynamic-update-slice_fusion.4
  141.7 0.7 bitcast_dynamic-update-slice_fusion.3
  142.4 7.4 %all-to-all-done.8 = bf16[16,16,512]{2,1,0:T(8,128)(2,1)S(1)} async-done(((bf16[16,16,512]{2,1,0:T(8,128)(2,1)}), bf16[16,16,512]{2,1,0:T(8,128)(2,1)S(1)}, u32[]{:S(2)}, u32[]{:S(2)}) %all-to-all-start.8) | async-done | bytes 262176 | tf_op jit(solution)/shard_map/all_to_all | solution.py:154
  149.8 2.8 %copy-done.4 = bf16[1,2048,1536]{2,1,0:T(8,128)(2,1)S(1)} copy-done((bf16[1,2048,1536]{2,1,0:T(8,128)(2,1)S(1)}, bf16[1,2048,1536]{2,1,0:T(8,128)(2,1)}, u32[]{:S(2)}) %copy-start.4) | copy-done | bytes 6291480
  152.5 3.7 %shard_map.81 = (bf16[4,4,16,512]{3,2,1,0:T(8,128)(2,1)}, bf16[2,64,512]{2,1,0:T(8,128)(2,1)S(1)}) custom-call(s32[2]{0:T(128)S(1)} %pad_add_fusion.where_ref, bf16[4,4,16,512]{3,2,1,0:T(8,128)(2,1)S(1)} %bitcast.102, f32[3,2048]{1,0:T(4,128)S(1)} %bitcast.101, bf16[2048,1536]{1,0:T(8,128)(2,1)S(1)} %bitcast.86, bf16[512,2048]{1,0:T(8,128)(2,1)S(1)} %bitcast.91, ...), custom_call_target="tpu_custom_call" | custom-call | tf_op jit(solution)/shard_map/pallas_call | solution.py:162
  156.3 3.5 %all-to-all-start.9 = ((bf16[16,16,512]{2,1,0:T(8,128)(2,1)}), bf16[16,16,512]{2,1,0:T(8,128)(2,1)S(1)}, u32[]{:S(2)}, u32[]{:S(2)}) async-start(bf16[16,16,512]{2,1,0:T(8,128)(2,1)} %bitcast.28), calls=%async_computation.9 | async-start | bytes 524288 | tf_op jit(solution)/shard_map/all_to_all | solution.py:154
  159.8 0.6 bitcast_dynamic-update-slice_fusion.2
  160.5 0.7 bitcast_dynamic-update-slice_fusion.1
  161.1 0.7 bitcast_dynamic-update-slice_fusion
  161.8 6.8 %all-to-all-done.9 = bf16[16,16,512]{2,1,0:T(8,128)(2,1)S(1)} async-done(((bf16[16,16,512]{2,1,0:T(8,128)(2,1)}), bf16[16,16,512]{2,1,0:T(8,128)(2,1)S(1)}, u32[]{:S(2)}, u32[]{:S(2)}) %all-to-all-start.9) | async-done | bytes 262176 | tf_op jit(solution)/shard_map/all_to_all | solution.py:154
  168.7 0.6 broadcast_in_dim.22
  169.3 3.3 %all-to-all-start.10 = ((bf16[8,1,8,512]{3,2,1,0:T(8,128)(2,1)}), bf16[8,1,8,512]{3,2,1,0:T(8,128)(2,1)S(1)}, u32[]{:S(2)}, u32[]{:S(2)}) async-start(bf16[8,1,8,512]{3,2,1,0:T(8,128)(2,1)} %bitcast.31), calls=%async_computation.10 | async-start | bytes 131072 | tf_op jit(solution)/shard_map/all_to_all | solution.py:211
  172.7 1.0 constant_dynamic-slice_fusion.1
  173.6 0.7 copy.11
  174.4 3.1 %all-to-all-done.10 = bf16[8,1,8,512]{3,2,1,0:T(8,128)(2,1)S(1)} async-done(((bf16[8,1,8,512]{3,2,1,0:T(8,128)(2,1)}), bf16[8,1,8,512]{3,2,1,0:T(8,128)(2,1)S(1)}, u32[]{:S(2)}, u32[]{:S(2)}) %all-to-all-start.10) | async-done | bytes 65568 | tf_op jit(solution)/shard_map/all_to_all | solution.py:211
  177.5 0.6 fusion.7
  (41 shorter events, 0.9 us)
Async XLA Ops:
  0.6 55.8 %copy-start.10 = (f32[1,2,128]{2,1,0:T(2,128)S(1)}, f32[1,2,128]{2,1,0:T(2,128)}, u32[]{:S(2)}) copy-start(f32[1,2,128]{2,1,0:T(2,128)} %param.10) | copy-start | bytes 3076
  0.6 55.8 %copy-start.8 = (bf16[1,1,2,4,1,4,8,512]{7,6,5,4,3,2,1,0:T(8,128)(2,1)S(1)}, bf16[1,1,2,4,1,4,8,512]{7,6,5,4,3,2,1,0:T(8,128)(2,1)}, u32[]{:S(2)}) copy-start(bf16[1,1,2,4,1,4,8,512]{7,6,5,4,3,2,1,0:T(8,128)(2,1)} %param.11) | copy-start | bytes 786436
  2.4 18.9 %all-to-all-start = ((bf16[16,16,512]{2,1,0:T(8,128)(2,1)}), bf16[16,16,512]{2,1,0:T(8,128)(2,1)S(1)}, u32[]{:S(2)}, u32[]{:S(2)}) async-start(bf16[16,16,512]{2,1,0:T(8,128)(2,1)} %bitcast.2), calls=%async_computation | async-start | bytes 524288 | tf_op jit(solution)/shard_map/all_to_all | solution.py:154
  21.3 2.8 %copy-start = (bf16[1,2048,1536]{2,1,0:T(8,128)(2,1)S(1)}, bf16[1,2048,1536]{2,1,0:T(8,128)(2,1)}, u32[]{:S(2)}) copy-start(bf16[1,2048,1536]{2,1,0:T(8,128)(2,1)} %param.8) | copy-start | bytes 18874372
  24.1 1.6 copy-start.5
  25.6 0.9 copy-start.7
  26.6 0.7 copy-start.9
  27.3 29.2 %copy-start.6 = (bf16[1,512,2048]{2,1,0:T(8,128)(2,1)S(1)}, bf16[1,512,2048]{2,1,0:T(8,128)(2,1)}, u32[]{:S(2)}) copy-start(bf16[1,512,2048]{2,1,0:T(8,128)(2,1)} %param.9) | copy-start | bytes 6291460
  43.8 12.7 %all-to-all-start.2 = ((bf16[16,16,512]{2,1,0:T(8,128)(2,1)}), bf16[16,16,512]{2,1,0:T(8,128)(2,1)S(1)}, u32[]{:S(2)}, u32[]{:S(2)}) async-start(bf16[16,16,512]{2,1,0:T(8,128)(2,1)} %bitcast.11), calls=%async_computation.2 | async-start | bytes 524288 | tf_op jit(solution)/shard_map/all_to_all | solution.py:154
  56.5 2.8 %copy-start.1 = (bf16[1,2048,1536]{2,1,0:T(8,128)(2,1)S(1)}, bf16[1,2048,1536]{2,1,0:T(8,128)(2,1)}, u32[]{:S(2)}) copy-start(bf16[1,2048,1536]{2,1,0:T(8,128)(2,1)} %param.8) | copy-start | bytes 18874372
  74.6 12.3 %all-to-all-start.4 = ((bf16[16,16,512]{2,1,0:T(8,128)(2,1)}), bf16[16,16,512]{2,1,0:T(8,128)(2,1)S(1)}, u32[]{:S(2)}, u32[]{:S(2)}) async-start(bf16[16,16,512]{2,1,0:T(8,128)(2,1)} %bitcast.16), calls=%async_computation.4 | async-start | bytes 524288 | tf_op jit(solution)/shard_map/all_to_all | solution.py:154
  86.9 2.8 %copy-start.2 = (bf16[1,2048,1536]{2,1,0:T(8,128)(2,1)S(1)}, bf16[1,2048,1536]{2,1,0:T(8,128)(2,1)}, u32[]{:S(2)}) copy-start(bf16[1,2048,1536]{2,1,0:T(8,128)(2,1)} %param.8) | copy-start | bytes 18874372
  105.3 12.3 %all-to-all-start.6 = ((bf16[16,16,512]{2,1,0:T(8,128)(2,1)}), bf16[16,16,512]{2,1,0:T(8,128)(2,1)S(1)}, u32[]{:S(2)}, u32[]{:S(2)}) async-start(bf16[16,16,512]{2,1,0:T(8,128)(2,1)} %bitcast.21), calls=%async_computation.6 | async-start | bytes 524288 | tf_op jit(solution)/shard_map/all_to_all | solution.py:154
  117.6 2.8 %copy-start.3 = (bf16[1,2048,1536]{2,1,0:T(8,128)(2,1)S(1)}, bf16[1,2048,1536]{2,1,0:T(8,128)(2,1)}, u32[]{:S(2)}) copy-start(bf16[1,2048,1536]{2,1,0:T(8,128)(2,1)} %param.8) | copy-start | bytes 18874372
  124.2 12.4 %all-to-all-start.7 = ((bf16[16,16,512]{2,1,0:T(8,128)(2,1)}), bf16[16,16,512]{2,1,0:T(8,128)(2,1)S(1)}, u32[]{:S(2)}, u32[]{:S(2)}) async-start(bf16[16,16,512]{2,1,0:T(8,128)(2,1)} %bitcast.23), calls=%async_computation.7 | async-start | bytes 524288 | tf_op jit(solution)/shard_map/all_to_all | solution.py:154
  137.4 12.3 %all-to-all-start.8 = ((bf16[16,16,512]{2,1,0:T(8,128)(2,1)}), bf16[16,16,512]{2,1,0:T(8,128)(2,1)S(1)}, u32[]{:S(2)}, u32[]{:S(2)}) async-start(bf16[16,16,512]{2,1,0:T(8,128)(2,1)} %bitcast.26), calls=%async_computation.8 | async-start | bytes 524288 | tf_op jit(solution)/shard_map/all_to_all | solution.py:154
  149.8 2.8 %copy-start.4 = (bf16[1,2048,1536]{2,1,0:T(8,128)(2,1)S(1)}, bf16[1,2048,1536]{2,1,0:T(8,128)(2,1)}, u32[]{:S(2)}) copy-start(bf16[1,2048,1536]{2,1,0:T(8,128)(2,1)} %param.8) | copy-start | bytes 18874372
  156.3 12.3 %all-to-all-start.9 = ((bf16[16,16,512]{2,1,0:T(8,128)(2,1)}), bf16[16,16,512]{2,1,0:T(8,128)(2,1)S(1)}, u32[]{:S(2)}, u32[]{:S(2)}) async-start(bf16[16,16,512]{2,1,0:T(8,128)(2,1)} %bitcast.28), calls=%async_computation.9 | async-start | bytes 524288 | tf_op jit(solution)/shard_map/all_to_all | solution.py:154
  169.3 8.2 %all-to-all-start.10 = ((bf16[8,1,8,512]{3,2,1,0:T(8,128)(2,1)}), bf16[8,1,8,512]{3,2,1,0:T(8,128)(2,1)S(1)}, u32[]{:S(2)}, u32[]{:S(2)}) async-start(bf16[8,1,8,512]{3,2,1,0:T(8,128)(2,1)} %bitcast.31), calls=%async_computation.10 | async-start | bytes 131072 | tf_op jit(solution)/shard_map/all_to_all | solution.py:211

commit v5 on v4

--- a/solution.py
+++ b/solution.py
@@ -104,6 +104,35 @@
         )
 
 
+def load_kernel(qkv_ref, out_ref, qkv_to, out_to, sems):
+    copies = (
+        pltpu.make_async_copy(qkv_ref, qkv_to, sems.at[0]),
+        pltpu.make_async_copy(out_ref, out_to, sems.at[1]),
+    )
+    for copy in copies:
+        copy.start()
+    for copy in copies:
+        copy.wait()
+
+
+def settle_kernel(parts_ref, streams_ref, entering_ref, streams_to, spread_to, last_to):
+    count, slices = parts_ref.shape[:2]
+    for section in range(count):
+        total = streams_ref[section].astype(jnp.float32)
+        for piece in range(slices):
+            total = total + parts_ref[section, piece].astype(jnp.float32)
+        total = total.astype(jnp.bfloat16)
+        if section == count - 1:
+            last_to[...] = total
+        else:
+            streams_to[section + 1] = total
+            for piece in range(slices):
+                spread_to[section + 1, piece] = total
+    streams_to[0] = entering_ref[...]
+    for piece in range(slices):
+        spread_to[0, piece] = entering_ref[...]
+
+
 def local(latent, modulation, qkv_weight, out_weight, norm_gain, stale_kv):
     seq_count = lax.axis_size("seq")
     seq_rank = lax.axis_index("seq")
@@ -154,11 +183,24 @@
         value = lax.all_to_all(value, ("pipe", "seq"), 0, 0, axis_index_groups=peers)
         return value.reshape(section_count, slice_count, block_rows, block_cols)
 
+    vmem = pl.BlockSpec(memory_space=pltpu.VMEM)
     in_vmem = functools.partial(pltpu.with_memory_space_constraint, memory_space=pltpu.VMEM)
-    qkv_slice, out_slice = in_vmem(qkv_slice), in_vmem(out_slice)
+    qkv_slice, out_slice = pl.pallas_call(
+        load_kernel,
+        out_shape=(
+            pltpu.VMEM(qkv_slice.shape, jnp.bfloat16),
+            pltpu.VMEM(out_slice.shape, jnp.bfloat16),
+        ),
+        in_specs=[pl.BlockSpec(memory_space=pltpu.HBM)] * 2,
+        out_specs=(vmem, vmem),
+        scratch_shapes=[pltpu.SemaphoreType.DMA((2,))],
+        compiler_params=pltpu.CompilerParams(vmem_limit_bytes=1024 * 1024),
+        cost_estimate=pl.CostEstimate(
+            flops=0, bytes_accessed=4 * (qkv_slice.size + out_slice.size), transcendentals=0
+        ),
+    )(*(pltpu.with_memory_space_constraint(w, pltpu.HBM) for w in (qkv_slice, out_slice)))
 
     def attend(group, features, prev):
-        vmem = pl.BlockSpec(memory_space=pltpu.VMEM)
         return pl.pallas_call(
             functools.partial(section_kernel, (patches, tok_dev, group_rows, head_dim)),
             out_shape=(
@@ -172,8 +214,8 @@
             jnp.stack((group, own_member)).astype(jnp.int32),
             features,
             modulation[0, 0],
-            qkv_slice,
-            out_slice,
+            in_vmem(qkv_slice),
+            in_vmem(out_slice),
             norm_gain[0],
             stale_rows,
             *prev,
@@ -182,24 +224,33 @@
     sources = lax.dynamic_slice_in_dim(
         latent.reshape(GROUPS, block_rows, model_width), section_rank * block_cols, block_cols, 2
     )
+    spread_shape = (section_count, slice_count, block_rows, block_cols)
     zeros = jnp.zeros_like(sources[0])
     streams = jnp.stack([sources[0]] + [zeros] * (section_count - 1))
+    spread = jnp.broadcast_to(streams[:, None], spread_shape)
+
+    def settle(parts, streams, entering):
+        return pl.pallas_call(
+            settle_kernel,
+            out_shape=tuple(
+                jax.ShapeDtypeStruct(shape, jnp.bfloat16)
+                for shape in (streams.shape, spread_shape, entering.shape)
+            ),
+            in_specs=[vmem] * 3,
+            out_specs=(vmem,) * 3,
+            compiler_params=pltpu.CompilerParams(vmem_limit_bytes=8 * 1024 * 1024),
+        )(parts, streams, entering)
+
     fresh_ticks = []
     finals = []
     for tick in range(GROUPS + section_count - 1):
-        features = exchange(
-            jnp.broadcast_to(
-                streams[:, None], (section_count, slice_count, block_rows, block_cols)
-            )
-        )
+        features = exchange(spread)
         prev = fresh_ticks[-(GROUPS - 1) :] if GROUPS > 1 else []
         partial_out, fresh = attend(tick - section_rank, features, prev)
         fresh_ticks.append(fresh)
-        parts = exchange(partial_out).astype(jnp.float32)
-        results = (streams.astype(jnp.float32) + jnp.sum(parts, axis=1)).astype(jnp.bfloat16)
-        finals.append(results[-1])
         entering = sources[tick + 1] if tick + 1 < GROUPS else zeros
-        streams = jnp.concatenate((entering[None], results[:-1]))
+        streams, spread, last = settle(exchange(partial_out), streams, entering)
+        finals.append(last)
 
     next_cache = lax.dynamic_slice_in_dim(jnp.stack(fresh_ticks), section_rank, GROUPS, 0)
     next_cache = next_cache.reshape(GROUPS, 2, slice_count, in_group, tok_dev, local_width)

time: 179 us -> 177 us (0.989)
  Pallas kernels: 16.6 us -> 23.7 us
  waiting for transfers between devices: 62.5 us -> 56.3 us
  local copies, waits for them, and re-layouts: 28.1 us -> 24.6 us
    pallas_call x0 -> x6, Pallas kernels: none -> 7.16 us  [the longest x5 3.73 us: settle(): pl.pallas_call(settle_kernel, out_shape=tuple((jax.ShapeDtypeStruct(shape...]
    all_to_all x7, waiting for transfers between devices: 59.3 us -> 53.1 us  [exchange(): lax.all_to_all(value, ('pipe', 'seq'), 0, 0, axis_index_groups=peers)]
    broadcast_in_dim x5 -> x2, local copies, waits for them, and re-layouts: 3.65 us -> 0.74 us  [the longest x1 0.73 us: local(): spread = jnp.broadcast_to(streams[:, None], spread_shape)]
    unnamed x27 -> x21, local copies, waits for them, and re-layouts: 20.5 us -> 20 us
  transfers between devices with their start and end apart: 8 -> 8, of which waited for: 8 -> 8; matrix products, arithmetic and copies ran while one was open for 3% -> 3% of each run, Pallas kernels for 0% -> 2%
where the time goes in v5:
time: 177 us; the launch traced here: 176 us
  waiting for transfers between devices  56.3 us (32%)
  blocking collectives  36.4 us (21%)
  starting transfers between devices  32.9 us (19%)
  local copies, waits for them, and re-layouts  24.6 us (14%)
  Pallas kernels  23.7 us (13%)
    all_to_all x7, waiting for transfers between devices, exchange(): lax.all_to_all(value, ('pipe', 'seq'), 0, 0, axis_index_groups=peers)  53.1 us
    all_to_all x3, blocking collectives, exchange(): lax.all_to_all(value, ('pipe', 'seq'), 0, 0, axis_index_groups=peers)  36.4 us
    all_to_all x7, starting transfers between devices, exchange(): lax.all_to_all(value, ('pipe', 'seq'), 0, 0, axis_index_groups=peers)  29.5 us
    unnamed x21, local copies, waits for them, and re-layouts  20 us
    pallas_call x5, Pallas kernels, attend(): pl.pallas_call(functools.partial(section_kernel, (patches, tok_dev, group...  16.6 us
    pallas_call x5, Pallas kernels, settle(): pl.pallas_call(settle_kernel, out_shape=tuple((jax.ShapeDtypeStruct(shape...  3.73 us
  transfers between devices with their start and end apart: 8, of which 8 were waited for; matrix products, arithmetic and copies ran while one was open for 3% of the time, Pallas kernels for 2%

profile of v5, /device:TPU:0, one launch (start us, length us, event | category | flops | bytes accessed | tf_op | source)
XLA Modules:
  0.0 175.7 jit_solution(12200409109307945209)
XLA Ops:
  0.8 0.7 dynamic-slice_bitcast_fusion
  1.6 0.7 broadcast_in_dim.18
  2.4 8.3 %all-to-all-start = ((bf16[16,16,512]{2,1,0:T(8,128)(2,1)}), bf16[16,16,512]{2,1,0:T(8,128)(2,1)S(1)}, u32[]{:S(2)}, u32[]{:S(2)}) async-start(bf16[16,16,512]{2,1,0:T(8,128)(2,1)} %bitcast.5), calls=%async_computation | async-start | bytes 524288 | tf_op jit(solution)/shard_map/all_to_all | solution.py:183
  10.7 0.8 copy.15
  11.4 3.4 %shard_map.77 = (bf16[2048,1536]{1,0:T(8,128)(2,1)S(1)}, bf16[512,2048]{1,0:T(8,128)(2,1)S(1)}) custom-call(bf16[2048,1536]{1,0:T(8,128)(2,1)} %bitcast.106, bf16[512,2048]{1,0:T(8,128)(2,1)} %bitcast.107), custom_call_target="tpu_custom_call" | custom-call | bytes 16777216 | tf_op jit(solution)/shard_map/pallas_call | solution.py:188
  14.9 2.6 %copy-done = bf16[2048,1536]{1,0:T(8,128)(2,1)} copy-done((bf16[2048,1536]{1,0:T(8,128)(2,1)}, bf16[2048,1536]{1,0:T(8,128)(2,1)S(1)}, u32[]{:S(2)}) %copy-start) | copy-done | bytes 6291480
  17.6 3.7 %all-to-all-done = bf16[16,16,512]{2,1,0:T(8,128)(2,1)S(1)} async-done(((bf16[16,16,512]{2,1,0:T(8,128)(2,1)}), bf16[16,16,512]{2,1,0:T(8,128)(2,1)S(1)}, u32[]{:S(2)}, u32[]{:S(2)}) %all-to-all-start) | async-done | bytes 262176 | tf_op jit(solution)/shard_map/all_to_all | solution.py:183
  21.3 2.8 %copy-done.1 = bf16[2048,1536]{1,0:T(8,128)(2,1)S(1)} copy-done((bf16[2048,1536]{1,0:T(8,128)(2,1)S(1)}, bf16[2048,1536]{1,0:T(8,128)(2,1)}, u32[]{:S(2)}) %copy-start.1) | copy-done | bytes 6291480
  24.1 3.0 %shard_map.78 = (bf16[4,4,16,512]{3,2,1,0:T(8,128)(2,1)S(1)}, bf16[2,64,512]{2,1,0:T(8,128)(2,1)S(1)}) custom-call(s32[2]{0:T(128)S(1)} %pad_add_fusion.1.where_ref, bf16[4,4,16,512]{3,2,1,0:T(8,128)(2,1)S(1)} %bitcast.87, f32[3,2048]{1,0:T(4,128)S(1)} %bitcast.81, bf16[2048,1536]{1,0:T(8,128)(2,1)S(1)} %copy-done.1, ...), custom_call_target="tpu_custom_call" | custom-call | tf_op jit(solution)/shard_map/pallas_call | solution.py:204
  27.1 13.1 %all_to_all.55 = bf16[16,16,512]{2,1,0:T(8,128)(2,1)S(1)} all-to-all(bf16[16,16,512]{2,1,0:T(8,128)(2,1)S(1)} %bitcast.96), channel_id=1, replica_groups=mesh['cfg'=2,'pipe'=4,'seq'=4] {'pipe','seq'}, dimensions={0} | all-to-all | bytes 524288 | tf_op jit(solution)/shard_map/all_to_all | solution.py:183
  40.2 0.7 shard_map.79
  40.9 3.5 %all-to-all-start.2 = ((bf16[16,16,512]{2,1,0:T(8,128)(2,1)}), bf16[16,16,512]{2,1,0:T(8,128)(2,1)S(1)}, u32[]{:S(2)}, u32[]{:S(2)}) async-start(bf16[16,16,512]{2,1,0:T(8,128)(2,1)} %bitcast.14), calls=%async_computation.2 | async-start | bytes 524288 | tf_op jit(solution)/shard_map/all_to_all | solution.py:183
  44.5 9.1 %all-to-all-done.2 = bf16[16,16,512]{2,1,0:T(8,128)(2,1)S(1)} async-done(((bf16[16,16,512]{2,1,0:T(8,128)(2,1)}), bf16[16,16,512]{2,1,0:T(8,128)(2,1)S(1)}, u32[]{:S(2)}, u32[]{:S(2)}) %all-to-all-start.2) | async-done | bytes 262176 | tf_op jit(solution)/shard_map/all_to_all | solution.py:183
  53.6 2.8 %copy-done.2 = bf16[2048,1536]{1,0:T(8,128)(2,1)S(1)} copy-done((bf16[2048,1536]{1,0:T(8,128)(2,1)S(1)}, bf16[2048,1536]{1,0:T(8,128)(2,1)}, u32[]{:S(2)}) %copy-start.2) | copy-done | bytes 6291480
  56.4 3.0 %shard_map.80 = (bf16[4,4,16,512]{3,2,1,0:T(8,128)(2,1)S(1)}, bf16[2,64,512]{2,1,0:T(8,128)(2,1)S(1)}) custom-call(s32[2]{0:T(128)S(1)} %pad_add_fusion.2.where_ref, bf16[4,4,16,512]{3,2,1,0:T(8,128)(2,1)S(1)} %bitcast.88, f32[3,2048]{1,0:T(4,128)S(1)} %bitcast.82, bf16[2048,1536]{1,0:T(8,128)(2,1)S(1)} %copy-done.2, ...), custom_call_target="tpu_custom_call" | custom-call | tf_op jit(solution)/shard_map/pallas_call | solution.py:204
  59.4 11.5 %all_to_all.56 = bf16[16,16,512]{2,1,0:T(8,128)(2,1)S(1)} all-to-all(bf16[16,16,512]{2,1,0:T(8,128)(2,1)S(1)} %bitcast.97), channel_id=1, replica_groups=mesh['cfg'=2,'pipe'=4,'seq'=4] {'pipe','seq'}, dimensions={0} | all-to-all | bytes 524288 | tf_op jit(solution)/shard_map/all_to_all | solution.py:183
  70.9 0.7 shard_map.81
  71.6 3.5 %all-to-all-start.4 = ((bf16[16,16,512]{2,1,0:T(8,128)(2,1)}), bf16[16,16,512]{2,1,0:T(8,128)(2,1)S(1)}, u32[]{:S(2)}, u32[]{:S(2)}) async-start(bf16[16,16,512]{2,1,0:T(8,128)(2,1)} %bitcast.18), calls=%async_computation.4 | async-start | bytes 524288 | tf_op jit(solution)/shard_map/all_to_all | solution.py:183
  75.3 8.7 %all-to-all-done.4 = bf16[16,16,512]{2,1,0:T(8,128)(2,1)S(1)} async-done(((bf16[16,16,512]{2,1,0:T(8,128)(2,1)}), bf16[16,16,512]{2,1,0:T(8,128)(2,1)S(1)}, u32[]{:S(2)}, u32[]{:S(2)}) %all-to-all-start.4) | async-done | bytes 262176 | tf_op jit(solution)/shard_map/all_to_all | solution.py:183
  84.0 2.8 %copy-done.3 = bf16[2048,1536]{1,0:T(8,128)(2,1)S(1)} copy-done((bf16[2048,1536]{1,0:T(8,128)(2,1)S(1)}, bf16[2048,1536]{1,0:T(8,128)(2,1)}, u32[]{:S(2)}) %copy-start.3) | copy-done | bytes 6291480
  86.8 3.0 %shard_map.82 = (bf16[4,4,16,512]{3,2,1,0:T(8,128)(2,1)S(1)}, bf16[2,64,512]{2,1,0:T(8,128)(2,1)S(1)}) custom-call(s32[2]{0:T(128)S(1)} %pad_add_fusion.3.where_ref, bf16[4,4,16,512]{3,2,1,0:T(8,128)(2,1)S(1)} %bitcast.90, f32[3,2048]{1,0:T(4,128)S(1)} %bitcast.83, bf16[2048,1536]{1,0:T(8,128)(2,1)S(1)} %copy-done.3, ...), custom_call_target="tpu_custom_call" | custom-call | tf_op jit(solution)/shard_map/pallas_call | solution.py:204
  89.8 11.8 %all_to_all.57 = bf16[16,16,512]{2,1,0:T(8,128)(2,1)S(1)} all-to-all(bf16[16,16,512]{2,1,0:T(8,128)(2,1)S(1)} %bitcast.98), channel_id=1, replica_groups=mesh['cfg'=2,'pipe'=4,'seq'=4] {'pipe','seq'}, dimensions={0} | all-to-all | bytes 524288 | tf_op jit(solution)/shard_map/all_to_all | solution.py:183
  101.6 0.7 shard_map.83
  102.3 3.5 %all-to-all-start.6 = ((bf16[16,16,512]{2,1,0:T(8,128)(2,1)}), bf16[16,16,512]{2,1,0:T(8,128)(2,1)S(1)}, u32[]{:S(2)}, u32[]{:S(2)}) async-start(bf16[16,16,512]{2,1,0:T(8,128)(2,1)} %bitcast.22), calls=%async_computation.6 | async-start | bytes 524288 | tf_op jit(solution)/shard_map/all_to_all | solution.py:183
  106.0 8.7 %all-to-all-done.6 = bf16[16,16,512]{2,1,0:T(8,128)(2,1)S(1)} async-done(((bf16[16,16,512]{2,1,0:T(8,128)(2,1)}), bf16[16,16,512]{2,1,0:T(8,128)(2,1)S(1)}, u32[]{:S(2)}, u32[]{:S(2)}) %all-to-all-start.6) | async-done | bytes 262176 | tf_op jit(solution)/shard_map/all_to_all | solution.py:183
  114.7 2.8 %copy-done.4 = bf16[2048,1536]{1,0:T(8,128)(2,1)S(1)} copy-done((bf16[2048,1536]{1,0:T(8,128)(2,1)S(1)}, bf16[2048,1536]{1,0:T(8,128)(2,1)}, u32[]{:S(2)}) %copy-start.4) | copy-done | bytes 6291480
  117.5 3.7 %shard_map.84 = (bf16[4,4,16,512]{3,2,1,0:T(8,128)(2,1)}, bf16[2,64,512]{2,1,0:T(8,128)(2,1)S(1)}) custom-call(s32[2]{0:T(128)S(1)} %pad_add_fusion.4.where_ref, bf16[4,4,16,512]{3,2,1,0:T(8,128)(2,1)S(1)} %bitcast.89, f32[3,2048]{1,0:T(4,128)S(1)} %bitcast.84, bf16[2048,1536]{1,0:T(8,128)(2,1)S(1)} %copy-done.4, ...), custom_call_target="tpu_custom_call" | custom-call | tf_op jit(solution)/shard_map/pallas_call | solution.py:204
  121.2 3.5 %all-to-all-start.7 = ((bf16[16,16,512]{2,1,0:T(8,128)(2,1)}), bf16[16,16,512]{2,1,0:T(8,128)(2,1)S(1)}, u32[]{:S(2)}, u32[]{:S(2)}) async-start(bf16[16,16,512]{2,1,0:T(8,128)(2,1)} %bitcast.24), calls=%async_computation.7 | async-start | bytes 524288 | tf_op jit(solution)/shard_map/all_to_all | solution.py:183
  124.7 8.8 %all-to-all-done.7 = bf16[16,16,512]{2,1,0:T(8,128)(2,1)S(1)} async-done(((bf16[16,16,512]{2,1,0:T(8,128)(2,1)}), bf16[16,16,512]{2,1,0:T(8,128)(2,1)S(1)}, u32[]{:S(2)}, u32[]{:S(2)}) %all-to-all-start.7) | async-done | bytes 262176 | tf_op jit(solution)/shard_map/all_to_all | solution.py:183
  133.5 0.7 shard_map.85
  134.3 3.5 %all-to-all-start.8 = ((bf16[16,16,512]{2,1,0:T(8,128)(2,1)}), bf16[16,16,512]{2,1,0:T(8,128)(2,1)S(1)}, u32[]{:S(2)}, u32[]{:S(2)}) async-start(bf16[16,16,512]{2,1,0:T(8,128)(2,1)} %bitcast.28), calls=%async_computation.8 | async-start | bytes 524288 | tf_op jit(solution)/shard_map/all_to_all | solution.py:183
  137.9 0.7 bitcast_dynamic-update-slice_fusion.4
  138.5 0.7 bitcast_dynamic-update-slice_fusion.3
  139.2 7.4 %all-to-all-done.8 = bf16[16,16,512]{2,1,0:T(8,128)(2,1)S(1)} async-done(((bf16[16,16,512]{2,1,0:T(8,128)(2,1)}), bf16[16,16,512]{2,1,0:T(8,128)(2,1)S(1)}, u32[]{:S(2)}, u32[]{:S(2)}) %all-to-all-start.8) | async-done | bytes 262176 | tf_op jit(solution)/shard_map/all_to_all | solution.py:183
  146.6 2.8 %copy-done.5 = bf16[2048,1536]{1,0:T(8,128)(2,1)S(1)} copy-done((bf16[2048,1536]{1,0:T(8,128)(2,1)S(1)}, bf16[2048,1536]{1,0:T(8,128)(2,1)}, u32[]{:S(2)}) %copy-start.5) | copy-done | bytes 6291480
  149.4 3.7 %shard_map.86 = (bf16[4,4,16,512]{3,2,1,0:T(8,128)(2,1)}, bf16[2,64,512]{2,1,0:T(8,128)(2,1)S(1)}) custom-call(s32[2]{0:T(128)S(1)} %pad_add_fusion.where_ref, bf16[4,4,16,512]{3,2,1,0:T(8,128)(2,1)S(1)} %bitcast.86, f32[3,2048]{1,0:T(4,128)S(1)} %bitcast.85, bf16[2048,1536]{1,0:T(8,128)(2,1)S(1)} %copy-done.5, ...), custom_call_target="tpu_custom_call" | custom-call | tf_op jit(solution)/shard_map/pallas_call | solution.py:204
  153.1 3.5 %all-to-all-start.9 = ((bf16[16,16,512]{2,1,0:T(8,128)(2,1)}), bf16[16,16,512]{2,1,0:T(8,128)(2,1)S(1)}, u32[]{:S(2)}, u32[]{:S(2)}) async-start(bf16[16,16,512]{2,1,0:T(8,128)(2,1)} %bitcast.30), calls=%async_computation.9 | async-start | bytes 524288 | tf_op jit(solution)/shard_map/all_to_all | solution.py:183
  156.7 0.7 bitcast_dynamic-update-slice_fusion.2
  157.3 0.7 bitcast_dynamic-update-slice_fusion.1
  158.0 0.7 bitcast_dynamic-update-slice_fusion
  158.6 6.8 %all-to-all-done.9 = bf16[16,16,512]{2,1,0:T(8,128)(2,1)S(1)} async-done(((bf16[16,16,512]{2,1,0:T(8,128)(2,1)}), bf16[16,16,512]{2,1,0:T(8,128)(2,1)S(1)}, u32[]{:S(2)}, u32[]{:S(2)}) %all-to-all-start.9) | async-done | bytes 262176 | tf_op jit(solution)/shard_map/all_to_all | solution.py:183
  165.4 0.8 shard_map.87
  166.2 0.6 broadcast_in_dim.21
  166.8 3.3 %all-to-all-start.10 = ((bf16[8,1,8,512]{3,2,1,0:T(8,128)(2,1)}), bf16[8,1,8,512]{3,2,1,0:T(8,128)(2,1)S(1)}, u32[]{:S(2)}, u32[]{:S(2)}) async-start(bf16[8,1,8,512]{3,2,1,0:T(8,128)(2,1)} %bitcast.34), calls=%async_computation.10 | async-start | bytes 131072 | tf_op jit(solution)/shard_map/all_to_all | solution.py:262
  170.2 1.0 constant_dynamic-slice_fusion.1
  171.2 0.7 copy.11
  171.9 3.1 %all-to-all-done.10 = bf16[8,1,8,512]{3,2,1,0:T(8,128)(2,1)S(1)} async-done(((bf16[8,1,8,512]{3,2,1,0:T(8,128)(2,1)}), bf16[8,1,8,512]{3,2,1,0:T(8,128)(2,1)S(1)}, u32[]{:S(2)}, u32[]{:S(2)}) %all-to-all-start.10) | async-done | bytes 65568 | tf_op jit(solution)/shard_map/all_to_all | solution.py:262
  175.1 0.6 fusion.3
  (22 shorter events, 0.7 us)
Async XLA Ops:
  0.6 20.6 %copy-start.6 = (bf16[1,1,2,4,1,4,8,512]{7,6,5,4,3,2,1,0:T(8,128)(2,1)S(1)}, bf16[1,1,2,4,1,4,8,512]{7,6,5,4,3,2,1,0:T(8,128)(2,1)}, u32[]{:S(2)}) copy-start(bf16[1,1,2,4,1,4,8,512]{7,6,5,4,3,2,1,0:T(8,128)(2,1)} %param.11) | copy-start | bytes 786436
  0.6 20.6 %copy-start.7 = (f32[1,2,128]{2,1,0:T(2,128)S(1)}, f32[1,2,128]{2,1,0:T(2,128)}, u32[]{:S(2)}) copy-start(f32[1,2,128]{2,1,0:T(2,128)} %param.10) | copy-start | bytes 3076
  2.4 18.9 %all-to-all-start = ((bf16[16,16,512]{2,1,0:T(8,128)(2,1)}), bf16[16,16,512]{2,1,0:T(8,128)(2,1)S(1)}, u32[]{:S(2)}, u32[]{:S(2)}) async-start(bf16[16,16,512]{2,1,0:T(8,128)(2,1)} %bitcast.5), calls=%async_computation | async-start | bytes 524288 | tf_op jit(solution)/shard_map/all_to_all | solution.py:183
  14.9 2.6 %copy-start = (bf16[2048,1536]{1,0:T(8,128)(2,1)}, bf16[2048,1536]{1,0:T(8,128)(2,1)S(1)}, u32[]{:S(2)}) copy-start(bf16[2048,1536]{1,0:T(8,128)(2,1)S(1)} %get-tuple-element.24.qkv_ref) | copy-start | bytes 18874372
  21.3 2.8 %copy-start.1 = (bf16[2048,1536]{1,0:T(8,128)(2,1)S(1)}, bf16[2048,1536]{1,0:T(8,128)(2,1)}, u32[]{:S(2)}) copy-start(bf16[2048,1536]{1,0:T(8,128)(2,1)} %copy-done) | copy-start | bytes 18874372
  40.9 12.7 %all-to-all-start.2 = ((bf16[16,16,512]{2,1,0:T(8,128)(2,1)}), bf16[16,16,512]{2,1,0:T(8,128)(2,1)S(1)}, u32[]{:S(2)}, u32[]{:S(2)}) async-start(bf16[16,16,512]{2,1,0:T(8,128)(2,1)} %bitcast.14), calls=%async_computation.2 | async-start | bytes 524288 | tf_op jit(solution)/shard_map/all_to_all | solution.py:183
  53.6 2.8 %copy-start.2 = (bf16[2048,1536]{1,0:T(8,128)(2,1)S(1)}, bf16[2048,1536]{1,0:T(8,128)(2,1)}, u32[]{:S(2)}) copy-start(bf16[2048,1536]{1,0:T(8,128)(2,1)} %copy-done) | copy-start | bytes 18874372
  71.6 12.3 %all-to-all-start.4 = ((bf16[16,16,512]{2,1,0:T(8,128)(2,1)}), bf16[16,16,512]{2,1,0:T(8,128)(2,1)S(1)}, u32[]{:S(2)}, u32[]{:S(2)}) async-start(bf16[16,16,512]{2,1,0:T(8,128)(2,1)} %bitcast.18), calls=%async_computation.4 | async-start | bytes 524288 | tf_op jit(solution)/shard_map/all_to_all | solution.py:183
  84.0 2.8 %copy-start.3 = (bf16[2048,1536]{1,0:T(8,128)(2,1)S(1)}, bf16[2048,1536]{1,0:T(8,128)(2,1)}, u32[]{:S(2)}) copy-start(bf16[2048,1536]{1,0:T(8,128)(2,1)} %copy-done) | copy-start | bytes 18874372
  102.3 12.3 %all-to-all-start.6 = ((bf16[16,16,512]{2,1,0:T(8,128)(2,1)}), bf16[16,16,512]{2,1,0:T(8,128)(2,1)S(1)}, u32[]{:S(2)}, u32[]{:S(2)}) async-start(bf16[16,16,512]{2,1,0:T(8,128)(2,1)} %bitcast.22), calls=%async_computation.6 | async-start | bytes 524288 | tf_op jit(solution)/shard_map/all_to_all | solution.py:183
  114.7 2.8 %copy-start.4 = (bf16[2048,1536]{1,0:T(8,128)(2,1)S(1)}, bf16[2048,1536]{1,0:T(8,128)(2,1)}, u32[]{:S(2)}) copy-start(bf16[2048,1536]{1,0:T(8,128)(2,1)} %copy-done) | copy-start | bytes 18874372
  121.2 12.3 %all-to-all-start.7 = ((bf16[16,16,512]{2,1,0:T(8,128)(2,1)}), bf16[16,16,512]{2,1,0:T(8,128)(2,1)S(1)}, u32[]{:S(2)}, u32[]{:S(2)}) async-start(bf16[16,16,512]{2,1,0:T(8,128)(2,1)} %bitcast.24), calls=%async_computation.7 | async-start | bytes 524288 | tf_op jit(solution)/shard_map/all_to_all | solution.py:183
  134.3 12.3 %all-to-all-start.8 = ((bf16[16,16,512]{2,1,0:T(8,128)(2,1)}), bf16[16,16,512]{2,1,0:T(8,128)(2,1)S(1)}, u32[]{:S(2)}, u32[]{:S(2)}) async-start(bf16[16,16,512]{2,1,0:T(8,128)(2,1)} %bitcast.28), calls=%async_computation.8 | async-start | bytes 524288 | tf_op jit(solution)/shard_map/all_to_all | solution.py:183
  146.6 2.8 %copy-start.5 = (bf16[2048,1536]{1,0:T(8,128)(2,1)S(1)}, bf16[2048,1536]{1,0:T(8,128)(2,1)}, u32[]{:S(2)}) copy-start(bf16[2048,1536]{1,0:T(8,128)(2,1)} %copy-done) | copy-start | bytes 18874372
  153.1 12.3 %all-to-all-start.9 = ((bf16[16,16,512]{2,1,0:T(8,128)(2,1)}), bf16[16,16,512]{2,1,0:T(8,128)(2,1)S(1)}, u32[]{:S(2)}, u32[]{:S(2)}) async-start(bf16[16,16,512]{2,1,0:T(8,128)(2,1)} %bitcast.30), calls=%async_computation.9 | async-start | bytes 524288 | tf_op jit(solution)/shard_map/all_to_all | solution.py:183
  166.8 8.2 %all-to-all-start.10 = ((bf16[8,1,8,512]{3,2,1,0:T(8,128)(2,1)}), bf16[8,1,8,512]{3,2,1,0:T(8,128)(2,1)S(1)}, u32[]{:S(2)}, u32[]{:S(2)}) async-start(bf16[8,1,8,512]{3,2,1,0:T(8,128)(2,1)} %bitcast.34), calls=%async_computation.10 | async-start | bytes 131072 | tf_op jit(solution)/shard_map/all_to_all | solution.py:262

commit v6 on v5

--- a/solution.py
+++ b/solution.py
@@ -31,15 +31,18 @@
     )
 
 
-def section_kernel(sizes, where_ref, rows_ref, mod_ref, qkv_ref, out_ref, gain_ref, stale_ref, *refs):
-    *prev_refs, partial_ref, fresh_ref = refs
-    patches, tok_dev, group_rows, head_dim = sizes
+def section_kernel(tick, sizes, where_ref, rows_ref, mod_ref, qkv_ref, out_ref, gain_ref, *refs):
+    *stale_refs, old_table_ref, partial_ref, table_ref = refs
+    tok_dev, head_dim = sizes
     blocks, slices, block_rows, block_cols = rows_ref.shape
     rows = slices * block_rows
     width = blocks * block_cols
     in_group = block_rows // tok_dev
-    heads = stale_ref.shape[2] // head_dim
-    group, own_member = where_ref[0], where_ref[1]
+    group_rows = slices * tok_dev
+    groups, local_width = table_ref.shape[1], table_ref.shape[3]
+    heads = local_width // head_dim
+    section, own_member = where_ref[0], where_ref[1]
+    group = tick - section
     parts = [rows_ref[q].reshape(rows, block_cols).astype(jnp.float32) for q in range(blocks)]
     mean = sum(jnp.sum(x, axis=-1, keepdims=True) for x in parts) / width
     parts = [x - mean for x in parts]
@@ -54,35 +57,39 @@
     modulated = jnp.concatenate(modulated, axis=1)
     mixed = jnp.dot(modulated, qkv_ref[...], preferred_element_type=jnp.float32)
 
-    def patch_in_group(shape, axis):
-        return lax.broadcasted_iota(jnp.int32, shape, axis) // tok_dev % in_group
-
-    square = (rows, rows)
-    masks = []
-    for back in range(len(prev_refs), 0, -1):
-        masks.append(jnp.broadcast_to(group >= back, square))
-    masks.append(patch_in_group(square, 1) <= patch_in_group(square, 0))
-    wide = (rows, stale_ref.shape[1])
-    key_at = lax.broadcasted_iota(jnp.int32, wide, 1)
-    masks.append(
-        jnp.logical_or(
-            key_at // group_rows % patches > group * in_group + patch_in_group(wide, 0),
-            key_at // (group_rows * patches) != own_member,
-        )
-    )
+    def by_patch(values):
+        values = values.reshape(slices, in_group, tok_dev, head_dim).swapaxes(0, 1)
+        return values.reshape(rows, head_dim).astype(jnp.bfloat16)
+
+    def query_patch(shape):
+        return lax.broadcasted_iota(jnp.int32, shape, 0) // tok_dev % in_group
+
+    square, wide = (rows, rows), (rows, groups * rows)
+    fresh_patch = lax.broadcasted_iota(jnp.int32, square, 1) // group_rows
+    old_patch = lax.broadcasted_iota(jnp.int32, wide, 1) // group_rows - group * in_group
+    masks = [
+        fresh_patch <= query_patch(square),
+        jnp.logical_or(old_patch < 0, old_patch > query_patch(wide)),
+    ]
+    for ref in stale_refs:
+        at = lax.broadcasted_iota(jnp.int32, (rows, ref.shape[1]), 1)
+        masks.append(at // (groups * rows) != own_member)
     attended = []
+    fresh = []
     for head in range(heads):
         at = slice(head * head_dim, (head + 1) * head_dim)
         query, key, value = (
             mixed[:, (3 * head + j) * head_dim : (3 * head + j + 1) * head_dim] for j in range(3)
         )
         query = head_norm(query, gain_ref[0:1, :]).astype(jnp.bfloat16)
-        key = head_norm(key, gain_ref[1:2, :]).astype(jnp.bfloat16)
-        value = value.astype(jnp.bfloat16)
-        fresh_ref[0, :, at] = key
-        fresh_ref[1, :, at] = value
-        keys = [ref[0, :, at] for ref in prev_refs] + [key, stale_ref[0, :, at]]
-        values = [ref[1, :, at] for ref in prev_refs] + [value, stale_ref[1, :, at]]
+        key = by_patch(head_norm(key, gain_ref[1:2, :]))
+        value = by_patch(value)
+        fresh.append((key, value))
+        keys, values = (
+            [new, old_table_ref[j, :, :, at].reshape(groups * rows, head_dim)]
+            + [ref[j, :, at] for ref in stale_refs]
+            for j, new in enumerate((key, value))
+        )
         total = 0.0
         summed = 0.0
         for mask, key_rows, value_rows in zip(masks, keys, values):
@@ -96,6 +103,19 @@
             )
         attended.append((summed / total).astype(jnp.bfloat16))
     attended = jnp.concatenate(attended, axis=1)
+
+    for at in range(groups):
+
+        @pl.when(group == at)
+        def _():
+            for j in range(2):
+                table_ref[j, at] = jnp.concatenate([pair[j] for pair in fresh], axis=1)
+
+        @pl.when(group != at)
+        def _():
+            for j in range(2):
+                table_ref[j, at] = old_table_ref[j, at]
+
     projected = jnp.dot(attended, out_ref[...], preferred_element_type=jnp.float32)
     projected = (mod_ref[2:3, :] * projected).astype(jnp.bfloat16)
     for q in range(blocks):
@@ -104,13 +124,26 @@
         )
 
 
-def load_kernel(qkv_ref, out_ref, qkv_to, out_to, sems):
+def start_kernel(where_ref, latent_ref, qkv_ref, out_ref, qkv_to, out_to, sources_to, streams_to, spread_to, sems):
     copies = (
         pltpu.make_async_copy(qkv_ref, qkv_to, sems.at[0]),
         pltpu.make_async_copy(out_ref, out_to, sems.at[1]),
     )
     for copy in copies:
         copy.start()
+    sections, slices, _, block_cols = spread_to.shape
+    for q in range(sections):
+
+        @pl.when(where_ref[0] == q)
+        def _():
+            sources_to[...] = latent_ref[:, :, q * block_cols : (q + 1) * block_cols]
+
+    first = sources_to[0]
+    for section in range(sections):
+        held = first if section == 0 else jnp.zeros_like(first)
+        streams_to[section] = held
+        for piece in range(slices):
+            spread_to[section, piece] = held
     for copy in copies:
         copy.wait()
 
@@ -161,7 +194,6 @@
         qkv_slice = join_pair(is_upper, qkv_slice, got_qkv, 1)
         out_slice = join_pair(is_upper, out_slice, got_out, 0)
         group_cache = join_pair(is_upper, group_cache, got_cache, 0)
-    stale_rows = group_cache.swapaxes(0, 1).reshape(2, -1, local_width)
     homes = section_count * slice_count
     in_group = patches // GROUPS
     block_rows = in_group * tok_dev
@@ -184,77 +216,76 @@
         return value.reshape(section_count, slice_count, block_rows, block_cols)
 
     vmem = pl.BlockSpec(memory_space=pltpu.VMEM)
+    smem = pl.BlockSpec(memory_space=pltpu.SMEM)
+    in_hbm = functools.partial(pltpu.with_memory_space_constraint, memory_space=pltpu.HBM)
     in_vmem = functools.partial(pltpu.with_memory_space_constraint, memory_space=pltpu.VMEM)
-    qkv_slice, out_slice = pl.pallas_call(
-        load_kernel,
+    where = jnp.stack((section_rank, own_member)).astype(jnp.int32)
+    sources = latent.reshape(GROUPS, block_rows, model_width)
+    stream_shape = (section_count, block_rows, block_cols)
+    spread_shape = (section_count, slice_count, block_rows, block_cols)
+    qkv_slice, out_slice, sources, streams, spread = pl.pallas_call(
+        start_kernel,
         out_shape=(
             pltpu.VMEM(qkv_slice.shape, jnp.bfloat16),
             pltpu.VMEM(out_slice.shape, jnp.bfloat16),
+            jax.ShapeDtypeStruct((GROUPS, block_rows, block_cols), jnp.bfloat16),
+            jax.ShapeDtypeStruct(stream_shape, jnp.bfloat16),
+            jax.ShapeDtypeStruct(spread_shape, jnp.bfloat16),
         ),
-        in_specs=[pl.BlockSpec(memory_space=pltpu.HBM)] * 2,
-        out_specs=(vmem, vmem),
+        in_specs=[smem, vmem] + [pl.BlockSpec(memory_space=pltpu.HBM)] * 2,
+        out_specs=(vmem,) * 5,
         scratch_shapes=[pltpu.SemaphoreType.DMA((2,))],
-        compiler_params=pltpu.CompilerParams(vmem_limit_bytes=1024 * 1024),
-        cost_estimate=pl.CostEstimate(
-            flops=0, bytes_accessed=4 * (qkv_slice.size + out_slice.size), transcendentals=0
-        ),
-    )(*(pltpu.with_memory_space_constraint(w, pltpu.HBM) for w in (qkv_slice, out_slice)))
-
-    def attend(group, features, prev):
-        return pl.pallas_call(
-            functools.partial(section_kernel, (patches, tok_dev, group_rows, head_dim)),
-            out_shape=(
-                jax.ShapeDtypeStruct(features.shape, jnp.bfloat16),
-                jax.ShapeDtypeStruct((2, rows, local_width), jnp.bfloat16),
-            ),
-            in_specs=[pl.BlockSpec(memory_space=pltpu.SMEM)] + [vmem] * (6 + len(prev)),
-            out_specs=(vmem, vmem),
-            compiler_params=pltpu.CompilerParams(vmem_limit_bytes=24 * 1024 * 1024),
-        )(
-            jnp.stack((group, own_member)).astype(jnp.int32),
+        compiler_params=pltpu.CompilerParams(vmem_limit_bytes=4 * 1024 * 1024),
+    )(where, sources, in_hbm(qkv_slice), in_hbm(out_slice))
+    stale_rows = []
+    if member_count > 1:
+        stale_rows = [group_cache.swapaxes(0, 1).reshape(2, -1, local_width)]
+    table = own_cache.reshape(2, GROUPS, rows, local_width)
+
+    def attend(tick, features, table):
+        operands = (
+            where,
             features,
             modulation[0, 0],
             in_vmem(qkv_slice),
             in_vmem(out_slice),
             norm_gain[0],
-            stale_rows,
-            *prev,
-        )
-
-    sources = lax.dynamic_slice_in_dim(
-        latent.reshape(GROUPS, block_rows, model_width), section_rank * block_cols, block_cols, 2
-    )
-    spread_shape = (section_count, slice_count, block_rows, block_cols)
-    zeros = jnp.zeros_like(sources[0])
-    streams = jnp.stack([sources[0]] + [zeros] * (section_count - 1))
-    spread = jnp.broadcast_to(streams[:, None], spread_shape)
+            *stale_rows,
+            table,
+        )
+        return pl.pallas_call(
+            functools.partial(section_kernel, tick, (tok_dev, head_dim)),
+            out_shape=(
+                jax.ShapeDtypeStruct(features.shape, jnp.bfloat16),
+                jax.ShapeDtypeStruct(table.shape, jnp.bfloat16),
+            ),
+            in_specs=[smem] + [vmem] * (len(operands) - 1),
+            out_specs=(vmem, vmem),
+            input_output_aliases={len(operands) - 1: 1},
+            compiler_params=pltpu.CompilerParams(vmem_limit_bytes=24 * 1024 * 1024),
+        )(*operands)
 
     def settle(parts, streams, entering):
         return pl.pallas_call(
             settle_kernel,
             out_shape=tuple(
                 jax.ShapeDtypeStruct(shape, jnp.bfloat16)
-                for shape in (streams.shape, spread_shape, entering.shape)
+                for shape in (stream_shape, spread_shape, entering.shape)
             ),
             in_specs=[vmem] * 3,
             out_specs=(vmem,) * 3,
             compiler_params=pltpu.CompilerParams(vmem_limit_bytes=8 * 1024 * 1024),
         )(parts, streams, entering)
 
-    fresh_ticks = []
     finals = []
     for tick in range(GROUPS + section_count - 1):
-        features = exchange(spread)
-        prev = fresh_ticks[-(GROUPS - 1) :] if GROUPS > 1 else []
-        partial_out, fresh = attend(tick - section_rank, features, prev)
-        fresh_ticks.append(fresh)
-        entering = sources[tick + 1] if tick + 1 < GROUPS else zeros
-        streams, spread, last = settle(exchange(partial_out), streams, entering)
+        partial_out, table = attend(tick, exchange(spread), table)
+        streams, spread, last = settle(
+            exchange(partial_out), streams, sources[min(tick + 1, GROUPS - 1)]
+        )
         finals.append(last)
 
-    next_cache = lax.dynamic_slice_in_dim(jnp.stack(fresh_ticks), section_rank, GROUPS, 0)
-    next_cache = next_cache.reshape(GROUPS, 2, slice_count, in_group, tok_dev, local_width)
-    next_cache = next_cache.transpose(1, 0, 3, 2, 4, 5).reshape(stale_kv.shape)
+    next_cache = table.reshape(stale_kv.shape)
     per_home = patches // section_count
     finals = jnp.stack(finals[section_count - 1 :])
     finals = finals.reshape(1, section_count, per_home, tok_dev, block_cols)

time: 177 us -> 178 us (level)
  blocking collectives: 36.4 us -> 98 us
  waiting for transfers between devices: 56.3 us -> 24.5 us
  starting transfers between devices: 32.9 us -> 15.2 us
  local copies, waits for them, and re-layouts: 24.6 us -> 11.5 us
  Pallas kernels: 23.7 us -> 26.8 us
    all_to_all x3 -> x8, blocking collectives: 36.4 us -> 98 us  [exchange(): lax.all_to_all(value, ('pipe', 'seq'), 0, 0, axis_index_groups=peers)]
    all_to_all x7 -> x2, waiting for transfers between devices: 53.1 us -> 19.7 us  [exchange(): lax.all_to_all(value, ('pipe', 'seq'), 0, 0, axis_index_groups=peers)]
    all_to_all x7 -> x2, starting transfers between devices: 29.5 us -> 11.8 us  [exchange(): lax.all_to_all(value, ('pipe', 'seq'), 0, 0, axis_index_groups=peers)]
    unnamed x21 -> x14, local copies, waits for them, and re-layouts: 20 us -> 10.8 us
    pallas_call x6, Pallas kernels: 20 us -> 24.2 us  [the longest x5 19.5 us: attend(): pl.pallas_call(functools.partial(section_kernel, tick, (tok_dev, head_dim...]
  transfers between devices with their start and end apart: 8 -> 3, of which waited for: 8 -> 3; matrix products, arithmetic and copies ran while one was open for 3% -> 0% of each run, Pallas kernels for 2% -> 0%
where the time goes in v6:
time: 178 us; the launch traced here: 177 us
  blocking collectives  98 us (55%)
  Pallas kernels  26.8 us (15%)
  waiting for transfers between devices  24.5 us (14%)
  starting transfers between devices  15.2 us (9%)
  local copies, waits for them, and re-layouts  11.5 us (6%)
    all_to_all x8, blocking collectives, exchange(): lax.all_to_all(value, ('pipe', 'seq'), 0, 0, axis_index_groups=peers)  98 us
    all_to_all x2, waiting for transfers between devices, exchange(): lax.all_to_all(value, ('pipe', 'seq'), 0, 0, axis_index_groups=peers)  19.7 us
    pallas_call x5, Pallas kernels, attend(): pl.pallas_call(functools.partial(section_kernel, tick, (tok_dev, head_dim...  19.5 us
    all_to_all x2, starting transfers between devices, exchange(): lax.all_to_all(value, ('pipe', 'seq'), 0, 0, axis_index_groups=peers)  11.8 us
    unnamed x14, local copies, waits for them, and re-layouts  10.8 us
    all_to_all x1, waiting for transfers between devices, local(): lax.all_to_all(finals.reshape((-1,) + finals.shape[2:]), ('cfg', 'pipe'),...  4.84 us
    pallas_call x1, Pallas kernels, local(): pl.pallas_call(start_kernel, out_shape=(pltpu.VMEM(qkv_slice.shape, jnp.b...  4.67 us
  transfers between devices with their start and end apart: 3, of which 3 were waited for; matrix products, arithmetic and copies ran while one was open for 0% of the time, Pallas kernels for 0%

profile of v6, /device:TPU:0, one launch (start us, length us, event | category | flops | bytes accessed | tf_op | source)
XLA Modules:
  0.0 177.4 jit_solution(992597481196773387)
XLA Ops:
  0.6 0.0 copy-start.5
  0.6 0.0 copy-start.4
  0.7 1.7 copy.25
  2.3 0.1 pad_add_fusion.where_ref
  2.4 0.0 copy-start.3
  2.4 0.9 copy-done.3
  3.3 4.7 %shard_map.77 = (bf16[2048,1536]{1,0:T(8,128)(2,1)S(1)}, bf16[512,2048]{1,0:T(8,128)(2,1)S(1)}, bf16[2,16,512]{2,1,0:T(8,128)(2,1)S(1)}, bf16[4,16,512]{2,1,0:T(8,128)(2,1)S(1)}, bf16[4,4,16,512]{3,2,1,0:T(8,128)(2,1)}) custom-call(s32[2]{0:T(128)S(1)} %pad_add_fusion.where_ref, bf16[2,16,2048]{2,1,0:T(8,128)(2,1)S(1)} %bitcast.81, ...), custom_call_target="tpu_custom_call" | custom-call | tf_op jit(solution)/shard_map/pallas_call | solution.py:226
  8.0 0.0 copy-start
  8.0 2.6 %copy-done = bf16[2048,1536]{1,0:T(8,128)(2,1)} copy-done((bf16[2048,1536]{1,0:T(8,128)(2,1)}, bf16[2048,1536]{1,0:T(8,128)(2,1)S(1)}, u32[]{:S(2)}) %copy-start) | copy-done | bytes 6291480
  10.6 8.3 %all-to-all-start = ((bf16[16,16,512]{2,1,0:T(8,128)(2,1)}), bf16[16,16,512]{2,1,0:T(8,128)(2,1)S(1)}, u32[]{:S(2)}, u32[]{:S(2)}) async-start(bf16[16,16,512]{2,1,0:T(8,128)(2,1)} %bitcast.4), calls=%async_computation | async-start | bytes 524288 | tf_op jit(solution)/shard_map/all_to_all | solution.py:215
  19.0 0.0 copy-done.5
  19.0 10.5 %all-to-all-done = bf16[16,16,512]{2,1,0:T(8,128)(2,1)S(1)} async-done(((bf16[16,16,512]{2,1,0:T(8,128)(2,1)}), bf16[16,16,512]{2,1,0:T(8,128)(2,1)S(1)}, u32[]{:S(2)}, u32[]{:S(2)}) %all-to-all-start) | async-done | bytes 262176 | tf_op jit(solution)/shard_map/all_to_all | solution.py:215
  29.5 0.0 copy-done.4
  29.5 0.0 copy-start.1
  29.5 2.8 %copy-done.1 = bf16[2048,1536]{1,0:T(8,128)(2,1)S(1)} copy-done((bf16[2048,1536]{1,0:T(8,128)(2,1)S(1)}, bf16[2048,1536]{1,0:T(8,128)(2,1)}, u32[]{:S(2)}) %copy-start.1) | copy-done | bytes 6291480
  32.3 4.3 %shard_map.78 = (bf16[4,4,16,512]{3,2,1,0:T(8,128)(2,1)}, bf16[2,2,64,512]{3,2,1,0:T(8,128)(2,1)}) custom-call(s32[2]{0:T(128)S(1)} %pad_add_fusion.where_ref, bf16[4,4,16,512]{3,2,1,0:T(8,128)(2,1)S(1)} %bitcast.63, f32[3,2048]{1,0:T(4,128)S(1)} %bitcast.58, bf16[2048,1536]{1,0:T(8,128)(2,1)S(1)} %copy-done.1, ...), custom_call_target="tpu_custom_call", output_to_operand_aliasing={{1}: (6, {})} | custom-call | tf_op jit(solution)/shard_map/pallas_call | solution.py:256
  36.6 3.5 %all-to-all-start.1 = ((bf16[16,16,512]{2,1,0:T(8,128)(2,1)}), bf16[16,16,512]{2,1,0:T(8,128)(2,1)S(1)}, u32[]{:S(2)}, u32[]{:S(2)}) async-start(bf16[16,16,512]{2,1,0:T(8,128)(2,1)} %bitcast.8), calls=%async_computation.1 | async-start | bytes 524288 | tf_op jit(solution)/shard_map/all_to_all | solution.py:215
  40.1 9.1 %all-to-all-done.1 = bf16[16,16,512]{2,1,0:T(8,128)(2,1)S(1)} async-done(((bf16[16,16,512]{2,1,0:T(8,128)(2,1)}), bf16[16,16,512]{2,1,0:T(8,128)(2,1)S(1)}, u32[]{:S(2)}, u32[]{:S(2)}) %all-to-all-start.1) | async-done | bytes 262176 | tf_op jit(solution)/shard_map/all_to_all | solution.py:215
  49.3 0.6 shard_map.79
  49.9 11.7 %all_to_all.55 = bf16[16,16,512]{2,1,0:T(8,128)(2,1)S(1)} all-to-all(bf16[16,16,512]{2,1,0:T(8,128)(2,1)S(1)} %bitcast.74), channel_id=1, replica_groups=mesh['cfg'=2,'pipe'=4,'seq'=4] {'pipe','seq'}, dimensions={0} | all-to-all | bytes 524288 | tf_op jit(solution)/shard_map/all_to_all | solution.py:215
  61.5 0.0 copy-start.2
  61.5 2.8 %copy-done.2 = bf16[2048,1536]{1,0:T(8,128)(2,1)S(1)} copy-done((bf16[2048,1536]{1,0:T(8,128)(2,1)S(1)}, bf16[2048,1536]{1,0:T(8,128)(2,1)}, u32[]{:S(2)}) %copy-start.2) | copy-done | bytes 6291480
  64.3 3.8 %shard_map.80 = (bf16[4,4,16,512]{3,2,1,0:T(8,128)(2,1)S(1)}, bf16[2,2,64,512]{3,2,1,0:T(8,128)(2,1)}) custom-call(s32[2]{0:T(128)S(1)} %pad_add_fusion.where_ref, bf16[4,4,16,512]{3,2,1,0:T(8,128)(2,1)S(1)} %bitcast.65, f32[3,2048]{1,0:T(4,128)S(1)} %bitcast.59, bf16[2048,1536]{1,0:T(8,128)(2,1)S(1)} %copy-done.2, ...), custom_call_target="tpu_custom_call", output_to_operand_aliasing={{1}: (6, {})} | custom-call | tf_op jit(solution)/shard_map/pallas_call | solution.py:256
  68.1 11.8 %all_to_all.56 = bf16[16,16,512]{2,1,0:T(8,128)(2,1)S(1)} all-to-all(bf16[16,16,512]{2,1,0:T(8,128)(2,1)S(1)} %bitcast.78), channel_id=1, replica_groups=mesh['cfg'=2,'pipe'=4,'seq'=4] {'pipe','seq'}, dimensions={0} | all-to-all | bytes 524288 | tf_op jit(solution)/shard_map/all_to_all | solution.py:215
  79.9 0.6 shard_map.81
  80.6 11.8 %all_to_all.57 = bf16[16,16,512]{2,1,0:T(8,128)(2,1)S(1)} all-to-all(bf16[16,16,512]{2,1,0:T(8,128)(2,1)S(1)} %bitcast.75), channel_id=1, replica_groups=mesh['cfg'=2,'pipe'=4,'seq'=4] {'pipe','seq'}, dimensions={0} | all-to-all | bytes 524288 | tf_op jit(solution)/shard_map/all_to_all | solution.py:215
  92.4 3.8 %shard_map.82 = (bf16[4,4,16,512]{3,2,1,0:T(8,128)(2,1)S(1)}, bf16[2,2,64,512]{3,2,1,0:T(8,128)(2,1)}) custom-call(s32[2]{0:T(128)S(1)} %pad_add_fusion.where_ref, bf16[4,4,16,512]{3,2,1,0:T(8,128)(2,1)S(1)} %bitcast.66, f32[3,2048]{1,0:T(4,128)S(1)} %bitcast.60, bf16[2048,1536]{1,0:T(8,128)(2,1)S(1)} %copy-done.2, ...), custom_call_target="tpu_custom_call", output_to_operand_aliasing={{1}: (6, {})} | custom-call | tf_op jit(solution)/shard_map/pallas_call | solution.py:256
  96.2 11.8 %all_to_all.58 = bf16[16,16,512]{2,1,0:T(8,128)(2,1)S(1)} all-to-all(bf16[16,16,512]{2,1,0:T(8,128)(2,1)S(1)} %bitcast.79), channel_id=1, replica_groups=mesh['cfg'=2,'pipe'=4,'seq'=4] {'pipe','seq'}, dimensions={0} | all-to-all | bytes 524288 | tf_op jit(solution)/shard_map/all_to_all | solution.py:215
  108.0 0.6 shard_map.83
  108.6 11.8 %all_to_all.59 = bf16[16,16,512]{2,1,0:T(8,128)(2,1)S(1)} all-to-all(bf16[16,16,512]{2,1,0:T(8,128)(2,1)S(1)} %bitcast.76), channel_id=1, replica_groups=mesh['cfg'=2,'pipe'=4,'seq'=4] {'pipe','seq'}, dimensions={0} | all-to-all | bytes 524288 | tf_op jit(solution)/shard_map/all_to_all | solution.py:215
  120.4 3.8 %shard_map.84 = (bf16[4,4,16,512]{3,2,1,0:T(8,128)(2,1)S(1)}, bf16[2,2,64,512]{3,2,1,0:T(8,128)(2,1)}) custom-call(s32[2]{0:T(128)S(1)} %pad_add_fusion.where_ref, bf16[4,4,16,512]{3,2,1,0:T(8,128)(2,1)S(1)} %bitcast.67, f32[3,2048]{1,0:T(4,128)S(1)} %bitcast.61, bf16[2048,1536]{1,0:T(8,128)(2,1)S(1)} %copy-done.2, ...), custom_call_target="tpu_custom_call", output_to_operand_aliasing={{1}: (6, {})} | custom-call | tf_op jit(solution)/shard_map/pallas_call | solution.py:256
  124.2 14.8 %all_to_all.60 = bf16[16,16,512]{2,1,0:T(8,128)(2,1)S(1)} all-to-all(bf16[16,16,512]{2,1,0:T(8,128)(2,1)S(1)} %bitcast.80), channel_id=1, replica_groups=mesh['cfg'=2,'pipe'=4,'seq'=4] {'pipe','seq'}, dimensions={0} | all-to-all | bytes 524288 | tf_op jit(solution)/shard_map/all_to_all | solution.py:215
  139.1 11.6 %all_to_all.61 = bf16[16,16,512]{2,1,0:T(8,128)(2,1)S(1)} all-to-all(bf16[16,16,512]{2,1,0:T(8,128)(2,1)S(1)} %bitcast.77), channel_id=1, replica_groups=mesh['cfg'=2,'pipe'=4,'seq'=4] {'pipe','seq'}, dimensions={0} | all-to-all | bytes 524288 | tf_op jit(solution)/shard_map/all_to_all | solution.py:215
  150.7 3.8 %shard_map.86 = (bf16[4,4,16,512]{3,2,1,0:T(8,128)(2,1)S(1)}, bf16[2,2,64,512]{3,2,1,0:T(8,128)(2,1)}) custom-call(s32[2]{0:T(128)S(1)} %pad_add_fusion.where_ref, bf16[4,4,16,512]{3,2,1,0:T(8,128)(2,1)S(1)} %bitcast.64, f32[3,2048]{1,0:T(4,128)S(1)} %bitcast.62, bf16[2048,1536]{1,0:T(8,128)(2,1)S(1)} %copy-done.2, ...), custom_call_target="tpu_custom_call", output_to_operand_aliasing={{1}: (6, {})} | custom-call | tf_op jit(solution)/shard_map/pallas_call | solution.py:256
  154.5 12.7 %all_to_all.62 = bf16[16,16,512]{2,1,0:T(8,128)(2,1)S(1)} all-to-all(bf16[16,16,512]{2,1,0:T(8,128)(2,1)S(1)} %bitcast.73), channel_id=1, replica_groups=mesh['cfg'=2,'pipe'=4,'seq'=4] {'pipe','seq'}, dimensions={0} | all-to-all | bytes 524288 | tf_op jit(solution)/shard_map/all_to_all | solution.py:215
  167.2 0.8 shard_map.87
  168.0 0.6 broadcast_in_dim.10
  168.6 3.3 %all-to-all-start.10 = ((bf16[8,1,8,512]{3,2,1,0:T(8,128)(2,1)}), bf16[8,1,8,512]{3,2,1,0:T(8,128)(2,1)S(1)}, u32[]{:S(2)}, u32[]{:S(2)}) async-start(bf16[8,1,8,512]{3,2,1,0:T(8,128)(2,1)} %bitcast.30), calls=%async_computation.10 | async-start | bytes 131072 | tf_op jit(solution)/shard_map/all_to_all | solution.py:293
  172.0 4.8 %all-to-all-done.10 = bf16[8,1,8,512]{3,2,1,0:T(8,128)(2,1)S(1)} async-done(((bf16[8,1,8,512]{3,2,1,0:T(8,128)(2,1)}), bf16[8,1,8,512]{3,2,1,0:T(8,128)(2,1)S(1)}, u32[]{:S(2)}, u32[]{:S(2)}) %all-to-all-start.10) | async-done | bytes 65568 | tf_op jit(solution)/shard_map/all_to_all | solution.py:293
  176.8 0.6 fusion.3
  (5 shorter events, 0.1 us)
Async XLA Ops:
  0.6 18.3 %copy-start.5 = (f32[1,1,3,2048]{3,1,2,0:T(1,128)S(1)}, f32[1,1,3,2048]{3,1,2,0:T(1,128)}, u32[]{:S(2)}) copy-start(f32[1,1,3,2048]{3,1,2,0:T(1,128)} %param.7) | copy-start | bytes 73732
  0.6 28.9 %copy-start.4 = (f32[1,2,128]{2,1,0:T(2,128)S(1)}, f32[1,2,128]{2,1,0:T(2,128)}, u32[]{:S(2)}) copy-start(f32[1,2,128]{2,1,0:T(2,128)} %param.10) | copy-start | bytes 3076
  2.4 0.9 copy-start.3
  8.0 2.7 %copy-start = (bf16[2048,1536]{1,0:T(8,128)(2,1)}, bf16[2048,1536]{1,0:T(8,128)(2,1)S(1)}, u32[]{:S(2)}) copy-start(bf16[2048,1536]{1,0:T(8,128)(2,1)S(1)} %get-tuple-element.28.qkv_ref) | copy-start | bytes 18874372
  10.6 18.9 %all-to-all-start = ((bf16[16,16,512]{2,1,0:T(8,128)(2,1)}), bf16[16,16,512]{2,1,0:T(8,128)(2,1)S(1)}, u32[]{:S(2)}, u32[]{:S(2)}) async-start(bf16[16,16,512]{2,1,0:T(8,128)(2,1)} %bitcast.4), calls=%async_computation | async-start | bytes 524288 | tf_op jit(solution)/shard_map/all_to_all | solution.py:215
  29.5 2.8 %copy-start.1 = (bf16[2048,1536]{1,0:T(8,128)(2,1)S(1)}, bf16[2048,1536]{1,0:T(8,128)(2,1)}, u32[]{:S(2)}) copy-start(bf16[2048,1536]{1,0:T(8,128)(2,1)} %copy-done) | copy-start | bytes 18874372
  36.6 12.7 %all-to-all-start.1 = ((bf16[16,16,512]{2,1,0:T(8,128)(2,1)}), bf16[16,16,512]{2,1,0:T(8,128)(2,1)S(1)}, u32[]{:S(2)}, u32[]{:S(2)}) async-start(bf16[16,16,512]{2,1,0:T(8,128)(2,1)} %bitcast.8), calls=%async_computation.1 | async-start | bytes 524288 | tf_op jit(solution)/shard_map/all_to_all | solution.py:215
  61.5 2.8 %copy-start.2 = (bf16[2048,1536]{1,0:T(8,128)(2,1)S(1)}, bf16[2048,1536]{1,0:T(8,128)(2,1)}, u32[]{:S(2)}) copy-start(bf16[2048,1536]{1,0:T(8,128)(2,1)} %copy-done) | copy-start | bytes 18874372
  168.6 8.2 %all-to-all-start.10 = ((bf16[8,1,8,512]{3,2,1,0:T(8,128)(2,1)}), bf16[8,1,8,512]{3,2,1,0:T(8,128)(2,1)S(1)}, u32[]{:S(2)}, u32[]{:S(2)}) async-start(bf16[8,1,8,512]{3,2,1,0:T(8,128)(2,1)} %bitcast.30), calls=%async_computation.10 | async-start | bytes 131072 | tf_op jit(solution)/shard_map/all_to_all | solution.py:293

commit v7 on v6

--- a/solution.py
+++ b/solution.py
@@ -50,9 +50,9 @@
     inverse = lax.rsqrt(spread + EPSILON)
     modulated = []
     for q, x in enumerate(parts):
-        at = pl.ds(q * block_cols, block_cols)
+        at = slice(q * block_cols, (q + 1) * block_cols)
         modulated.append(
-            (x * inverse * (1.0 + mod_ref[1:2, at]) + mod_ref[0:1, at]).astype(jnp.bfloat16)
+            (x * inverse * (1.0 + mod_ref[1, :, at]) + mod_ref[0, :, at]).astype(jnp.bfloat16)
         )
     modulated = jnp.concatenate(modulated, axis=1)
     mixed = jnp.dot(modulated, qkv_ref[...], preferred_element_type=jnp.float32)
@@ -104,6 +104,13 @@
         attended.append((summed / total).astype(jnp.bfloat16))
     attended = jnp.concatenate(attended, axis=1)
 
+    projected = jnp.dot(attended, out_ref[...], preferred_element_type=jnp.float32)
+    projected = (mod_ref[2] * projected).astype(jnp.bfloat16)
+    for q in range(blocks):
+        partial_ref[q] = projected[:, q * block_cols : (q + 1) * block_cols].reshape(
+            slices, block_rows, block_cols
+        )
+
     for at in range(groups):
 
         @pl.when(group == at)
@@ -116,19 +123,15 @@
             for j in range(2):
                 table_ref[j, at] = old_table_ref[j, at]
 
-    projected = jnp.dot(attended, out_ref[...], preferred_element_type=jnp.float32)
-    projected = (mod_ref[2:3, :] * projected).astype(jnp.bfloat16)
-    for q in range(blocks):
-        partial_ref[q] = projected[:, q * block_cols : (q + 1) * block_cols].reshape(
-            slices, block_rows, block_cols
-        )
-
-
-def start_kernel(where_ref, latent_ref, qkv_ref, out_ref, qkv_to, out_to, sources_to, streams_to, spread_to, sems):
-    copies = (
-        pltpu.make_async_copy(qkv_ref, qkv_to, sems.at[0]),
-        pltpu.make_async_copy(out_ref, out_to, sems.at[1]),
-    )
+
+def start_kernel(where_ref, latent_ref, *refs):
+    loads = (len(refs) - 4) // 2
+    from_refs, to_refs = refs[:loads], refs[loads : 2 * loads]
+    sources_to, streams_to, spread_to, sems = refs[2 * loads :]
+    copies = [
+        pltpu.make_async_copy(from_ref, to_ref, sems.at[at])
+        for at, (from_ref, to_ref) in enumerate(zip(from_refs, to_refs))
+    ]
     for copy in copies:
         copy.start()
     sections, slices, _, block_cols = spread_to.shape
@@ -148,22 +151,33 @@
         copy.wait()
 
 
-def settle_kernel(parts_ref, streams_ref, entering_ref, streams_to, spread_to, last_to):
+def added(parts_ref, streams_ref, section):
+    total = streams_ref[section].astype(jnp.float32)
+    for piece in range(parts_ref.shape[1]):
+        total = total + parts_ref[section, piece].astype(jnp.float32)
+    return total.astype(jnp.bfloat16)
+
+
+def settle_kernel(entering, parts_ref, streams_ref, sources_ref, streams_to, spread_to, last_to):
     count, slices = parts_ref.shape[:2]
     for section in range(count):
-        total = streams_ref[section].astype(jnp.float32)
+        if section == 0:
+            held = sources_ref[entering]
+        else:
+            held = added(parts_ref, streams_ref, section - 1)
+        streams_to[section] = held
         for piece in range(slices):
-            total = total + parts_ref[section, piece].astype(jnp.float32)
-        total = total.astype(jnp.bfloat16)
-        if section == count - 1:
-            last_to[...] = total
-        else:
-            streams_to[section + 1] = total
-            for piece in range(slices):
-                spread_to[section + 1, piece] = total
-    streams_to[0] = entering_ref[...]
-    for piece in range(slices):
-        spread_to[0, piece] = entering_ref[...]
+            spread_to[section, piece] = held
+    last_to[...] = added(parts_ref, streams_ref, count - 1)
+
+
+def close_kernel(parts_ref, streams_ref, *refs):
+    *last_refs, finals_to = refs
+    lasts = [ref[...] for ref in last_refs]
+    lasts.append(added(parts_ref, streams_ref, parts_ref.shape[0] - 1))
+    finals = jnp.concatenate(lasts).reshape(finals_to.shape[1:])
+    for branch in range(finals_to.shape[0]):
+        finals_to[branch] = finals
 
 
 def local(latent, modulation, qkv_weight, out_weight, norm_gain, stale_kv):
@@ -223,33 +237,38 @@
     sources = latent.reshape(GROUPS, block_rows, model_width)
     stream_shape = (section_count, block_rows, block_cols)
     spread_shape = (section_count, slice_count, block_rows, block_cols)
-    qkv_slice, out_slice, sources, streams, spread = pl.pallas_call(
+    loads = (
+        qkv_slice,
+        out_slice,
+        modulation.reshape(3, 1, model_width),
+        norm_gain[0],
+        own_cache.reshape(2, GROUPS, rows, local_width),
+    )
+    qkv_slice, out_slice, modulation, norm_gain, table, sources, streams, spread = pl.pallas_call(
         start_kernel,
-        out_shape=(
-            pltpu.VMEM(qkv_slice.shape, jnp.bfloat16),
-            pltpu.VMEM(out_slice.shape, jnp.bfloat16),
-            jax.ShapeDtypeStruct((GROUPS, block_rows, block_cols), jnp.bfloat16),
+        out_shape=tuple(pltpu.VMEM(value.shape, value.dtype) for value in loads)
+        + (
+            pltpu.VMEM((GROUPS, block_rows, block_cols), jnp.bfloat16),
             jax.ShapeDtypeStruct(stream_shape, jnp.bfloat16),
             jax.ShapeDtypeStruct(spread_shape, jnp.bfloat16),
         ),
-        in_specs=[smem, vmem] + [pl.BlockSpec(memory_space=pltpu.HBM)] * 2,
-        out_specs=(vmem,) * 5,
-        scratch_shapes=[pltpu.SemaphoreType.DMA((2,))],
+        in_specs=[smem, vmem] + [pl.BlockSpec(memory_space=pltpu.HBM)] * len(loads),
+        out_specs=(vmem,) * (len(loads) + 3),
+        scratch_shapes=[pltpu.SemaphoreType.DMA((len(loads),))],
         compiler_params=pltpu.CompilerParams(vmem_limit_bytes=4 * 1024 * 1024),
-    )(where, sources, in_hbm(qkv_slice), in_hbm(out_slice))
+    )(where, sources, *map(in_hbm, loads))
     stale_rows = []
     if member_count > 1:
         stale_rows = [group_cache.swapaxes(0, 1).reshape(2, -1, local_width)]
-    table = own_cache.reshape(2, GROUPS, rows, local_width)
 
     def attend(tick, features, table):
         operands = (
             where,
             features,
-            modulation[0, 0],
+            in_vmem(modulation),
             in_vmem(qkv_slice),
             in_vmem(out_slice),
-            norm_gain[0],
+            in_vmem(norm_gain),
             *stale_rows,
             table,
         )
@@ -265,31 +284,37 @@
             compiler_params=pltpu.CompilerParams(vmem_limit_bytes=24 * 1024 * 1024),
         )(*operands)
 
-    def settle(parts, streams, entering):
+    def settle(entering, parts, streams):
         return pl.pallas_call(
-            settle_kernel,
+            functools.partial(settle_kernel, entering),
             out_shape=tuple(
                 jax.ShapeDtypeStruct(shape, jnp.bfloat16)
-                for shape in (stream_shape, spread_shape, entering.shape)
+                for shape in (stream_shape, spread_shape, stream_shape[1:])
             ),
             in_specs=[vmem] * 3,
             out_specs=(vmem,) * 3,
             compiler_params=pltpu.CompilerParams(vmem_limit_bytes=8 * 1024 * 1024),
-        )(parts, streams, entering)
-
-    finals = []
-    for tick in range(GROUPS + section_count - 1):
+        )(parts, streams, in_vmem(sources))
+
+    lasts = []
+    ticks = GROUPS + section_count - 1
+    for tick in range(ticks):
         partial_out, table = attend(tick, exchange(spread), table)
-        streams, spread, last = settle(
-            exchange(partial_out), streams, sources[min(tick + 1, GROUPS - 1)]
-        )
-        finals.append(last)
+        parts = exchange(partial_out)
+        if tick < ticks - 1:
+            streams, spread, last = settle(min(tick + 1, GROUPS - 1), parts, streams)
+            lasts.append(last)
 
     next_cache = table.reshape(stale_kv.shape)
     per_home = patches // section_count
-    finals = jnp.stack(finals[section_count - 1 :])
-    finals = finals.reshape(1, section_count, per_home, tok_dev, block_cols)
-    finals = jnp.broadcast_to(finals, (2,) + finals.shape[1:])
+    finals = pl.pallas_call(
+        close_kernel,
+        out_shape=jax.ShapeDtypeStruct((2, patches, tok_dev, block_cols), jnp.bfloat16),
+        in_specs=[vmem] * (GROUPS + 1),
+        out_specs=vmem,
+        compiler_params=pltpu.CompilerParams(vmem_limit_bytes=8 * 1024 * 1024),
+    )(parts, streams, *lasts[section_count - 1 :])
+    finals = finals.reshape(2, section_count, per_home, tok_dev, block_cols)
     got = lax.all_to_all(
         finals.reshape((-1,) + finals.shape[2:]), ("cfg", "pipe"), 0, 0
     ).reshape(finals.shape)

time: 178 us -> 163 us (0.916)
  blocking collectives: 98 us -> 130 us
  waiting for transfers between devices: 24.5 us -> 4.13 us
  starting transfers between devices: 15.2 us -> 3.35 us
  local copies, waits for them, and re-layouts: 11.5 us -> 1.61 us
  Pallas kernels: 26.8 us -> 22 us
    all_to_all x8 -> x10, blocking collectives: 98 us -> 130 us  [exchange(): lax.all_to_all(value, ('pipe', 'seq'), 0, 0, axis_index_groups=peers)]
    all_to_all x2 -> x0, waiting for transfers between devices: 19.7 us -> none  [exchange(): lax.all_to_all(value, ('pipe', 'seq'), 0, 0, axis_index_groups=peers)]
    all_to_all x2 -> x0, starting transfers between devices: 11.8 us -> none  [exchange(): lax.all_to_all(value, ('pipe', 'seq'), 0, 0, axis_index_groups=peers)]
    unnamed x14 -> x3, local copies, waits for them, and re-layouts: 10.8 us -> 1.61 us
    pallas_call x5, Pallas kernels: 19.5 us -> 15.4 us  [attend(): pl.pallas_call(functools.partial(section_kernel, tick, (tok_dev, head_dim...]
  transfers between devices with their start and end apart: 3 -> 1, of which waited for: 3 -> 1; matrix products, arithmetic and copies ran while one was open for 0% -> 0% of each run, Pallas kernels for 0% -> 0%
where the time goes in v7:
time: 163 us
  blocking collectives  130 us (80%)
  Pallas kernels  22 us (13%)
  waiting for transfers between devices  4.13 us (3%)
  starting transfers between devices  3.35 us (2%)
    all_to_all x10, blocking collectives, exchange(): lax.all_to_all(value, ('pipe', 'seq'), 0, 0, axis_index_groups=peers)  130 us
    pallas_call x5, Pallas kernels, attend(): pl.pallas_call(functools.partial(section_kernel, tick, (tok_dev, head_dim...  15.4 us
    all_to_all x1, waiting for transfers between devices, local(): lax.all_to_all(finals.reshape((-1,) + finals.shape[2:]), ('cfg', 'pipe'),...  4.13 us
    pallas_call x1, Pallas kernels, local(): pl.pallas_call(start_kernel, out_shape=tuple((pltpu.VMEM(value.shape, val...  4 us
    all_to_all x1, starting transfers between devices, local(): lax.all_to_all(finals.reshape((-1,) + finals.shape[2:]), ('cfg', 'pipe'),...  3.35 us
  transfers between devices with their start and end apart: 1, of which 1 were waited for; matrix products, arithmetic and copies ran while one was open for 0% of the time, Pallas kernels for 0%

profile of v7, /device:TPU:0, one launch (start us, length us, event | category | flops | bytes accessed | tf_op | source)
XLA Modules:
  0.0 162.5 jit_solution(12541457088414344039)
XLA Ops:
  0.6 0.1 pad_add_fusion.where_ref
  0.7 0.0 copy-start
  0.7 0.9 copy-done
  1.6 4.0 %shard_map.77 = (bf16[2048,1536]{1,0:T(8,128)(2,1)S(1)}, bf16[512,2048]{1,0:T(8,128)(2,1)S(1)}, f32[3,1,2048]{2,1,0:T(1,128)S(1)}, f32[2,128]{1,0:T(2,128)S(1)},...) custom-call(s32[2]{0:T(128)S(1)} %pad_add_fusion.where_ref, ...), custom_call_target="tpu_custom_call" | custom-call | tf_op jit(solution)/shard_map/pallas_call | solution.py:247
  5.6 18.7 %all_to_all.55 = bf16[16,16,512]{2,1,0:T(8,128)(2,1)S(1)} all-to-all(bf16[16,16,512]{2,1,0:T(8,128)(2,1)S(1)} %bitcast.65), channel_id=1, replica_groups=mesh['cfg'=2,'pipe'=4,'seq'=4] {'pipe','seq'}, dimensions={0} | all-to-all | bytes 524288 | tf_op jit(solution)/shard_map/all_to_all | solution.py:229
  24.3 3.1 %shard_map.78 = (bf16[4,4,16,512]{3,2,1,0:T(8,128)(2,1)S(1)}, bf16[2,2,64,512]{3,2,1,0:T(8,128)(2,1)S(1)}) custom-call(s32[2]{0:T(128)S(1)} %pad_add_fusion.where_ref, bf16[4,4,16,512]{3,2,1,0:T(8,128)(2,1)S(1)} %bitcast.58, f32[3,1,2048]{2,1,0:T(1,128)S(1)} %get-tuple-element.30.mod_ref, ...), custom_call_target="tpu_custom_call", output_to_operand_aliasing={{1}: (6, {})} | custom-call | tf_op jit(solution)/shard_map/pallas_call | solution.py:275
  27.4 12.6 %all_to_all.56 = bf16[16,16,512]{2,1,0:T(8,128)(2,1)S(1)} all-to-all(bf16[16,16,512]{2,1,0:T(8,128)(2,1)S(1)} %bitcast.70), channel_id=1, replica_groups=mesh['cfg'=2,'pipe'=4,'seq'=4] {'pipe','seq'}, dimensions={0} | all-to-all | bytes 524288 | tf_op jit(solution)/shard_map/all_to_all | solution.py:229
  40.0 0.6 shard_map.79
  40.6 12.4 %all_to_all.57 = bf16[16,16,512]{2,1,0:T(8,128)(2,1)S(1)} all-to-all(bf16[16,16,512]{2,1,0:T(8,128)(2,1)S(1)} %bitcast.67), channel_id=1, replica_groups=mesh['cfg'=2,'pipe'=4,'seq'=4] {'pipe','seq'}, dimensions={0} | all-to-all | bytes 524288 | tf_op jit(solution)/shard_map/all_to_all | solution.py:229
  53.1 3.1 %shard_map.80 = (bf16[4,4,16,512]{3,2,1,0:T(8,128)(2,1)S(1)}, bf16[2,2,64,512]{3,2,1,0:T(8,128)(2,1)S(1)}) custom-call(s32[2]{0:T(128)S(1)} %pad_add_fusion.where_ref, bf16[4,4,16,512]{3,2,1,0:T(8,128)(2,1)S(1)} %bitcast.55, f32[3,1,2048]{2,1,0:T(1,128)S(1)} %get-tuple-element.30.mod_ref, ...), custom_call_target="tpu_custom_call", output_to_operand_aliasing={{1}: (6, {})} | custom-call | tf_op jit(solution)/shard_map/pallas_call | solution.py:275
  56.2 12.3 %all_to_all.58 = bf16[16,16,512]{2,1,0:T(8,128)(2,1)S(1)} all-to-all(bf16[16,16,512]{2,1,0:T(8,128)(2,1)S(1)} %bitcast.71), channel_id=1, replica_groups=mesh['cfg'=2,'pipe'=4,'seq'=4] {'pipe','seq'}, dimensions={0} | all-to-all | bytes 524288 | tf_op jit(solution)/shard_map/all_to_all | solution.py:229
  68.5 0.6 shard_map.81
  69.1 12.3 %all_to_all.59 = bf16[16,16,512]{2,1,0:T(8,128)(2,1)S(1)} all-to-all(bf16[16,16,512]{2,1,0:T(8,128)(2,1)S(1)} %bitcast.68), channel_id=1, replica_groups=mesh['cfg'=2,'pipe'=4,'seq'=4] {'pipe','seq'}, dimensions={0} | all-to-all | bytes 524288 | tf_op jit(solution)/shard_map/all_to_all | solution.py:229
  81.5 3.1 %shard_map.82 = (bf16[4,4,16,512]{3,2,1,0:T(8,128)(2,1)S(1)}, bf16[2,2,64,512]{3,2,1,0:T(8,128)(2,1)S(1)}) custom-call(s32[2]{0:T(128)S(1)} %pad_add_fusion.where_ref, bf16[4,4,16,512]{3,2,1,0:T(8,128)(2,1)S(1)} %bitcast.56, f32[3,1,2048]{2,1,0:T(1,128)S(1)} %get-tuple-element.30.mod_ref, ...), custom_call_target="tpu_custom_call", output_to_operand_aliasing={{1}: (6, {})} | custom-call | tf_op jit(solution)/shard_map/pallas_call | solution.py:275
  84.5 12.3 %all_to_all.60 = bf16[16,16,512]{2,1,0:T(8,128)(2,1)S(1)} all-to-all(bf16[16,16,512]{2,1,0:T(8,128)(2,1)S(1)} %bitcast.72), channel_id=1, replica_groups=mesh['cfg'=2,'pipe'=4,'seq'=4] {'pipe','seq'}, dimensions={0} | all-to-all | bytes 524288 | tf_op jit(solution)/shard_map/all_to_all | solution.py:229
  96.9 0.6 shard_map.83
  97.5 12.3 %all_to_all.61 = bf16[16,16,512]{2,1,0:T(8,128)(2,1)S(1)} all-to-all(bf16[16,16,512]{2,1,0:T(8,128)(2,1)S(1)} %bitcast.69), channel_id=1, replica_groups=mesh['cfg'=2,'pipe'=4,'seq'=4] {'pipe','seq'}, dimensions={0} | all-to-all | bytes 524288 | tf_op jit(solution)/shard_map/all_to_all | solution.py:229
  109.8 3.1 %shard_map.84 = (bf16[4,4,16,512]{3,2,1,0:T(8,128)(2,1)S(1)}, bf16[2,2,64,512]{3,2,1,0:T(8,128)(2,1)S(1)}) custom-call(s32[2]{0:T(128)S(1)} %pad_add_fusion.where_ref, bf16[4,4,16,512]{3,2,1,0:T(8,128)(2,1)S(1)} %bitcast.57, f32[3,1,2048]{2,1,0:T(1,128)S(1)} %get-tuple-element.30.mod_ref, ...), custom_call_target="tpu_custom_call", output_to_operand_aliasing={{1}: (6, {})} | custom-call | tf_op jit(solution)/shard_map/pallas_call | solution.py:275
  112.9 12.3 %all_to_all.62 = bf16[16,16,512]{2,1,0:T(8,128)(2,1)S(1)} all-to-all(bf16[16,16,512]{2,1,0:T(8,128)(2,1)S(1)} %bitcast.73), channel_id=1, replica_groups=mesh['cfg'=2,'pipe'=4,'seq'=4] {'pipe','seq'}, dimensions={0} | all-to-all | bytes 524288 | tf_op jit(solution)/shard_map/all_to_all | solution.py:229
  125.3 12.3 %all_to_all.63 = bf16[16,16,512]{2,1,0:T(8,128)(2,1)S(1)} all-to-all(bf16[16,16,512]{2,1,0:T(8,128)(2,1)S(1)} %bitcast.66), channel_id=1, replica_groups=mesh['cfg'=2,'pipe'=4,'seq'=4] {'pipe','seq'}, dimensions={0} | all-to-all | bytes 524288 | tf_op jit(solution)/shard_map/all_to_all | solution.py:229
  137.6 3.1 %shard_map.86 = (bf16[4,4,16,512]{3,2,1,0:T(8,128)(2,1)S(1)}, bf16[2,2,64,512]{3,2,1,0:T(8,128)(2,1)S(1)}) custom-call(s32[2]{0:T(128)S(1)} %pad_add_fusion.where_ref, bf16[4,4,16,512]{3,2,1,0:T(8,128)(2,1)S(1)} %bitcast.54, f32[3,1,2048]{2,1,0:T(1,128)S(1)} %get-tuple-element.30.mod_ref, ...), custom_call_target="tpu_custom_call", output_to_operand_aliasing={{1}: (6, {})} | custom-call | tf_op jit(solution)/shard_map/pallas_call | solution.py:275
  140.7 12.3 %all_to_all.64 = bf16[16,16,512]{2,1,0:T(8,128)(2,1)S(1)} all-to-all(bf16[16,16,512]{2,1,0:T(8,128)(2,1)S(1)} %bitcast.64), channel_id=1, replica_groups=mesh['cfg'=2,'pipe'=4,'seq'=4] {'pipe','seq'}, dimensions={0} | all-to-all | bytes 524288 | tf_op jit(solution)/shard_map/all_to_all | solution.py:229
  153.1 0.6 shard_map.87
  153.7 3.3 %all-to-all-start.10 = ((bf16[8,1,8,512]{3,2,1,0:T(8,128)(2,1)}), bf16[8,1,8,512]{3,2,1,0:T(8,128)(2,1)S(1)}, u32[]{:S(2)}, u32[]{:S(2)}) async-start(bf16[8,1,8,512]{3,2,1,0:T(8,128)(2,1)} %bitcast.28), calls=%async_computation.10 | async-start | bytes 131072 | tf_op jit(solution)/shard_map/all_to_all | solution.py:318
  157.1 0.7 copy.23
  157.8 4.1 %all-to-all-done.10 = bf16[8,1,8,512]{3,2,1,0:T(8,128)(2,1)S(1)} async-done(((bf16[8,1,8,512]{3,2,1,0:T(8,128)(2,1)}), bf16[8,1,8,512]{3,2,1,0:T(8,128)(2,1)S(1)}, u32[]{:S(2)}, u32[]{:S(2)}) %all-to-all-start.10) | async-done | bytes 65568 | tf_op jit(solution)/shard_map/all_to_all | solution.py:318
  161.9 0.6 fusion.3
  (2 shorter events, 0.1 us)
Async XLA Ops:
  0.7 0.9 copy-start
  153.7 8.2 %all-to-all-start.10 = ((bf16[8,1,8,512]{3,2,1,0:T(8,128)(2,1)}), bf16[8,1,8,512]{3,2,1,0:T(8,128)(2,1)S(1)}, u32[]{:S(2)}, u32[]{:S(2)}) async-start(bf16[8,1,8,512]{3,2,1,0:T(8,128)(2,1)} %bitcast.28), calls=%async_computation.10 | async-start | bytes 131072 | tf_op jit(solution)/shard_map/all_to_all | solution.py:318

commit v8 on v7

--- a/solution.py
+++ b/solution.py
@@ -11,6 +11,7 @@
 GUIDANCE_SCALE = 6.0
 EPSILON = 1e-06
 GROUPS = 2
+PIECES = 8
 
 
 def swapped(value, axis, bit):
@@ -132,8 +133,24 @@
         pltpu.make_async_copy(from_ref, to_ref, sems.at[at])
         for at, (from_ref, to_ref) in enumerate(zip(from_refs, to_refs))
     ]
-    for copy in copies:
+    for copy in copies[1:]:
         copy.start()
+    piece_rows = from_refs[0].shape[0] // PIECES
+
+    @pl.when(where_ref[2] == 0)
+    def _():
+        copies[0].start()
+        copies[0].wait()
+
+    @pl.when(where_ref[2] == 1)
+    def _():
+        @pl.loop(0, PIECES)
+        def _(step):
+            at = pl.ds(step * piece_rows, piece_rows)
+            piece = pltpu.make_async_copy(from_refs[0].at[at], to_refs[0].at[at], sems.at[0])
+            piece.start()
+            piece.wait()
+
     sections, slices, _, block_cols = spread_to.shape
     for q in range(sections):
 
@@ -147,7 +164,7 @@
         streams_to[section] = held
         for piece in range(slices):
             spread_to[section, piece] = held
-    for copy in copies:
+    for copy in copies[1:]:
         copy.wait()
 
 
@@ -233,7 +250,7 @@
     smem = pl.BlockSpec(memory_space=pltpu.SMEM)
     in_hbm = functools.partial(pltpu.with_memory_space_constraint, memory_space=pltpu.HBM)
     in_vmem = functools.partial(pltpu.with_memory_space_constraint, memory_space=pltpu.VMEM)
-    where = jnp.stack((section_rank, own_member)).astype(jnp.int32)
+    where = jnp.stack((section_rank, own_member, branch_rank)).astype(jnp.int32)
     sources = latent.reshape(GROUPS, block_rows, model_width)
     stream_shape = (section_count, block_rows, block_cols)
     spread_shape = (section_count, slice_count, block_rows, block_cols)

time: 163 us -> 166 us (1.018)
  blocking collectives: 130 us -> 133 us
    all_to_all x10, blocking collectives: 130 us -> 133 us  [exchange(): lax.all_to_all(value, ('pipe', 'seq'), 0, 0, axis_index_groups=peers)]
where the time goes in v8:
time: 166 us
  blocking collectives  133 us (80%)
  Pallas kernels  22.1 us (13%)
  waiting for transfers between devices  4.13 us (2%)
  starting transfers between devices  3.35 us (2%)
    all_to_all x10, blocking collectives, exchange(): lax.all_to_all(value, ('pipe', 'seq'), 0, 0, axis_index_groups=peers)  133 us
    pallas_call x5, Pallas kernels, attend(): pl.pallas_call(functools.partial(section_kernel, tick, (tok_dev, head_dim...  15.4 us
    pallas_call x1, Pallas kernels, local(): pl.pallas_call(start_kernel, out_shape=tuple((pltpu.VMEM(value.shape, val...  4.15 us
    all_to_all x1, waiting for transfers between devices, local(): lax.all_to_all(finals.reshape((-1,) + finals.shape[2:]), ('cfg', 'pipe'),...  4.13 us
    all_to_all x1, starting transfers between devices, local(): lax.all_to_all(finals.reshape((-1,) + finals.shape[2:]), ('cfg', 'pipe'),...  3.35 us
  transfers between devices with their start and end apart: 1, of which 1 were waited for; matrix products, arithmetic and copies ran while one was open for 0% of the time, Pallas kernels for 0%

profile of v8, /device:TPU:0, one launch (start us, length us, event | category | flops | bytes accessed | tf_op | source)
XLA Modules:
  0.0 165.5 jit_solution(5319216670396006718)
XLA Ops:
  0.6 0.1 pad_add_fusion.where_ref
  0.7 0.0 copy-start
  0.7 0.9 copy-done
  1.6 4.2 %shard_map.77 = (bf16[2048,1536]{1,0:T(8,128)(2,1)S(1)}, bf16[512,2048]{1,0:T(8,128)(2,1)S(1)}, f32[3,1,2048]{2,1,0:T(1,128)S(1)}, f32[2,128]{1,0:T(2,128)S(1)},...) custom-call(s32[3]{0:T(128)S(1)} %pad_add_fusion.where_ref, ...), custom_call_target="tpu_custom_call" | custom-call | tf_op jit(solution)/shard_map/pallas_call | solution.py:264
  5.8 17.0 %all_to_all.55 = bf16[16,16,512]{2,1,0:T(8,128)(2,1)S(1)} all-to-all(bf16[16,16,512]{2,1,0:T(8,128)(2,1)S(1)} %bitcast.66), channel_id=1, replica_groups=mesh['cfg'=2,'pipe'=4,'seq'=4] {'pipe','seq'}, dimensions={0} | all-to-all | bytes 524288 | tf_op jit(solution)/shard_map/all_to_all | solution.py:246
  22.7 3.1 %shard_map.78 = (bf16[4,4,16,512]{3,2,1,0:T(8,128)(2,1)S(1)}, bf16[2,2,64,512]{3,2,1,0:T(8,128)(2,1)S(1)}) custom-call(s32[3]{0:T(128)S(1)} %pad_add_fusion.where_ref, bf16[4,4,16,512]{3,2,1,0:T(8,128)(2,1)S(1)} %bitcast.59, f32[3,1,2048]{2,1,0:T(1,128)S(1)} %get-tuple-element.30.mod_ref, ...), custom_call_target="tpu_custom_call", output_to_operand_aliasing={{1}: (6, {})} | custom-call | tf_op jit(solution)/shard_map/pallas_call | solution.py:292
  25.8 11.8 %all_to_all.56 = bf16[16,16,512]{2,1,0:T(8,128)(2,1)S(1)} all-to-all(bf16[16,16,512]{2,1,0:T(8,128)(2,1)S(1)} %bitcast.71), channel_id=1, replica_groups=mesh['cfg'=2,'pipe'=4,'seq'=4] {'pipe','seq'}, dimensions={0} | all-to-all | bytes 524288 | tf_op jit(solution)/shard_map/all_to_all | solution.py:246
  37.6 0.6 shard_map.79
  38.3 13.1 %all_to_all.57 = bf16[16,16,512]{2,1,0:T(8,128)(2,1)S(1)} all-to-all(bf16[16,16,512]{2,1,0:T(8,128)(2,1)S(1)} %bitcast.68), channel_id=1, replica_groups=mesh['cfg'=2,'pipe'=4,'seq'=4] {'pipe','seq'}, dimensions={0} | all-to-all | bytes 524288 | tf_op jit(solution)/shard_map/all_to_all | solution.py:246
  51.4 3.1 %shard_map.80 = (bf16[4,4,16,512]{3,2,1,0:T(8,128)(2,1)S(1)}, bf16[2,2,64,512]{3,2,1,0:T(8,128)(2,1)S(1)}) custom-call(s32[3]{0:T(128)S(1)} %pad_add_fusion.where_ref, bf16[4,4,16,512]{3,2,1,0:T(8,128)(2,1)S(1)} %bitcast.56, f32[3,1,2048]{2,1,0:T(1,128)S(1)} %get-tuple-element.30.mod_ref, ...), custom_call_target="tpu_custom_call", output_to_operand_aliasing={{1}: (6, {})} | custom-call | tf_op jit(solution)/shard_map/pallas_call | solution.py:292
  54.4 15.3 %all_to_all.58 = bf16[16,16,512]{2,1,0:T(8,128)(2,1)S(1)} all-to-all(bf16[16,16,512]{2,1,0:T(8,128)(2,1)S(1)} %bitcast.72), channel_id=1, replica_groups=mesh['cfg'=2,'pipe'=4,'seq'=4] {'pipe','seq'}, dimensions={0} | all-to-all | bytes 524288 | tf_op jit(solution)/shard_map/all_to_all | solution.py:246
  69.8 0.6 shard_map.81
  70.4 13.5 %all_to_all.59 = bf16[16,16,512]{2,1,0:T(8,128)(2,1)S(1)} all-to-all(bf16[16,16,512]{2,1,0:T(8,128)(2,1)S(1)} %bitcast.69), channel_id=1, replica_groups=mesh['cfg'=2,'pipe'=4,'seq'=4] {'pipe','seq'}, dimensions={0} | all-to-all | bytes 524288 | tf_op jit(solution)/shard_map/all_to_all | solution.py:246
  83.9 3.1 %shard_map.82 = (bf16[4,4,16,512]{3,2,1,0:T(8,128)(2,1)S(1)}, bf16[2,2,64,512]{3,2,1,0:T(8,128)(2,1)S(1)}) custom-call(s32[3]{0:T(128)S(1)} %pad_add_fusion.where_ref, bf16[4,4,16,512]{3,2,1,0:T(8,128)(2,1)S(1)} %bitcast.57, f32[3,1,2048]{2,1,0:T(1,128)S(1)} %get-tuple-element.30.mod_ref, ...), custom_call_target="tpu_custom_call", output_to_operand_aliasing={{1}: (6, {})} | custom-call | tf_op jit(solution)/shard_map/pallas_call | solution.py:292
  87.0 12.8 %all_to_all.60 = bf16[16,16,512]{2,1,0:T(8,128)(2,1)S(1)} all-to-all(bf16[16,16,512]{2,1,0:T(8,128)(2,1)S(1)} %bitcast.73), channel_id=1, replica_groups=mesh['cfg'=2,'pipe'=4,'seq'=4] {'pipe','seq'}, dimensions={0} | all-to-all | bytes 524288 | tf_op jit(solution)/shard_map/all_to_all | solution.py:246
  99.8 0.6 shard_map.83
  100.4 12.4 %all_to_all.61 = bf16[16,16,512]{2,1,0:T(8,128)(2,1)S(1)} all-to-all(bf16[16,16,512]{2,1,0:T(8,128)(2,1)S(1)} %bitcast.70), channel_id=1, replica_groups=mesh['cfg'=2,'pipe'=4,'seq'=4] {'pipe','seq'}, dimensions={0} | all-to-all | bytes 524288 | tf_op jit(solution)/shard_map/all_to_all | solution.py:246
  112.8 3.1 %shard_map.84 = (bf16[4,4,16,512]{3,2,1,0:T(8,128)(2,1)S(1)}, bf16[2,2,64,512]{3,2,1,0:T(8,128)(2,1)S(1)}) custom-call(s32[3]{0:T(128)S(1)} %pad_add_fusion.where_ref, bf16[4,4,16,512]{3,2,1,0:T(8,128)(2,1)S(1)} %bitcast.58, f32[3,1,2048]{2,1,0:T(1,128)S(1)} %get-tuple-element.30.mod_ref, ...), custom_call_target="tpu_custom_call", output_to_operand_aliasing={{1}: (6, {})} | custom-call | tf_op jit(solution)/shard_map/pallas_call | solution.py:292
  115.9 12.3 %all_to_all.62 = bf16[16,16,512]{2,1,0:T(8,128)(2,1)S(1)} all-to-all(bf16[16,16,512]{2,1,0:T(8,128)(2,1)S(1)} %bitcast.74), channel_id=1, replica_groups=mesh['cfg'=2,'pipe'=4,'seq'=4] {'pipe','seq'}, dimensions={0} | all-to-all | bytes 524288 | tf_op jit(solution)/shard_map/all_to_all | solution.py:246
  128.3 12.3 %all_to_all.63 = bf16[16,16,512]{2,1,0:T(8,128)(2,1)S(1)} all-to-all(bf16[16,16,512]{2,1,0:T(8,128)(2,1)S(1)} %bitcast.67), channel_id=1, replica_groups=mesh['cfg'=2,'pipe'=4,'seq'=4] {'pipe','seq'}, dimensions={0} | all-to-all | bytes 524288 | tf_op jit(solution)/shard_map/all_to_all | solution.py:246
  140.6 3.1 %shard_map.86 = (bf16[4,4,16,512]{3,2,1,0:T(8,128)(2,1)S(1)}, bf16[2,2,64,512]{3,2,1,0:T(8,128)(2,1)S(1)}) custom-call(s32[3]{0:T(128)S(1)} %pad_add_fusion.where_ref, bf16[4,4,16,512]{3,2,1,0:T(8,128)(2,1)S(1)} %bitcast.55, f32[3,1,2048]{2,1,0:T(1,128)S(1)} %get-tuple-element.30.mod_ref, ...), custom_call_target="tpu_custom_call", output_to_operand_aliasing={{1}: (6, {})} | custom-call | tf_op jit(solution)/shard_map/pallas_call | solution.py:292
  143.7 12.3 %all_to_all.64 = bf16[16,16,512]{2,1,0:T(8,128)(2,1)S(1)} all-to-all(bf16[16,16,512]{2,1,0:T(8,128)(2,1)S(1)} %bitcast.65), channel_id=1, replica_groups=mesh['cfg'=2,'pipe'=4,'seq'=4] {'pipe','seq'}, dimensions={0} | all-to-all | bytes 524288 | tf_op jit(solution)/shard_map/all_to_all | solution.py:246
  156.1 0.6 shard_map.87
  156.7 3.3 %all-to-all-start.10 = ((bf16[8,1,8,512]{3,2,1,0:T(8,128)(2,1)}), bf16[8,1,8,512]{3,2,1,0:T(8,128)(2,1)S(1)}, u32[]{:S(2)}, u32[]{:S(2)}) async-start(bf16[8,1,8,512]{3,2,1,0:T(8,128)(2,1)} %bitcast.29), calls=%async_computation.10 | async-start | bytes 131072 | tf_op jit(solution)/shard_map/all_to_all | solution.py:335
  160.1 0.7 copy.23
  160.8 4.1 %all-to-all-done.10 = bf16[8,1,8,512]{3,2,1,0:T(8,128)(2,1)S(1)} async-done(((bf16[8,1,8,512]{3,2,1,0:T(8,128)(2,1)}), bf16[8,1,8,512]{3,2,1,0:T(8,128)(2,1)S(1)}, u32[]{:S(2)}, u32[]{:S(2)}) %all-to-all-start.10) | async-done | bytes 65568 | tf_op jit(solution)/shard_map/all_to_all | solution.py:335
  164.9 0.6 fusion.3
  (2 shorter events, 0.1 us)
Async XLA Ops:
  0.7 0.9 copy-start
  156.7 8.2 %all-to-all-start.10 = ((bf16[8,1,8,512]{3,2,1,0:T(8,128)(2,1)}), bf16[8,1,8,512]{3,2,1,0:T(8,128)(2,1)S(1)}, u32[]{:S(2)}, u32[]{:S(2)}) async-start(bf16[8,1,8,512]{3,2,1,0:T(8,128)(2,1)} %bitcast.29), calls=%async_computation.10 | async-start | bytes 131072 | tf_op jit(solution)/shard_map/all_to_all | solution.py:335

commit v9 on v7

--- a/solution.py
+++ b/solution.py
@@ -33,6 +33,7 @@
 
 def section_kernel(tick, sizes, where_ref, rows_ref, mod_ref, qkv_ref, out_ref, gain_ref, *refs):
     *stale_refs, old_table_ref, partial_ref, table_ref = refs
+    closing = len(partial_ref.shape) == 5
     tok_dev, head_dim = sizes
     blocks, slices, block_rows, block_cols = rows_ref.shape
     rows = slices * block_rows
@@ -41,7 +42,7 @@
     group_rows = slices * tok_dev
     groups, local_width = table_ref.shape[1], table_ref.shape[3]
     heads = local_width // head_dim
-    section, own_member = where_ref[0], where_ref[1]
+    section, own_member, own_slice = where_ref[0], where_ref[1], where_ref[2]
     group = tick - section
     parts = [rows_ref[q].reshape(rows, block_cols).astype(jnp.float32) for q in range(blocks)]
     mean = sum(jnp.sum(x, axis=-1, keepdims=True) for x in parts) / width
@@ -105,11 +106,14 @@
     attended = jnp.concatenate(attended, axis=1)
 
     projected = jnp.dot(attended, out_ref[...], preferred_element_type=jnp.float32)
-    projected = (mod_ref[2] * projected).astype(jnp.bfloat16)
-    for q in range(blocks):
-        partial_ref[q] = projected[:, q * block_cols : (q + 1) * block_cols].reshape(
-            slices, block_rows, block_cols
-        )
+    projected = mod_ref[2] * projected
+    if closing:
+        close_into(partial_ref, projected, rows_ref, section, own_slice, in_group)
+    else:
+        out_cols = partial_ref.shape[3]
+        for q in range(partial_ref.shape[0]):
+            piece = projected[:, q * out_cols : (q + 1) * out_cols].astype(jnp.bfloat16)
+            partial_ref[q] = piece.reshape(slices, block_rows, out_cols)
 
     for at in range(groups):
 
@@ -122,6 +126,40 @@
         def _():
             for j in range(2):
                 table_ref[j, at] = old_table_ref[j, at]
+
+
+def close_into(closing_ref, projected, rows_ref, section, own_slice, in_group):
+    branches, patches, slices = closing_ref.shape[:3]
+    blocks, _, block_rows, block_cols = rows_ref.shape
+    tok_dev = block_rows // in_group
+    per_branch = blocks // branches
+
+    @pl.when(section >= patches)
+    def _():
+        for piece in range(slices):
+            own = (own_slice == piece).astype(jnp.float32)
+            by_block = []
+            for q in range(blocks):
+                rows = projected[
+                    piece * block_rows : (piece + 1) * block_rows,
+                    q * block_cols : (q + 1) * block_cols,
+                ]
+                rows = rows + own * rows_ref[q, piece].astype(jnp.float32)
+                by_block.append(rows.reshape(in_group, tok_dev, block_cols))
+            for branch in range(branches):
+                for patch in range(patches):
+                    held = [by_block[branch * per_branch + k][patch] for k in range(per_branch)]
+                    closing_ref[branch, patch, piece] = jnp.concatenate(held).astype(jnp.bfloat16)
+
+    @pl.when(section < patches)
+    def _():
+        finished = [rows_ref[q, own_slice].astype(jnp.float32)[:tok_dev] for q in range(blocks)]
+        for branch in range(branches):
+            held = jnp.concatenate(finished[branch * per_branch : (branch + 1) * per_branch])
+            held = held.astype(jnp.bfloat16)
+            for patch in range(patches):
+                for piece in range(slices):
+                    closing_ref[branch, patch, piece] = held
 
 
 def start_kernel(where_ref, latent_ref, *refs):
@@ -134,19 +172,18 @@
     ]
     for copy in copies:
         copy.start()
-    sections, slices, _, block_cols = spread_to.shape
+    sections, _, block_cols = streams_to.shape
+    for piece in range(spread_to.shape[0]):
+        spread_to[piece] = latent_ref[0]
     for q in range(sections):
 
         @pl.when(where_ref[0] == q)
         def _():
             sources_to[...] = latent_ref[:, :, q * block_cols : (q + 1) * block_cols]
 
-    first = sources_to[0]
-    for section in range(sections):
-        held = first if section == 0 else jnp.zeros_like(first)
-        streams_to[section] = held
-        for piece in range(slices):
-            spread_to[section, piece] = held
+    streams_to[0] = sources_to[0]
+    for section in range(1, sections):
+        streams_to[section] = jnp.zeros(streams_to.shape[1:], streams_to.dtype)
     for copy in copies:
         copy.wait()
 
@@ -155,29 +192,63 @@
     total = streams_ref[section].astype(jnp.float32)
     for piece in range(parts_ref.shape[1]):
         total = total + parts_ref[section, piece].astype(jnp.float32)
-    return total.astype(jnp.bfloat16)
-
-
-def settle_kernel(entering, parts_ref, streams_ref, sources_ref, streams_to, spread_to, last_to):
+    return total
+
+
+def settle_kernel(entering, parts_ref, streams_ref, sources_ref, streams_to, spread_to):
     count, slices = parts_ref.shape[:2]
     for section in range(count):
         if section == 0:
             held = sources_ref[entering]
         else:
-            held = added(parts_ref, streams_ref, section - 1)
+            held = added(parts_ref, streams_ref, section - 1).astype(jnp.bfloat16)
         streams_to[section] = held
         for piece in range(slices):
             spread_to[section, piece] = held
-    last_to[...] = added(parts_ref, streams_ref, count - 1)
-
-
-def close_kernel(parts_ref, streams_ref, *refs):
-    *last_refs, finals_to = refs
-    lasts = [ref[...] for ref in last_refs]
-    lasts.append(added(parts_ref, streams_ref, parts_ref.shape[0] - 1))
-    finals = jnp.concatenate(lasts).reshape(finals_to.shape[1:])
-    for branch in range(finals_to.shape[0]):
-        finals_to[branch] = finals
+
+
+def settle_last_kernel(in_group, parts_ref, streams_ref, spread_to):
+    count, slices = parts_ref.shape[:2]
+    finished = added(parts_ref, streams_ref, count - 1)
+    tok_dev = finished.shape[0] // in_group
+    last = added(parts_ref, streams_ref, count - 2).astype(jnp.bfloat16)
+    for section in range(count):
+        held = last
+        if section < in_group:
+            held = finished[section * tok_dev : (section + 1) * tok_dev]
+            held = jnp.concatenate([held] * in_group).astype(jnp.bfloat16)
+        for piece in range(slices):
+            spread_to[section, piece] = held
+
+
+def guide_kernel(where_ref, closing_ref, guided_ref):
+    branches, patches, slices, block_rows, block_cols = closing_ref.shape
+    tok_dev = guided_ref.shape[0]
+    section, own_slice = where_ref[0], where_ref[2]
+
+    def combine(pair):
+        conditional, unconditional = pair
+        rows = unconditional + GUIDANCE_SCALE * (conditional - unconditional)
+        for at in range(block_rows // tok_dev):
+            guided_ref[:, at * block_cols : (at + 1) * block_cols] = rows[
+                at * tok_dev : (at + 1) * tok_dev
+            ].astype(jnp.bfloat16)
+
+    @pl.when(section >= patches)
+    def _():
+        pair = []
+        for branch in range(branches):
+            total = 0.0
+            for piece in range(slices):
+                total = total + closing_ref[branch, patches - 1, piece].astype(jnp.float32)
+            pair.append(total.astype(jnp.bfloat16).astype(jnp.float32))
+        combine(pair)
+
+    @pl.when(section < patches)
+    def _():
+        combine(
+            [closing_ref[branch, section, own_slice].astype(jnp.float32) for branch in range(branches)]
+        )
 
 
 def local(latent, modulation, qkv_weight, out_weight, norm_gain, stale_kv):
@@ -185,7 +256,6 @@
     seq_rank = lax.axis_index("seq")
     section_count = lax.axis_size("pipe")
     section_rank = lax.axis_index("pipe")
-    branch_rank = lax.axis_index("cfg")
     patches, tok_dev, model_width = latent.shape
     head_dim = norm_gain.shape[2]
     slice_count = min(seq_count, 8)
@@ -213,16 +283,20 @@
     block_rows = in_group * tok_dev
     block_cols = model_width // section_count
     rows = slice_count * block_rows
-    peers = None
-    if member_count > 1:
-        peers = [
-            [
-                q * seq_count + a + member_count * b
-                for q in range(section_count)
-                for b in range(slice_count)
-            ]
-            for a in range(member_count)
+    half = section_count // 2
+    groups_of = range(member_count)
+    in_slices = [[a + member_count * b for b in range(slice_count)] for a in groups_of]
+    peers = [[q * seq_count + at for q in range(section_count) for at in g] for g in in_slices]
+    closing_peers = [
+        [
+            (c * section_count + q) * seq_count + at
+            for c in range(2)
+            for q in range(h * half, (h + 1) * half)
+            for at in g
         ]
+        for h in range(2)
+        for g in in_slices
+    ]
 
     def exchange(value):
         value = value.reshape(homes, block_rows, block_cols)
@@ -233,7 +307,7 @@
     smem = pl.BlockSpec(memory_space=pltpu.SMEM)
     in_hbm = functools.partial(pltpu.with_memory_space_constraint, memory_space=pltpu.HBM)
     in_vmem = functools.partial(pltpu.with_memory_space_constraint, memory_space=pltpu.VMEM)
-    where = jnp.stack((section_rank, own_member)).astype(jnp.int32)
+    where = jnp.stack((section_rank, own_member, seq_rank // member_count)).astype(jnp.int32)
     sources = latent.reshape(GROUPS, block_rows, model_width)
     stream_shape = (section_count, block_rows, block_cols)
     spread_shape = (section_count, slice_count, block_rows, block_cols)
@@ -250,7 +324,7 @@
         + (
             pltpu.VMEM((GROUPS, block_rows, block_cols), jnp.bfloat16),
             jax.ShapeDtypeStruct(stream_shape, jnp.bfloat16),
-            jax.ShapeDtypeStruct(spread_shape, jnp.bfloat16),
+            jax.ShapeDtypeStruct((slice_count, block_rows, model_width), jnp.bfloat16),
         ),
         in_specs=[smem, vmem] + [pl.BlockSpec(memory_space=pltpu.HBM)] * len(loads),
         out_specs=(vmem,) * (len(loads) + 3),
@@ -261,7 +335,7 @@
     if member_count > 1:
         stale_rows = [group_cache.swapaxes(0, 1).reshape(2, -1, local_width)]
 
-    def attend(tick, features, table):
+    def attend(tick, features, table, partial_shape):
         operands = (
             where,
             features,
@@ -275,7 +349,7 @@
         return pl.pallas_call(
             functools.partial(section_kernel, tick, (tok_dev, head_dim)),
             out_shape=(
-                jax.ShapeDtypeStruct(features.shape, jnp.bfloat16),
+                jax.ShapeDtypeStruct(partial_shape, jnp.bfloat16),
                 jax.ShapeDtypeStruct(table.shape, jnp.bfloat16),
             ),
             in_specs=[smem] + [vmem] * (len(operands) - 1),
@@ -284,45 +358,43 @@
             compiler_params=pltpu.CompilerParams(vmem_limit_bytes=24 * 1024 * 1024),
         )(*operands)
 
-    def settle(entering, parts, streams):
+    def small(kernel, in_specs, *out_shapes):
         return pl.pallas_call(
-            functools.partial(settle_kernel, entering),
-            out_shape=tuple(
-                jax.ShapeDtypeStruct(shape, jnp.bfloat16)
-                for shape in (stream_shape, spread_shape, stream_shape[1:])
-            ),
-            in_specs=[vmem] * 3,
-            out_specs=(vmem,) * 3,
+            kernel,
+            out_shape=tuple(jax.ShapeDtypeStruct(shape, jnp.bfloat16) for shape in out_shapes),
+            in_specs=in_specs,
+            out_specs=(vmem,) * len(out_shapes),
             compiler_params=pltpu.CompilerParams(vmem_limit_bytes=8 * 1024 * 1024),
-        )(parts, streams, in_vmem(sources))
-
-    lasts = []
+        )
+
     ticks = GROUPS + section_count - 1
-    for tick in range(ticks):
-        partial_out, table = attend(tick, exchange(spread), table)
+    closing_shape = (2, half, slice_count, block_rows, block_cols)
+    features = lax.all_to_all(spread, "seq", 0, 0, axis_index_groups=in_slices)[None]
+    for tick in range(ticks - 1):
+        partial_out, table = attend(tick, features, table, spread_shape)
         parts = exchange(partial_out)
-        if tick < ticks - 1:
-            streams, spread, last = settle(min(tick + 1, GROUPS - 1), parts, streams)
-            lasts.append(last)
-
-    next_cache = table.reshape(stale_kv.shape)
-    per_home = patches // section_count
-    finals = pl.pallas_call(
-        close_kernel,
-        out_shape=jax.ShapeDtypeStruct((2, patches, tok_dev, block_cols), jnp.bfloat16),
-        in_specs=[vmem] * (GROUPS + 1),
-        out_specs=vmem,
-        compiler_params=pltpu.CompilerParams(vmem_limit_bytes=8 * 1024 * 1024),
-    )(parts, streams, *lasts[section_count - 1 :])
-    finals = finals.reshape(2, section_count, per_home, tok_dev, block_cols)
-    got = lax.all_to_all(
-        finals.reshape((-1,) + finals.shape[2:]), ("cfg", "pipe"), 0, 0
-    ).reshape(finals.shape)
-    half = section_count // 2
-    got = lax.dynamic_slice_in_dim(got, branch_rank * half, half, 1).astype(jnp.float32)
-    guided = (got[1] + GUIDANCE_SCALE * (got[0] - got[1])).astype(jnp.bfloat16)
-    guided = guided.transpose(1, 2, 0, 3).reshape(per_home, tok_dev, half * block_cols)
-    return (guided, next_cache)
+        if tick < ticks - 2:
+            streams, spread = small(
+                functools.partial(settle_kernel, min(tick + 1, GROUPS - 1)),
+                [vmem] * 3,
+                stream_shape,
+                spread_shape,
+            )(parts, streams, in_vmem(sources))
+        else:
+            (spread,) = small(
+                functools.partial(settle_last_kernel, in_group), [vmem] * 2, spread_shape
+            )(parts, streams)
+        features = exchange(spread)
+    closing, table = attend(ticks - 1, features, table, closing_shape)
+    closing = lax.all_to_all(
+        closing.reshape((-1,) + closing_shape[3:]),
+        ("cfg", "pipe", "seq"),
+        0,
+        0,
+        axis_index_groups=closing_peers,
+    ).reshape(closing_shape)
+    (guided,) = small(guide_kernel, [smem, vmem], (tok_dev, model_width // 2))(where, closing)
+    return (guided[None], table.reshape(stale_kv.shape))
 
 
 def solution(mesh):

time: 163 us -> 153 us (0.939)
  blocking collectives: 130 us -> 116 us
  waiting for transfers between devices: 4.13 us -> 9.32 us
    all_to_all x10 -> x8, blocking collectives: 130 us -> 101 us  [exchange(): lax.all_to_all(value, ('pipe', 'seq'), 0, 0, axis_index_groups=peers)]
    all_to_all x0 -> x1, blocking collectives: none -> 15 us  [local(): lax.all_to_all(spread, 'seq', 0, 0, axis_index_groups=in_slices)[None]]
    all_to_all x1, waiting for transfers between devices: 4.13 us -> 9.32 us  [local(): lax.all_to_all(closing.reshape((-1,) + closing_shape[3:]), ('cfg', 'pipe'...]
where the time goes in v9:
time: 153 us
  blocking collectives  116 us (76%)
  Pallas kernels  21.5 us (14%)
  waiting for transfers between devices  9.32 us (6%)
  starting transfers between devices  3.53 us (2%)
  local copies, waits for them, and re-layouts  1.61 us (1%)
    all_to_all x8, blocking collectives, exchange(): lax.all_to_all(value, ('pipe', 'seq'), 0, 0, axis_index_groups=peers)  101 us
    pallas_call x5, Pallas kernels, attend(): pl.pallas_call(functools.partial(section_kernel, tick, (tok_dev, head_dim...  16.1 us
    all_to_all x1, blocking collectives, local(): lax.all_to_all(spread, 'seq', 0, 0, axis_index_groups=in_slices)[None]  15 us
    all_to_all x1, waiting for transfers between devices, local(): lax.all_to_all(closing.reshape((-1,) + closing_shape[3:]), ('cfg', 'pipe'...  9.32 us
    pallas_call x1, Pallas kernels, local(): pl.pallas_call(start_kernel, out_shape=tuple((pltpu.VMEM(value.shape, val...  4 us
    all_to_all x1, starting transfers between devices, local(): lax.all_to_all(closing.reshape((-1,) + closing_shape[3:]), ('cfg', 'pipe'...  3.53 us
  transfers between devices with their start and end apart: 1, of which 1 were waited for; matrix products, arithmetic and copies ran while one was open for 0% of the time, Pallas kernels for 0%

profile of v9, /device:TPU:0, one launch (start us, length us, event | category | flops | bytes accessed | tf_op | source)
XLA Modules:
  0.0 152.8 jit_solution(16571838346863506199)
XLA Ops:
  0.6 0.1 pad_add_fusion.where_ref
  0.7 0.0 copy-start
  0.7 0.9 copy-done
  1.6 4.0 %shard_map.77 = (bf16[2048,1536]{1,0:T(8,128)(2,1)S(1)}, bf16[512,2048]{1,0:T(8,128)(2,1)S(1)}, f32[3,1,2048]{2,1,0:T(1,128)S(1)}, f32[2,128]{1,0:T(2,128)S(1)},...) custom-call(s32[3]{0:T(128)S(1)} %pad_add_fusion.where_ref, ...), custom_call_target="tpu_custom_call" | custom-call | tf_op jit(solution)/shard_map/pallas_call | solution.py:321
  5.6 15.0 %all_to_all.50 = bf16[4,16,2048]{2,1,0:T(8,128)(2,1)S(1)} all-to-all(bf16[4,16,2048]{2,1,0:T(8,128)(2,1)S(1)} %get-tuple-element.26), channel_id=1, replica_groups={{0,1,2,3},{4,5,6,7},{8,9,10,11},{12,13,14,15},{16,17,18,19},{20,21,22,2..., dimensions={0} | all-to-all | bytes 524288 | tf_op jit(solution)/shard_map/all_to_all | solution.py:372
  20.6 3.1 %shard_map.78 = (bf16[4,4,16,512]{3,2,1,0:T(8,128)(2,1)S(1)}, bf16[2,2,64,512]{3,2,1,0:T(8,128)(2,1)S(1)}) custom-call(s32[3]{0:T(128)S(1)} %pad_add_fusion.where_ref, bf16[1,4,16,2048]{3,2,1,0:T(8,128)(2,1)S(1)} %bitcast.36, f32[3,1,2048]{2,1,0:T(1,128)S(1)} %get-tuple-element.27.mod_ref, ...), custom_call_target="tpu_custom_call", output_to_operand_aliasing={{1}: (6, {})} | custom-call | tf_op jit(solution)/shard_map/pallas_call | solution.py:349
  23.7 14.6 %all_to_all.51 = bf16[16,16,512]{2,1,0:T(8,128)(2,1)S(1)} all-to-all(bf16[16,16,512]{2,1,0:T(8,128)(2,1)S(1)} %bitcast.44), channel_id=1, replica_groups={{0,1,2,3,4,5,6,7,8,9,10,11,12,13,14,15},{16,17,18,19,20,21,22,23,24,25,..., dimensions={0} | all-to-all | bytes 524288 | tf_op jit(solution)/shard_map/all_to_all | solution.py:303
  38.4 12.4 %all_to_all.52 = bf16[16,16,512]{2,1,0:T(8,128)(2,1)S(1)} all-to-all(bf16[16,16,512]{2,1,0:T(8,128)(2,1)S(1)} %bitcast.45), channel_id=1, replica_groups={{0,1,2,3,4,5,6,7,8,9,10,11,12,13,14,15},{16,17,18,19,20,21,22,23,24,25,..., dimensions={0} | all-to-all | bytes 524288 | tf_op jit(solution)/shard_map/all_to_all | solution.py:303
  50.8 3.1 %shard_map.80 = (bf16[4,4,16,512]{3,2,1,0:T(8,128)(2,1)S(1)}, bf16[2,2,64,512]{3,2,1,0:T(8,128)(2,1)S(1)}) custom-call(s32[3]{0:T(128)S(1)} %pad_add_fusion.where_ref, bf16[4,4,16,512]{3,2,1,0:T(8,128)(2,1)S(1)} %bitcast.33, f32[3,1,2048]{2,1,0:T(1,128)S(1)} %get-tuple-element.27.mod_ref, ...), custom_call_target="tpu_custom_call", output_to_operand_aliasing={{1}: (6, {})} | custom-call | tf_op jit(solution)/shard_map/pallas_call | solution.py:349
  53.9 12.3 %all_to_all.53 = bf16[16,16,512]{2,1,0:T(8,128)(2,1)S(1)} all-to-all(bf16[16,16,512]{2,1,0:T(8,128)(2,1)S(1)} %bitcast.46), channel_id=1, replica_groups={{0,1,2,3,4,5,6,7,8,9,10,11,12,13,14,15},{16,17,18,19,20,21,22,23,24,25,..., dimensions={0} | all-to-all | bytes 524288 | tf_op jit(solution)/shard_map/all_to_all | solution.py:303
  66.3 12.3 %all_to_all.54 = bf16[16,16,512]{2,1,0:T(8,128)(2,1)S(1)} all-to-all(bf16[16,16,512]{2,1,0:T(8,128)(2,1)S(1)} %bitcast.47), channel_id=1, replica_groups={{0,1,2,3,4,5,6,7,8,9,10,11,12,13,14,15},{16,17,18,19,20,21,22,23,24,25,..., dimensions={0} | all-to-all | bytes 524288 | tf_op jit(solution)/shard_map/all_to_all | solution.py:303
  78.6 3.1 %shard_map.82 = (bf16[4,4,16,512]{3,2,1,0:T(8,128)(2,1)S(1)}, bf16[2,2,64,512]{3,2,1,0:T(8,128)(2,1)S(1)}) custom-call(s32[3]{0:T(128)S(1)} %pad_add_fusion.where_ref, bf16[4,4,16,512]{3,2,1,0:T(8,128)(2,1)S(1)} %bitcast.34, f32[3,1,2048]{2,1,0:T(1,128)S(1)} %get-tuple-element.27.mod_ref, ...), custom_call_target="tpu_custom_call", output_to_operand_aliasing={{1}: (6, {})} | custom-call | tf_op jit(solution)/shard_map/pallas_call | solution.py:349
  81.7 12.3 %all_to_all.55 = bf16[16,16,512]{2,1,0:T(8,128)(2,1)S(1)} all-to-all(bf16[16,16,512]{2,1,0:T(8,128)(2,1)S(1)} %bitcast.48), channel_id=1, replica_groups={{0,1,2,3,4,5,6,7,8,9,10,11,12,13,14,15},{16,17,18,19,20,21,22,23,24,25,..., dimensions={0} | all-to-all | bytes 524288 | tf_op jit(solution)/shard_map/all_to_all | solution.py:303
  94.1 12.3 %all_to_all.56 = bf16[16,16,512]{2,1,0:T(8,128)(2,1)S(1)} all-to-all(bf16[16,16,512]{2,1,0:T(8,128)(2,1)S(1)} %bitcast.43), channel_id=1, replica_groups={{0,1,2,3,4,5,6,7,8,9,10,11,12,13,14,15},{16,17,18,19,20,21,22,23,24,25,..., dimensions={0} | all-to-all | bytes 524288 | tf_op jit(solution)/shard_map/all_to_all | solution.py:303
  106.5 3.1 %shard_map.84 = (bf16[4,4,16,512]{3,2,1,0:T(8,128)(2,1)S(1)}, bf16[2,2,64,512]{3,2,1,0:T(8,128)(2,1)S(1)}) custom-call(s32[3]{0:T(128)S(1)} %pad_add_fusion.where_ref, bf16[4,4,16,512]{3,2,1,0:T(8,128)(2,1)S(1)} %bitcast.35, f32[3,1,2048]{2,1,0:T(1,128)S(1)} %get-tuple-element.27.mod_ref, ...), custom_call_target="tpu_custom_call", output_to_operand_aliasing={{1}: (6, {})} | custom-call | tf_op jit(solution)/shard_map/pallas_call | solution.py:349
  109.5 12.3 %all_to_all.57 = bf16[16,16,512]{2,1,0:T(8,128)(2,1)S(1)} all-to-all(bf16[16,16,512]{2,1,0:T(8,128)(2,1)S(1)} %bitcast.49), channel_id=1, replica_groups={{0,1,2,3,4,5,6,7,8,9,10,11,12,13,14,15},{16,17,18,19,20,21,22,23,24,25,..., dimensions={0} | all-to-all | bytes 524288 | tf_op jit(solution)/shard_map/all_to_all | solution.py:303
  121.9 12.3 %all_to_all.58 = bf16[16,16,512]{2,1,0:T(8,128)(2,1)S(1)} all-to-all(bf16[16,16,512]{2,1,0:T(8,128)(2,1)S(1)} %bitcast.42), channel_id=1, replica_groups={{0,1,2,3,4,5,6,7,8,9,10,11,12,13,14,15},{16,17,18,19,20,21,22,23,24,25,..., dimensions={0} | all-to-all | bytes 524288 | tf_op jit(solution)/shard_map/all_to_all | solution.py:303
  134.2 3.8 %shard_map.86 = (bf16[2,2,4,16,512]{4,3,2,1,0:T(8,128)(2,1)}, bf16[2,2,64,512]{3,2,1,0:T(8,128)(2,1)S(1)}) custom-call(s32[3]{0:T(128)S(1)} %pad_add_fusion.where_ref, bf16[4,4,16,512]{3,2,1,0:T(8,128)(2,1)S(1)} %bitcast.32, f32[3,1,2048]{2,1,0:T(1,128)S(1)} %get-tuple-element.27.mod_ref, ...), custom_call_target="tpu_custom_call", output_to_operand_aliasing={{1}: (6, {})} | custom-call | tf_op jit(solution)/shard_map/pallas_call | solution.py:349
  138.1 3.5 %all-to-all-start.9 = ((bf16[16,16,512]{2,1,0:T(8,128)(2,1)}), bf16[16,16,512]{2,1,0:T(8,128)(2,1)S(1)}, u32[]{:S(2)}, u32[]{:S(2)}) async-start(bf16[16,16,512]{2,1,0:T(8,128)(2,1)} %bitcast.25), calls=%async_computation.9 | async-start | bytes 524288 | tf_op jit(solution)/shard_map/all_to_all | solution.py:389
  141.6 0.7 copy.19
  142.3 9.3 %all-to-all-done.9 = bf16[16,16,512]{2,1,0:T(8,128)(2,1)S(1)} async-done(((bf16[16,16,512]{2,1,0:T(8,128)(2,1)}), bf16[16,16,512]{2,1,0:T(8,128)(2,1)S(1)}, u32[]{:S(2)}, u32[]{:S(2)}) %all-to-all-start.9) | async-done | bytes 262176 | tf_op jit(solution)/shard_map/all_to_all | solution.py:389
  151.6 1.2 shard_map.87
  (4 shorter events, 0.1 us)
Async XLA Ops:
  0.7 0.9 copy-start
  138.1 13.6 %all-to-all-start.9 = ((bf16[16,16,512]{2,1,0:T(8,128)(2,1)}), bf16[16,16,512]{2,1,0:T(8,128)(2,1)S(1)}, u32[]{:S(2)}, u32[]{:S(2)}) async-start(bf16[16,16,512]{2,1,0:T(8,128)(2,1)} %bitcast.25), calls=%async_computation.9 | async-start | bytes 524288 | tf_op jit(solution)/shard_map/all_to_all | solution.py:389

commit v10 on v9

--- a/solution.py
+++ b/solution.py
@@ -11,6 +11,7 @@
 GUIDANCE_SCALE = 6.0
 EPSILON = 1e-06
 GROUPS = 2
+PIECES = 4
 
 
 def swapped(value, axis, bit):
@@ -32,6 +33,10 @@
 
 
 def section_kernel(tick, sizes, where_ref, rows_ref, mod_ref, qkv_ref, out_ref, gain_ref, *refs):
+    loading = tick == 0
+    weights_from = (qkv_ref, out_ref)
+    if loading:
+        *refs, qkv_ref, out_ref, sems = refs
     *stale_refs, old_table_ref, partial_ref, table_ref = refs
     closing = len(partial_ref.shape) == 5
     tok_dev, head_dim = sizes
@@ -44,6 +49,19 @@
     heads = local_width // head_dim
     section, own_member, own_slice = where_ref[0], where_ref[1], where_ref[2]
     group = tick - section
+    copies = []
+    if loading:
+        piece_rows = qkv_ref.shape[0] // PIECES
+        for at in range(PIECES):
+            piece = pl.ds(at * piece_rows, piece_rows)
+            copies.append(
+                pltpu.make_async_copy(
+                    weights_from[0].at[piece], qkv_ref.at[piece], sems.at[at]
+                )
+            )
+        copies.append(pltpu.make_async_copy(weights_from[1], out_ref, sems.at[PIECES]))
+        for copy in copies:
+            copy.start()
     parts = [rows_ref[q].reshape(rows, block_cols).astype(jnp.float32) for q in range(blocks)]
     mean = sum(jnp.sum(x, axis=-1, keepdims=True) for x in parts) / width
     parts = [x - mean for x in parts]
@@ -56,7 +74,16 @@
             (x * inverse * (1.0 + mod_ref[1, :, at]) + mod_ref[0, :, at]).astype(jnp.bfloat16)
         )
     modulated = jnp.concatenate(modulated, axis=1)
-    mixed = jnp.dot(modulated, qkv_ref[...], preferred_element_type=jnp.float32)
+    if loading:
+        mixed = 0.0
+        for at in range(PIECES):
+            copies[at].wait()
+            piece = slice(at * piece_rows, (at + 1) * piece_rows)
+            mixed = mixed + jnp.dot(
+                modulated[:, piece], qkv_ref[piece, :], preferred_element_type=jnp.float32
+            )
+    else:
+        mixed = jnp.dot(modulated, qkv_ref[...], preferred_element_type=jnp.float32)
 
     def by_patch(values):
         values = values.reshape(slices, in_group, tok_dev, head_dim).swapaxes(0, 1)
@@ -105,6 +132,8 @@
         attended.append((summed / total).astype(jnp.bfloat16))
     attended = jnp.concatenate(attended, axis=1)
 
+    if loading:
+        copies[PIECES].wait()
     projected = jnp.dot(attended, out_ref[...], preferred_element_type=jnp.float32)
     projected = mod_ref[2] * projected
     if closing:
@@ -166,26 +195,22 @@
     loads = (len(refs) - 4) // 2
     from_refs, to_refs = refs[:loads], refs[loads : 2 * loads]
     sources_to, streams_to, spread_to, sems = refs[2 * loads :]
+    sections, _, block_cols = streams_to.shape
+    own_cols = pl.ds(pl.multiple_of(where_ref[0] * block_cols, block_cols), block_cols)
+    pairs = [(latent_ref.at[0], spread_to.at[piece]) for piece in range(spread_to.shape[0])]
+    pairs.append((latent_ref.at[:, :, own_cols], sources_to))
+    pairs.extend(zip(from_refs, to_refs))
     copies = [
         pltpu.make_async_copy(from_ref, to_ref, sems.at[at])
-        for at, (from_ref, to_ref) in enumerate(zip(from_refs, to_refs))
+        for at, (from_ref, to_ref) in enumerate(pairs)
     ]
     for copy in copies:
         copy.start()
-    sections, _, block_cols = streams_to.shape
-    for piece in range(spread_to.shape[0]):
-        spread_to[piece] = latent_ref[0]
-    for q in range(sections):
-
-        @pl.when(where_ref[0] == q)
-        def _():
-            sources_to[...] = latent_ref[:, :, q * block_cols : (q + 1) * block_cols]
-
-    streams_to[0] = sources_to[0]
     for section in range(1, sections):
         streams_to[section] = jnp.zeros(streams_to.shape[1:], streams_to.dtype)
     for copy in copies:
         copy.wait()
+    streams_to[0] = sources_to[0]
 
 
 def added(parts_ref, streams_ref, section):
@@ -305,6 +330,7 @@
 
     vmem = pl.BlockSpec(memory_space=pltpu.VMEM)
     smem = pl.BlockSpec(memory_space=pltpu.SMEM)
+    hbm = pl.BlockSpec(memory_space=pltpu.HBM)
     in_hbm = functools.partial(pltpu.with_memory_space_constraint, memory_space=pltpu.HBM)
     in_vmem = functools.partial(pltpu.with_memory_space_constraint, memory_space=pltpu.VMEM)
     where = jnp.stack((section_rank, own_member, seq_rank // member_count)).astype(jnp.int32)
@@ -312,13 +338,11 @@
     stream_shape = (section_count, block_rows, block_cols)
     spread_shape = (section_count, slice_count, block_rows, block_cols)
     loads = (
-        qkv_slice,
-        out_slice,
         modulation.reshape(3, 1, model_width),
         norm_gain[0],
         own_cache.reshape(2, GROUPS, rows, local_width),
     )
-    qkv_slice, out_slice, modulation, norm_gain, table, sources, streams, spread = pl.pallas_call(
+    modulation, norm_gain, table, sources, streams, spread = pl.pallas_call(
         start_kernel,
         out_shape=tuple(pltpu.VMEM(value.shape, value.dtype) for value in loads)
         + (
@@ -326,34 +350,42 @@
             jax.ShapeDtypeStruct(stream_shape, jnp.bfloat16),
             jax.ShapeDtypeStruct((slice_count, block_rows, model_width), jnp.bfloat16),
         ),
-        in_specs=[smem, vmem] + [pl.BlockSpec(memory_space=pltpu.HBM)] * len(loads),
+        in_specs=[smem] + [hbm] * (len(loads) + 1),
         out_specs=(vmem,) * (len(loads) + 3),
-        scratch_shapes=[pltpu.SemaphoreType.DMA((len(loads),))],
+        scratch_shapes=[pltpu.SemaphoreType.DMA((len(loads) + slice_count + 1,))],
         compiler_params=pltpu.CompilerParams(vmem_limit_bytes=4 * 1024 * 1024),
-    )(where, sources, *map(in_hbm, loads))
+    )(where, in_hbm(sources), *map(in_hbm, loads))
     stale_rows = []
     if member_count > 1:
         stale_rows = [group_cache.swapaxes(0, 1).reshape(2, -1, local_width)]
 
-    def attend(tick, features, table, partial_shape):
+    def attend(tick, features, table, weights, partial_shape):
+        loading = tick == 0
         operands = (
             where,
             features,
             in_vmem(modulation),
-            in_vmem(qkv_slice),
-            in_vmem(out_slice),
+            *map(in_hbm if loading else in_vmem, weights),
             in_vmem(norm_gain),
             *stale_rows,
             table,
         )
+        in_specs = [smem] + [vmem] * (len(operands) - 1)
+        out_shape = (
+            jax.ShapeDtypeStruct(partial_shape, jnp.bfloat16),
+            jax.ShapeDtypeStruct(table.shape, jnp.bfloat16),
+        )
+        scratch = []
+        if loading:
+            in_specs[3:5] = [hbm, hbm]
+            out_shape += tuple(pltpu.VMEM(w.shape, jnp.bfloat16) for w in weights)
+            scratch = [pltpu.SemaphoreType.DMA((PIECES + 1,))]
         return pl.pallas_call(
             functools.partial(section_kernel, tick, (tok_dev, head_dim)),
-            out_shape=(
-                jax.ShapeDtypeStruct(partial_shape, jnp.bfloat16),
-                jax.ShapeDtypeStruct(table.shape, jnp.bfloat16),
-            ),
-            in_specs=[smem] + [vmem] * (len(operands) - 1),
-            out_specs=(vmem, vmem),
+            out_shape=out_shape,
+            in_specs=in_specs,
+            out_specs=(vmem,) * len(out_shape),
+            scratch_shapes=scratch,
             input_output_aliases={len(operands) - 1: 1},
             compiler_params=pltpu.CompilerParams(vmem_limit_bytes=24 * 1024 * 1024),
         )(*operands)
@@ -370,8 +402,10 @@
     ticks = GROUPS + section_count - 1
     closing_shape = (2, half, slice_count, block_rows, block_cols)
     features = lax.all_to_all(spread, "seq", 0, 0, axis_index_groups=in_slices)[None]
+    weights = [qkv_slice, out_slice]
     for tick in range(ticks - 1):
-        partial_out, table = attend(tick, features, table, spread_shape)
+        partial_out, table, *loaded = attend(tick, features, table, weights, spread_shape)
+        weights = loaded or weights
         parts = exchange(partial_out)
         if tick < ticks - 2:
             streams, spread = small(
@@ -385,7 +419,7 @@
                 functools.partial(settle_last_kernel, in_group), [vmem] * 2, spread_shape
             )(parts, streams)
         features = exchange(spread)
-    closing, table = attend(ticks - 1, features, table, closing_shape)
+    closing, table = attend(ticks - 1, features, table, weights, closing_shape)
     closing = lax.all_to_all(
         closing.reshape((-1,) + closing_shape[3:]),
         ("cfg", "pipe", "seq"),

time: 153 us -> 152 us (level)
    pallas_call x1, Pallas kernels: 4 us -> 1.75 us  [local(): pl.pallas_call(start_kernel, out_shape=tuple((pltpu.VMEM(value.shape, val...]
    pallas_call x5, Pallas kernels: 16.1 us -> 18.1 us  [attend(): pl.pallas_call(functools.partial(section_kernel, tick, (tok_dev, head_dim...]
where the time goes in v10:
time: 152 us
  blocking collectives  116 us (76%)
  Pallas kernels  21.2 us (14%)
  waiting for transfers between devices  9.32 us (6%)
  starting transfers between devices  3.53 us (2%)
    all_to_all x8, blocking collectives, exchange(): lax.all_to_all(value, ('pipe', 'seq'), 0, 0, axis_index_groups=peers)  101 us
    pallas_call x5, Pallas kernels, attend(): pl.pallas_call(functools.partial(section_kernel, tick, (tok_dev, head_dim...  18.1 us
    all_to_all x1, blocking collectives, local(): lax.all_to_all(spread, 'seq', 0, 0, axis_index_groups=in_slices)[None]  15 us
    all_to_all x1, waiting for transfers between devices, local(): lax.all_to_all(closing.reshape((-1,) + closing_shape[3:]), ('cfg', 'pipe'...  9.32 us
    all_to_all x1, starting transfers between devices, local(): lax.all_to_all(closing.reshape((-1,) + closing_shape[3:]), ('cfg', 'pipe'...  3.53 us
  transfers between devices with their start and end apart: 1, of which 1 were waited for; matrix products, arithmetic and copies ran while one was open for 0% of the time, Pallas kernels for 0%

profile of v10, /device:TPU:0, one launch (start us, length us, event | category | flops | bytes accessed | tf_op | source)
XLA Modules:
  0.0 151.6 jit_solution(14685646850002822345)
XLA Ops:
  0.6 0.1 pad_add_fusion.where_ref
  0.7 1.7 %shard_map.77 = (f32[3,1,2048]{2,1,0:T(1,128)S(1)}, f32[2,128]{1,0:T(2,128)S(1)}, bf16[2,2,64,512]{3,2,1,0:T(8,128)(2,1)S(1)}, bf16[2,16,512]{2,1,0:T(8,128)(2,1...) custom-call(s32[3]{0:T(128)S(1)} %pad_add_fusion.where_ref, bf16[2,16,2048]{2,1,0:T(8,128)(2,1)} %bitcast.53, ...), custom_call_target="tpu_custom_call" | custom-call | tf_op jit(solution)/shard_map/pallas_call | solution.py:345
  2.5 15.0 %all_to_all.50 = bf16[4,16,2048]{2,1,0:T(8,128)(2,1)S(1)} all-to-all(bf16[4,16,2048]{2,1,0:T(8,128)(2,1)S(1)} %get-tuple-element.26), channel_id=1, replica_groups={{0,1,2,3},{4,5,6,7},{8,9,10,11},{12,13,14,15},{16,17,18,19},{20,21,22,2..., dimensions={0} | all-to-all | bytes 524288 | tf_op jit(solution)/shard_map/all_to_all | solution.py:404
  17.5 5.0 %shard_map.78 = (bf16[4,4,16,512]{3,2,1,0:T(8,128)(2,1)S(1)}, bf16[2,2,64,512]{3,2,1,0:T(8,128)(2,1)S(1)}, bf16[2048,1536]{1,0:T(8,128)(2,1)S(1)}, bf16[512,2048]{1,0:T(8,128)(2,1)S(1)}) custom-call(s32[3]{0:T(128)S(1)} %pad_add_fusion.where_ref, bf16[1,4,16,2048]{3,2,1,0:T(8,128)(2,1)S(1)} %bitcast.33, ...), custom_call_target="tpu_custom_call", output_to_operand_aliasing={{1}: (6, {})} | custom-call | tf_op jit(solution)/shard_map/pallas_call | solution.py:383
  22.5 14.6 %all_to_all.51 = bf16[16,16,512]{2,1,0:T(8,128)(2,1)S(1)} all-to-all(bf16[16,16,512]{2,1,0:T(8,128)(2,1)S(1)} %bitcast.43), channel_id=1, replica_groups={{0,1,2,3,4,5,6,7,8,9,10,11,12,13,14,15},{16,17,18,19,20,21,22,23,24,25,..., dimensions={0} | all-to-all | bytes 524288 | tf_op jit(solution)/shard_map/all_to_all | solution.py:328
  37.2 12.4 %all_to_all.52 = bf16[16,16,512]{2,1,0:T(8,128)(2,1)S(1)} all-to-all(bf16[16,16,512]{2,1,0:T(8,128)(2,1)S(1)} %bitcast.45), channel_id=1, replica_groups={{0,1,2,3,4,5,6,7,8,9,10,11,12,13,14,15},{16,17,18,19,20,21,22,23,24,25,..., dimensions={0} | all-to-all | bytes 524288 | tf_op jit(solution)/shard_map/all_to_all | solution.py:328
  49.6 3.1 %shard_map.80 = (bf16[4,4,16,512]{3,2,1,0:T(8,128)(2,1)S(1)}, bf16[2,2,64,512]{3,2,1,0:T(8,128)(2,1)S(1)}) custom-call(s32[3]{0:T(128)S(1)} %pad_add_fusion.where_ref, bf16[4,4,16,512]{3,2,1,0:T(8,128)(2,1)S(1)} %bitcast.34, f32[3,1,2048]{2,1,0:T(1,128)S(1)} %get-tuple-element.27.mod_ref, ...), custom_call_target="tpu_custom_call", output_to_operand_aliasing={{1}: (6, {})} | custom-call | tf_op jit(solution)/shard_map/pallas_call | solution.py:383
  52.7 12.3 %all_to_all.53 = bf16[16,16,512]{2,1,0:T(8,128)(2,1)S(1)} all-to-all(bf16[16,16,512]{2,1,0:T(8,128)(2,1)S(1)} %bitcast.46), channel_id=1, replica_groups={{0,1,2,3,4,5,6,7,8,9,10,11,12,13,14,15},{16,17,18,19,20,21,22,23,24,25,..., dimensions={0} | all-to-all | bytes 524288 | tf_op jit(solution)/shard_map/all_to_all | solution.py:328
  65.1 12.3 %all_to_all.54 = bf16[16,16,512]{2,1,0:T(8,128)(2,1)S(1)} all-to-all(bf16[16,16,512]{2,1,0:T(8,128)(2,1)S(1)} %bitcast.47), channel_id=1, replica_groups={{0,1,2,3,4,5,6,7,8,9,10,11,12,13,14,15},{16,17,18,19,20,21,22,23,24,25,..., dimensions={0} | all-to-all | bytes 524288 | tf_op jit(solution)/shard_map/all_to_all | solution.py:328
  77.4 3.1 %shard_map.82 = (bf16[4,4,16,512]{3,2,1,0:T(8,128)(2,1)S(1)}, bf16[2,2,64,512]{3,2,1,0:T(8,128)(2,1)S(1)}) custom-call(s32[3]{0:T(128)S(1)} %pad_add_fusion.where_ref, bf16[4,4,16,512]{3,2,1,0:T(8,128)(2,1)S(1)} %bitcast.35, f32[3,1,2048]{2,1,0:T(1,128)S(1)} %get-tuple-element.27.mod_ref, ...), custom_call_target="tpu_custom_call", output_to_operand_aliasing={{1}: (6, {})} | custom-call | tf_op jit(solution)/shard_map/pallas_call | solution.py:383
  80.5 12.3 %all_to_all.55 = bf16[16,16,512]{2,1,0:T(8,128)(2,1)S(1)} all-to-all(bf16[16,16,512]{2,1,0:T(8,128)(2,1)S(1)} %bitcast.48), channel_id=1, replica_groups={{0,1,2,3,4,5,6,7,8,9,10,11,12,13,14,15},{16,17,18,19,20,21,22,23,24,25,..., dimensions={0} | all-to-all | bytes 524288 | tf_op jit(solution)/shard_map/all_to_all | solution.py:328
  92.9 12.3 %all_to_all.56 = bf16[16,16,512]{2,1,0:T(8,128)(2,1)S(1)} all-to-all(bf16[16,16,512]{2,1,0:T(8,128)(2,1)S(1)} %bitcast.44), channel_id=1, replica_groups={{0,1,2,3,4,5,6,7,8,9,10,11,12,13,14,15},{16,17,18,19,20,21,22,23,24,25,..., dimensions={0} | all-to-all | bytes 524288 | tf_op jit(solution)/shard_map/all_to_all | solution.py:328
  105.2 3.1 %shard_map.84 = (bf16[4,4,16,512]{3,2,1,0:T(8,128)(2,1)S(1)}, bf16[2,2,64,512]{3,2,1,0:T(8,128)(2,1)S(1)}) custom-call(s32[3]{0:T(128)S(1)} %pad_add_fusion.where_ref, bf16[4,4,16,512]{3,2,1,0:T(8,128)(2,1)S(1)} %bitcast.36, f32[3,1,2048]{2,1,0:T(1,128)S(1)} %get-tuple-element.27.mod_ref, ...), custom_call_target="tpu_custom_call", output_to_operand_aliasing={{1}: (6, {})} | custom-call | tf_op jit(solution)/shard_map/pallas_call | solution.py:383
  108.3 12.3 %all_to_all.57 = bf16[16,16,512]{2,1,0:T(8,128)(2,1)S(1)} all-to-all(bf16[16,16,512]{2,1,0:T(8,128)(2,1)S(1)} %bitcast.49), channel_id=1, replica_groups={{0,1,2,3,4,5,6,7,8,9,10,11,12,13,14,15},{16,17,18,19,20,21,22,23,24,25,..., dimensions={0} | all-to-all | bytes 524288 | tf_op jit(solution)/shard_map/all_to_all | solution.py:328
  120.7 12.3 %all_to_all.58 = bf16[16,16,512]{2,1,0:T(8,128)(2,1)S(1)} all-to-all(bf16[16,16,512]{2,1,0:T(8,128)(2,1)S(1)} %bitcast.42), channel_id=1, replica_groups={{0,1,2,3,4,5,6,7,8,9,10,11,12,13,14,15},{16,17,18,19,20,21,22,23,24,25,..., dimensions={0} | all-to-all | bytes 524288 | tf_op jit(solution)/shard_map/all_to_all | solution.py:328
  133.0 3.8 %shard_map.86 = (bf16[2,2,4,16,512]{4,3,2,1,0:T(8,128)(2,1)}, bf16[2,2,64,512]{3,2,1,0:T(8,128)(2,1)S(1)}) custom-call(s32[3]{0:T(128)S(1)} %pad_add_fusion.where_ref, bf16[4,4,16,512]{3,2,1,0:T(8,128)(2,1)S(1)} %bitcast.32, f32[3,1,2048]{2,1,0:T(1,128)S(1)} %get-tuple-element.27.mod_ref, ...), custom_call_target="tpu_custom_call", output_to_operand_aliasing={{1}: (6, {})} | custom-call | tf_op jit(solution)/shard_map/pallas_call | solution.py:383
  136.8 3.5 %all-to-all-start.9 = ((bf16[16,16,512]{2,1,0:T(8,128)(2,1)}), bf16[16,16,512]{2,1,0:T(8,128)(2,1)S(1)}, u32[]{:S(2)}, u32[]{:S(2)}) async-start(bf16[16,16,512]{2,1,0:T(8,128)(2,1)} %bitcast.25), calls=%async_computation.9 | async-start | bytes 524288 | tf_op jit(solution)/shard_map/all_to_all | solution.py:423
  140.4 0.7 copy.19
  141.1 9.3 %all-to-all-done.9 = bf16[16,16,512]{2,1,0:T(8,128)(2,1)S(1)} async-done(((bf16[16,16,512]{2,1,0:T(8,128)(2,1)}), bf16[16,16,512]{2,1,0:T(8,128)(2,1)S(1)}, u32[]{:S(2)}, u32[]{:S(2)}) %all-to-all-start.9) | async-done | bytes 262176 | tf_op jit(solution)/shard_map/all_to_all | solution.py:423
  150.4 1.2 shard_map.87
  (4 shorter events, 0.1 us)
Async XLA Ops:
  136.8 13.6 %all-to-all-start.9 = ((bf16[16,16,512]{2,1,0:T(8,128)(2,1)}), bf16[16,16,512]{2,1,0:T(8,128)(2,1)S(1)}, u32[]{:S(2)}, u32[]{:S(2)}) async-start(bf16[16,16,512]{2,1,0:T(8,128)(2,1)} %bitcast.25), calls=%async_computation.9 | async-start | bytes 524288 | tf_op jit(solution)/shard_map/all_to_all | solution.py:423

commit v11 on v10

--- a/solution.py
+++ b/solution.py
@@ -11,7 +11,8 @@
 GUIDANCE_SCALE = 6.0
 EPSILON = 1e-06
 GROUPS = 2
-PIECES = 4
+PIECES = 8
+IN_FLIGHT = 3
 
 
 def swapped(value, axis, bit):
@@ -60,7 +61,7 @@
                 )
             )
         copies.append(pltpu.make_async_copy(weights_from[1], out_ref, sems.at[PIECES]))
-        for copy in copies:
+        for copy in copies[:IN_FLIGHT]:
             copy.start()
     parts = [rows_ref[q].reshape(rows, block_cols).astype(jnp.float32) for q in range(blocks)]
     mean = sum(jnp.sum(x, axis=-1, keepdims=True) for x in parts) / width
@@ -78,6 +79,8 @@
         mixed = 0.0
         for at in range(PIECES):
             copies[at].wait()
+            if at + IN_FLIGHT < len(copies):
+                copies[at + IN_FLIGHT].start()
             piece = slice(at * piece_rows, (at + 1) * piece_rows)
             mixed = mixed + jnp.dot(
                 modulated[:, piece], qkv_ref[piece, :], preferred_element_type=jnp.float32
@@ -92,44 +95,50 @@
     def query_patch(shape):
         return lax.broadcasted_iota(jnp.int32, shape, 0) // tok_dev % in_group
 
-    square, wide = (rows, rows), (rows, groups * rows)
-    fresh_patch = lax.broadcasted_iota(jnp.int32, square, 1) // group_rows
-    old_patch = lax.broadcasted_iota(jnp.int32, wide, 1) // group_rows - group * in_group
+    fresh_shape, old_shape = (rows, rows), (rows, groups * rows)
+    fresh_patch = lax.broadcasted_iota(jnp.int32, fresh_shape, 1) // group_rows
+    old_patch = lax.broadcasted_iota(jnp.int32, old_shape, 1) // group_rows - group * in_group
     masks = [
-        fresh_patch <= query_patch(square),
-        jnp.logical_or(old_patch < 0, old_patch > query_patch(wide)),
+        (fresh_patch <= query_patch(fresh_shape)).astype(jnp.float32),
+        jnp.logical_or(old_patch < 0, old_patch > query_patch(old_shape)).astype(jnp.float32),
     ]
     for ref in stale_refs:
         at = lax.broadcasted_iota(jnp.int32, (rows, ref.shape[1]), 1)
-        masks.append(at // (groups * rows) != own_member)
-    attended = []
-    fresh = []
-    for head in range(heads):
-        at = slice(head * head_dim, (head + 1) * head_dim)
-        query, key, value = (
-            mixed[:, (3 * head + j) * head_dim : (3 * head + j + 1) * head_dim] for j in range(3)
-        )
-        query = head_norm(query, gain_ref[0:1, :]).astype(jnp.bfloat16)
-        key = by_patch(head_norm(key, gain_ref[1:2, :]))
-        value = by_patch(value)
-        fresh.append((key, value))
-        keys, values = (
-            [new, old_table_ref[j, :, :, at].reshape(groups * rows, head_dim)]
-            + [ref[j, :, at] for ref in stale_refs]
-            for j, new in enumerate((key, value))
-        )
-        total = 0.0
-        summed = 0.0
-        for mask, key_rows, value_rows in zip(masks, keys, values):
-            scores = lax.dot_general(
-                query, key_rows, (((1,), (1,)), ((), ())), preferred_element_type=jnp.float32
-            )
-            weights = jnp.where(mask, jnp.exp(scores / math.sqrt(head_dim)), 0.0)
-            total = total + jnp.sum(weights, axis=-1, keepdims=True)
-            summed = summed + jnp.dot(
-                weights.astype(jnp.bfloat16), value_rows, preferred_element_type=jnp.float32
-            )
-        attended.append((summed / total).astype(jnp.bfloat16))
+        masks.append((at // (groups * rows) != own_member).astype(jnp.float32))
+    mask = jnp.concatenate(masks, axis=1)
+
+    def column(head, kind):
+        at = (3 * head + kind) * head_dim
+        return mixed[:, at : at + head_dim]
+
+    every = range(heads)
+    at_head = [slice(head * head_dim, (head + 1) * head_dim) for head in every]
+    queries = [head_norm(column(h, 0), gain_ref[0:1, :]).astype(jnp.bfloat16) for h in every]
+    fresh = [
+        (by_patch(head_norm(column(h, 1), gain_ref[1:2, :])), by_patch(column(h, 2))) for h in every
+    ]
+
+    def entries(head, kind):
+        old = old_table_ref[kind, :, :, at_head[head]].reshape(groups * rows, head_dim)
+        stale = [ref[kind, :, at_head[head]] for ref in stale_refs]
+        return jnp.concatenate([fresh[head][kind], old] + stale)
+
+    scores = [
+        lax.dot_general(
+            queries[h],
+            entries(h, 0),
+            (((1,), (1,)), ((), ())),
+            preferred_element_type=jnp.float32,
+        )
+        for h in every
+    ]
+    weights = [mask * jnp.exp(s / math.sqrt(head_dim)) for s in scores]
+    totals = [jnp.sum(w, axis=-1, keepdims=True) for w in weights]
+    summed = [
+        jnp.dot(weights[h].astype(jnp.bfloat16), entries(h, 1), preferred_element_type=jnp.float32)
+        for h in every
+    ]
+    attended = [(a / t).astype(jnp.bfloat16) for a, t in zip(summed, totals)]
     attended = jnp.concatenate(attended, axis=1)
 
     if loading:
@@ -246,7 +255,9 @@
             spread_to[section, piece] = held
 
 
-def guide_kernel(where_ref, closing_ref, guided_ref):
+def guide_kernel(where_ref, closing_ref, table_ref, guided_ref, table_to, sem):
+    copy = pltpu.make_async_copy(table_ref, table_to, sem)
+    copy.start()
     branches, patches, slices, block_rows, block_cols = closing_ref.shape
     tok_dev = guided_ref.shape[0]
     section, own_slice = where_ref[0], where_ref[2]
@@ -274,6 +285,8 @@
         combine(
             [closing_ref[branch, section, own_slice].astype(jnp.float32) for branch in range(branches)]
         )
+
+    copy.wait()
 
 
 def local(latent, modulation, qkv_weight, out_weight, norm_gain, stale_kv):
@@ -427,7 +440,17 @@
         0,
         axis_index_groups=closing_peers,
     ).reshape(closing_shape)
-    (guided,) = small(guide_kernel, [smem, vmem], (tok_dev, model_width // 2))(where, closing)
+    guided, table = pl.pallas_call(
+        guide_kernel,
+        out_shape=(
+            jax.ShapeDtypeStruct((tok_dev, model_width // 2), jnp.bfloat16),
+            jax.ShapeDtypeStruct(table.shape, jnp.bfloat16),
+        ),
+        in_specs=[smem, vmem, vmem],
+        out_specs=(vmem, hbm),
+        scratch_shapes=[pltpu.SemaphoreType.DMA],
+        compiler_params=pltpu.CompilerParams(vmem_limit_bytes=8 * 1024 * 1024),
+    )(where, closing, table)
     return (guided[None], table.reshape(stale_kv.shape))
 
 

time: 152 us -> 151 us (level)
  blocking collectives: 116 us -> 129 us
  waiting for transfers between devices: 9.32 us -> 0 us
  starting transfers between devices: 3.53 us -> 0 us
    all_to_all x0 -> x1, blocking collectives: none -> 12.7 us  [local(): lax.all_to_all(closing.reshape((-1,) + closing_shape[3:]), ('cfg', 'pipe'...]
    all_to_all x1 -> x0, waiting for transfers between devices: 9.32 us -> none  [local(): lax.all_to_all(closing.reshape((-1,) + closing_shape[3:]), ('cfg', 'pipe'...]
    all_to_all x1 -> x0, starting transfers between devices: 3.53 us -> none  [local(): lax.all_to_all(closing.reshape((-1,) + closing_shape[3:]), ('cfg', 'pipe'...]
  transfers between devices with their start and end apart: 1 -> 0, of which waited for: 1 -> 0; matrix products, arithmetic and copies ran while one was open for 0% -> 0% of each run, Pallas kernels for 0% -> 0%
where the time goes in v11:
time: 151 us; the launch traced here: 150 us
  blocking collectives  129 us (85%)
  Pallas kernels  20.7 us (14%)
    all_to_all x8, blocking collectives, exchange(): lax.all_to_all(value, ('pipe', 'seq'), 0, 0, axis_index_groups=peers)  101 us
    pallas_call x5, Pallas kernels, attend(): pl.pallas_call(functools.partial(section_kernel, tick, (tok_dev, head_dim...  17 us
    all_to_all x1, blocking collectives, local(): lax.all_to_all(spread, 'seq', 0, 0, axis_index_groups=in_slices)[None]  15 us
    all_to_all x1, blocking collectives, local(): lax.all_to_all(closing.reshape((-1,) + closing_shape[3:]), ('cfg', 'pipe'...  12.7 us

profile of v11, /device:TPU:0, one launch (start us, length us, event | category | flops | bytes accessed | tf_op | source)
XLA Modules:
  0.0 150.2 jit_solution(6705933041782035315)
XLA Ops:
  0.6 0.1 pad_add_fusion.where_ref
  0.7 1.7 %shard_map.77 = (f32[3,1,2048]{2,1,0:T(1,128)S(1)}, f32[2,128]{1,0:T(2,128)S(1)}, bf16[2,2,64,512]{3,2,1,0:T(8,128)(2,1)S(1)}, bf16[2,16,512]{2,1,0:T(8,128)(2,1...) custom-call(s32[3]{0:T(128)S(1)} %pad_add_fusion.where_ref, bf16[2,16,2048]{2,1,0:T(8,128)(2,1)} %bitcast.53, ...), custom_call_target="tpu_custom_call" | custom-call | tf_op jit(solution)/shard_map/pallas_call | solution.py:358
  2.5 15.0 %all_to_all.50 = bf16[4,16,2048]{2,1,0:T(8,128)(2,1)S(1)} all-to-all(bf16[4,16,2048]{2,1,0:T(8,128)(2,1)S(1)} %get-tuple-element.28), channel_id=1, replica_groups={{0,1,2,3},{4,5,6,7},{8,9,10,11},{12,13,14,15},{16,17,18,19},{20,21,22,2..., dimensions={0} | all-to-all | bytes 524288 | tf_op jit(solution)/shard_map/all_to_all | solution.py:417
  17.5 5.7 %shard_map.78 = (bf16[4,4,16,512]{3,2,1,0:T(8,128)(2,1)S(1)}, bf16[2,2,64,512]{3,2,1,0:T(8,128)(2,1)S(1)}, bf16[2048,1536]{1,0:T(8,128)(2,1)S(1)}, bf16[512,2048]{1,0:T(8,128)(2,1)S(1)}) custom-call(s32[3]{0:T(128)S(1)} %pad_add_fusion.where_ref, bf16[1,4,16,2048]{3,2,1,0:T(8,128)(2,1)S(1)} %bitcast.32, ...), custom_call_target="tpu_custom_call", output_to_operand_aliasing={{1}: (6, {})} | custom-call | tf_op jit(solution)/shard_map/pallas_call | solution.py:396
  23.2 14.6 %all_to_all.51 = bf16[16,16,512]{2,1,0:T(8,128)(2,1)S(1)} all-to-all(bf16[16,16,512]{2,1,0:T(8,128)(2,1)S(1)} %bitcast.43), channel_id=1, replica_groups={{0,1,2,3,4,5,6,7,8,9,10,11,12,13,14,15},{16,17,18,19,20,21,22,23,24,25,..., dimensions={0} | all-to-all | bytes 524288 | tf_op jit(solution)/shard_map/all_to_all | solution.py:341
  37.9 12.4 %all_to_all.52 = bf16[16,16,512]{2,1,0:T(8,128)(2,1)S(1)} all-to-all(bf16[16,16,512]{2,1,0:T(8,128)(2,1)S(1)} %bitcast.45), channel_id=1, replica_groups={{0,1,2,3,4,5,6,7,8,9,10,11,12,13,14,15},{16,17,18,19,20,21,22,23,24,25,..., dimensions={0} | all-to-all | bytes 524288 | tf_op jit(solution)/shard_map/all_to_all | solution.py:341
  50.3 2.8 %shard_map.80 = (bf16[4,4,16,512]{3,2,1,0:T(8,128)(2,1)S(1)}, bf16[2,2,64,512]{3,2,1,0:T(8,128)(2,1)S(1)}) custom-call(s32[3]{0:T(128)S(1)} %pad_add_fusion.where_ref, bf16[4,4,16,512]{3,2,1,0:T(8,128)(2,1)S(1)} %bitcast.33, f32[3,1,2048]{2,1,0:T(1,128)S(1)} %get-tuple-element.29.mod_ref, ...), custom_call_target="tpu_custom_call", output_to_operand_aliasing={{1}: (6, {})} | custom-call | tf_op jit(solution)/shard_map/pallas_call | solution.py:396
  53.1 12.3 %all_to_all.53 = bf16[16,16,512]{2,1,0:T(8,128)(2,1)S(1)} all-to-all(bf16[16,16,512]{2,1,0:T(8,128)(2,1)S(1)} %bitcast.46), channel_id=1, replica_groups={{0,1,2,3,4,5,6,7,8,9,10,11,12,13,14,15},{16,17,18,19,20,21,22,23,24,25,..., dimensions={0} | all-to-all | bytes 524288 | tf_op jit(solution)/shard_map/all_to_all | solution.py:341
  65.5 12.3 %all_to_all.54 = bf16[16,16,512]{2,1,0:T(8,128)(2,1)S(1)} all-to-all(bf16[16,16,512]{2,1,0:T(8,128)(2,1)S(1)} %bitcast.47), channel_id=1, replica_groups={{0,1,2,3,4,5,6,7,8,9,10,11,12,13,14,15},{16,17,18,19,20,21,22,23,24,25,..., dimensions={0} | all-to-all | bytes 524288 | tf_op jit(solution)/shard_map/all_to_all | solution.py:341
  77.8 2.8 %shard_map.82 = (bf16[4,4,16,512]{3,2,1,0:T(8,128)(2,1)S(1)}, bf16[2,2,64,512]{3,2,1,0:T(8,128)(2,1)S(1)}) custom-call(s32[3]{0:T(128)S(1)} %pad_add_fusion.where_ref, bf16[4,4,16,512]{3,2,1,0:T(8,128)(2,1)S(1)} %bitcast.34, f32[3,1,2048]{2,1,0:T(1,128)S(1)} %get-tuple-element.29.mod_ref, ...), custom_call_target="tpu_custom_call", output_to_operand_aliasing={{1}: (6, {})} | custom-call | tf_op jit(solution)/shard_map/pallas_call | solution.py:396
  80.6 12.3 %all_to_all.55 = bf16[16,16,512]{2,1,0:T(8,128)(2,1)S(1)} all-to-all(bf16[16,16,512]{2,1,0:T(8,128)(2,1)S(1)} %bitcast.48), channel_id=1, replica_groups={{0,1,2,3,4,5,6,7,8,9,10,11,12,13,14,15},{16,17,18,19,20,21,22,23,24,25,..., dimensions={0} | all-to-all | bytes 524288 | tf_op jit(solution)/shard_map/all_to_all | solution.py:341
  93.0 12.3 %all_to_all.56 = bf16[16,16,512]{2,1,0:T(8,128)(2,1)S(1)} all-to-all(bf16[16,16,512]{2,1,0:T(8,128)(2,1)S(1)} %bitcast.44), channel_id=1, replica_groups={{0,1,2,3,4,5,6,7,8,9,10,11,12,13,14,15},{16,17,18,19,20,21,22,23,24,25,..., dimensions={0} | all-to-all | bytes 524288 | tf_op jit(solution)/shard_map/all_to_all | solution.py:341
  105.4 2.8 %shard_map.84 = (bf16[4,4,16,512]{3,2,1,0:T(8,128)(2,1)S(1)}, bf16[2,2,64,512]{3,2,1,0:T(8,128)(2,1)S(1)}) custom-call(s32[3]{0:T(128)S(1)} %pad_add_fusion.where_ref, bf16[4,4,16,512]{3,2,1,0:T(8,128)(2,1)S(1)} %bitcast.35, f32[3,1,2048]{2,1,0:T(1,128)S(1)} %get-tuple-element.29.mod_ref, ...), custom_call_target="tpu_custom_call", output_to_operand_aliasing={{1}: (6, {})} | custom-call | tf_op jit(solution)/shard_map/pallas_call | solution.py:396
  108.2 12.3 %all_to_all.57 = bf16[16,16,512]{2,1,0:T(8,128)(2,1)S(1)} all-to-all(bf16[16,16,512]{2,1,0:T(8,128)(2,1)S(1)} %bitcast.49), channel_id=1, replica_groups={{0,1,2,3,4,5,6,7,8,9,10,11,12,13,14,15},{16,17,18,19,20,21,22,23,24,25,..., dimensions={0} | all-to-all | bytes 524288 | tf_op jit(solution)/shard_map/all_to_all | solution.py:341
  120.5 12.3 %all_to_all.58 = bf16[16,16,512]{2,1,0:T(8,128)(2,1)S(1)} all-to-all(bf16[16,16,512]{2,1,0:T(8,128)(2,1)S(1)} %bitcast.41), channel_id=1, replica_groups={{0,1,2,3,4,5,6,7,8,9,10,11,12,13,14,15},{16,17,18,19,20,21,22,23,24,25,..., dimensions={0} | all-to-all | bytes 524288 | tf_op jit(solution)/shard_map/all_to_all | solution.py:341
  132.9 2.8 %shard_map.86 = (bf16[2,2,4,16,512]{4,3,2,1,0:T(8,128)(2,1)S(1)}, bf16[2,2,64,512]{3,2,1,0:T(8,128)(2,1)S(1)}) custom-call(s32[3]{0:T(128)S(1)} %pad_add_fusion.where_ref, bf16[4,4,16,512]{3,2,1,0:T(8,128)(2,1)S(1)} %bitcast.31, f32[3,1,2048]{2,1,0:T(1,128)S(1)} %get-tuple-element.29.mod_ref, ...), custom_call_target="tpu_custom_call", output_to_operand_aliasing={{1}: (6, {})} | custom-call | tf_op jit(solution)/shard_map/pallas_call | solution.py:396
  135.7 12.7 %all_to_all.59 = bf16[16,16,512]{2,1,0:T(8,128)(2,1)S(1)} all-to-all(bf16[16,16,512]{2,1,0:T(8,128)(2,1)S(1)} %bitcast.42), channel_id=1, replica_groups={{0,1,2,3,4,5,6,7,16,17,18,19,20,21,22,23},{8,9,10,11,12,13,14,15,24,25,..., dimensions={0} | all-to-all | bytes 524288 | tf_op jit(solution)/shard_map/all_to_all | solution.py:436
  148.4 1.9 %shard_map.87 = (bf16[8,1024]{1,0:T(8,128)(2,1)}, bf16[2,2,64,512]{3,2,1,0:T(8,128)(2,1)}) custom-call(s32[3]{0:T(128)S(1)} %pad_add_fusion.where_ref, bf16[2,2,4,16,512]{4,3,2,1,0:T(8,128)(2,1)S(1)} %bitcast.36, bf16[2,2,64,512]{3,2,1,0:T(8,128)(2,1)S(1)} %get-tuple-element.51.table_ref), custom_call_target="tpu_custom_call" | custom-call | tf_op jit(solution)/shard_map/pallas_call | solution.py:443
  (4 shorter events, 0.1 us)

commit v12 on v11

--- a/solution.py
+++ b/solution.py
@@ -11,8 +11,6 @@
 GUIDANCE_SCALE = 6.0
 EPSILON = 1e-06
 GROUPS = 2
-PIECES = 8
-IN_FLIGHT = 3
 
 
 def swapped(value, axis, bit):
@@ -34,10 +32,6 @@
 
 
 def section_kernel(tick, sizes, where_ref, rows_ref, mod_ref, qkv_ref, out_ref, gain_ref, *refs):
-    loading = tick == 0
-    weights_from = (qkv_ref, out_ref)
-    if loading:
-        *refs, qkv_ref, out_ref, sems = refs
     *stale_refs, old_table_ref, partial_ref, table_ref = refs
     closing = len(partial_ref.shape) == 5
     tok_dev, head_dim = sizes
@@ -50,19 +44,6 @@
     heads = local_width // head_dim
     section, own_member, own_slice = where_ref[0], where_ref[1], where_ref[2]
     group = tick - section
-    copies = []
-    if loading:
-        piece_rows = qkv_ref.shape[0] // PIECES
-        for at in range(PIECES):
-            piece = pl.ds(at * piece_rows, piece_rows)
-            copies.append(
-                pltpu.make_async_copy(
-                    weights_from[0].at[piece], qkv_ref.at[piece], sems.at[at]
-                )
-            )
-        copies.append(pltpu.make_async_copy(weights_from[1], out_ref, sems.at[PIECES]))
-        for copy in copies[:IN_FLIGHT]:
-            copy.start()
     parts = [rows_ref[q].reshape(rows, block_cols).astype(jnp.float32) for q in range(blocks)]
     mean = sum(jnp.sum(x, axis=-1, keepdims=True) for x in parts) / width
     parts = [x - mean for x in parts]
@@ -75,18 +56,7 @@
             (x * inverse * (1.0 + mod_ref[1, :, at]) + mod_ref[0, :, at]).astype(jnp.bfloat16)
         )
     modulated = jnp.concatenate(modulated, axis=1)
-    if loading:
-        mixed = 0.0
-        for at in range(PIECES):
-            copies[at].wait()
-            if at + IN_FLIGHT < len(copies):
-                copies[at + IN_FLIGHT].start()
-            piece = slice(at * piece_rows, (at + 1) * piece_rows)
-            mixed = mixed + jnp.dot(
-                modulated[:, piece], qkv_ref[piece, :], preferred_element_type=jnp.float32
-            )
-    else:
-        mixed = jnp.dot(modulated, qkv_ref[...], preferred_element_type=jnp.float32)
+    mixed = jnp.dot(modulated, qkv_ref[...], preferred_element_type=jnp.float32)
 
     def by_patch(values):
         values = values.reshape(slices, in_group, tok_dev, head_dim).swapaxes(0, 1)
@@ -141,8 +111,6 @@
     attended = [(a / t).astype(jnp.bfloat16) for a, t in zip(summed, totals)]
     attended = jnp.concatenate(attended, axis=1)
 
-    if loading:
-        copies[PIECES].wait()
     projected = jnp.dot(attended, out_ref[...], preferred_element_type=jnp.float32)
     projected = mod_ref[2] * projected
     if closing:
@@ -200,7 +168,8 @@
                     closing_ref[branch, patch, piece] = held
 
 
-def start_kernel(where_ref, latent_ref, *refs):
+def start_kernel(where_ref, latent_ref, qkv_ref, out_ref, *refs):
+    del qkv_ref, out_ref
     loads = (len(refs) - 4) // 2
     from_refs, to_refs = refs[:loads], refs[loads : 2 * loads]
     sources_to, streams_to, spread_to, sems = refs[2 * loads :]
@@ -363,42 +332,34 @@
             jax.ShapeDtypeStruct(stream_shape, jnp.bfloat16),
             jax.ShapeDtypeStruct((slice_count, block_rows, model_width), jnp.bfloat16),
         ),
-        in_specs=[smem] + [hbm] * (len(loads) + 1),
+        in_specs=[smem] + [hbm] * (len(loads) + 3),
         out_specs=(vmem,) * (len(loads) + 3),
         scratch_shapes=[pltpu.SemaphoreType.DMA((len(loads) + slice_count + 1,))],
         compiler_params=pltpu.CompilerParams(vmem_limit_bytes=4 * 1024 * 1024),
-    )(where, in_hbm(sources), *map(in_hbm, loads))
+    )(where, in_hbm(sources), in_hbm(qkv_slice), in_hbm(out_slice), *map(in_hbm, loads))
     stale_rows = []
     if member_count > 1:
         stale_rows = [group_cache.swapaxes(0, 1).reshape(2, -1, local_width)]
 
-    def attend(tick, features, table, weights, partial_shape):
-        loading = tick == 0
+    def attend(tick, features, table, partial_shape):
         operands = (
             where,
             features,
             in_vmem(modulation),
-            *map(in_hbm if loading else in_vmem, weights),
+            in_vmem(qkv_slice),
+            in_vmem(out_slice),
             in_vmem(norm_gain),
             *stale_rows,
             table,
         )
-        in_specs = [smem] + [vmem] * (len(operands) - 1)
-        out_shape = (
-            jax.ShapeDtypeStruct(partial_shape, jnp.bfloat16),
-            jax.ShapeDtypeStruct(table.shape, jnp.bfloat16),
-        )
-        scratch = []
-        if loading:
-            in_specs[3:5] = [hbm, hbm]
-            out_shape += tuple(pltpu.VMEM(w.shape, jnp.bfloat16) for w in weights)
-            scratch = [pltpu.SemaphoreType.DMA((PIECES + 1,))]
         return pl.pallas_call(
             functools.partial(section_kernel, tick, (tok_dev, head_dim)),
-            out_shape=out_shape,
-            in_specs=in_specs,
-            out_specs=(vmem,) * len(out_shape),
-            scratch_shapes=scratch,
+            out_shape=(
+                jax.ShapeDtypeStruct(partial_shape, jnp.bfloat16),
+                jax.ShapeDtypeStruct(table.shape, jnp.bfloat16),
+            ),
+            in_specs=[smem] + [vmem] * (len(operands) - 1),
+            out_specs=(vmem, vmem),
             input_output_aliases={len(operands) - 1: 1},
             compiler_params=pltpu.CompilerParams(vmem_limit_bytes=24 * 1024 * 1024),
         )(*operands)
@@ -415,10 +376,8 @@
     ticks = GROUPS + section_count - 1
     closing_shape = (2, half, slice_count, block_rows, block_cols)
     features = lax.all_to_all(spread, "seq", 0, 0, axis_index_groups=in_slices)[None]
-    weights = [qkv_slice, out_slice]
     for tick in range(ticks - 1):
-        partial_out, table, *loaded = attend(tick, features, table, weights, spread_shape)
-        weights = loaded or weights
+        partial_out, table = attend(tick, features, table, spread_shape)
         parts = exchange(partial_out)
         if tick < ticks - 2:
             streams, spread = small(
@@ -432,7 +391,7 @@
                 functools.partial(settle_last_kernel, in_group), [vmem] * 2, spread_shape
             )(parts, streams)
         features = exchange(spread)
-    closing, table = attend(ticks - 1, features, table, weights, closing_shape)
+    closing, table = attend(ticks - 1, features, table, closing_shape)
     closing = lax.all_to_all(
         closing.reshape((-1,) + closing_shape[3:]),
         ("cfg", "pipe", "seq"),

time: 151 us -> 148 us (0.980)
  Pallas kernels: 20.7 us -> 18.1 us
    pallas_call x5, Pallas kernels: 17 us -> 14.1 us  [attend(): pl.pallas_call(functools.partial(section_kernel, tick, (tok_dev, head_dim...]
where the time goes in v12:
time: 148 us
  blocking collectives  129 us (87%)
  Pallas kernels  18.1 us (12%)
    all_to_all x8, blocking collectives, exchange(): lax.all_to_all(value, ('pipe', 'seq'), 0, 0, axis_index_groups=peers)  101 us
    all_to_all x1, blocking collectives, local(): lax.all_to_all(spread, 'seq', 0, 0, axis_index_groups=in_slices)[None]  15.1 us
    pallas_call x5, Pallas kernels, attend(): pl.pallas_call(functools.partial(section_kernel, tick, (tok_dev, head_dim...  14.1 us
    all_to_all x1, blocking collectives, local(): lax.all_to_all(closing.reshape((-1,) + closing_shape[3:]), ('cfg', 'pipe'...  12.7 us

profile of v12, /device:TPU:0, one launch (start us, length us, event | category | flops | bytes accessed | tf_op | source)
XLA Modules:
  0.0 147.8 jit_solution(6441174923302370192)
XLA Ops:
  0.6 0.0 copy-start.1
  0.6 0.0 copy-start
  0.7 0.1 pad_add_fusion.where_ref
  0.7 2.0 %shard_map.77 = (f32[3,1,2048]{2,1,0:T(1,128)S(1)}, f32[2,128]{1,0:T(2,128)S(1)}, bf16[2,2,64,512]{3,2,1,0:T(8,128)(2,1)S(1)}, bf16[2,16,512]{2,1,0:T(8,128)(2,1...) custom-call(s32[3]{0:T(128)S(1)} %pad_add_fusion.where_ref, bf16[2,16,2048]{2,1,0:T(8,128)(2,1)} %bitcast.63, ...), custom_call_target="tpu_custom_call" | custom-call | tf_op jit(solution)/shard_map/pallas_call | solution.py:327
  2.8 15.1 %all_to_all.50 = bf16[4,16,2048]{2,1,0:T(8,128)(2,1)S(1)} all-to-all(bf16[4,16,2048]{2,1,0:T(8,128)(2,1)S(1)} %get-tuple-element.26), channel_id=1, replica_groups={{0,1,2,3},{4,5,6,7},{8,9,10,11},{12,13,14,15},{16,17,18,19},{20,21,22,2..., dimensions={0} | all-to-all | bytes 524288 | tf_op jit(solution)/shard_map/all_to_all | solution.py:378
  17.9 0.0 copy-done.1
  17.9 0.0 copy-done
  17.9 2.8 %shard_map.78 = (bf16[4,4,16,512]{3,2,1,0:T(8,128)(2,1)S(1)}, bf16[2,2,64,512]{3,2,1,0:T(8,128)(2,1)S(1)}) custom-call(s32[3]{0:T(128)S(1)} %pad_add_fusion.where_ref, bf16[1,4,16,2048]{3,2,1,0:T(8,128)(2,1)S(1)} %bitcast.47, f32[3,1,2048]{2,1,0:T(1,128)S(1)} %get-tuple-element.27.mod_ref, ...), custom_call_target="tpu_custom_call", output_to_operand_aliasing={{1}: (6, {})} | custom-call | tf_op jit(solution)/shard_map/pallas_call | solution.py:355
  20.7 14.6 %all_to_all.51 = bf16[16,16,512]{2,1,0:T(8,128)(2,1)S(1)} all-to-all(bf16[16,16,512]{2,1,0:T(8,128)(2,1)S(1)} %bitcast.56), channel_id=1, replica_groups={{0,1,2,3,4,5,6,7,8,9,10,11,12,13,14,15},{16,17,18,19,20,21,22,23,24,25,..., dimensions={0} | all-to-all | bytes 524288 | tf_op jit(solution)/shard_map/all_to_all | solution.py:310
  35.4 12.4 %all_to_all.52 = bf16[16,16,512]{2,1,0:T(8,128)(2,1)S(1)} all-to-all(bf16[16,16,512]{2,1,0:T(8,128)(2,1)S(1)} %bitcast.57), channel_id=1, replica_groups={{0,1,2,3,4,5,6,7,8,9,10,11,12,13,14,15},{16,17,18,19,20,21,22,23,24,25,..., dimensions={0} | all-to-all | bytes 524288 | tf_op jit(solution)/shard_map/all_to_all | solution.py:310
  47.8 2.8 %shard_map.80 = (bf16[4,4,16,512]{3,2,1,0:T(8,128)(2,1)S(1)}, bf16[2,2,64,512]{3,2,1,0:T(8,128)(2,1)S(1)}) custom-call(s32[3]{0:T(128)S(1)} %pad_add_fusion.where_ref, bf16[4,4,16,512]{3,2,1,0:T(8,128)(2,1)S(1)} %bitcast.44, f32[3,1,2048]{2,1,0:T(1,128)S(1)} %get-tuple-element.27.mod_ref, ...), custom_call_target="tpu_custom_call", output_to_operand_aliasing={{1}: (6, {})} | custom-call | tf_op jit(solution)/shard_map/pallas_call | solution.py:355
  50.6 12.3 %all_to_all.53 = bf16[16,16,512]{2,1,0:T(8,128)(2,1)S(1)} all-to-all(bf16[16,16,512]{2,1,0:T(8,128)(2,1)S(1)} %bitcast.58), channel_id=1, replica_groups={{0,1,2,3,4,5,6,7,8,9,10,11,12,13,14,15},{16,17,18,19,20,21,22,23,24,25,..., dimensions={0} | all-to-all | bytes 524288 | tf_op jit(solution)/shard_map/all_to_all | solution.py:310
  63.0 12.3 %all_to_all.54 = bf16[16,16,512]{2,1,0:T(8,128)(2,1)S(1)} all-to-all(bf16[16,16,512]{2,1,0:T(8,128)(2,1)S(1)} %bitcast.59), channel_id=1, replica_groups={{0,1,2,3,4,5,6,7,8,9,10,11,12,13,14,15},{16,17,18,19,20,21,22,23,24,25,..., dimensions={0} | all-to-all | bytes 524288 | tf_op jit(solution)/shard_map/all_to_all | solution.py:310
  75.4 2.8 %shard_map.82 = (bf16[4,4,16,512]{3,2,1,0:T(8,128)(2,1)S(1)}, bf16[2,2,64,512]{3,2,1,0:T(8,128)(2,1)S(1)}) custom-call(s32[3]{0:T(128)S(1)} %pad_add_fusion.where_ref, bf16[4,4,16,512]{3,2,1,0:T(8,128)(2,1)S(1)} %bitcast.45, f32[3,1,2048]{2,1,0:T(1,128)S(1)} %get-tuple-element.27.mod_ref, ...), custom_call_target="tpu_custom_call", output_to_operand_aliasing={{1}: (6, {})} | custom-call | tf_op jit(solution)/shard_map/pallas_call | solution.py:355
  78.2 12.3 %all_to_all.55 = bf16[16,16,512]{2,1,0:T(8,128)(2,1)S(1)} all-to-all(bf16[16,16,512]{2,1,0:T(8,128)(2,1)S(1)} %bitcast.60), channel_id=1, replica_groups={{0,1,2,3,4,5,6,7,8,9,10,11,12,13,14,15},{16,17,18,19,20,21,22,23,24,25,..., dimensions={0} | all-to-all | bytes 524288 | tf_op jit(solution)/shard_map/all_to_all | solution.py:310
  90.6 12.3 %all_to_all.56 = bf16[16,16,512]{2,1,0:T(8,128)(2,1)S(1)} all-to-all(bf16[16,16,512]{2,1,0:T(8,128)(2,1)S(1)} %bitcast.55), channel_id=1, replica_groups={{0,1,2,3,4,5,6,7,8,9,10,11,12,13,14,15},{16,17,18,19,20,21,22,23,24,25,..., dimensions={0} | all-to-all | bytes 524288 | tf_op jit(solution)/shard_map/all_to_all | solution.py:310
  102.9 2.8 %shard_map.84 = (bf16[4,4,16,512]{3,2,1,0:T(8,128)(2,1)S(1)}, bf16[2,2,64,512]{3,2,1,0:T(8,128)(2,1)S(1)}) custom-call(s32[3]{0:T(128)S(1)} %pad_add_fusion.where_ref, bf16[4,4,16,512]{3,2,1,0:T(8,128)(2,1)S(1)} %bitcast.46, f32[3,1,2048]{2,1,0:T(1,128)S(1)} %get-tuple-element.27.mod_ref, ...), custom_call_target="tpu_custom_call", output_to_operand_aliasing={{1}: (6, {})} | custom-call | tf_op jit(solution)/shard_map/pallas_call | solution.py:355
  105.7 12.3 %all_to_all.57 = bf16[16,16,512]{2,1,0:T(8,128)(2,1)S(1)} all-to-all(bf16[16,16,512]{2,1,0:T(8,128)(2,1)S(1)} %bitcast.61), channel_id=1, replica_groups={{0,1,2,3,4,5,6,7,8,9,10,11,12,13,14,15},{16,17,18,19,20,21,22,23,24,25,..., dimensions={0} | all-to-all | bytes 524288 | tf_op jit(solution)/shard_map/all_to_all | solution.py:310
  118.1 12.3 %all_to_all.58 = bf16[16,16,512]{2,1,0:T(8,128)(2,1)S(1)} all-to-all(bf16[16,16,512]{2,1,0:T(8,128)(2,1)S(1)} %bitcast.53), channel_id=1, replica_groups={{0,1,2,3,4,5,6,7,8,9,10,11,12,13,14,15},{16,17,18,19,20,21,22,23,24,25,..., dimensions={0} | all-to-all | bytes 524288 | tf_op jit(solution)/shard_map/all_to_all | solution.py:310
  130.4 2.8 %shard_map.86 = (bf16[2,2,4,16,512]{4,3,2,1,0:T(8,128)(2,1)S(1)}, bf16[2,2,64,512]{3,2,1,0:T(8,128)(2,1)S(1)}) custom-call(s32[3]{0:T(128)S(1)} %pad_add_fusion.where_ref, bf16[4,4,16,512]{3,2,1,0:T(8,128)(2,1)S(1)} %bitcast.43, f32[3,1,2048]{2,1,0:T(1,128)S(1)} %get-tuple-element.27.mod_ref, ...), custom_call_target="tpu_custom_call", output_to_operand_aliasing={{1}: (6, {})} | custom-call | tf_op jit(solution)/shard_map/pallas_call | solution.py:355
  133.2 12.7 %all_to_all.59 = bf16[16,16,512]{2,1,0:T(8,128)(2,1)S(1)} all-to-all(bf16[16,16,512]{2,1,0:T(8,128)(2,1)S(1)} %bitcast.54), channel_id=1, replica_groups={{0,1,2,3,4,5,6,7,16,17,18,19,20,21,22,23},{8,9,10,11,12,13,14,15,24,25,..., dimensions={0} | all-to-all | bytes 524288 | tf_op jit(solution)/shard_map/all_to_all | solution.py:395
  145.9 1.9 %shard_map.87 = (bf16[8,1024]{1,0:T(8,128)(2,1)}, bf16[2,2,64,512]{3,2,1,0:T(8,128)(2,1)}) custom-call(s32[3]{0:T(128)S(1)} %pad_add_fusion.where_ref, bf16[2,2,4,16,512]{4,3,2,1,0:T(8,128)(2,1)S(1)} %bitcast.48, bf16[2,2,64,512]{3,2,1,0:T(8,128)(2,1)S(1)} %get-tuple-element.47.table_ref), custom_call_target="tpu_custom_call" | custom-call | tf_op jit(solution)/shard_map/pallas_call | solution.py:402
  (4 shorter events, 0.1 us)
Async XLA Ops:
  0.6 17.3 %copy-start.1 = (bf16[1,512,2048]{2,1,0:T(8,128)(2,1)S(1)}, bf16[1,512,2048]{2,1,0:T(8,128)(2,1)}, u32[]{:S(2)}) copy-start(bf16[1,512,2048]{2,1,0:T(8,128)(2,1)} %param.9) | copy-start | bytes 6291460
  0.6 17.3 %copy-start = (bf16[1,2048,1536]{2,1,0:T(8,128)(2,1)S(1)}, bf16[1,2048,1536]{2,1,0:T(8,128)(2,1)}, u32[]{:S(2)}) copy-start(bf16[1,2048,1536]{2,1,0:T(8,128)(2,1)} %param.8) | copy-start | bytes 18874372

commit v13 on v12

--- a/solution.py
+++ b/solution.py
@@ -31,16 +31,17 @@
     )
 
 
-def section_kernel(tick, sizes, where_ref, rows_ref, mod_ref, qkv_ref, out_ref, gain_ref, *refs):
+def section_kernel(tick, closing, sizes, where_ref, rows_ref, mod_ref, qkv_ref, out_ref, gain_ref, *refs):
+    if closing:
+        *refs, held_ref, sems = refs
     *stale_refs, old_table_ref, partial_ref, table_ref = refs
-    closing = len(partial_ref.shape) == 5
     tok_dev, head_dim = sizes
     blocks, slices, block_rows, block_cols = rows_ref.shape
     rows = slices * block_rows
     width = blocks * block_cols
     in_group = block_rows // tok_dev
     group_rows = slices * tok_dev
-    groups, local_width = table_ref.shape[1], table_ref.shape[3]
+    groups, local_width = old_table_ref.shape[1], old_table_ref.shape[3]
     heads = local_width // head_dim
     section, own_member, own_slice = where_ref[0], where_ref[1], where_ref[2]
     group = tick - section
@@ -56,7 +57,16 @@
             (x * inverse * (1.0 + mod_ref[1, :, at]) + mod_ref[0, :, at]).astype(jnp.bfloat16)
         )
     modulated = jnp.concatenate(modulated, axis=1)
-    mixed = jnp.dot(modulated, qkv_ref[...], preferred_element_type=jnp.float32)
+    pair = 2 if heads % 2 == 0 else 1
+    pair_width = 3 * pair * head_dim
+    mixed = [
+        jnp.dot(
+            modulated,
+            qkv_ref[:, at * pair_width : (at + 1) * pair_width],
+            preferred_element_type=jnp.float32,
+        )
+        for at in range(heads // pair)
+    ]
 
     def by_patch(values):
         values = values.reshape(slices, in_group, tok_dev, head_dim).swapaxes(0, 1)
@@ -78,40 +88,57 @@
     mask = jnp.concatenate(masks, axis=1)
 
     def column(head, kind):
-        at = (3 * head + kind) * head_dim
-        return mixed[:, at : at + head_dim]
-
-    every = range(heads)
-    at_head = [slice(head * head_dim, (head + 1) * head_dim) for head in every]
-    queries = [head_norm(column(h, 0), gain_ref[0:1, :]).astype(jnp.bfloat16) for h in every]
-    fresh = [
-        (by_patch(head_norm(column(h, 1), gain_ref[1:2, :])), by_patch(column(h, 2))) for h in every
-    ]
-
-    def entries(head, kind):
-        old = old_table_ref[kind, :, :, at_head[head]].reshape(groups * rows, head_dim)
-        stale = [ref[kind, :, at_head[head]] for ref in stale_refs]
-        return jnp.concatenate([fresh[head][kind], old] + stale)
-
-    scores = [
-        lax.dot_general(
-            queries[h],
-            entries(h, 0),
-            (((1,), (1,)), ((), ())),
+        at = (3 * (head % pair) + kind) * head_dim
+        return mixed[head // pair][:, at : at + head_dim]
+
+    at_head = [slice(head * head_dim, (head + 1) * head_dim) for head in range(heads)]
+    fresh = []
+
+    def attend(head):
+        at = at_head[head]
+        query = head_norm(column(head, 0), gain_ref[0:1, :]).astype(jnp.bfloat16)
+        key = by_patch(head_norm(column(head, 1), gain_ref[1:2, :]))
+        fresh.append((key, by_patch(column(head, 2))))
+
+        def entries(kind):
+            old = old_table_ref[kind, :, :, at].reshape(groups * rows, head_dim)
+            return jnp.concatenate([fresh[head][kind], old] + [ref[kind, :, at] for ref in stale_refs])
+
+        scores = lax.dot_general(
+            query, entries(0), (((1,), (1,)), ((), ())), preferred_element_type=jnp.float32
+        )
+        weights = mask * jnp.exp(scores / math.sqrt(head_dim))
+        total = jnp.sum(weights, axis=-1, keepdims=True)
+        summed = jnp.dot(
+            weights.astype(jnp.bfloat16), entries(1), preferred_element_type=jnp.float32
+        )
+        return (summed / total).astype(jnp.bfloat16)
+
+    attended = [attend(head) for head in range(heads)]
+
+    def fresh_rows(kind):
+        return jnp.concatenate([entry[kind] for entry in fresh], axis=1)
+
+    copies = []
+    if closing:
+        last = groups - 1
+        for kind in range(2):
+            held_ref[kind] = jnp.where(group == last, fresh_rows(kind), old_table_ref[kind, last])
+        copies = [
+            pltpu.make_async_copy(held_ref, table_ref.at[:, last], sems.at[0]),
+            pltpu.make_async_copy(
+                old_table_ref.at[:, pl.ds(0, last)], table_ref.at[:, pl.ds(0, last)], sems.at[1]
+            ),
+        ]
+        for copy in copies:
+            copy.start()
+    projected = 0.0
+    for at in range(heads // pair):
+        projected = projected + jnp.dot(
+            jnp.concatenate(attended[at * pair : (at + 1) * pair], axis=1),
+            out_ref[at * pair * head_dim : (at + 1) * pair * head_dim, :],
             preferred_element_type=jnp.float32,
         )
-        for h in every
-    ]
-    weights = [mask * jnp.exp(s / math.sqrt(head_dim)) for s in scores]
-    totals = [jnp.sum(w, axis=-1, keepdims=True) for w in weights]
-    summed = [
-        jnp.dot(weights[h].astype(jnp.bfloat16), entries(h, 1), preferred_element_type=jnp.float32)
-        for h in every
-    ]
-    attended = [(a / t).astype(jnp.bfloat16) for a, t in zip(summed, totals)]
-    attended = jnp.concatenate(attended, axis=1)
-
-    projected = jnp.dot(attended, out_ref[...], preferred_element_type=jnp.float32)
     projected = mod_ref[2] * projected
     if closing:
         close_into(partial_ref, projected, rows_ref, section, own_slice, in_group)
@@ -121,17 +148,19 @@
             piece = projected[:, q * out_cols : (q + 1) * out_cols].astype(jnp.bfloat16)
             partial_ref[q] = piece.reshape(slices, block_rows, out_cols)
 
-    for at in range(groups):
+    for copy in copies:
+        copy.wait()
+    for at in range(0 if closing else groups):
 
         @pl.when(group == at)
         def _():
-            for j in range(2):
-                table_ref[j, at] = jnp.concatenate([pair[j] for pair in fresh], axis=1)
+            for kind in range(2):
+                table_ref[kind, at] = fresh_rows(kind)
 
         @pl.when(group != at)
         def _():
-            for j in range(2):
-                table_ref[j, at] = old_table_ref[j, at]
+            for kind in range(2):
+                table_ref[kind, at] = old_table_ref[kind, at]
 
 
 def close_into(closing_ref, projected, rows_ref, section, own_slice, in_group):
@@ -224,9 +253,7 @@
             spread_to[section, piece] = held
 
 
-def guide_kernel(where_ref, closing_ref, table_ref, guided_ref, table_to, sem):
-    copy = pltpu.make_async_copy(table_ref, table_to, sem)
-    copy.start()
+def guide_kernel(where_ref, closing_ref, guided_ref):
     branches, patches, slices, block_rows, block_cols = closing_ref.shape
     tok_dev = guided_ref.shape[0]
     section, own_slice = where_ref[0], where_ref[2]
@@ -254,8 +281,6 @@
         combine(
             [closing_ref[branch, section, own_slice].astype(jnp.float32) for branch in range(branches)]
         )
-
-    copy.wait()
 
 
 def local(latent, modulation, qkv_weight, out_weight, norm_gain, stale_kv):
@@ -341,6 +366,8 @@
     if member_count > 1:
         stale_rows = [group_cache.swapaxes(0, 1).reshape(2, -1, local_width)]
 
+    ticks = GROUPS + section_count - 1
+
     def attend(tick, features, table, partial_shape):
         operands = (
             where,
@@ -352,15 +379,20 @@
             *stale_rows,
             table,
         )
+        closing = tick == ticks - 1
+        scratch = []
+        if closing:
+            scratch = [pltpu.VMEM((2, rows, local_width), jnp.bfloat16), pltpu.SemaphoreType.DMA((2,))]
         return pl.pallas_call(
-            functools.partial(section_kernel, tick, (tok_dev, head_dim)),
+            functools.partial(section_kernel, tick, closing, (tok_dev, head_dim)),
             out_shape=(
                 jax.ShapeDtypeStruct(partial_shape, jnp.bfloat16),
                 jax.ShapeDtypeStruct(table.shape, jnp.bfloat16),
             ),
             in_specs=[smem] + [vmem] * (len(operands) - 1),
-            out_specs=(vmem, vmem),
-            input_output_aliases={len(operands) - 1: 1},
+            out_specs=(vmem, hbm if closing else vmem),
+            scratch_shapes=scratch,
+            input_output_aliases={} if closing else {len(operands) - 1: 1},
             compiler_params=pltpu.CompilerParams(vmem_limit_bytes=24 * 1024 * 1024),
         )(*operands)
 
@@ -373,7 +405,6 @@
             compiler_params=pltpu.CompilerParams(vmem_limit_bytes=8 * 1024 * 1024),
         )
 
-    ticks = GROUPS + section_count - 1
     closing_shape = (2, half, slice_count, block_rows, block_cols)
     features = lax.all_to_all(spread, "seq", 0, 0, axis_index_groups=in_slices)[None]
     for tick in range(ticks - 1):
@@ -399,17 +430,7 @@
         0,
         axis_index_groups=closing_peers,
     ).reshape(closing_shape)
-    guided, table = pl.pallas_call(
-        guide_kernel,
-        out_shape=(
-            jax.ShapeDtypeStruct((tok_dev, model_width // 2), jnp.bfloat16),
-            jax.ShapeDtypeStruct(table.shape, jnp.bfloat16),
-        ),
-        in_specs=[smem, vmem, vmem],
-        out_specs=(vmem, hbm),
-        scratch_shapes=[pltpu.SemaphoreType.DMA],
-        compiler_params=pltpu.CompilerParams(vmem_limit_bytes=8 * 1024 * 1024),
-    )(where, closing, table)
+    (guided,) = small(guide_kernel, [smem, vmem], (tok_dev, model_width // 2))(where, closing)
     return (guided[None], table.reshape(stale_kv.shape))
 
 

time: 148 us -> 150 us (1.014)
  Pallas kernels: 18.1 us -> 19.6 us
    pallas_call x6, Pallas kernels: 15.9 us -> 17.4 us  [the longest x5 16.3 us: attend(): pl.pallas_call(functools.partial(section_kernel, tick, closing, (tok_dev,...]
where the time goes in v13:
time: 150 us; the launch traced here: 149 us
  blocking collectives  129 us (86%)
  Pallas kernels  19.6 us (13%)
    all_to_all x8, blocking collectives, exchange(): lax.all_to_all(value, ('pipe', 'seq'), 0, 0, axis_index_groups=peers)  101 us
    pallas_call x5, Pallas kernels, attend(): pl.pallas_call(functools.partial(section_kernel, tick, closing, (tok_dev,...  16.3 us
    all_to_all x1, blocking collectives, local(): lax.all_to_all(spread, 'seq', 0, 0, axis_index_groups=in_slices)[None]  15.1 us
    all_to_all x1, blocking collectives, local(): lax.all_to_all(closing.reshape((-1,) + closing_shape[3:]), ('cfg', 'pipe'...  12.7 us

profile of v13, /device:TPU:0, one launch (start us, length us, event | category | flops | bytes accessed | tf_op | source)
XLA Modules:
  0.0 149.3 jit_solution(18119008036041506343)
XLA Ops:
  0.6 0.0 copy-start.1
  0.6 0.0 copy-start
  0.7 0.1 pad_add_fusion.where_ref
  0.7 2.0 %shard_map.77 = (f32[3,1,2048]{2,1,0:T(1,128)S(1)}, f32[2,128]{1,0:T(2,128)S(1)}, bf16[2,2,64,512]{3,2,1,0:T(8,128)(2,1)S(1)}, bf16[2,16,512]{2,1,0:T(8,128)(2,1...) custom-call(s32[3]{0:T(128)S(1)} %pad_add_fusion.where_ref, bf16[2,16,2048]{2,1,0:T(8,128)(2,1)} %bitcast.63, ...), custom_call_target="tpu_custom_call" | custom-call | tf_op jit(solution)/shard_map/pallas_call | solution.py:352
  2.8 15.1 %all_to_all.50 = bf16[4,16,2048]{2,1,0:T(8,128)(2,1)S(1)} all-to-all(bf16[4,16,2048]{2,1,0:T(8,128)(2,1)S(1)} %get-tuple-element.24), channel_id=1, replica_groups={{0,1,2,3},{4,5,6,7},{8,9,10,11},{12,13,14,15},{16,17,18,19},{20,21,22,2..., dimensions={0} | all-to-all | bytes 524288 | tf_op jit(solution)/shard_map/all_to_all | solution.py:409
  17.9 0.0 copy-done.1
  17.9 0.0 copy-done
  17.9 3.2 %shard_map.78 = (bf16[4,4,16,512]{3,2,1,0:T(8,128)(2,1)S(1)}, bf16[2,2,64,512]{3,2,1,0:T(8,128)(2,1)S(1)}) custom-call(s32[3]{0:T(128)S(1)} %pad_add_fusion.where_ref, bf16[1,4,16,2048]{3,2,1,0:T(8,128)(2,1)S(1)} %bitcast.47, f32[3,1,2048]{2,1,0:T(1,128)S(1)} %get-tuple-element.25.mod_ref, ...), custom_call_target="tpu_custom_call", output_to_operand_aliasing={{1}: (6, {})} | custom-call | tf_op jit(solution)/shard_map/pallas_call | solution.py:386
  21.1 14.6 %all_to_all.51 = bf16[16,16,512]{2,1,0:T(8,128)(2,1)S(1)} all-to-all(bf16[16,16,512]{2,1,0:T(8,128)(2,1)S(1)} %bitcast.56), channel_id=1, replica_groups={{0,1,2,3,4,5,6,7,8,9,10,11,12,13,14,15},{16,17,18,19,20,21,22,23,24,25,..., dimensions={0} | all-to-all | bytes 524288 | tf_op jit(solution)/shard_map/all_to_all | solution.py:335
  35.7 12.4 %all_to_all.52 = bf16[16,16,512]{2,1,0:T(8,128)(2,1)S(1)} all-to-all(bf16[16,16,512]{2,1,0:T(8,128)(2,1)S(1)} %bitcast.57), channel_id=1, replica_groups={{0,1,2,3,4,5,6,7,8,9,10,11,12,13,14,15},{16,17,18,19,20,21,22,23,24,25,..., dimensions={0} | all-to-all | bytes 524288 | tf_op jit(solution)/shard_map/all_to_all | solution.py:335
  48.2 3.1 %shard_map.80 = (bf16[4,4,16,512]{3,2,1,0:T(8,128)(2,1)S(1)}, bf16[2,2,64,512]{3,2,1,0:T(8,128)(2,1)S(1)}) custom-call(s32[3]{0:T(128)S(1)} %pad_add_fusion.where_ref, bf16[4,4,16,512]{3,2,1,0:T(8,128)(2,1)S(1)} %bitcast.44, f32[3,1,2048]{2,1,0:T(1,128)S(1)} %get-tuple-element.25.mod_ref, ...), custom_call_target="tpu_custom_call", output_to_operand_aliasing={{1}: (6, {})} | custom-call | tf_op jit(solution)/shard_map/pallas_call | solution.py:386
  51.3 12.3 %all_to_all.53 = bf16[16,16,512]{2,1,0:T(8,128)(2,1)S(1)} all-to-all(bf16[16,16,512]{2,1,0:T(8,128)(2,1)S(1)} %bitcast.58), channel_id=1, replica_groups={{0,1,2,3,4,5,6,7,8,9,10,11,12,13,14,15},{16,17,18,19,20,21,22,23,24,25,..., dimensions={0} | all-to-all | bytes 524288 | tf_op jit(solution)/shard_map/all_to_all | solution.py:335
  63.7 12.3 %all_to_all.54 = bf16[16,16,512]{2,1,0:T(8,128)(2,1)S(1)} all-to-all(bf16[16,16,512]{2,1,0:T(8,128)(2,1)S(1)} %bitcast.59), channel_id=1, replica_groups={{0,1,2,3,4,5,6,7,8,9,10,11,12,13,14,15},{16,17,18,19,20,21,22,23,24,25,..., dimensions={0} | all-to-all | bytes 524288 | tf_op jit(solution)/shard_map/all_to_all | solution.py:335
  76.0 3.1 %shard_map.82 = (bf16[4,4,16,512]{3,2,1,0:T(8,128)(2,1)S(1)}, bf16[2,2,64,512]{3,2,1,0:T(8,128)(2,1)S(1)}) custom-call(s32[3]{0:T(128)S(1)} %pad_add_fusion.where_ref, bf16[4,4,16,512]{3,2,1,0:T(8,128)(2,1)S(1)} %bitcast.45, f32[3,1,2048]{2,1,0:T(1,128)S(1)} %get-tuple-element.25.mod_ref, ...), custom_call_target="tpu_custom_call", output_to_operand_aliasing={{1}: (6, {})} | custom-call | tf_op jit(solution)/shard_map/pallas_call | solution.py:386
  79.2 12.3 %all_to_all.55 = bf16[16,16,512]{2,1,0:T(8,128)(2,1)S(1)} all-to-all(bf16[16,16,512]{2,1,0:T(8,128)(2,1)S(1)} %bitcast.60), channel_id=1, replica_groups={{0,1,2,3,4,5,6,7,8,9,10,11,12,13,14,15},{16,17,18,19,20,21,22,23,24,25,..., dimensions={0} | all-to-all | bytes 524288 | tf_op jit(solution)/shard_map/all_to_all | solution.py:335
  91.6 12.3 %all_to_all.56 = bf16[16,16,512]{2,1,0:T(8,128)(2,1)S(1)} all-to-all(bf16[16,16,512]{2,1,0:T(8,128)(2,1)S(1)} %bitcast.55), channel_id=1, replica_groups={{0,1,2,3,4,5,6,7,8,9,10,11,12,13,14,15},{16,17,18,19,20,21,22,23,24,25,..., dimensions={0} | all-to-all | bytes 524288 | tf_op jit(solution)/shard_map/all_to_all | solution.py:335
  103.9 3.1 %shard_map.84 = (bf16[4,4,16,512]{3,2,1,0:T(8,128)(2,1)S(1)}, bf16[2,2,64,512]{3,2,1,0:T(8,128)(2,1)S(1)}) custom-call(s32[3]{0:T(128)S(1)} %pad_add_fusion.where_ref, bf16[4,4,16,512]{3,2,1,0:T(8,128)(2,1)S(1)} %bitcast.46, f32[3,1,2048]{2,1,0:T(1,128)S(1)} %get-tuple-element.25.mod_ref, ...), custom_call_target="tpu_custom_call", output_to_operand_aliasing={{1}: (6, {})} | custom-call | tf_op jit(solution)/shard_map/pallas_call | solution.py:386
  107.1 12.3 %all_to_all.57 = bf16[16,16,512]{2,1,0:T(8,128)(2,1)S(1)} all-to-all(bf16[16,16,512]{2,1,0:T(8,128)(2,1)S(1)} %bitcast.61), channel_id=1, replica_groups={{0,1,2,3,4,5,6,7,8,9,10,11,12,13,14,15},{16,17,18,19,20,21,22,23,24,25,..., dimensions={0} | all-to-all | bytes 524288 | tf_op jit(solution)/shard_map/all_to_all | solution.py:335
  119.4 12.3 %all_to_all.58 = bf16[16,16,512]{2,1,0:T(8,128)(2,1)S(1)} all-to-all(bf16[16,16,512]{2,1,0:T(8,128)(2,1)S(1)} %bitcast.52), channel_id=1, replica_groups={{0,1,2,3,4,5,6,7,8,9,10,11,12,13,14,15},{16,17,18,19,20,21,22,23,24,25,..., dimensions={0} | all-to-all | bytes 524288 | tf_op jit(solution)/shard_map/all_to_all | solution.py:335
  131.8 3.7 %shard_map.86 = (bf16[2,2,4,16,512]{4,3,2,1,0:T(8,128)(2,1)S(1)}, bf16[2,2,64,512]{3,2,1,0:T(8,128)(2,1)}) custom-call(s32[3]{0:T(128)S(1)} %pad_add_fusion.where_ref, bf16[4,4,16,512]{3,2,1,0:T(8,128)(2,1)S(1)} %bitcast.43, f32[3,1,2048]{2,1,0:T(1,128)S(1)} %get-tuple-element.25.mod_ref, bf16[2048,1536]{1,0:T(8,128)(2,1)S(1)} %bitcast.36, ...), custom_call_target="tpu_custom_call" | custom-call | tf_op jit(solution)/shard_map/pallas_call | solution.py:386
  135.5 12.7 %all_to_all.59 = bf16[16,16,512]{2,1,0:T(8,128)(2,1)S(1)} all-to-all(bf16[16,16,512]{2,1,0:T(8,128)(2,1)S(1)} %bitcast.54), channel_id=1, replica_groups={{0,1,2,3,4,5,6,7,16,17,18,19,20,21,22,23},{8,9,10,11,12,13,14,15,24,25,..., dimensions={0} | all-to-all | bytes 524288 | tf_op jit(solution)/shard_map/all_to_all | solution.py:426
  148.1 1.2 shard_map.87
  (4 shorter events, 0.1 us)
Async XLA Ops:
  0.6 17.3 %copy-start.1 = (bf16[1,512,2048]{2,1,0:T(8,128)(2,1)S(1)}, bf16[1,512,2048]{2,1,0:T(8,128)(2,1)}, u32[]{:S(2)}) copy-start(bf16[1,512,2048]{2,1,0:T(8,128)(2,1)} %param.9) | copy-start | bytes 6291460
  0.6 17.3 %copy-start = (bf16[1,2048,1536]{2,1,0:T(8,128)(2,1)S(1)}, bf16[1,2048,1536]{2,1,0:T(8,128)(2,1)}, u32[]{:S(2)}) copy-start(bf16[1,2048,1536]{2,1,0:T(8,128)(2,1)} %param.8) | copy-start | bytes 18874372

commit v14 on v12

--- a/solution.py
+++ b/solution.py
@@ -45,9 +45,9 @@
     section, own_member, own_slice = where_ref[0], where_ref[1], where_ref[2]
     group = tick - section
     parts = [rows_ref[q].reshape(rows, block_cols).astype(jnp.float32) for q in range(blocks)]
-    mean = sum(jnp.sum(x, axis=-1, keepdims=True) for x in parts) / width
+    mean = jnp.sum(sum(parts), axis=-1, keepdims=True) * (1.0 / width)
     parts = [x - mean for x in parts]
-    spread = sum(jnp.sum(x * x, axis=-1, keepdims=True) for x in parts) / width
+    spread = jnp.sum(sum(x * x for x in parts), axis=-1, keepdims=True) * (1.0 / width)
     inverse = lax.rsqrt(spread + EPSILON)
     modulated = []
     for q, x in enumerate(parts):
@@ -58,9 +58,13 @@
     modulated = jnp.concatenate(modulated, axis=1)
     mixed = jnp.dot(modulated, qkv_ref[...], preferred_element_type=jnp.float32)
 
+    def stacked(kind):
+        at = [(3 * head + kind) * head_dim for head in range(heads)]
+        return jnp.stack([mixed[:, start : start + head_dim] for start in at])
+
     def by_patch(values):
-        values = values.reshape(slices, in_group, tok_dev, head_dim).swapaxes(0, 1)
-        return values.reshape(rows, head_dim).astype(jnp.bfloat16)
+        values = values.reshape(heads, slices, in_group, tok_dev, head_dim).swapaxes(1, 2)
+        return values.reshape(heads, rows, head_dim).astype(jnp.bfloat16)
 
     def query_patch(shape):
         return lax.broadcasted_iota(jnp.int32, shape, 0) // tok_dev % in_group
@@ -77,39 +81,32 @@
         masks.append((at // (groups * rows) != own_member).astype(jnp.float32))
     mask = jnp.concatenate(masks, axis=1)
 
-    def column(head, kind):
-        at = (3 * head + kind) * head_dim
-        return mixed[:, at : at + head_dim]
-
-    every = range(heads)
-    at_head = [slice(head * head_dim, (head + 1) * head_dim) for head in every]
-    queries = [head_norm(column(h, 0), gain_ref[0:1, :]).astype(jnp.bfloat16) for h in every]
-    fresh = [
-        (by_patch(head_norm(column(h, 1), gain_ref[1:2, :])), by_patch(column(h, 2))) for h in every
-    ]
+    queries = head_norm(stacked(0), gain_ref[0:1, :]).astype(jnp.bfloat16)
+    fresh = (by_patch(head_norm(stacked(1), gain_ref[1:2, :])), by_patch(stacked(2)))
 
     def entries(head, kind):
-        old = old_table_ref[kind, :, :, at_head[head]].reshape(groups * rows, head_dim)
-        stale = [ref[kind, :, at_head[head]] for ref in stale_refs]
-        return jnp.concatenate([fresh[head][kind], old] + stale)
+        at = slice(head * head_dim, (head + 1) * head_dim)
+        old = old_table_ref[kind, :, :, at].reshape(groups * rows, head_dim)
+        return jnp.concatenate([fresh[kind][head], old] + [ref[kind, :, at] for ref in stale_refs])
 
     scores = [
         lax.dot_general(
-            queries[h],
-            entries(h, 0),
+            queries[head],
+            entries(head, 0),
             (((1,), (1,)), ((), ())),
             preferred_element_type=jnp.float32,
         )
-        for h in every
+        for head in range(heads)
     ]
-    weights = [mask * jnp.exp(s / math.sqrt(head_dim)) for s in scores]
-    totals = [jnp.sum(w, axis=-1, keepdims=True) for w in weights]
+    weights = mask[None] * jnp.exp(jnp.stack(scores) * (1.0 / math.sqrt(head_dim)))
+    inverse = 1.0 / jnp.sum(weights, axis=-1, keepdims=True)
+    weights = weights.astype(jnp.bfloat16)
     summed = [
-        jnp.dot(weights[h].astype(jnp.bfloat16), entries(h, 1), preferred_element_type=jnp.float32)
-        for h in every
+        jnp.dot(weights[head], entries(head, 1), preferred_element_type=jnp.float32)
+        for head in range(heads)
     ]
-    attended = [(a / t).astype(jnp.bfloat16) for a, t in zip(summed, totals)]
-    attended = jnp.concatenate(attended, axis=1)
+    attended = (jnp.stack(summed) * inverse).astype(jnp.bfloat16)
+    attended = jnp.concatenate([attended[head] for head in range(heads)], axis=1)
 
     projected = jnp.dot(attended, out_ref[...], preferred_element_type=jnp.float32)
     projected = mod_ref[2] * projected
@@ -126,7 +123,7 @@
         @pl.when(group == at)
         def _():
             for j in range(2):
-                table_ref[j, at] = jnp.concatenate([pair[j] for pair in fresh], axis=1)
+                table_ref[j, at] = jnp.concatenate([fresh[j][head] for head in range(heads)], axis=1)
 
         @pl.when(group != at)
         def _():

time: 148 us -> 148 us (level)
  no operation moved by 1% of the time
where the time goes in v14:
time: 148 us
  blocking collectives  129 us (87%)
  Pallas kernels  18.1 us (12%)
    all_to_all x8, blocking collectives, exchange(): lax.all_to_all(value, ('pipe', 'seq'), 0, 0, axis_index_groups=peers)  101 us
    all_to_all x1, blocking collectives, local(): lax.all_to_all(spread, 'seq', 0, 0, axis_index_groups=in_slices)[None]  15.1 us
    pallas_call x5, Pallas kernels, attend(): pl.pallas_call(functools.partial(section_kernel, tick, (tok_dev, head_dim...  14.1 us
    all_to_all x1, blocking collectives, local(): lax.all_to_all(closing.reshape((-1,) + closing_shape[3:]), ('cfg', 'pipe'...  12.7 us

profile of v14, /device:TPU:0, one launch (start us, length us, event | category | flops | bytes accessed | tf_op | source)
XLA Modules:
  0.0 147.8 jit_solution(13171203832727999424)
XLA Ops:
  0.6 0.0 copy-start.1
  0.6 0.0 copy-start
  0.7 0.1 pad_add_fusion.where_ref
  0.7 2.0 %shard_map.77 = (f32[3,1,2048]{2,1,0:T(1,128)S(1)}, f32[2,128]{1,0:T(2,128)S(1)}, bf16[2,2,64,512]{3,2,1,0:T(8,128)(2,1)S(1)}, bf16[2,16,512]{2,1,0:T(8,128)(2,1...) custom-call(s32[3]{0:T(128)S(1)} %pad_add_fusion.where_ref, bf16[2,16,2048]{2,1,0:T(8,128)(2,1)} %bitcast.63, ...), custom_call_target="tpu_custom_call" | custom-call | tf_op jit(solution)/shard_map/pallas_call | solution.py:324
  2.8 15.1 %all_to_all.50 = bf16[4,16,2048]{2,1,0:T(8,128)(2,1)S(1)} all-to-all(bf16[4,16,2048]{2,1,0:T(8,128)(2,1)S(1)} %get-tuple-element.26), channel_id=1, replica_groups={{0,1,2,3},{4,5,6,7},{8,9,10,11},{12,13,14,15},{16,17,18,19},{20,21,22,2..., dimensions={0} | all-to-all | bytes 524288 | tf_op jit(solution)/shard_map/all_to_all | solution.py:375
  17.9 0.0 copy-done.1
  17.9 0.0 copy-done
  17.9 2.8 %shard_map.78 = (bf16[4,4,16,512]{3,2,1,0:T(8,128)(2,1)S(1)}, bf16[2,2,64,512]{3,2,1,0:T(8,128)(2,1)S(1)}) custom-call(s32[3]{0:T(128)S(1)} %pad_add_fusion.where_ref, bf16[1,4,16,2048]{3,2,1,0:T(8,128)(2,1)S(1)} %bitcast.47, f32[3,1,2048]{2,1,0:T(1,128)S(1)} %get-tuple-element.27.mod_ref, ...), custom_call_target="tpu_custom_call", output_to_operand_aliasing={{1}: (6, {})} | custom-call | tf_op jit(solution)/shard_map/pallas_call | solution.py:352
  20.7 14.6 %all_to_all.51 = bf16[16,16,512]{2,1,0:T(8,128)(2,1)S(1)} all-to-all(bf16[16,16,512]{2,1,0:T(8,128)(2,1)S(1)} %bitcast.56), channel_id=1, replica_groups={{0,1,2,3,4,5,6,7,8,9,10,11,12,13,14,15},{16,17,18,19,20,21,22,23,24,25,..., dimensions={0} | all-to-all | bytes 524288 | tf_op jit(solution)/shard_map/all_to_all | solution.py:307
  35.4 12.4 %all_to_all.52 = bf16[16,16,512]{2,1,0:T(8,128)(2,1)S(1)} all-to-all(bf16[16,16,512]{2,1,0:T(8,128)(2,1)S(1)} %bitcast.57), channel_id=1, replica_groups={{0,1,2,3,4,5,6,7,8,9,10,11,12,13,14,15},{16,17,18,19,20,21,22,23,24,25,..., dimensions={0} | all-to-all | bytes 524288 | tf_op jit(solution)/shard_map/all_to_all | solution.py:307
  47.8 2.8 %shard_map.80 = (bf16[4,4,16,512]{3,2,1,0:T(8,128)(2,1)S(1)}, bf16[2,2,64,512]{3,2,1,0:T(8,128)(2,1)S(1)}) custom-call(s32[3]{0:T(128)S(1)} %pad_add_fusion.where_ref, bf16[4,4,16,512]{3,2,1,0:T(8,128)(2,1)S(1)} %bitcast.44, f32[3,1,2048]{2,1,0:T(1,128)S(1)} %get-tuple-element.27.mod_ref, ...), custom_call_target="tpu_custom_call", output_to_operand_aliasing={{1}: (6, {})} | custom-call | tf_op jit(solution)/shard_map/pallas_call | solution.py:352
  50.6 12.3 %all_to_all.53 = bf16[16,16,512]{2,1,0:T(8,128)(2,1)S(1)} all-to-all(bf16[16,16,512]{2,1,0:T(8,128)(2,1)S(1)} %bitcast.58), channel_id=1, replica_groups={{0,1,2,3,4,5,6,7,8,9,10,11,12,13,14,15},{16,17,18,19,20,21,22,23,24,25,..., dimensions={0} | all-to-all | bytes 524288 | tf_op jit(solution)/shard_map/all_to_all | solution.py:307
  63.0 12.3 %all_to_all.54 = bf16[16,16,512]{2,1,0:T(8,128)(2,1)S(1)} all-to-all(bf16[16,16,512]{2,1,0:T(8,128)(2,1)S(1)} %bitcast.59), channel_id=1, replica_groups={{0,1,2,3,4,5,6,7,8,9,10,11,12,13,14,15},{16,17,18,19,20,21,22,23,24,25,..., dimensions={0} | all-to-all | bytes 524288 | tf_op jit(solution)/shard_map/all_to_all | solution.py:307
  75.4 2.8 %shard_map.82 = (bf16[4,4,16,512]{3,2,1,0:T(8,128)(2,1)S(1)}, bf16[2,2,64,512]{3,2,1,0:T(8,128)(2,1)S(1)}) custom-call(s32[3]{0:T(128)S(1)} %pad_add_fusion.where_ref, bf16[4,4,16,512]{3,2,1,0:T(8,128)(2,1)S(1)} %bitcast.45, f32[3,1,2048]{2,1,0:T(1,128)S(1)} %get-tuple-element.27.mod_ref, ...), custom_call_target="tpu_custom_call", output_to_operand_aliasing={{1}: (6, {})} | custom-call | tf_op jit(solution)/shard_map/pallas_call | solution.py:352
  78.2 12.3 %all_to_all.55 = bf16[16,16,512]{2,1,0:T(8,128)(2,1)S(1)} all-to-all(bf16[16,16,512]{2,1,0:T(8,128)(2,1)S(1)} %bitcast.60), channel_id=1, replica_groups={{0,1,2,3,4,5,6,7,8,9,10,11,12,13,14,15},{16,17,18,19,20,21,22,23,24,25,..., dimensions={0} | all-to-all | bytes 524288 | tf_op jit(solution)/shard_map/all_to_all | solution.py:307
  90.6 12.3 %all_to_all.56 = bf16[16,16,512]{2,1,0:T(8,128)(2,1)S(1)} all-to-all(bf16[16,16,512]{2,1,0:T(8,128)(2,1)S(1)} %bitcast.55), channel_id=1, replica_groups={{0,1,2,3,4,5,6,7,8,9,10,11,12,13,14,15},{16,17,18,19,20,21,22,23,24,25,..., dimensions={0} | all-to-all | bytes 524288 | tf_op jit(solution)/shard_map/all_to_all | solution.py:307
  102.9 2.8 %shard_map.84 = (bf16[4,4,16,512]{3,2,1,0:T(8,128)(2,1)S(1)}, bf16[2,2,64,512]{3,2,1,0:T(8,128)(2,1)S(1)}) custom-call(s32[3]{0:T(128)S(1)} %pad_add_fusion.where_ref, bf16[4,4,16,512]{3,2,1,0:T(8,128)(2,1)S(1)} %bitcast.46, f32[3,1,2048]{2,1,0:T(1,128)S(1)} %get-tuple-element.27.mod_ref, ...), custom_call_target="tpu_custom_call", output_to_operand_aliasing={{1}: (6, {})} | custom-call | tf_op jit(solution)/shard_map/pallas_call | solution.py:352
  105.7 12.3 %all_to_all.57 = bf16[16,16,512]{2,1,0:T(8,128)(2,1)S(1)} all-to-all(bf16[16,16,512]{2,1,0:T(8,128)(2,1)S(1)} %bitcast.61), channel_id=1, replica_groups={{0,1,2,3,4,5,6,7,8,9,10,11,12,13,14,15},{16,17,18,19,20,21,22,23,24,25,..., dimensions={0} | all-to-all | bytes 524288 | tf_op jit(solution)/shard_map/all_to_all | solution.py:307
  118.1 12.3 %all_to_all.58 = bf16[16,16,512]{2,1,0:T(8,128)(2,1)S(1)} all-to-all(bf16[16,16,512]{2,1,0:T(8,128)(2,1)S(1)} %bitcast.53), channel_id=1, replica_groups={{0,1,2,3,4,5,6,7,8,9,10,11,12,13,14,15},{16,17,18,19,20,21,22,23,24,25,..., dimensions={0} | all-to-all | bytes 524288 | tf_op jit(solution)/shard_map/all_to_all | solution.py:307
  130.4 2.8 %shard_map.86 = (bf16[2,2,4,16,512]{4,3,2,1,0:T(8,128)(2,1)S(1)}, bf16[2,2,64,512]{3,2,1,0:T(8,128)(2,1)S(1)}) custom-call(s32[3]{0:T(128)S(1)} %pad_add_fusion.where_ref, bf16[4,4,16,512]{3,2,1,0:T(8,128)(2,1)S(1)} %bitcast.43, f32[3,1,2048]{2,1,0:T(1,128)S(1)} %get-tuple-element.27.mod_ref, ...), custom_call_target="tpu_custom_call", output_to_operand_aliasing={{1}: (6, {})} | custom-call | tf_op jit(solution)/shard_map/pallas_call | solution.py:352
  133.2 12.7 %all_to_all.59 = bf16[16,16,512]{2,1,0:T(8,128)(2,1)S(1)} all-to-all(bf16[16,16,512]{2,1,0:T(8,128)(2,1)S(1)} %bitcast.54), channel_id=1, replica_groups={{0,1,2,3,4,5,6,7,16,17,18,19,20,21,22,23},{8,9,10,11,12,13,14,15,24,25,..., dimensions={0} | all-to-all | bytes 524288 | tf_op jit(solution)/shard_map/all_to_all | solution.py:392
  145.9 1.9 %shard_map.87 = (bf16[8,1024]{1,0:T(8,128)(2,1)}, bf16[2,2,64,512]{3,2,1,0:T(8,128)(2,1)}) custom-call(s32[3]{0:T(128)S(1)} %pad_add_fusion.where_ref, bf16[2,2,4,16,512]{4,3,2,1,0:T(8,128)(2,1)S(1)} %bitcast.48, bf16[2,2,64,512]{3,2,1,0:T(8,128)(2,1)S(1)} %get-tuple-element.47.table_ref), custom_call_target="tpu_custom_call" | custom-call | tf_op jit(solution)/shard_map/pallas_call | solution.py:399
  (4 shorter events, 0.1 us)
Async XLA Ops:
  0.6 17.3 %copy-start.1 = (bf16[1,512,2048]{2,1,0:T(8,128)(2,1)S(1)}, bf16[1,512,2048]{2,1,0:T(8,128)(2,1)}, u32[]{:S(2)}) copy-start(bf16[1,512,2048]{2,1,0:T(8,128)(2,1)} %param.9) | copy-start | bytes 6291460
  0.6 17.3 %copy-start = (bf16[1,2048,1536]{2,1,0:T(8,128)(2,1)S(1)}, bf16[1,2048,1536]{2,1,0:T(8,128)(2,1)}, u32[]{:S(2)}) copy-start(bf16[1,2048,1536]{2,1,0:T(8,128)(2,1)} %param.8) | copy-start | bytes 18874372

commit v15 on v14

--- a/solution.py
+++ b/solution.py
@@ -34,6 +34,7 @@
 def section_kernel(tick, sizes, where_ref, rows_ref, mod_ref, qkv_ref, out_ref, gain_ref, *refs):
     *stale_refs, old_table_ref, partial_ref, table_ref = refs
     closing = len(partial_ref.shape) == 5
+    folding = tick == 1
     tok_dev, head_dim = sizes
     blocks, slices, block_rows, block_cols = rows_ref.shape
     rows = slices * block_rows
@@ -110,6 +111,13 @@
 
     projected = jnp.dot(attended, out_ref[...], preferred_element_type=jnp.float32)
     projected = mod_ref[2] * projected
+    if folding:
+        at_slice = lax.broadcasted_iota(jnp.int32, (rows, 1), 0) // block_rows
+        own = (at_slice == own_slice).astype(jnp.float32)
+        projected = projected + own * jnp.concatenate(
+            [rows_ref[q].reshape(rows, block_cols).astype(jnp.float32) for q in range(blocks)],
+            axis=1,
+        )
     if closing:
         close_into(partial_ref, projected, rows_ref, section, own_slice, in_group)
     else:
@@ -167,11 +175,11 @@
 
 def start_kernel(where_ref, latent_ref, qkv_ref, out_ref, *refs):
     del qkv_ref, out_ref
-    loads = (len(refs) - 4) // 2
+    loads = (len(refs) - 3) // 2
     from_refs, to_refs = refs[:loads], refs[loads : 2 * loads]
-    sources_to, streams_to, spread_to, sems = refs[2 * loads :]
-    sections, _, block_cols = streams_to.shape
-    own_cols = pl.ds(pl.multiple_of(where_ref[0] * block_cols, block_cols), block_cols)
+    sources_to, spread_to, sems = refs[2 * loads :]
+    half_cols = sources_to.shape[2]
+    own_cols = pl.ds(pl.multiple_of(where_ref[0] % 2 * half_cols, half_cols), half_cols)
     pairs = [(latent_ref.at[0], spread_to.at[piece]) for piece in range(spread_to.shape[0])]
     pairs.append((latent_ref.at[:, :, own_cols], sources_to))
     pairs.extend(zip(from_refs, to_refs))
@@ -181,27 +189,29 @@
     ]
     for copy in copies:
         copy.start()
-    for section in range(1, sections):
-        streams_to[section] = jnp.zeros(streams_to.shape[1:], streams_to.dtype)
     for copy in copies:
         copy.wait()
-    streams_to[0] = sources_to[0]
-
-
-def added(parts_ref, streams_ref, section):
-    total = streams_ref[section].astype(jnp.float32)
+
+
+def added(parts_ref, section, *streams_refs):
+    total = sum(parts_ref[section, piece].astype(jnp.float32) for piece in range(parts_ref.shape[1]))
+    for ref in streams_refs:
+        total = total + ref[section].astype(jnp.float32)
+    return total
+
+
+def settle_first_kernel(parts_ref, sources_ref, spread_to):
+    first = added(parts_ref, 0, sources_ref).astype(jnp.bfloat16)
     for piece in range(parts_ref.shape[1]):
-        total = total + parts_ref[section, piece].astype(jnp.float32)
-    return total
-
-
-def settle_kernel(entering, parts_ref, streams_ref, sources_ref, streams_to, spread_to):
+        spread_to[0, piece] = sources_ref[1]
+        spread_to[1, piece] = first
+
+
+def settle_kernel(parts_ref, *refs):
+    *streams_refs, streams_to, spread_to = refs
     count, slices = parts_ref.shape[:2]
     for section in range(count):
-        if section == 0:
-            held = sources_ref[entering]
-        else:
-            held = added(parts_ref, streams_ref, section - 1).astype(jnp.bfloat16)
+        held = added(parts_ref, max(section - 1, 0), *streams_refs).astype(jnp.bfloat16)
         streams_to[section] = held
         for piece in range(slices):
             spread_to[section, piece] = held
@@ -209,9 +219,9 @@
 
 def settle_last_kernel(in_group, parts_ref, streams_ref, spread_to):
     count, slices = parts_ref.shape[:2]
-    finished = added(parts_ref, streams_ref, count - 1)
+    finished = added(parts_ref, count - 1, streams_ref)
     tok_dev = finished.shape[0] // in_group
-    last = added(parts_ref, streams_ref, count - 2).astype(jnp.bfloat16)
+    last = added(parts_ref, count - 2, streams_ref).astype(jnp.bfloat16)
     for section in range(count):
         held = last
         if section < in_group:
@@ -302,10 +312,16 @@
         for g in in_slices
     ]
 
-    def exchange(value):
-        value = value.reshape(homes, block_rows, block_cols)
-        value = lax.all_to_all(value, ("pipe", "seq"), 0, 0, axis_index_groups=peers)
-        return value.reshape(section_count, slice_count, block_rows, block_cols)
+    pair_peers = [
+        [q * seq_count + at for q in range(first, first + 2) for at in g]
+        for first in range(0, section_count, 2)
+        for g in in_slices
+    ]
+
+    def exchange(value, among=peers):
+        flat = value.reshape((-1,) + value.shape[2:])
+        flat = lax.all_to_all(flat, ("pipe", "seq"), 0, 0, axis_index_groups=among)
+        return flat.reshape(value.shape)
 
     vmem = pl.BlockSpec(memory_space=pltpu.VMEM)
     smem = pl.BlockSpec(memory_space=pltpu.SMEM)
@@ -321,16 +337,15 @@
         norm_gain[0],
         own_cache.reshape(2, GROUPS, rows, local_width),
     )
-    modulation, norm_gain, table, sources, streams, spread = pl.pallas_call(
+    modulation, norm_gain, table, sources, spread = pl.pallas_call(
         start_kernel,
         out_shape=tuple(pltpu.VMEM(value.shape, value.dtype) for value in loads)
         + (
-            pltpu.VMEM((GROUPS, block_rows, block_cols), jnp.bfloat16),
-            jax.ShapeDtypeStruct(stream_shape, jnp.bfloat16),
+            pltpu.VMEM((GROUPS, block_rows, model_width // 2), jnp.bfloat16),
             jax.ShapeDtypeStruct((slice_count, block_rows, model_width), jnp.bfloat16),
         ),
         in_specs=[smem] + [hbm] * (len(loads) + 3),
-        out_specs=(vmem,) * (len(loads) + 3),
+        out_specs=(vmem,) * (len(loads) + 2),
         scratch_shapes=[pltpu.SemaphoreType.DMA((len(loads) + slice_count + 1,))],
         compiler_params=pltpu.CompilerParams(vmem_limit_bytes=4 * 1024 * 1024),
     )(where, in_hbm(sources), in_hbm(qkv_slice), in_hbm(out_slice), *map(in_hbm, loads))
@@ -373,21 +388,23 @@
     ticks = GROUPS + section_count - 1
     closing_shape = (2, half, slice_count, block_rows, block_cols)
     features = lax.all_to_all(spread, "seq", 0, 0, axis_index_groups=in_slices)[None]
-    for tick in range(ticks - 1):
+    pair_shape = (2, slice_count, block_rows, model_width // 2)
+    partial_out, table = attend(0, features, table, pair_shape)
+    parts = exchange(partial_out, pair_peers)
+    (spread,) = small(settle_first_kernel, [vmem] * 2, pair_shape)(parts, in_vmem(sources))
+    features = exchange(spread, pair_peers)
+    streams = []
+    for tick in range(1, ticks - 2):
         partial_out, table = attend(tick, features, table, spread_shape)
-        parts = exchange(partial_out)
-        if tick < ticks - 2:
-            streams, spread = small(
-                functools.partial(settle_kernel, min(tick + 1, GROUPS - 1)),
-                [vmem] * 3,
-                stream_shape,
-                spread_shape,
-            )(parts, streams, in_vmem(sources))
-        else:
-            (spread,) = small(
-                functools.partial(settle_last_kernel, in_group), [vmem] * 2, spread_shape
-            )(parts, streams)
+        held = [exchange(partial_out)] + streams
+        stream, spread = small(settle_kernel, [vmem] * len(held), stream_shape, spread_shape)(*held)
+        streams = [stream]
         features = exchange(spread)
+    partial_out, table = attend(ticks - 2, features, table, spread_shape)
+    (spread,) = small(
+        functools.partial(settle_last_kernel, in_group), [vmem] * 2, spread_shape
+    )(exchange(partial_out), *streams)
+    features = exchange(spread)
     closing, table = attend(ticks - 1, features, table, closing_shape)
     closing = lax.all_to_all(
         closing.reshape((-1,) + closing_shape[3:]),

time: 148 us -> 144 us (0.973)
  blocking collectives: 129 us -> 125 us
    all_to_all x8, blocking collectives: 101 us -> 97.2 us  [exchange(): flat = lax.all_to_all(flat, ('pipe', 'seq'), 0, 0, axis_index_groups=among)]
where the time goes in v15:
time: 144 us
  blocking collectives  125 us (87%)
  Pallas kernels  18.1 us (13%)
    all_to_all x8, blocking collectives, exchange(): flat = lax.all_to_all(flat, ('pipe', 'seq'), 0, 0, axis_index_groups=among)  97.2 us
    all_to_all x1, blocking collectives, local(): lax.all_to_all(spread, 'seq', 0, 0, axis_index_groups=in_slices)[None]  15.1 us
    pallas_call x5, Pallas kernels, attend(): pl.pallas_call(functools.partial(section_kernel, tick, (tok_dev, head_dim...  14.1 us
    all_to_all x1, blocking collectives, local(): lax.all_to_all(closing.reshape((-1,) + closing_shape[3:]), ('cfg', 'pipe'...  12.7 us

profile of v15, /device:TPU:0, one launch (start us, length us, event | category | flops | bytes accessed | tf_op | source)
XLA Modules:
  0.0 143.9 jit_solution(12241729243325539795)
XLA Ops:
  0.6 0.0 copy-start.1
  0.6 0.0 copy-start
  0.7 0.1 pad_add_fusion.where_ref
  0.7 2.1 %shard_map.77 = (f32[3,1,2048]{2,1,0:T(1,128)S(1)}, f32[2,128]{1,0:T(2,128)S(1)}, bf16[2,2,64,512]{3,2,1,0:T(8,128)(2,1)S(1)}, bf16[2,16,1024]{2,1,0:T(8,128)(2,1)S(1)}, bf16[4,16,2048]{2,1,0:T(8,128)(2,1)S(1)}) custom-call(s32[3]{0:T(128)S(1)} %pad_add_fusion.where_ref, bf16[2,16,2048]{2,1,0:T(8,128)(2,1)} %bitcast.63, bf16[2048,1536]{1,0:T(8,128)(2,1)} %bitcast.31, ...), custom_call_target="tpu_custom_call" | custom-call | tf_op jit(solution)/shard_map/pallas_call | solution.py:340
  2.8 15.1 %all_to_all.50 = bf16[4,16,2048]{2,1,0:T(8,128)(2,1)S(1)} all-to-all(bf16[4,16,2048]{2,1,0:T(8,128)(2,1)S(1)} %get-tuple-element.23), channel_id=1, replica_groups={{0,1,2,3},{4,5,6,7},{8,9,10,11},{12,13,14,15},{16,17,18,19},{20,21,22,2..., dimensions={0} | all-to-all | bytes 524288 | tf_op jit(solution)/shard_map/all_to_all | solution.py:390
  17.9 0.0 copy-done.1
  17.9 0.0 copy-done
  17.9 2.8 %shard_map.78 = (bf16[2,4,16,1024]{3,2,1,0:T(8,128)(2,1)S(1)}, bf16[2,2,64,512]{3,2,1,0:T(8,128)(2,1)S(1)}) custom-call(s32[3]{0:T(128)S(1)} %pad_add_fusion.where_ref, bf16[1,4,16,2048]{3,2,1,0:T(8,128)(2,1)S(1)} %bitcast.47, f32[3,1,2048]{2,1,0:T(1,128)S(1)} %get-tuple-element.24.mod_ref, ...), custom_call_target="tpu_custom_call", output_to_operand_aliasing={{1}: (6, {})} | custom-call | tf_op jit(solution)/shard_map/pallas_call | solution.py:367
  20.7 13.0 %all_to_all.51 = bf16[8,16,1024]{2,1,0:T(8,128)(2,1)S(1)} all-to-all(bf16[8,16,1024]{2,1,0:T(8,128)(2,1)S(1)} %bitcast.56), channel_id=1, replica_groups={{0,1,2,3,4,5,6,7},{8,9,10,11,12,13,14,15},{16,17,18,19,20,21,22,23},{24..., dimensions={0} | all-to-all | bytes 524288 | tf_op jit(solution)/shard_map/all_to_all | solution.py:323
  33.7 11.1 %all_to_all.52 = bf16[8,16,1024]{2,1,0:T(8,128)(2,1)S(1)} all-to-all(bf16[8,16,1024]{2,1,0:T(8,128)(2,1)S(1)} %bitcast.53), channel_id=1, replica_groups={{0,1,2,3,4,5,6,7},{8,9,10,11,12,13,14,15},{16,17,18,19,20,21,22,23},{24..., dimensions={0} | all-to-all | bytes 524288 | tf_op jit(solution)/shard_map/all_to_all | solution.py:323
  44.8 2.8 %shard_map.80 = (bf16[4,4,16,512]{3,2,1,0:T(8,128)(2,1)S(1)}, bf16[2,2,64,512]{3,2,1,0:T(8,128)(2,1)S(1)}) custom-call(s32[3]{0:T(128)S(1)} %pad_add_fusion.where_ref, bf16[2,4,16,1024]{3,2,1,0:T(8,128)(2,1)S(1)} %bitcast.44, f32[3,1,2048]{2,1,0:T(1,128)S(1)} %get-tuple-element.24.mod_ref, ...), custom_call_target="tpu_custom_call", output_to_operand_aliasing={{1}: (6, {})} | custom-call | tf_op jit(solution)/shard_map/pallas_call | solution.py:367
  47.6 11.5 %all_to_all.53 = bf16[16,16,512]{2,1,0:T(8,128)(2,1)S(1)} all-to-all(bf16[16,16,512]{2,1,0:T(8,128)(2,1)S(1)} %bitcast.57), channel_id=1, replica_groups={{0,1,2,3,4,5,6,7,8,9,10,11,12,13,14,15},{16,17,18,19,20,21,22,23,24,25,..., dimensions={0} | all-to-all | bytes 524288 | tf_op jit(solution)/shard_map/all_to_all | solution.py:323
  59.2 11.8 %all_to_all.54 = bf16[16,16,512]{2,1,0:T(8,128)(2,1)S(1)} all-to-all(bf16[16,16,512]{2,1,0:T(8,128)(2,1)S(1)} %bitcast.61), channel_id=1, replica_groups={{0,1,2,3,4,5,6,7,8,9,10,11,12,13,14,15},{16,17,18,19,20,21,22,23,24,25,..., dimensions={0} | all-to-all | bytes 524288 | tf_op jit(solution)/shard_map/all_to_all | solution.py:323
  71.0 2.8 %shard_map.82 = (bf16[4,4,16,512]{3,2,1,0:T(8,128)(2,1)S(1)}, bf16[2,2,64,512]{3,2,1,0:T(8,128)(2,1)S(1)}) custom-call(s32[3]{0:T(128)S(1)} %pad_add_fusion.where_ref, bf16[4,4,16,512]{3,2,1,0:T(8,128)(2,1)S(1)} %bitcast.45, f32[3,1,2048]{2,1,0:T(1,128)S(1)} %get-tuple-element.24.mod_ref, ...), custom_call_target="tpu_custom_call", output_to_operand_aliasing={{1}: (6, {})} | custom-call | tf_op jit(solution)/shard_map/pallas_call | solution.py:367
  73.8 11.9 %all_to_all.55 = bf16[16,16,512]{2,1,0:T(8,128)(2,1)S(1)} all-to-all(bf16[16,16,512]{2,1,0:T(8,128)(2,1)S(1)} %bitcast.58), channel_id=1, replica_groups={{0,1,2,3,4,5,6,7,8,9,10,11,12,13,14,15},{16,17,18,19,20,21,22,23,24,25,..., dimensions={0} | all-to-all | bytes 524288 | tf_op jit(solution)/shard_map/all_to_all | solution.py:323
  85.8 11.7 %all_to_all.56 = bf16[16,16,512]{2,1,0:T(8,128)(2,1)S(1)} all-to-all(bf16[16,16,512]{2,1,0:T(8,128)(2,1)S(1)} %bitcast.59), channel_id=1, replica_groups={{0,1,2,3,4,5,6,7,8,9,10,11,12,13,14,15},{16,17,18,19,20,21,22,23,24,25,..., dimensions={0} | all-to-all | bytes 524288 | tf_op jit(solution)/shard_map/all_to_all | solution.py:323
  97.5 2.8 %shard_map.84 = (bf16[4,4,16,512]{3,2,1,0:T(8,128)(2,1)S(1)}, bf16[2,2,64,512]{3,2,1,0:T(8,128)(2,1)S(1)}) custom-call(s32[3]{0:T(128)S(1)} %pad_add_fusion.where_ref, bf16[4,4,16,512]{3,2,1,0:T(8,128)(2,1)S(1)} %bitcast.46, f32[3,1,2048]{2,1,0:T(1,128)S(1)} %get-tuple-element.24.mod_ref, ...), custom_call_target="tpu_custom_call", output_to_operand_aliasing={{1}: (6, {})} | custom-call | tf_op jit(solution)/shard_map/pallas_call | solution.py:367
  100.3 13.5 %all_to_all.57 = bf16[16,16,512]{2,1,0:T(8,128)(2,1)S(1)} all-to-all(bf16[16,16,512]{2,1,0:T(8,128)(2,1)S(1)} %bitcast.60), channel_id=1, replica_groups={{0,1,2,3,4,5,6,7,8,9,10,11,12,13,14,15},{16,17,18,19,20,21,22,23,24,25,..., dimensions={0} | all-to-all | bytes 524288 | tf_op jit(solution)/shard_map/all_to_all | solution.py:323
  113.8 12.7 %all_to_all.58 = bf16[16,16,512]{2,1,0:T(8,128)(2,1)S(1)} all-to-all(bf16[16,16,512]{2,1,0:T(8,128)(2,1)S(1)} %bitcast.54), channel_id=1, replica_groups={{0,1,2,3,4,5,6,7,8,9,10,11,12,13,14,15},{16,17,18,19,20,21,22,23,24,25,..., dimensions={0} | all-to-all | bytes 524288 | tf_op jit(solution)/shard_map/all_to_all | solution.py:323
  126.5 2.8 %shard_map.86 = (bf16[2,2,4,16,512]{4,3,2,1,0:T(8,128)(2,1)S(1)}, bf16[2,2,64,512]{3,2,1,0:T(8,128)(2,1)S(1)}) custom-call(s32[3]{0:T(128)S(1)} %pad_add_fusion.where_ref, bf16[4,4,16,512]{3,2,1,0:T(8,128)(2,1)S(1)} %bitcast.43, f32[3,1,2048]{2,1,0:T(1,128)S(1)} %get-tuple-element.24.mod_ref, ...), custom_call_target="tpu_custom_call", output_to_operand_aliasing={{1}: (6, {})} | custom-call | tf_op jit(solution)/shard_map/pallas_call | solution.py:367
  129.4 12.7 %all_to_all.59 = bf16[16,16,512]{2,1,0:T(8,128)(2,1)S(1)} all-to-all(bf16[16,16,512]{2,1,0:T(8,128)(2,1)S(1)} %bitcast.55), channel_id=1, replica_groups={{0,1,2,3,4,5,6,7,16,17,18,19,20,21,22,23},{8,9,10,11,12,13,14,15,24,25,..., dimensions={0} | all-to-all | bytes 524288 | tf_op jit(solution)/shard_map/all_to_all | solution.py:409
  142.0 1.9 %shard_map.87 = (bf16[8,1024]{1,0:T(8,128)(2,1)}, bf16[2,2,64,512]{3,2,1,0:T(8,128)(2,1)}) custom-call(s32[3]{0:T(128)S(1)} %pad_add_fusion.where_ref, bf16[2,2,4,16,512]{4,3,2,1,0:T(8,128)(2,1)S(1)} %bitcast.48, bf16[2,2,64,512]{3,2,1,0:T(8,128)(2,1)S(1)} %get-tuple-element.41.table_ref), custom_call_target="tpu_custom_call" | custom-call | tf_op jit(solution)/shard_map/pallas_call | solution.py:416
  (4 shorter events, 0.1 us)
Async XLA Ops:
  0.6 17.3 %copy-start.1 = (bf16[1,512,2048]{2,1,0:T(8,128)(2,1)S(1)}, bf16[1,512,2048]{2,1,0:T(8,128)(2,1)}, u32[]{:S(2)}) copy-start(bf16[1,512,2048]{2,1,0:T(8,128)(2,1)} %param.9) | copy-start | bytes 6291460
  0.6 17.3 %copy-start = (bf16[1,2048,1536]{2,1,0:T(8,128)(2,1)S(1)}, bf16[1,2048,1536]{2,1,0:T(8,128)(2,1)}, u32[]{:S(2)}) copy-start(bf16[1,2048,1536]{2,1,0:T(8,128)(2,1)} %param.8) | copy-start | bytes 18874372

commit v16 on v15

--- a/solution.py
+++ b/solution.py
@@ -173,19 +173,12 @@
                     closing_ref[branch, patch, piece] = held
 
 
-def start_kernel(where_ref, latent_ref, qkv_ref, out_ref, *refs):
-    del qkv_ref, out_ref
-    loads = (len(refs) - 3) // 2
-    from_refs, to_refs = refs[:loads], refs[loads : 2 * loads]
-    sources_to, spread_to, sems = refs[2 * loads :]
-    half_cols = sources_to.shape[2]
-    own_cols = pl.ds(pl.multiple_of(where_ref[0] % 2 * half_cols, half_cols), half_cols)
-    pairs = [(latent_ref.at[0], spread_to.at[piece]) for piece in range(spread_to.shape[0])]
-    pairs.append((latent_ref.at[:, :, own_cols], sources_to))
-    pairs.extend(zip(from_refs, to_refs))
+def start_kernel(where_ref, latent_ref, *refs):
+    del where_ref
+    spread_to, sems = refs[-2:]
     copies = [
-        pltpu.make_async_copy(from_ref, to_ref, sems.at[at])
-        for at, (from_ref, to_ref) in enumerate(pairs)
+        pltpu.make_async_copy(latent_ref.at[0], spread_to.at[piece], sems.at[piece])
+        for piece in range(spread_to.shape[0])
     ]
     for copy in copies:
         copy.start()
@@ -200,11 +193,18 @@
     return total
 
 
-def settle_first_kernel(parts_ref, sources_ref, spread_to):
-    first = added(parts_ref, 0, sources_ref).astype(jnp.bfloat16)
-    for piece in range(parts_ref.shape[1]):
-        spread_to[0, piece] = sources_ref[1]
-        spread_to[1, piece] = first
+def settle_first_kernel(where_ref, parts_ref, latent_ref, spread_to):
+    first = added(parts_ref, 0)
+    half_cols = first.shape[1]
+    for half in range(2):
+
+        @pl.when(where_ref[0] % 2 == half)
+        def _():
+            at = slice(half * half_cols, (half + 1) * half_cols)
+            held = (first + latent_ref[0, :, at].astype(jnp.float32)).astype(jnp.bfloat16)
+            for piece in range(parts_ref.shape[1]):
+                spread_to[0, piece] = latent_ref[1, :, at]
+                spread_to[1, piece] = held
 
 
 def settle_kernel(parts_ref, *refs):
@@ -332,23 +332,18 @@
     sources = latent.reshape(GROUPS, block_rows, model_width)
     stream_shape = (section_count, block_rows, block_cols)
     spread_shape = (section_count, slice_count, block_rows, block_cols)
-    loads = (
-        modulation.reshape(3, 1, model_width),
-        norm_gain[0],
-        own_cache.reshape(2, GROUPS, rows, local_width),
-    )
-    modulation, norm_gain, table, sources, spread = pl.pallas_call(
+    modulation = modulation.reshape(3, 1, model_width)
+    norm_gain = norm_gain[0]
+    table = own_cache.reshape(2, GROUPS, rows, local_width)
+    named = (sources, qkv_slice, out_slice, modulation, norm_gain, table)
+    spread = pl.pallas_call(
         start_kernel,
-        out_shape=tuple(pltpu.VMEM(value.shape, value.dtype) for value in loads)
-        + (
-            pltpu.VMEM((GROUPS, block_rows, model_width // 2), jnp.bfloat16),
-            jax.ShapeDtypeStruct((slice_count, block_rows, model_width), jnp.bfloat16),
-        ),
-        in_specs=[smem] + [hbm] * (len(loads) + 3),
-        out_specs=(vmem,) * (len(loads) + 2),
-        scratch_shapes=[pltpu.SemaphoreType.DMA((len(loads) + slice_count + 1,))],
+        out_shape=jax.ShapeDtypeStruct((slice_count, block_rows, model_width), jnp.bfloat16),
+        in_specs=[smem] + [hbm] * len(named),
+        out_specs=vmem,
+        scratch_shapes=[pltpu.SemaphoreType.DMA((slice_count,))],
         compiler_params=pltpu.CompilerParams(vmem_limit_bytes=4 * 1024 * 1024),
-    )(where, in_hbm(sources), in_hbm(qkv_slice), in_hbm(out_slice), *map(in_hbm, loads))
+    )(where, *map(in_hbm, named))
     stale_rows = []
     if member_count > 1:
         stale_rows = [group_cache.swapaxes(0, 1).reshape(2, -1, local_width)]
@@ -362,7 +357,7 @@
             in_vmem(out_slice),
             in_vmem(norm_gain),
             *stale_rows,
-            table,
+            in_vmem(table),
         )
         return pl.pallas_call(
             functools.partial(section_kernel, tick, (tok_dev, head_dim)),
@@ -372,7 +367,6 @@
             ),
             in_specs=[smem] + [vmem] * (len(operands) - 1),
             out_specs=(vmem, vmem),
-            input_output_aliases={len(operands) - 1: 1},
             compiler_params=pltpu.CompilerParams(vmem_limit_bytes=24 * 1024 * 1024),
         )(*operands)
 
@@ -391,7 +385,9 @@
     pair_shape = (2, slice_count, block_rows, model_width // 2)
     partial_out, table = attend(0, features, table, pair_shape)
     parts = exchange(partial_out, pair_peers)
-    (spread,) = small(settle_first_kernel, [vmem] * 2, pair_shape)(parts, in_vmem(sources))
+    (spread,) = small(settle_first_kernel, [smem, vmem, vmem], pair_shape)(
+        where, parts, in_vmem(sources)
+    )
     features = exchange(spread, pair_peers)
     streams = []
     for tick in range(1, ticks - 2):

time: 144 us -> 145 us (level)
  no operation moved by 1% of the time
where the time goes in v16:
time: 145 us; the launch traced here: 144 us
  blocking collectives  125 us (86%)
  Pallas kernels  18.3 us (13%)
    all_to_all x8, blocking collectives, exchange(): flat = lax.all_to_all(flat, ('pipe', 'seq'), 0, 0, axis_index_groups=among)  97.2 us
    all_to_all x1, blocking collectives, local(): lax.all_to_all(spread, 'seq', 0, 0, axis_index_groups=in_slices)[None]  15.1 us
    pallas_call x5, Pallas kernels, attend(): pl.pallas_call(functools.partial(section_kernel, tick, (tok_dev, head_dim...  13.9 us
    all_to_all x1, blocking collectives, local(): lax.all_to_all(closing.reshape((-1,) + closing_shape[3:]), ('cfg', 'pipe'...  12.7 us

profile of v16, /device:TPU:0, one launch (start us, length us, event | category | flops | bytes accessed | tf_op | source)
XLA Modules:
  0.0 144.2 jit_solution(9108193463851998762)
XLA Ops:
  0.6 0.0 copy-start.2
  0.6 0.0 copy-start.5
  0.7 0.0 copy-start.1
  0.7 0.0 copy-start.3
  0.7 0.0 copy-start
  0.7 0.1 pad_add_fusion.where_ref
  0.8 1.8 %shard_map.77 = bf16[4,16,2048]{2,1,0:T(8,128)(2,1)S(1)} custom-call(s32[3]{0:T(128)S(1)} %pad_add_fusion.where_ref, bf16[2,16,2048]{2,1,0:T(8,128)(2,1)} %bitcast.63, bf16[2048,1536]{1,0:T(8,128)(2,1)} %bitcast.31, bf16[512,2048]{1,0:T(8,128)(2,1)} %bitcast.37, f32[3,1,2048]{2,1,0:T(1,128)} %bitcast.57, f32[2,128]{1,0:T(2,128)} %bitcast.72, ...), custom_call_target="tpu_custom_call" | custom-call | tf_op jit(solution)/shard_map/pallas_call | solution.py:339
  2.6 0.0 copy-start.4
  2.6 15.1 %all_to_all.50 = bf16[4,16,2048]{2,1,0:T(8,128)(2,1)S(1)} all-to-all(bf16[4,16,2048]{2,1,0:T(8,128)(2,1)S(1)} %shard_map.77), channel_id=1, replica_groups={{0,1,2,3},{4,5,6,7},{8,9,10,11},{12,13,14,15},{16,17,18,19},{20,21,22,2..., dimensions={0} | all-to-all | bytes 524288 | tf_op jit(solution)/shard_map/all_to_all | solution.py:384
  17.8 0.0 copy-done.2
  17.8 0.0 copy-done.5
  17.8 0.0 copy-done.1
  17.8 0.0 copy-done.3
  17.8 0.0 copy-done
  17.8 2.8 %shard_map.78 = (bf16[2,4,16,1024]{3,2,1,0:T(8,128)(2,1)S(1)}, bf16[2,2,64,512]{3,2,1,0:T(8,128)(2,1)S(1)}) custom-call(s32[3]{0:T(128)S(1)} %pad_add_fusion.where_ref, bf16[1,4,16,2048]{3,2,1,0:T(8,128)(2,1)S(1)} %bitcast.49, f32[3,1,2048]{2,1,0:T(1,128)S(1)} %bitcast.58, bf16[2048,1536]{1,0:T(8,128)(2,1)S(1)} %bitcast.32, bf16[512,2048]{1,0:T(8,128)(2,1)S(1)} %bitcast.38, ...), custom_call_target="tpu_custom_call" | custom-call | tf_op jit(solution)/shard_map/pallas_call | solution.py:362
  20.6 13.0 %all_to_all.51 = bf16[8,16,1024]{2,1,0:T(8,128)(2,1)S(1)} all-to-all(bf16[8,16,1024]{2,1,0:T(8,128)(2,1)S(1)} %bitcast.70), channel_id=1, replica_groups={{0,1,2,3,4,5,6,7},{8,9,10,11,12,13,14,15},{16,17,18,19,20,21,22,23},{24..., dimensions={0} | all-to-all | bytes 524288 | tf_op jit(solution)/shard_map/all_to_all | solution.py:323
  33.6 0.0 copy-done.4
  33.6 0.6 shard_map.79
  34.1 11.1 %all_to_all.52 = bf16[8,16,1024]{2,1,0:T(8,128)(2,1)S(1)} all-to-all(bf16[8,16,1024]{2,1,0:T(8,128)(2,1)S(1)} %bitcast.56), channel_id=1, replica_groups={{0,1,2,3,4,5,6,7},{8,9,10,11,12,13,14,15},{16,17,18,19,20,21,22,23},{24..., dimensions={0} | all-to-all | bytes 524288 | tf_op jit(solution)/shard_map/all_to_all | solution.py:323
  45.2 2.8 %shard_map.80 = (bf16[4,4,16,512]{3,2,1,0:T(8,128)(2,1)S(1)}, bf16[2,2,64,512]{3,2,1,0:T(8,128)(2,1)S(1)}) custom-call(s32[3]{0:T(128)S(1)} %pad_add_fusion.where_ref, bf16[2,4,16,1024]{3,2,1,0:T(8,128)(2,1)S(1)} %bitcast.45, f32[3,1,2048]{2,1,0:T(1,128)S(1)} %bitcast.59, bf16[2048,1536]{1,0:T(8,128)(2,1)S(1)} %bitcast.33, bf16[512,2048]{1,0:T(8,128)(2,1)S(1)} %bitcast.39, ...), custom_call_target="tpu_custom_call" | custom-call | tf_op jit(solution)/shard_map/pallas_call | solution.py:362
  48.0 11.5 %all_to_all.53 = bf16[16,16,512]{2,1,0:T(8,128)(2,1)S(1)} all-to-all(bf16[16,16,512]{2,1,0:T(8,128)(2,1)S(1)} %bitcast.65), channel_id=1, replica_groups={{0,1,2,3,4,5,6,7,8,9,10,11,12,13,14,15},{16,17,18,19,20,21,22,23,24,25,..., dimensions={0} | all-to-all | bytes 524288 | tf_op jit(solution)/shard_map/all_to_all | solution.py:323
  59.6 11.8 %all_to_all.54 = bf16[16,16,512]{2,1,0:T(8,128)(2,1)S(1)} all-to-all(bf16[16,16,512]{2,1,0:T(8,128)(2,1)S(1)} %bitcast.71), channel_id=1, replica_groups={{0,1,2,3,4,5,6,7,8,9,10,11,12,13,14,15},{16,17,18,19,20,21,22,23,24,25,..., dimensions={0} | all-to-all | bytes 524288 | tf_op jit(solution)/shard_map/all_to_all | solution.py:323
  71.4 2.8 %shard_map.82 = (bf16[4,4,16,512]{3,2,1,0:T(8,128)(2,1)S(1)}, bf16[2,2,64,512]{3,2,1,0:T(8,128)(2,1)S(1)}) custom-call(s32[3]{0:T(128)S(1)} %pad_add_fusion.where_ref, bf16[4,4,16,512]{3,2,1,0:T(8,128)(2,1)S(1)} %bitcast.46, f32[3,1,2048]{2,1,0:T(1,128)S(1)} %bitcast.60, bf16[2048,1536]{1,0:T(8,128)(2,1)S(1)} %bitcast.34, bf16[512,2048]{1,0:T(8,128)(2,1)S(1)} %bitcast.40, ...), custom_call_target="tpu_custom_call" | custom-call | tf_op jit(solution)/shard_map/pallas_call | solution.py:362
  74.2 11.9 %all_to_all.55 = bf16[16,16,512]{2,1,0:T(8,128)(2,1)S(1)} all-to-all(bf16[16,16,512]{2,1,0:T(8,128)(2,1)S(1)} %bitcast.66), channel_id=1, replica_groups={{0,1,2,3,4,5,6,7,8,9,10,11,12,13,14,15},{16,17,18,19,20,21,22,23,24,25,..., dimensions={0} | all-to-all | bytes 524288 | tf_op jit(solution)/shard_map/all_to_all | solution.py:323
  86.1 11.7 %all_to_all.56 = bf16[16,16,512]{2,1,0:T(8,128)(2,1)S(1)} all-to-all(bf16[16,16,512]{2,1,0:T(8,128)(2,1)S(1)} %bitcast.67), channel_id=1, replica_groups={{0,1,2,3,4,5,6,7,8,9,10,11,12,13,14,15},{16,17,18,19,20,21,22,23,24,25,..., dimensions={0} | all-to-all | bytes 524288 | tf_op jit(solution)/shard_map/all_to_all | solution.py:323
  97.8 2.8 %shard_map.84 = (bf16[4,4,16,512]{3,2,1,0:T(8,128)(2,1)S(1)}, bf16[2,2,64,512]{3,2,1,0:T(8,128)(2,1)S(1)}) custom-call(s32[3]{0:T(128)S(1)} %pad_add_fusion.where_ref, bf16[4,4,16,512]{3,2,1,0:T(8,128)(2,1)S(1)} %bitcast.47, f32[3,1,2048]{2,1,0:T(1,128)S(1)} %bitcast.61, bf16[2048,1536]{1,0:T(8,128)(2,1)S(1)} %bitcast.35, bf16[512,2048]{1,0:T(8,128)(2,1)S(1)} %bitcast.41, ...), custom_call_target="tpu_custom_call" | custom-call | tf_op jit(solution)/shard_map/pallas_call | solution.py:362
  100.6 13.5 %all_to_all.57 = bf16[16,16,512]{2,1,0:T(8,128)(2,1)S(1)} all-to-all(bf16[16,16,512]{2,1,0:T(8,128)(2,1)S(1)} %bitcast.68), channel_id=1, replica_groups={{0,1,2,3,4,5,6,7,8,9,10,11,12,13,14,15},{16,17,18,19,20,21,22,23,24,25,..., dimensions={0} | all-to-all | bytes 524288 | tf_op jit(solution)/shard_map/all_to_all | solution.py:323
  114.2 12.7 %all_to_all.58 = bf16[16,16,512]{2,1,0:T(8,128)(2,1)S(1)} all-to-all(bf16[16,16,512]{2,1,0:T(8,128)(2,1)S(1)} %bitcast.54), channel_id=1, replica_groups={{0,1,2,3,4,5,6,7,8,9,10,11,12,13,14,15},{16,17,18,19,20,21,22,23,24,25,..., dimensions={0} | all-to-all | bytes 524288 | tf_op jit(solution)/shard_map/all_to_all | solution.py:323
  126.9 2.8 %shard_map.86 = (bf16[2,2,4,16,512]{4,3,2,1,0:T(8,128)(2,1)S(1)}, bf16[2,2,64,512]{3,2,1,0:T(8,128)(2,1)S(1)}) custom-call(s32[3]{0:T(128)S(1)} %pad_add_fusion.where_ref, bf16[4,4,16,512]{3,2,1,0:T(8,128)(2,1)S(1)} %bitcast.48, f32[3,1,2048]{2,1,0:T(1,128)S(1)} %bitcast.62, bf16[2048,1536]{1,0:T(8,128)(2,1)S(1)} %bitcast.36, ...), custom_call_target="tpu_custom_call" | custom-call | tf_op jit(solution)/shard_map/pallas_call | solution.py:362
  129.7 12.7 %all_to_all.59 = bf16[16,16,512]{2,1,0:T(8,128)(2,1)S(1)} all-to-all(bf16[16,16,512]{2,1,0:T(8,128)(2,1)S(1)} %bitcast.69), channel_id=1, replica_groups={{0,1,2,3,4,5,6,7,16,17,18,19,20,21,22,23},{8,9,10,11,12,13,14,15,24,25,..., dimensions={0} | all-to-all | bytes 524288 | tf_op jit(solution)/shard_map/all_to_all | solution.py:405
  142.3 1.9 %shard_map.87 = (bf16[8,1024]{1,0:T(8,128)(2,1)}, bf16[2,2,64,512]{3,2,1,0:T(8,128)(2,1)}) custom-call(s32[3]{0:T(128)S(1)} %pad_add_fusion.where_ref, bf16[2,2,4,16,512]{4,3,2,1,0:T(8,128)(2,1)S(1)} %bitcast.50, bf16[2,2,64,512]{3,2,1,0:T(8,128)(2,1)S(1)} %get-tuple-element.31.table_ref), custom_call_target="tpu_custom_call" | custom-call | tf_op jit(solution)/shard_map/pallas_call | solution.py:412
  (3 shorter events, 0.1 us)
Async XLA Ops:
  0.6 17.1 %copy-start.2 = (bf16[1,1,2,4,1,4,8,512]{7,6,5,4,3,2,1,0:T(8,128)(2,1)S(1)}, bf16[1,1,2,4,1,4,8,512]{7,6,5,4,3,2,1,0:T(8,128)(2,1)}, u32[]{:S(2)}) copy-start(bf16[1,1,2,4,1,4,8,512]{7,6,5,4,3,2,1,0:T(8,128)(2,1)} %param.11) | copy-start | bytes 786436
  0.6 17.1 %copy-start.5 = (f32[1,2,128]{2,1,0:T(2,128)S(1)}, f32[1,2,128]{2,1,0:T(2,128)}, u32[]{:S(2)}) copy-start(f32[1,2,128]{2,1,0:T(2,128)} %param.10) | copy-start | bytes 3076
  0.7 17.1 %copy-start.1 = (bf16[1,512,2048]{2,1,0:T(8,128)(2,1)S(1)}, bf16[1,512,2048]{2,1,0:T(8,128)(2,1)}, u32[]{:S(2)}) copy-start(bf16[1,512,2048]{2,1,0:T(8,128)(2,1)} %param.9) | copy-start | bytes 6291460
  0.7 17.1 %copy-start.3 = (f32[1,1,3,2048]{3,1,2,0:T(1,128)S(1)}, f32[1,1,3,2048]{3,1,2,0:T(1,128)}, u32[]{:S(2)}) copy-start(f32[1,1,3,2048]{3,1,2,0:T(1,128)} %param.7) | copy-start | bytes 73732
  0.7 17.1 %copy-start = (bf16[1,2048,1536]{2,1,0:T(8,128)(2,1)S(1)}, bf16[1,2048,1536]{2,1,0:T(8,128)(2,1)}, u32[]{:S(2)}) copy-start(bf16[1,2048,1536]{2,1,0:T(8,128)(2,1)} %param.8) | copy-start | bytes 18874372
  2.6 30.9 %copy-start.4 = (bf16[4,8,2048]{2,1,0:T(8,128)(2,1)S(1)}, bf16[4,8,2048]{2,1,0:T(8,128)(2,1)}, u32[]{:S(2)}) copy-start(bf16[4,8,2048]{2,1,0:T(8,128)(2,1)} %param.6) | copy-start | bytes 393220

commit v17 on v16

--- a/solution.py
+++ b/solution.py
@@ -31,11 +31,16 @@
     )
 
 
-def section_kernel(tick, sizes, where_ref, rows_ref, mod_ref, qkv_ref, out_ref, gain_ref, *refs):
+def position(members):
+    rank = lax.axis_index("seq")
+    return lax.axis_index("pipe"), rank % members, rank // members
+
+
+def section_kernel(tick, sizes, rows_ref, mod_ref, qkv_ref, out_ref, gain_ref, *refs):
     *stale_refs, old_table_ref, partial_ref, table_ref = refs
     closing = len(partial_ref.shape) == 5
     folding = tick == 1
-    tok_dev, head_dim = sizes
+    tok_dev, head_dim, members = sizes
     blocks, slices, block_rows, block_cols = rows_ref.shape
     rows = slices * block_rows
     width = blocks * block_cols
@@ -43,7 +48,7 @@
     group_rows = slices * tok_dev
     groups, local_width = table_ref.shape[1], table_ref.shape[3]
     heads = local_width // head_dim
-    section, own_member, own_slice = where_ref[0], where_ref[1], where_ref[2]
+    section, own_member, own_slice = position(members)
     group = tick - section
     parts = [rows_ref[q].reshape(rows, block_cols).astype(jnp.float32) for q in range(blocks)]
     mean = jnp.sum(sum(parts), axis=-1, keepdims=True) * (1.0 / width)
@@ -173,17 +178,10 @@
                     closing_ref[branch, patch, piece] = held
 
 
-def start_kernel(where_ref, latent_ref, *refs):
-    del where_ref
-    spread_to, sems = refs[-2:]
-    copies = [
-        pltpu.make_async_copy(latent_ref.at[0], spread_to.at[piece], sems.at[piece])
-        for piece in range(spread_to.shape[0])
-    ]
-    for copy in copies:
-        copy.start()
-    for copy in copies:
-        copy.wait()
+def start_kernel(latent_ref, *refs):
+    spread_to = refs[-1]
+    for piece in range(spread_to.shape[0]):
+        spread_to[piece] = latent_ref[0]
 
 
 def added(parts_ref, section, *streams_refs):
@@ -193,12 +191,12 @@
     return total
 
 
-def settle_first_kernel(where_ref, parts_ref, latent_ref, spread_to):
+def settle_first_kernel(parts_ref, latent_ref, spread_to):
     first = added(parts_ref, 0)
     half_cols = first.shape[1]
     for half in range(2):
 
-        @pl.when(where_ref[0] % 2 == half)
+        @pl.when(lax.axis_index("pipe") % 2 == half)
         def _():
             at = slice(half * half_cols, (half + 1) * half_cols)
             held = (first + latent_ref[0, :, at].astype(jnp.float32)).astype(jnp.bfloat16)
@@ -231,12 +229,12 @@
             spread_to[section, piece] = held
 
 
-def guide_kernel(where_ref, closing_ref, table_ref, guided_ref, table_to, sem):
+def guide_kernel(members, closing_ref, table_ref, guided_ref, table_to, sem):
     copy = pltpu.make_async_copy(table_ref, table_to, sem)
     copy.start()
     branches, patches, slices, block_rows, block_cols = closing_ref.shape
     tok_dev = guided_ref.shape[0]
-    section, own_slice = where_ref[0], where_ref[2]
+    section, _, own_slice = position(members)
 
     def combine(pair):
         conditional, unconditional = pair
@@ -269,7 +267,6 @@
     seq_count = lax.axis_size("seq")
     seq_rank = lax.axis_index("seq")
     section_count = lax.axis_size("pipe")
-    section_rank = lax.axis_index("pipe")
     patches, tok_dev, model_width = latent.shape
     head_dim = norm_gain.shape[2]
     slice_count = min(seq_count, 8)
@@ -324,33 +321,29 @@
         return flat.reshape(value.shape)
 
     vmem = pl.BlockSpec(memory_space=pltpu.VMEM)
-    smem = pl.BlockSpec(memory_space=pltpu.SMEM)
     hbm = pl.BlockSpec(memory_space=pltpu.HBM)
     in_hbm = functools.partial(pltpu.with_memory_space_constraint, memory_space=pltpu.HBM)
     in_vmem = functools.partial(pltpu.with_memory_space_constraint, memory_space=pltpu.VMEM)
-    where = jnp.stack((section_rank, own_member, seq_rank // member_count)).astype(jnp.int32)
     sources = latent.reshape(GROUPS, block_rows, model_width)
     stream_shape = (section_count, block_rows, block_cols)
     spread_shape = (section_count, slice_count, block_rows, block_cols)
     modulation = modulation.reshape(3, 1, model_width)
     norm_gain = norm_gain[0]
     table = own_cache.reshape(2, GROUPS, rows, local_width)
-    named = (sources, qkv_slice, out_slice, modulation, norm_gain, table)
+    named = (qkv_slice, out_slice, modulation, norm_gain, table)
     spread = pl.pallas_call(
         start_kernel,
         out_shape=jax.ShapeDtypeStruct((slice_count, block_rows, model_width), jnp.bfloat16),
-        in_specs=[smem] + [hbm] * len(named),
+        in_specs=[vmem] + [hbm] * len(named),
         out_specs=vmem,
-        scratch_shapes=[pltpu.SemaphoreType.DMA((slice_count,))],
         compiler_params=pltpu.CompilerParams(vmem_limit_bytes=4 * 1024 * 1024),
-    )(where, *map(in_hbm, named))
+    )(in_vmem(sources), *map(in_hbm, named))
     stale_rows = []
     if member_count > 1:
         stale_rows = [group_cache.swapaxes(0, 1).reshape(2, -1, local_width)]
 
     def attend(tick, features, table, partial_shape):
         operands = (
-            where,
             features,
             in_vmem(modulation),
             in_vmem(qkv_slice),
@@ -360,12 +353,12 @@
             in_vmem(table),
         )
         return pl.pallas_call(
-            functools.partial(section_kernel, tick, (tok_dev, head_dim)),
+            functools.partial(section_kernel, tick, (tok_dev, head_dim, member_count)),
             out_shape=(
                 jax.ShapeDtypeStruct(partial_shape, jnp.bfloat16),
                 jax.ShapeDtypeStruct(table.shape, jnp.bfloat16),
             ),
-            in_specs=[smem] + [vmem] * (len(operands) - 1),
+            in_specs=[vmem] * len(operands),
             out_specs=(vmem, vmem),
             compiler_params=pltpu.CompilerParams(vmem_limit_bytes=24 * 1024 * 1024),
         )(*operands)
@@ -385,9 +378,7 @@
     pair_shape = (2, slice_count, block_rows, model_width // 2)
     partial_out, table = attend(0, features, table, pair_shape)
     parts = exchange(partial_out, pair_peers)
-    (spread,) = small(settle_first_kernel, [smem, vmem, vmem], pair_shape)(
-        where, parts, in_vmem(sources)
-    )
+    (spread,) = small(settle_first_kernel, [vmem] * 2, pair_shape)(parts, in_vmem(sources))
     features = exchange(spread, pair_peers)
     streams = []
     for tick in range(1, ticks - 2):
@@ -410,16 +401,16 @@
         axis_index_groups=closing_peers,
     ).reshape(closing_shape)
     guided, table = pl.pallas_call(
-        guide_kernel,
+        functools.partial(guide_kernel, member_count),
         out_shape=(
             jax.ShapeDtypeStruct((tok_dev, model_width // 2), jnp.bfloat16),
             jax.ShapeDtypeStruct(table.shape, jnp.bfloat16),
         ),
-        in_specs=[smem, vmem, vmem],
+        in_specs=[vmem, vmem],
         out_specs=(vmem, hbm),
         scratch_shapes=[pltpu.SemaphoreType.DMA],
         compiler_params=pltpu.CompilerParams(vmem_limit_bytes=8 * 1024 * 1024),
-    )(where, closing, table)
+    )(closing, table)
     return (guided[None], table.reshape(stale_kv.shape))
 
 

time: 145 us -> 140 us (0.966)
  Pallas kernels: 18.3 us -> 12.8 us
    pallas_call x5, Pallas kernels: 13.9 us -> 11.4 us  [attend(): pl.pallas_call(functools.partial(section_kernel, tick, (tok_dev, head_dim...]
    pallas_call x1, Pallas kernels: 1.85 us -> 0.02 us  [local(): pl.pallas_call(start_kernel, out_shape=jax.ShapeDtypeStruct((slice_count,...]
where the time goes in v17:
time: 140 us
  blocking collectives  125 us (89%)
  Pallas kernels  12.8 us (9%)
    all_to_all x8, blocking collectives, exchange(): flat = lax.all_to_all(flat, ('pipe', 'seq'), 0, 0, axis_index_groups=among)  97.2 us
    all_to_all x1, blocking collectives, local(): lax.all_to_all(spread, 'seq', 0, 0, axis_index_groups=in_slices)[None]  15.3 us
    all_to_all x1, blocking collectives, local(): lax.all_to_all(closing.reshape((-1,) + closing_shape[3:]), ('cfg', 'pipe'...  12.7 us
    pallas_call x5, Pallas kernels, attend(): pl.pallas_call(functools.partial(section_kernel, tick, (tok_dev, head_dim...  11.4 us

profile of v17, /device:TPU:0, one launch (start us, length us, event | category | flops | bytes accessed | tf_op | source)
XLA Modules:
  0.0 139.8 jit_solution(4393607154339328867)
XLA Ops:
  0.6 0.0 copy-start.2
  0.6 0.0 copy-start.1
  0.7 0.0 copy-start
  0.7 0.0 copy-start.3
  0.7 0.0 copy-start.4
  0.7 1.0 copy-done.4
  1.7 0.0 copy-start.6
  1.8 0.0 copy-start.5
  1.8 15.3 %all_to_all.50 = bf16[4,16,2048]{2,1,0:T(8,128)(2,1)S(1)} all-to-all(bf16[4,16,2048]{2,1,0:T(8,128)(2,1)S(1)} %shard_map.77), channel_id=1, replica_groups={{0,1,2,3},{4,5,6,7},{8,9,10,11},{12,13,14,15},{16,17,18,19},{20,21,22,2..., dimensions={0} | all-to-all | bytes 524288 | tf_op jit(solution)/shard_map/all_to_all | solution.py:377
  17.0 0.0 copy-done.2
  17.0 0.0 copy-done.1
  17.0 0.0 copy-done
  17.0 0.0 copy-done.3
  17.0 0.0 copy-done.6
  17.0 2.3 %shard_map.78 = (bf16[2,4,16,1024]{3,2,1,0:T(8,128)(2,1)S(1)}, bf16[2,2,64,512]{3,2,1,0:T(8,128)(2,1)S(1)}) custom-call(bf16[1,4,16,2048]{3,2,1,0:T(8,128)(2,1)S(1)} %bitcast.47, f32[3,1,2048]{2,1,0:T(1,128)S(1)} %bitcast.56, bf16[2048,1536]{1,0:T(8,128)(2,1)S(1)} %bitcast.30, bf16[512,2048]{1,0:T(8,128)(2,1)S(1)} %bitcast.36, f32[2,128]{1,0:T(2,128)S(1)} %bitcast.71, ...), custom_call_target="tpu_custom_call" | custom-call | tf_op jit(solution)/shard_map/pallas_call | solution.py:355
  19.3 13.0 %all_to_all.51 = bf16[8,16,1024]{2,1,0:T(8,128)(2,1)S(1)} all-to-all(bf16[8,16,1024]{2,1,0:T(8,128)(2,1)S(1)} %bitcast.68), channel_id=1, replica_groups={{0,1,2,3,4,5,6,7},{8,9,10,11,12,13,14,15},{16,17,18,19,20,21,22,23},{24..., dimensions={0} | all-to-all | bytes 524288 | tf_op jit(solution)/shard_map/all_to_all | solution.py:320
  32.3 0.0 copy-done.5
  32.3 11.1 %all_to_all.52 = bf16[8,16,1024]{2,1,0:T(8,128)(2,1)S(1)} all-to-all(bf16[8,16,1024]{2,1,0:T(8,128)(2,1)S(1)} %bitcast.54), channel_id=1, replica_groups={{0,1,2,3,4,5,6,7},{8,9,10,11,12,13,14,15},{16,17,18,19,20,21,22,23},{24..., dimensions={0} | all-to-all | bytes 524288 | tf_op jit(solution)/shard_map/all_to_all | solution.py:320
  43.4 2.3 %shard_map.80 = (bf16[4,4,16,512]{3,2,1,0:T(8,128)(2,1)S(1)}, bf16[2,2,64,512]{3,2,1,0:T(8,128)(2,1)S(1)}) custom-call(bf16[2,4,16,1024]{3,2,1,0:T(8,128)(2,1)S(1)} %bitcast.43, f32[3,1,2048]{2,1,0:T(1,128)S(1)} %bitcast.57, bf16[2048,1536]{1,0:T(8,128)(2,1)S(1)} %bitcast.31, bf16[512,2048]{1,0:T(8,128)(2,1)S(1)} %bitcast.37, f32[2,128]{1,0:T(2,128)S(1)} %bitcast.72, ...), custom_call_target="tpu_custom_call" | custom-call | tf_op jit(solution)/shard_map/pallas_call | solution.py:355
  45.7 11.5 %all_to_all.53 = bf16[16,16,512]{2,1,0:T(8,128)(2,1)S(1)} all-to-all(bf16[16,16,512]{2,1,0:T(8,128)(2,1)S(1)} %bitcast.63), channel_id=1, replica_groups={{0,1,2,3,4,5,6,7,8,9,10,11,12,13,14,15},{16,17,18,19,20,21,22,23,24,25,..., dimensions={0} | all-to-all | bytes 524288 | tf_op jit(solution)/shard_map/all_to_all | solution.py:320
  57.2 11.8 %all_to_all.54 = bf16[16,16,512]{2,1,0:T(8,128)(2,1)S(1)} all-to-all(bf16[16,16,512]{2,1,0:T(8,128)(2,1)S(1)} %bitcast.69), channel_id=1, replica_groups={{0,1,2,3,4,5,6,7,8,9,10,11,12,13,14,15},{16,17,18,19,20,21,22,23,24,25,..., dimensions={0} | all-to-all | bytes 524288 | tf_op jit(solution)/shard_map/all_to_all | solution.py:320
  69.0 2.3 %shard_map.82 = (bf16[4,4,16,512]{3,2,1,0:T(8,128)(2,1)S(1)}, bf16[2,2,64,512]{3,2,1,0:T(8,128)(2,1)S(1)}) custom-call(bf16[4,4,16,512]{3,2,1,0:T(8,128)(2,1)S(1)} %bitcast.44, f32[3,1,2048]{2,1,0:T(1,128)S(1)} %bitcast.58, bf16[2048,1536]{1,0:T(8,128)(2,1)S(1)} %bitcast.32, bf16[512,2048]{1,0:T(8,128)(2,1)S(1)} %bitcast.38, f32[2,128]{1,0:T(2,128)S(1)} %bitcast.73, ...), custom_call_target="tpu_custom_call" | custom-call | tf_op jit(solution)/shard_map/pallas_call | solution.py:355
  71.3 11.9 %all_to_all.55 = bf16[16,16,512]{2,1,0:T(8,128)(2,1)S(1)} all-to-all(bf16[16,16,512]{2,1,0:T(8,128)(2,1)S(1)} %bitcast.64), channel_id=1, replica_groups={{0,1,2,3,4,5,6,7,8,9,10,11,12,13,14,15},{16,17,18,19,20,21,22,23,24,25,..., dimensions={0} | all-to-all | bytes 524288 | tf_op jit(solution)/shard_map/all_to_all | solution.py:320
  83.3 11.7 %all_to_all.56 = bf16[16,16,512]{2,1,0:T(8,128)(2,1)S(1)} all-to-all(bf16[16,16,512]{2,1,0:T(8,128)(2,1)S(1)} %bitcast.65), channel_id=1, replica_groups={{0,1,2,3,4,5,6,7,8,9,10,11,12,13,14,15},{16,17,18,19,20,21,22,23,24,25,..., dimensions={0} | all-to-all | bytes 524288 | tf_op jit(solution)/shard_map/all_to_all | solution.py:320
  95.0 2.3 %shard_map.84 = (bf16[4,4,16,512]{3,2,1,0:T(8,128)(2,1)S(1)}, bf16[2,2,64,512]{3,2,1,0:T(8,128)(2,1)S(1)}) custom-call(bf16[4,4,16,512]{3,2,1,0:T(8,128)(2,1)S(1)} %bitcast.45, f32[3,1,2048]{2,1,0:T(1,128)S(1)} %bitcast.59, bf16[2048,1536]{1,0:T(8,128)(2,1)S(1)} %bitcast.33, bf16[512,2048]{1,0:T(8,128)(2,1)S(1)} %bitcast.39, f32[2,128]{1,0:T(2,128)S(1)} %bitcast.74, ...), custom_call_target="tpu_custom_call" | custom-call | tf_op jit(solution)/shard_map/pallas_call | solution.py:355
  97.3 13.5 %all_to_all.57 = bf16[16,16,512]{2,1,0:T(8,128)(2,1)S(1)} all-to-all(bf16[16,16,512]{2,1,0:T(8,128)(2,1)S(1)} %bitcast.66), channel_id=1, replica_groups={{0,1,2,3,4,5,6,7,8,9,10,11,12,13,14,15},{16,17,18,19,20,21,22,23,24,25,..., dimensions={0} | all-to-all | bytes 524288 | tf_op jit(solution)/shard_map/all_to_all | solution.py:320
  110.8 12.7 %all_to_all.58 = bf16[16,16,512]{2,1,0:T(8,128)(2,1)S(1)} all-to-all(bf16[16,16,512]{2,1,0:T(8,128)(2,1)S(1)} %bitcast.52), channel_id=1, replica_groups={{0,1,2,3,4,5,6,7,8,9,10,11,12,13,14,15},{16,17,18,19,20,21,22,23,24,25,..., dimensions={0} | all-to-all | bytes 524288 | tf_op jit(solution)/shard_map/all_to_all | solution.py:320
  123.5 2.3 %shard_map.86 = (bf16[2,2,4,16,512]{4,3,2,1,0:T(8,128)(2,1)S(1)}, bf16[2,2,64,512]{3,2,1,0:T(8,128)(2,1)S(1)}) custom-call(bf16[4,4,16,512]{3,2,1,0:T(8,128)(2,1)S(1)} %bitcast.46, f32[3,1,2048]{2,1,0:T(1,128)S(1)} %bitcast.60, bf16[2048,1536]{1,0:T(8,128)(2,1)S(1)} %bitcast.34, bf16[512,2048]{1,0:T(8,128)(2,1)S(1)} %bitcast.40, f32[2,128]{1,0:T(2,128)S(1)} %bitcast.75, ...), custom_call_target="tpu_custom_call" | custom-call | tf_op jit(solution)/shard_map/pallas_call | solution.py:355
  125.8 12.7 %all_to_all.59 = bf16[16,16,512]{2,1,0:T(8,128)(2,1)S(1)} all-to-all(bf16[16,16,512]{2,1,0:T(8,128)(2,1)S(1)} %bitcast.67), channel_id=1, replica_groups={{0,1,2,3,4,5,6,7,16,17,18,19,20,21,22,23},{8,9,10,11,12,13,14,15,24,25,..., dimensions={0} | all-to-all | bytes 524288 | tf_op jit(solution)/shard_map/all_to_all | solution.py:396
  138.5 1.3 shard_map.87
  (5 shorter events, 0.1 us)
Async XLA Ops:
  0.6 16.4 %copy-start.2 = (bf16[1,1,2,4,1,4,8,512]{7,6,5,4,3,2,1,0:T(8,128)(2,1)S(1)}, bf16[1,1,2,4,1,4,8,512]{7,6,5,4,3,2,1,0:T(8,128)(2,1)}, u32[]{:S(2)}) copy-start(bf16[1,1,2,4,1,4,8,512]{7,6,5,4,3,2,1,0:T(8,128)(2,1)} %param.11) | copy-start | bytes 786436
  0.6 16.4 %copy-start.1 = (bf16[1,512,2048]{2,1,0:T(8,128)(2,1)S(1)}, bf16[1,512,2048]{2,1,0:T(8,128)(2,1)}, u32[]{:S(2)}) copy-start(bf16[1,512,2048]{2,1,0:T(8,128)(2,1)} %param.9) | copy-start | bytes 6291460
  0.7 16.4 %copy-start = (bf16[1,2048,1536]{2,1,0:T(8,128)(2,1)S(1)}, bf16[1,2048,1536]{2,1,0:T(8,128)(2,1)}, u32[]{:S(2)}) copy-start(bf16[1,2048,1536]{2,1,0:T(8,128)(2,1)} %param.8) | copy-start | bytes 18874372
  0.7 16.4 %copy-start.3 = (f32[1,1,3,2048]{3,1,2,0:T(1,128)S(1)}, f32[1,1,3,2048]{3,1,2,0:T(1,128)}, u32[]{:S(2)}) copy-start(f32[1,1,3,2048]{3,1,2,0:T(1,128)} %param.7) | copy-start | bytes 73732
  0.7 1.1 copy-start.4
  1.7 15.3 %copy-start.6 = (f32[1,2,128]{2,1,0:T(2,128)S(1)}, f32[1,2,128]{2,1,0:T(2,128)}, u32[]{:S(2)}) copy-start(f32[1,2,128]{2,1,0:T(2,128)} %param.10) | copy-start | bytes 3076
  1.8 30.5 %copy-start.5 = (bf16[4,8,2048]{2,1,0:T(8,128)(2,1)S(1)}, bf16[4,8,2048]{2,1,0:T(8,128)(2,1)}, u32[]{:S(2)}) copy-start(bf16[4,8,2048]{2,1,0:T(8,128)(2,1)} %param.6) | copy-start | bytes 393220

commit v18 on v17

--- a/solution.py
+++ b/solution.py
@@ -131,17 +131,10 @@
             piece = projected[:, q * out_cols : (q + 1) * out_cols].astype(jnp.bfloat16)
             partial_ref[q] = piece.reshape(slices, block_rows, out_cols)
 
-    for at in range(groups):
-
-        @pl.when(group == at)
-        def _():
-            for j in range(2):
-                table_ref[j, at] = jnp.concatenate([fresh[j][head] for head in range(heads)], axis=1)
-
-        @pl.when(group != at)
-        def _():
-            for j in range(2):
-                table_ref[j, at] = old_table_ref[j, at]
+    for kind in range(2):
+        rows_of = jnp.concatenate([fresh[kind][head] for head in range(heads)], axis=1)
+        for at in range(groups):
+            table_ref[kind, at] = jnp.where(group == at, rows_of, old_table_ref[kind, at])
 
 
 def close_into(closing_ref, projected, rows_ref, section, own_slice, in_group):
@@ -180,8 +173,15 @@
 
 def start_kernel(latent_ref, *refs):
     spread_to = refs[-1]
-    for piece in range(spread_to.shape[0]):
-        spread_to[piece] = latent_ref[0]
+    half_cols = spread_to.shape[3]
+    for half in range(2):
+
+        @pl.when(lax.axis_index("pipe") % 2 == half)
+        def _():
+            held = latent_ref[0, :, half * half_cols : (half + 1) * half_cols]
+            for line in range(2):
+                for piece in range(spread_to.shape[1]):
+                    spread_to[line, piece] = held
 
 
 def added(parts_ref, section, *streams_refs):
@@ -327,13 +327,14 @@
     sources = latent.reshape(GROUPS, block_rows, model_width)
     stream_shape = (section_count, block_rows, block_cols)
     spread_shape = (section_count, slice_count, block_rows, block_cols)
+    pair_shape = (2, slice_count, block_rows, model_width // 2)
     modulation = modulation.reshape(3, 1, model_width)
     norm_gain = norm_gain[0]
     table = own_cache.reshape(2, GROUPS, rows, local_width)
     named = (qkv_slice, out_slice, modulation, norm_gain, table)
     spread = pl.pallas_call(
         start_kernel,
-        out_shape=jax.ShapeDtypeStruct((slice_count, block_rows, model_width), jnp.bfloat16),
+        out_shape=jax.ShapeDtypeStruct(pair_shape, jnp.bfloat16),
         in_specs=[vmem] + [hbm] * len(named),
         out_specs=vmem,
         compiler_params=pltpu.CompilerParams(vmem_limit_bytes=4 * 1024 * 1024),
@@ -374,8 +375,7 @@
 
     ticks = GROUPS + section_count - 1
     closing_shape = (2, half, slice_count, block_rows, block_cols)
-    features = lax.all_to_all(spread, "seq", 0, 0, axis_index_groups=in_slices)[None]
-    pair_shape = (2, slice_count, block_rows, model_width // 2)
+    features = exchange(spread, pair_peers)
     partial_out, table = attend(0, features, table, pair_shape)
     parts = exchange(partial_out, pair_peers)
     (spread,) = small(settle_first_kernel, [vmem] * 2, pair_shape)(parts, in_vmem(sources))

time: 140 us -> 141 us (level)
    all_to_all x8 -> x9, blocking collectives: 97.2 us -> 113 us  [exchange(): flat = lax.all_to_all(flat, ('pipe', 'seq'), 0, 0, axis_index_groups=among)]
    all_to_all x1 -> x0, blocking collectives: 15.3 us -> none  [local(): lax.all_to_all(spread, 'seq', 0, 0, axis_index_groups=in_slices)[None]]
where the time goes in v18:
time: 141 us; the launch traced here: 140 us
  blocking collectives  126 us (89%)
  Pallas kernels  12.7 us (9%)
    all_to_all x9, blocking collectives, exchange(): flat = lax.all_to_all(flat, ('pipe', 'seq'), 0, 0, axis_index_groups=among)  113 us
    all_to_all x1, blocking collectives, local(): lax.all_to_all(closing.reshape((-1,) + closing_shape[3:]), ('cfg', 'pipe'...  12.7 us
    pallas_call x5, Pallas kernels, attend(): pl.pallas_call(functools.partial(section_kernel, tick, (tok_dev, head_dim...  11.3 us

profile of v18, /device:TPU:0, one launch (start us, length us, event | category | flops | bytes accessed | tf_op | source)
XLA Modules:
  0.0 140.4 jit_solution(13819903507329008572)
XLA Ops:
  0.6 0.0 copy-start.2
  0.6 0.0 copy-start.1
  0.7 0.0 copy-start
  0.7 0.0 copy-start.3
  0.7 0.0 copy-start.4
  0.7 1.0 copy-done.4
  1.7 0.0 copy-start.6
  1.8 0.0 copy-start.5
  1.8 17.1 %all_to_all.50 = bf16[8,16,1024]{2,1,0:T(8,128)(2,1)S(1)} all-to-all(bf16[8,16,1024]{2,1,0:T(8,128)(2,1)S(1)} %bitcast.49), channel_id=1, replica_groups={{0,1,2,3,4,5,6,7},{8,9,10,11,12,13,14,15},{16,17,18,19,20,21,22,23},{24..., dimensions={0} | all-to-all | bytes 524288 | tf_op jit(solution)/shard_map/all_to_all | solution.py:320
  18.9 0.0 copy-done.2
  18.9 0.0 copy-done.1
  18.9 0.0 copy-done
  18.9 0.0 copy-done.3
  18.9 0.0 copy-done.6
  18.9 2.3 %shard_map.78 = (bf16[2,4,16,1024]{3,2,1,0:T(8,128)(2,1)S(1)}, bf16[2,2,64,512]{3,2,1,0:T(8,128)(2,1)S(1)}) custom-call(bf16[2,4,16,1024]{3,2,1,0:T(8,128)(2,1)S(1)} %bitcast.48, f32[3,1,2048]{2,1,0:T(1,128)S(1)} %bitcast.58, bf16[2048,1536]{1,0:T(8,128)(2,1)S(1)} %bitcast.31, bf16[512,2048]{1,0:T(8,128)(2,1)S(1)} %bitcast.37, f32[2,128]{1,0:T(2,128)S(1)} %bitcast.73, ...), custom_call_target="tpu_custom_call" | custom-call | tf_op jit(solution)/shard_map/pallas_call | solution.py:356
  21.1 11.8 %all_to_all.51 = bf16[8,16,1024]{2,1,0:T(8,128)(2,1)S(1)} all-to-all(bf16[8,16,1024]{2,1,0:T(8,128)(2,1)S(1)} %bitcast.70), channel_id=1, replica_groups={{0,1,2,3,4,5,6,7},{8,9,10,11,12,13,14,15},{16,17,18,19,20,21,22,23},{24..., dimensions={0} | all-to-all | bytes 524288 | tf_op jit(solution)/shard_map/all_to_all | solution.py:320
  33.0 0.0 copy-done.5
  33.0 11.0 %all_to_all.52 = bf16[8,16,1024]{2,1,0:T(8,128)(2,1)S(1)} all-to-all(bf16[8,16,1024]{2,1,0:T(8,128)(2,1)S(1)} %bitcast.56), channel_id=1, replica_groups={{0,1,2,3,4,5,6,7},{8,9,10,11,12,13,14,15},{16,17,18,19,20,21,22,23},{24..., dimensions={0} | all-to-all | bytes 524288 | tf_op jit(solution)/shard_map/all_to_all | solution.py:320
  44.0 2.2 %shard_map.80 = (bf16[4,4,16,512]{3,2,1,0:T(8,128)(2,1)S(1)}, bf16[2,2,64,512]{3,2,1,0:T(8,128)(2,1)S(1)}) custom-call(bf16[2,4,16,1024]{3,2,1,0:T(8,128)(2,1)S(1)} %bitcast.44, f32[3,1,2048]{2,1,0:T(1,128)S(1)} %bitcast.59, bf16[2048,1536]{1,0:T(8,128)(2,1)S(1)} %bitcast.32, bf16[512,2048]{1,0:T(8,128)(2,1)S(1)} %bitcast.38, f32[2,128]{1,0:T(2,128)S(1)} %bitcast.74, ...), custom_call_target="tpu_custom_call" | custom-call | tf_op jit(solution)/shard_map/pallas_call | solution.py:356
  46.3 11.5 %all_to_all.53 = bf16[16,16,512]{2,1,0:T(8,128)(2,1)S(1)} all-to-all(bf16[16,16,512]{2,1,0:T(8,128)(2,1)S(1)} %bitcast.65), channel_id=1, replica_groups={{0,1,2,3,4,5,6,7,8,9,10,11,12,13,14,15},{16,17,18,19,20,21,22,23,24,25,..., dimensions={0} | all-to-all | bytes 524288 | tf_op jit(solution)/shard_map/all_to_all | solution.py:320
  57.8 11.8 %all_to_all.54 = bf16[16,16,512]{2,1,0:T(8,128)(2,1)S(1)} all-to-all(bf16[16,16,512]{2,1,0:T(8,128)(2,1)S(1)} %bitcast.71), channel_id=1, replica_groups={{0,1,2,3,4,5,6,7,8,9,10,11,12,13,14,15},{16,17,18,19,20,21,22,23,24,25,..., dimensions={0} | all-to-all | bytes 524288 | tf_op jit(solution)/shard_map/all_to_all | solution.py:320
  69.7 2.2 %shard_map.82 = (bf16[4,4,16,512]{3,2,1,0:T(8,128)(2,1)S(1)}, bf16[2,2,64,512]{3,2,1,0:T(8,128)(2,1)S(1)}) custom-call(bf16[4,4,16,512]{3,2,1,0:T(8,128)(2,1)S(1)} %bitcast.45, f32[3,1,2048]{2,1,0:T(1,128)S(1)} %bitcast.60, bf16[2048,1536]{1,0:T(8,128)(2,1)S(1)} %bitcast.33, bf16[512,2048]{1,0:T(8,128)(2,1)S(1)} %bitcast.39, f32[2,128]{1,0:T(2,128)S(1)} %bitcast.75, ...), custom_call_target="tpu_custom_call" | custom-call | tf_op jit(solution)/shard_map/pallas_call | solution.py:356
  71.9 11.9 %all_to_all.55 = bf16[16,16,512]{2,1,0:T(8,128)(2,1)S(1)} all-to-all(bf16[16,16,512]{2,1,0:T(8,128)(2,1)S(1)} %bitcast.66), channel_id=1, replica_groups={{0,1,2,3,4,5,6,7,8,9,10,11,12,13,14,15},{16,17,18,19,20,21,22,23,24,25,..., dimensions={0} | all-to-all | bytes 524288 | tf_op jit(solution)/shard_map/all_to_all | solution.py:320
  83.9 11.7 %all_to_all.56 = bf16[16,16,512]{2,1,0:T(8,128)(2,1)S(1)} all-to-all(bf16[16,16,512]{2,1,0:T(8,128)(2,1)S(1)} %bitcast.67), channel_id=1, replica_groups={{0,1,2,3,4,5,6,7,8,9,10,11,12,13,14,15},{16,17,18,19,20,21,22,23,24,25,..., dimensions={0} | all-to-all | bytes 524288 | tf_op jit(solution)/shard_map/all_to_all | solution.py:320
  95.6 2.2 %shard_map.84 = (bf16[4,4,16,512]{3,2,1,0:T(8,128)(2,1)S(1)}, bf16[2,2,64,512]{3,2,1,0:T(8,128)(2,1)S(1)}) custom-call(bf16[4,4,16,512]{3,2,1,0:T(8,128)(2,1)S(1)} %bitcast.46, f32[3,1,2048]{2,1,0:T(1,128)S(1)} %bitcast.61, bf16[2048,1536]{1,0:T(8,128)(2,1)S(1)} %bitcast.34, bf16[512,2048]{1,0:T(8,128)(2,1)S(1)} %bitcast.40, f32[2,128]{1,0:T(2,128)S(1)} %bitcast.76, ...), custom_call_target="tpu_custom_call" | custom-call | tf_op jit(solution)/shard_map/pallas_call | solution.py:356
  97.9 13.5 %all_to_all.57 = bf16[16,16,512]{2,1,0:T(8,128)(2,1)S(1)} all-to-all(bf16[16,16,512]{2,1,0:T(8,128)(2,1)S(1)} %bitcast.68), channel_id=1, replica_groups={{0,1,2,3,4,5,6,7,8,9,10,11,12,13,14,15},{16,17,18,19,20,21,22,23,24,25,..., dimensions={0} | all-to-all | bytes 524288 | tf_op jit(solution)/shard_map/all_to_all | solution.py:320
  111.4 12.7 %all_to_all.58 = bf16[16,16,512]{2,1,0:T(8,128)(2,1)S(1)} all-to-all(bf16[16,16,512]{2,1,0:T(8,128)(2,1)S(1)} %bitcast.54), channel_id=1, replica_groups={{0,1,2,3,4,5,6,7,8,9,10,11,12,13,14,15},{16,17,18,19,20,21,22,23,24,25,..., dimensions={0} | all-to-all | bytes 524288 | tf_op jit(solution)/shard_map/all_to_all | solution.py:320
  124.1 2.3 %shard_map.86 = (bf16[2,2,4,16,512]{4,3,2,1,0:T(8,128)(2,1)S(1)}, bf16[2,2,64,512]{3,2,1,0:T(8,128)(2,1)S(1)}) custom-call(bf16[4,4,16,512]{3,2,1,0:T(8,128)(2,1)S(1)} %bitcast.47, f32[3,1,2048]{2,1,0:T(1,128)S(1)} %bitcast.62, bf16[2048,1536]{1,0:T(8,128)(2,1)S(1)} %bitcast.35, bf16[512,2048]{1,0:T(8,128)(2,1)S(1)} %bitcast.41, f32[2,128]{1,0:T(2,128)S(1)} %bitcast.77, ...), custom_call_target="tpu_custom_call" | custom-call | tf_op jit(solution)/shard_map/pallas_call | solution.py:356
  126.4 12.7 %all_to_all.59 = bf16[16,16,512]{2,1,0:T(8,128)(2,1)S(1)} all-to-all(bf16[16,16,512]{2,1,0:T(8,128)(2,1)S(1)} %bitcast.69), channel_id=1, replica_groups={{0,1,2,3,4,5,6,7,16,17,18,19,20,21,22,23},{8,9,10,11,12,13,14,15,24,25,..., dimensions={0} | all-to-all | bytes 524288 | tf_op jit(solution)/shard_map/all_to_all | solution.py:396
  139.1 1.3 shard_map.87
  (5 shorter events, 0.1 us)
Async XLA Ops:
  0.6 18.2 %copy-start.2 = (bf16[1,1,2,4,1,4,8,512]{7,6,5,4,3,2,1,0:T(8,128)(2,1)S(1)}, bf16[1,1,2,4,1,4,8,512]{7,6,5,4,3,2,1,0:T(8,128)(2,1)}, u32[]{:S(2)}) copy-start(bf16[1,1,2,4,1,4,8,512]{7,6,5,4,3,2,1,0:T(8,128)(2,1)} %param.11) | copy-start | bytes 786436
  0.6 18.2 %copy-start.1 = (bf16[1,512,2048]{2,1,0:T(8,128)(2,1)S(1)}, bf16[1,512,2048]{2,1,0:T(8,128)(2,1)}, u32[]{:S(2)}) copy-start(bf16[1,512,2048]{2,1,0:T(8,128)(2,1)} %param.9) | copy-start | bytes 6291460
  0.7 18.2 %copy-start = (bf16[1,2048,1536]{2,1,0:T(8,128)(2,1)S(1)}, bf16[1,2048,1536]{2,1,0:T(8,128)(2,1)}, u32[]{:S(2)}) copy-start(bf16[1,2048,1536]{2,1,0:T(8,128)(2,1)} %param.8) | copy-start | bytes 18874372
  0.7 18.2 %copy-start.3 = (f32[1,1,3,2048]{3,1,2,0:T(1,128)S(1)}, f32[1,1,3,2048]{3,1,2,0:T(1,128)}, u32[]{:S(2)}) copy-start(f32[1,1,3,2048]{3,1,2,0:T(1,128)} %param.7) | copy-start | bytes 73732
  0.7 1.1 copy-start.4
  1.7 17.2 %copy-start.6 = (f32[1,2,128]{2,1,0:T(2,128)S(1)}, f32[1,2,128]{2,1,0:T(2,128)}, u32[]{:S(2)}) copy-start(f32[1,2,128]{2,1,0:T(2,128)} %param.10) | copy-start | bytes 3076
  1.8 31.2 %copy-start.5 = (bf16[4,8,2048]{2,1,0:T(8,128)(2,1)S(1)}, bf16[4,8,2048]{2,1,0:T(8,128)(2,1)}, u32[]{:S(2)}) copy-start(bf16[4,8,2048]{2,1,0:T(8,128)(2,1)} %param.6) | copy-start | bytes 393220

commit v19 on v18

--- a/solution.py
+++ b/solution.py
@@ -172,16 +172,7 @@
 
 
 def start_kernel(latent_ref, *refs):
-    spread_to = refs[-1]
-    half_cols = spread_to.shape[3]
-    for half in range(2):
-
-        @pl.when(lax.axis_index("pipe") % 2 == half)
-        def _():
-            held = latent_ref[0, :, half * half_cols : (half + 1) * half_cols]
-            for line in range(2):
-                for piece in range(spread_to.shape[1]):
-                    spread_to[line, piece] = held
+    refs[-1][...] = latent_ref[0]
 
 
 def added(parts_ref, section, *streams_refs):
@@ -332,9 +323,9 @@
     norm_gain = norm_gain[0]
     table = own_cache.reshape(2, GROUPS, rows, local_width)
     named = (qkv_slice, out_slice, modulation, norm_gain, table)
-    spread = pl.pallas_call(
+    own_rows = pl.pallas_call(
         start_kernel,
-        out_shape=jax.ShapeDtypeStruct(pair_shape, jnp.bfloat16),
+        out_shape=jax.ShapeDtypeStruct((block_rows, model_width), jnp.bfloat16),
         in_specs=[vmem] + [hbm] * len(named),
         out_specs=vmem,
         compiler_params=pltpu.CompilerParams(vmem_limit_bytes=4 * 1024 * 1024),
@@ -375,7 +366,7 @@
 
     ticks = GROUPS + section_count - 1
     closing_shape = (2, half, slice_count, block_rows, block_cols)
-    features = exchange(spread, pair_peers)
+    features = lax.all_gather(own_rows, "seq", axis_index_groups=in_slices)[None]
     partial_out, table = attend(0, features, table, pair_shape)
     parts = exchange(partial_out, pair_peers)
     (spread,) = small(settle_first_kernel, [vmem] * 2, pair_shape)(parts, in_vmem(sources))

time: 141 us -> 145 us (1.028)
  blocking collectives: 126 us -> 130 us
    all_gather x0 -> x1, blocking collectives: none -> 15.8 us  [local(): lax.all_gather(own_rows, 'seq', axis_index_groups=in_slices)[None]]
    all_to_all x9 -> x8, blocking collectives: 113 us -> 101 us  [exchange(): flat = lax.all_to_all(flat, ('pipe', 'seq'), 0, 0, axis_index_groups=among)]
where the time goes in v19:
time: 145 us; the launch traced here: 144 us
  blocking collectives  130 us (90%)
  Pallas kernels  12.7 us (9%)
    all_to_all x8, blocking collectives, exchange(): flat = lax.all_to_all(flat, ('pipe', 'seq'), 0, 0, axis_index_groups=among)  101 us
    all_gather x1, blocking collectives, local(): lax.all_gather(own_rows, 'seq', axis_index_groups=in_slices)[None]  15.8 us
    all_to_all x1, blocking collectives, local(): lax.all_to_all(closing.reshape((-1,) + closing_shape[3:]), ('cfg', 'pipe'...  12.7 us
    pallas_call x5, Pallas kernels, attend(): pl.pallas_call(functools.partial(section_kernel, tick, (tok_dev, head_dim...  11.3 us

profile of v19, /device:TPU:0, one launch (start us, length us, event | category | flops | bytes accessed | tf_op | source)
XLA Modules:
  0.0 144.3 jit_solution(7882980459958644990)
XLA Ops:
  0.6 0.0 copy-start.2
  0.6 0.0 copy-start.1
  0.7 0.0 copy-start
  0.7 0.0 copy-start.3
  0.7 0.0 copy-start.4
  0.7 1.0 copy-done.4
  1.7 0.0 copy-start.6
  1.7 0.0 copy-start.5
  1.7 15.8 %all-gather = bf16[64,2048]{1,0:T(8,128)(2,1)S(1)} all-gather(bf16[16,2048]{1,0:T(8,128)(2,1)S(1)} %shard_map.77), channel_id=2, replica_groups={{0,1,2,3},{4,5,6,7},{8,9,10,11},{12,13,14,15},{16,17,18,19},{20,21,22,2..., dimensions={0}, use_global_device_ids=true | all-gather | bytes 327680 | tf_op jit(solution)/shard_map/all_gather | solution.py:369
  17.5 0.0 copy-done.2
  17.5 0.0 copy-done.1
  17.5 0.0 copy-done
  17.5 0.0 copy-done.3
  17.5 0.0 copy-done.6
  17.5 2.2 %shard_map.78 = (bf16[2,4,16,1024]{3,2,1,0:T(8,128)(2,1)S(1)}, bf16[2,2,64,512]{3,2,1,0:T(8,128)(2,1)S(1)}) custom-call(bf16[1,4,16,2048]{3,2,1,0:T(8,128)(2,1)S(1)} %bitcast.43, f32[3,1,2048]{2,1,0:T(1,128)S(1)} %bitcast.56, bf16[2048,1536]{1,0:T(8,128)(2,1)S(1)} %bitcast.30, bf16[512,2048]{1,0:T(8,128)(2,1)S(1)} %bitcast.36, f32[2,128]{1,0:T(2,128)S(1)} %bitcast.71, ...), custom_call_target="tpu_custom_call" | custom-call | tf_op jit(solution)/shard_map/pallas_call | solution.py:347
  19.8 14.5 %all_to_all.45 = bf16[8,16,1024]{2,1,0:T(8,128)(2,1)S(1)} all-to-all(bf16[8,16,1024]{2,1,0:T(8,128)(2,1)S(1)} %bitcast.68), channel_id=1, replica_groups={{0,1,2,3,4,5,6,7},{8,9,10,11,12,13,14,15},{16,17,18,19,20,21,22,23},{24..., dimensions={0} | all-to-all | bytes 524288 | tf_op jit(solution)/shard_map/all_to_all | solution.py:311
  34.3 0.0 copy-done.5
  34.3 11.0 %all_to_all.46 = bf16[8,16,1024]{2,1,0:T(8,128)(2,1)S(1)} all-to-all(bf16[8,16,1024]{2,1,0:T(8,128)(2,1)S(1)} %bitcast.54), channel_id=1, replica_groups={{0,1,2,3,4,5,6,7},{8,9,10,11,12,13,14,15},{16,17,18,19,20,21,22,23},{24..., dimensions={0} | all-to-all | bytes 524288 | tf_op jit(solution)/shard_map/all_to_all | solution.py:311
  45.3 2.2 %shard_map.80 = (bf16[4,4,16,512]{3,2,1,0:T(8,128)(2,1)S(1)}, bf16[2,2,64,512]{3,2,1,0:T(8,128)(2,1)S(1)}) custom-call(bf16[2,4,16,1024]{3,2,1,0:T(8,128)(2,1)S(1)} %bitcast.44, f32[3,1,2048]{2,1,0:T(1,128)S(1)} %bitcast.57, bf16[2048,1536]{1,0:T(8,128)(2,1)S(1)} %bitcast.31, bf16[512,2048]{1,0:T(8,128)(2,1)S(1)} %bitcast.37, f32[2,128]{1,0:T(2,128)S(1)} %bitcast.72, ...), custom_call_target="tpu_custom_call" | custom-call | tf_op jit(solution)/shard_map/pallas_call | solution.py:347
  47.5 11.7 %all_to_all.47 = bf16[16,16,512]{2,1,0:T(8,128)(2,1)S(1)} all-to-all(bf16[16,16,512]{2,1,0:T(8,128)(2,1)S(1)} %bitcast.63), channel_id=1, replica_groups={{0,1,2,3,4,5,6,7,8,9,10,11,12,13,14,15},{16,17,18,19,20,21,22,23,24,25,..., dimensions={0} | all-to-all | bytes 524288 | tf_op jit(solution)/shard_map/all_to_all | solution.py:311
  59.3 11.8 %all_to_all.48 = bf16[16,16,512]{2,1,0:T(8,128)(2,1)S(1)} all-to-all(bf16[16,16,512]{2,1,0:T(8,128)(2,1)S(1)} %bitcast.69), channel_id=1, replica_groups={{0,1,2,3,4,5,6,7,8,9,10,11,12,13,14,15},{16,17,18,19,20,21,22,23,24,25,..., dimensions={0} | all-to-all | bytes 524288 | tf_op jit(solution)/shard_map/all_to_all | solution.py:311
  71.1 2.2 %shard_map.82 = (bf16[4,4,16,512]{3,2,1,0:T(8,128)(2,1)S(1)}, bf16[2,2,64,512]{3,2,1,0:T(8,128)(2,1)S(1)}) custom-call(bf16[4,4,16,512]{3,2,1,0:T(8,128)(2,1)S(1)} %bitcast.45, f32[3,1,2048]{2,1,0:T(1,128)S(1)} %bitcast.58, bf16[2048,1536]{1,0:T(8,128)(2,1)S(1)} %bitcast.32, bf16[512,2048]{1,0:T(8,128)(2,1)S(1)} %bitcast.38, f32[2,128]{1,0:T(2,128)S(1)} %bitcast.73, ...), custom_call_target="tpu_custom_call" | custom-call | tf_op jit(solution)/shard_map/pallas_call | solution.py:347
  73.4 14.5 %all_to_all.49 = bf16[16,16,512]{2,1,0:T(8,128)(2,1)S(1)} all-to-all(bf16[16,16,512]{2,1,0:T(8,128)(2,1)S(1)} %bitcast.64), channel_id=1, replica_groups={{0,1,2,3,4,5,6,7,8,9,10,11,12,13,14,15},{16,17,18,19,20,21,22,23,24,25,..., dimensions={0} | all-to-all | bytes 524288 | tf_op jit(solution)/shard_map/all_to_all | solution.py:311
  87.9 13.4 %all_to_all.50 = bf16[16,16,512]{2,1,0:T(8,128)(2,1)S(1)} all-to-all(bf16[16,16,512]{2,1,0:T(8,128)(2,1)S(1)} %bitcast.65), channel_id=1, replica_groups={{0,1,2,3,4,5,6,7,8,9,10,11,12,13,14,15},{16,17,18,19,20,21,22,23,24,25,..., dimensions={0} | all-to-all | bytes 524288 | tf_op jit(solution)/shard_map/all_to_all | solution.py:311
  101.3 2.2 %shard_map.84 = (bf16[4,4,16,512]{3,2,1,0:T(8,128)(2,1)S(1)}, bf16[2,2,64,512]{3,2,1,0:T(8,128)(2,1)S(1)}) custom-call(bf16[4,4,16,512]{3,2,1,0:T(8,128)(2,1)S(1)} %bitcast.46, f32[3,1,2048]{2,1,0:T(1,128)S(1)} %bitcast.59, bf16[2048,1536]{1,0:T(8,128)(2,1)S(1)} %bitcast.33, bf16[512,2048]{1,0:T(8,128)(2,1)S(1)} %bitcast.39, f32[2,128]{1,0:T(2,128)S(1)} %bitcast.74, ...), custom_call_target="tpu_custom_call" | custom-call | tf_op jit(solution)/shard_map/pallas_call | solution.py:347
  103.6 12.6 %all_to_all.51 = bf16[16,16,512]{2,1,0:T(8,128)(2,1)S(1)} all-to-all(bf16[16,16,512]{2,1,0:T(8,128)(2,1)S(1)} %bitcast.66), channel_id=1, replica_groups={{0,1,2,3,4,5,6,7,8,9,10,11,12,13,14,15},{16,17,18,19,20,21,22,23,24,25,..., dimensions={0} | all-to-all | bytes 524288 | tf_op jit(solution)/shard_map/all_to_all | solution.py:311
  116.2 11.8 %all_to_all.52 = bf16[16,16,512]{2,1,0:T(8,128)(2,1)S(1)} all-to-all(bf16[16,16,512]{2,1,0:T(8,128)(2,1)S(1)} %bitcast.52), channel_id=1, replica_groups={{0,1,2,3,4,5,6,7,8,9,10,11,12,13,14,15},{16,17,18,19,20,21,22,23,24,25,..., dimensions={0} | all-to-all | bytes 524288 | tf_op jit(solution)/shard_map/all_to_all | solution.py:311
  128.1 2.3 %shard_map.86 = (bf16[2,2,4,16,512]{4,3,2,1,0:T(8,128)(2,1)S(1)}, bf16[2,2,64,512]{3,2,1,0:T(8,128)(2,1)S(1)}) custom-call(bf16[4,4,16,512]{3,2,1,0:T(8,128)(2,1)S(1)} %bitcast.47, f32[3,1,2048]{2,1,0:T(1,128)S(1)} %bitcast.60, bf16[2048,1536]{1,0:T(8,128)(2,1)S(1)} %bitcast.34, bf16[512,2048]{1,0:T(8,128)(2,1)S(1)} %bitcast.40, f32[2,128]{1,0:T(2,128)S(1)} %bitcast.75, ...), custom_call_target="tpu_custom_call" | custom-call | tf_op jit(solution)/shard_map/pallas_call | solution.py:347
  130.4 12.7 %all_to_all.53 = bf16[16,16,512]{2,1,0:T(8,128)(2,1)S(1)} all-to-all(bf16[16,16,512]{2,1,0:T(8,128)(2,1)S(1)} %bitcast.67), channel_id=1, replica_groups={{0,1,2,3,4,5,6,7,16,17,18,19,20,21,22,23},{8,9,10,11,12,13,14,15,24,25,..., dimensions={0} | all-to-all | bytes 524288 | tf_op jit(solution)/shard_map/all_to_all | solution.py:387
  143.0 1.3 shard_map.87
  (5 shorter events, 0.1 us)
Async XLA Ops:
  0.6 16.9 %copy-start.2 = (bf16[1,1,2,4,1,4,8,512]{7,6,5,4,3,2,1,0:T(8,128)(2,1)S(1)}, bf16[1,1,2,4,1,4,8,512]{7,6,5,4,3,2,1,0:T(8,128)(2,1)}, u32[]{:S(2)}) copy-start(bf16[1,1,2,4,1,4,8,512]{7,6,5,4,3,2,1,0:T(8,128)(2,1)} %param.11) | copy-start | bytes 786436
  0.6 16.9 %copy-start.1 = (bf16[1,512,2048]{2,1,0:T(8,128)(2,1)S(1)}, bf16[1,512,2048]{2,1,0:T(8,128)(2,1)}, u32[]{:S(2)}) copy-start(bf16[1,512,2048]{2,1,0:T(8,128)(2,1)} %param.9) | copy-start | bytes 6291460
  0.7 16.9 %copy-start = (bf16[1,2048,1536]{2,1,0:T(8,128)(2,1)S(1)}, bf16[1,2048,1536]{2,1,0:T(8,128)(2,1)}, u32[]{:S(2)}) copy-start(bf16[1,2048,1536]{2,1,0:T(8,128)(2,1)} %param.8) | copy-start | bytes 18874372
  0.7 16.9 %copy-start.3 = (f32[1,1,3,2048]{3,1,2,0:T(1,128)S(1)}, f32[1,1,3,2048]{3,1,2,0:T(1,128)}, u32[]{:S(2)}) copy-start(f32[1,1,3,2048]{3,1,2,0:T(1,128)} %param.7) | copy-start | bytes 73732
  0.7 1.1 copy-start.4
  1.7 15.8 %copy-start.6 = (f32[1,2,128]{2,1,0:T(2,128)S(1)}, f32[1,2,128]{2,1,0:T(2,128)}, u32[]{:S(2)}) copy-start(f32[1,2,128]{2,1,0:T(2,128)} %param.10) | copy-start | bytes 3076
  1.7 32.5 %copy-start.5 = (bf16[4,8,2048]{2,1,0:T(8,128)(2,1)S(1)}, bf16[4,8,2048]{2,1,0:T(8,128)(2,1)}, u32[]{:S(2)}) copy-start(bf16[4,8,2048]{2,1,0:T(8,128)(2,1)} %param.6) | copy-start | bytes 393220

commit v20 on v19

--- a/solution.py
+++ b/solution.py
@@ -172,7 +172,9 @@
 
 
 def start_kernel(latent_ref, *refs):
-    refs[-1][...] = latent_ref[0]
+    spread_to = refs[-1]
+    for piece in range(spread_to.shape[0]):
+        spread_to[piece] = latent_ref[...]
 
 
 def added(parts_ref, section, *streams_refs):
@@ -318,18 +320,17 @@
     sources = latent.reshape(GROUPS, block_rows, model_width)
     stream_shape = (section_count, block_rows, block_cols)
     spread_shape = (section_count, slice_count, block_rows, block_cols)
-    pair_shape = (2, slice_count, block_rows, model_width // 2)
     modulation = modulation.reshape(3, 1, model_width)
     norm_gain = norm_gain[0]
     table = own_cache.reshape(2, GROUPS, rows, local_width)
-    named = (qkv_slice, out_slice, modulation, norm_gain, table)
-    own_rows = pl.pallas_call(
+    named = (qkv_slice, out_slice, modulation, norm_gain, table, sources)
+    spread = pl.pallas_call(
         start_kernel,
-        out_shape=jax.ShapeDtypeStruct((block_rows, model_width), jnp.bfloat16),
+        out_shape=jax.ShapeDtypeStruct((slice_count, block_rows, model_width), jnp.bfloat16),
         in_specs=[vmem] + [hbm] * len(named),
         out_specs=vmem,
         compiler_params=pltpu.CompilerParams(vmem_limit_bytes=4 * 1024 * 1024),
-    )(in_vmem(sources), *map(in_hbm, named))
+    )(sources[0], *map(in_hbm, named))
     stale_rows = []
     if member_count > 1:
         stale_rows = [group_cache.swapaxes(0, 1).reshape(2, -1, local_width)]
@@ -366,7 +367,8 @@
 
     ticks = GROUPS + section_count - 1
     closing_shape = (2, half, slice_count, block_rows, block_cols)
-    features = lax.all_gather(own_rows, "seq", axis_index_groups=in_slices)[None]
+    features = lax.all_to_all(spread, "seq", 0, 0, axis_index_groups=in_slices)[None]
+    pair_shape = (2, slice_count, block_rows, model_width // 2)
     partial_out, table = attend(0, features, table, pair_shape)
     parts = exchange(partial_out, pair_peers)
     (spread,) = small(settle_first_kernel, [vmem] * 2, pair_shape)(parts, in_vmem(sources))

time: 145 us -> 140 us (0.966)
  blocking collectives: 130 us -> 125 us
    all_gather x1 -> x0, blocking collectives: 15.8 us -> none  [local(): lax.all_gather(own_rows, 'seq', axis_index_groups=in_slices)[None]]
    all_to_all x0 -> x1, blocking collectives: none -> 15.3 us  [local(): lax.all_to_all(spread, 'seq', 0, 0, axis_index_groups=in_slices)[None]]
    all_to_all x8, blocking collectives: 101 us -> 97.2 us  [exchange(): flat = lax.all_to_all(flat, ('pipe', 'seq'), 0, 0, axis_index_groups=among)]
where the time goes in v20:
time: 140 us
  blocking collectives  125 us (89%)
  Pallas kernels  12.7 us (9%)
    all_to_all x8, blocking collectives, exchange(): flat = lax.all_to_all(flat, ('pipe', 'seq'), 0, 0, axis_index_groups=among)  97.2 us
    all_to_all x1, blocking collectives, local(): lax.all_to_all(spread, 'seq', 0, 0, axis_index_groups=in_slices)[None]  15.3 us
    all_to_all x1, blocking collectives, local(): lax.all_to_all(closing.reshape((-1,) + closing_shape[3:]), ('cfg', 'pipe'...  12.7 us
    pallas_call x5, Pallas kernels, attend(): pl.pallas_call(functools.partial(section_kernel, tick, (tok_dev, head_dim...  11.3 us

profile of v20, /device:TPU:0, one launch (start us, length us, event | category | flops | bytes accessed | tf_op | source)
XLA Modules:
  0.0 139.6 jit_solution(6286807875464439913)
XLA Ops:
  0.6 0.0 copy-start.2
  0.6 0.0 copy-start.5
  0.7 0.0 copy-start.1
  0.7 0.0 copy-start
  0.7 0.0 copy-start.3
  0.7 1.0 slice_bitcast_fusion.latent_ref
  1.7 0.0 copy-start.4
  1.7 15.3 %all_to_all.50 = bf16[4,16,2048]{2,1,0:T(8,128)(2,1)S(1)} all-to-all(bf16[4,16,2048]{2,1,0:T(8,128)(2,1)S(1)} %shard_map.77), channel_id=1, replica_groups={{0,1,2,3},{4,5,6,7},{8,9,10,11},{12,13,14,15},{16,17,18,19},{20,21,22,2..., dimensions={0} | all-to-all | bytes 524288 | tf_op jit(solution)/shard_map/all_to_all | solution.py:370
  17.0 0.0 copy-done.2
  17.0 0.0 copy-done.5
  17.0 0.0 copy-done.1
  17.0 0.0 copy-done
  17.0 0.0 copy-done.3
  17.0 2.3 %shard_map.78 = (bf16[2,4,16,1024]{3,2,1,0:T(8,128)(2,1)S(1)}, bf16[2,2,64,512]{3,2,1,0:T(8,128)(2,1)S(1)}) custom-call(bf16[1,4,16,2048]{3,2,1,0:T(8,128)(2,1)S(1)} %bitcast.49, f32[3,1,2048]{2,1,0:T(1,128)S(1)} %bitcast.58, bf16[2048,1536]{1,0:T(8,128)(2,1)S(1)} %bitcast.32, bf16[512,2048]{1,0:T(8,128)(2,1)S(1)} %bitcast.38, f32[2,128]{1,0:T(2,128)S(1)} %bitcast.73, ...), custom_call_target="tpu_custom_call" | custom-call | tf_op jit(solution)/shard_map/pallas_call | solution.py:348
  19.3 13.0 %all_to_all.51 = bf16[8,16,1024]{2,1,0:T(8,128)(2,1)S(1)} all-to-all(bf16[8,16,1024]{2,1,0:T(8,128)(2,1)S(1)} %bitcast.70), channel_id=1, replica_groups={{0,1,2,3,4,5,6,7},{8,9,10,11,12,13,14,15},{16,17,18,19,20,21,22,23},{24..., dimensions={0} | all-to-all | bytes 524288 | tf_op jit(solution)/shard_map/all_to_all | solution.py:313
  32.2 0.0 copy-done.4
  32.3 11.1 %all_to_all.52 = bf16[8,16,1024]{2,1,0:T(8,128)(2,1)S(1)} all-to-all(bf16[8,16,1024]{2,1,0:T(8,128)(2,1)S(1)} %bitcast.56), channel_id=1, replica_groups={{0,1,2,3,4,5,6,7},{8,9,10,11,12,13,14,15},{16,17,18,19,20,21,22,23},{24..., dimensions={0} | all-to-all | bytes 524288 | tf_op jit(solution)/shard_map/all_to_all | solution.py:313
  43.3 2.2 %shard_map.80 = (bf16[4,4,16,512]{3,2,1,0:T(8,128)(2,1)S(1)}, bf16[2,2,64,512]{3,2,1,0:T(8,128)(2,1)S(1)}) custom-call(bf16[2,4,16,1024]{3,2,1,0:T(8,128)(2,1)S(1)} %bitcast.45, f32[3,1,2048]{2,1,0:T(1,128)S(1)} %bitcast.59, bf16[2048,1536]{1,0:T(8,128)(2,1)S(1)} %bitcast.33, bf16[512,2048]{1,0:T(8,128)(2,1)S(1)} %bitcast.39, f32[2,128]{1,0:T(2,128)S(1)} %bitcast.74, ...), custom_call_target="tpu_custom_call" | custom-call | tf_op jit(solution)/shard_map/pallas_call | solution.py:348
  45.6 11.5 %all_to_all.53 = bf16[16,16,512]{2,1,0:T(8,128)(2,1)S(1)} all-to-all(bf16[16,16,512]{2,1,0:T(8,128)(2,1)S(1)} %bitcast.65), channel_id=1, replica_groups={{0,1,2,3,4,5,6,7,8,9,10,11,12,13,14,15},{16,17,18,19,20,21,22,23,24,25,..., dimensions={0} | all-to-all | bytes 524288 | tf_op jit(solution)/shard_map/all_to_all | solution.py:313
  57.1 11.8 %all_to_all.54 = bf16[16,16,512]{2,1,0:T(8,128)(2,1)S(1)} all-to-all(bf16[16,16,512]{2,1,0:T(8,128)(2,1)S(1)} %bitcast.71), channel_id=1, replica_groups={{0,1,2,3,4,5,6,7,8,9,10,11,12,13,14,15},{16,17,18,19,20,21,22,23,24,25,..., dimensions={0} | all-to-all | bytes 524288 | tf_op jit(solution)/shard_map/all_to_all | solution.py:313
  68.9 2.2 %shard_map.82 = (bf16[4,4,16,512]{3,2,1,0:T(8,128)(2,1)S(1)}, bf16[2,2,64,512]{3,2,1,0:T(8,128)(2,1)S(1)}) custom-call(bf16[4,4,16,512]{3,2,1,0:T(8,128)(2,1)S(1)} %bitcast.46, f32[3,1,2048]{2,1,0:T(1,128)S(1)} %bitcast.60, bf16[2048,1536]{1,0:T(8,128)(2,1)S(1)} %bitcast.34, bf16[512,2048]{1,0:T(8,128)(2,1)S(1)} %bitcast.40, f32[2,128]{1,0:T(2,128)S(1)} %bitcast.75, ...), custom_call_target="tpu_custom_call" | custom-call | tf_op jit(solution)/shard_map/pallas_call | solution.py:348
  71.2 11.9 %all_to_all.55 = bf16[16,16,512]{2,1,0:T(8,128)(2,1)S(1)} all-to-all(bf16[16,16,512]{2,1,0:T(8,128)(2,1)S(1)} %bitcast.66), channel_id=1, replica_groups={{0,1,2,3,4,5,6,7,8,9,10,11,12,13,14,15},{16,17,18,19,20,21,22,23,24,25,..., dimensions={0} | all-to-all | bytes 524288 | tf_op jit(solution)/shard_map/all_to_all | solution.py:313
  83.2 11.7 %all_to_all.56 = bf16[16,16,512]{2,1,0:T(8,128)(2,1)S(1)} all-to-all(bf16[16,16,512]{2,1,0:T(8,128)(2,1)S(1)} %bitcast.67), channel_id=1, replica_groups={{0,1,2,3,4,5,6,7,8,9,10,11,12,13,14,15},{16,17,18,19,20,21,22,23,24,25,..., dimensions={0} | all-to-all | bytes 524288 | tf_op jit(solution)/shard_map/all_to_all | solution.py:313
  94.9 2.2 %shard_map.84 = (bf16[4,4,16,512]{3,2,1,0:T(8,128)(2,1)S(1)}, bf16[2,2,64,512]{3,2,1,0:T(8,128)(2,1)S(1)}) custom-call(bf16[4,4,16,512]{3,2,1,0:T(8,128)(2,1)S(1)} %bitcast.47, f32[3,1,2048]{2,1,0:T(1,128)S(1)} %bitcast.61, bf16[2048,1536]{1,0:T(8,128)(2,1)S(1)} %bitcast.35, bf16[512,2048]{1,0:T(8,128)(2,1)S(1)} %bitcast.41, f32[2,128]{1,0:T(2,128)S(1)} %bitcast.76, ...), custom_call_target="tpu_custom_call" | custom-call | tf_op jit(solution)/shard_map/pallas_call | solution.py:348
  97.1 13.5 %all_to_all.57 = bf16[16,16,512]{2,1,0:T(8,128)(2,1)S(1)} all-to-all(bf16[16,16,512]{2,1,0:T(8,128)(2,1)S(1)} %bitcast.68), channel_id=1, replica_groups={{0,1,2,3,4,5,6,7,8,9,10,11,12,13,14,15},{16,17,18,19,20,21,22,23,24,25,..., dimensions={0} | all-to-all | bytes 524288 | tf_op jit(solution)/shard_map/all_to_all | solution.py:313
  110.7 12.7 %all_to_all.58 = bf16[16,16,512]{2,1,0:T(8,128)(2,1)S(1)} all-to-all(bf16[16,16,512]{2,1,0:T(8,128)(2,1)S(1)} %bitcast.54), channel_id=1, replica_groups={{0,1,2,3,4,5,6,7,8,9,10,11,12,13,14,15},{16,17,18,19,20,21,22,23,24,25,..., dimensions={0} | all-to-all | bytes 524288 | tf_op jit(solution)/shard_map/all_to_all | solution.py:313
  123.4 2.3 %shard_map.86 = (bf16[2,2,4,16,512]{4,3,2,1,0:T(8,128)(2,1)S(1)}, bf16[2,2,64,512]{3,2,1,0:T(8,128)(2,1)S(1)}) custom-call(bf16[4,4,16,512]{3,2,1,0:T(8,128)(2,1)S(1)} %bitcast.48, f32[3,1,2048]{2,1,0:T(1,128)S(1)} %bitcast.62, bf16[2048,1536]{1,0:T(8,128)(2,1)S(1)} %bitcast.36, bf16[512,2048]{1,0:T(8,128)(2,1)S(1)} %bitcast.42, f32[2,128]{1,0:T(2,128)S(1)} %bitcast.77, ...), custom_call_target="tpu_custom_call" | custom-call | tf_op jit(solution)/shard_map/pallas_call | solution.py:348
  125.7 12.7 %all_to_all.59 = bf16[16,16,512]{2,1,0:T(8,128)(2,1)S(1)} all-to-all(bf16[16,16,512]{2,1,0:T(8,128)(2,1)S(1)} %bitcast.69), channel_id=1, replica_groups={{0,1,2,3,4,5,6,7,16,17,18,19,20,21,22,23},{8,9,10,11,12,13,14,15,24,25,..., dimensions={0} | all-to-all | bytes 524288 | tf_op jit(solution)/shard_map/all_to_all | solution.py:389
  138.3 1.3 shard_map.87
  (5 shorter events, 0.1 us)
Async XLA Ops:
  0.6 16.4 %copy-start.2 = (bf16[1,1,2,4,1,4,8,512]{7,6,5,4,3,2,1,0:T(8,128)(2,1)S(1)}, bf16[1,1,2,4,1,4,8,512]{7,6,5,4,3,2,1,0:T(8,128)(2,1)}, u32[]{:S(2)}) copy-start(bf16[1,1,2,4,1,4,8,512]{7,6,5,4,3,2,1,0:T(8,128)(2,1)} %param.11) | copy-start | bytes 786436
  0.6 16.3 %copy-start.5 = (f32[1,2,128]{2,1,0:T(2,128)S(1)}, f32[1,2,128]{2,1,0:T(2,128)}, u32[]{:S(2)}) copy-start(f32[1,2,128]{2,1,0:T(2,128)} %param.10) | copy-start | bytes 3076
  0.7 16.3 %copy-start.1 = (bf16[1,512,2048]{2,1,0:T(8,128)(2,1)S(1)}, bf16[1,512,2048]{2,1,0:T(8,128)(2,1)}, u32[]{:S(2)}) copy-start(bf16[1,512,2048]{2,1,0:T(8,128)(2,1)} %param.9) | copy-start | bytes 6291460
  0.7 16.3 %copy-start = (bf16[1,2048,1536]{2,1,0:T(8,128)(2,1)S(1)}, bf16[1,2048,1536]{2,1,0:T(8,128)(2,1)}, u32[]{:S(2)}) copy-start(bf16[1,2048,1536]{2,1,0:T(8,128)(2,1)} %param.8) | copy-start | bytes 18874372
  0.7 16.3 %copy-start.3 = (f32[1,1,3,2048]{3,1,2,0:T(1,128)S(1)}, f32[1,1,3,2048]{3,1,2,0:T(1,128)}, u32[]{:S(2)}) copy-start(f32[1,1,3,2048]{3,1,2,0:T(1,128)} %param.7) | copy-start | bytes 73732
  1.7 30.5 %copy-start.4 = (bf16[4,8,2048]{2,1,0:T(8,128)(2,1)S(1)}, bf16[4,8,2048]{2,1,0:T(8,128)(2,1)}, u32[]{:S(2)}) copy-start(bf16[4,8,2048]{2,1,0:T(8,128)(2,1)} %param.6) | copy-start | bytes 393220

commit v21 on v20

--- a/solution.py
+++ b/solution.py
@@ -41,7 +41,7 @@
     closing = len(partial_ref.shape) == 5
     folding = tick == 1
     tok_dev, head_dim, members = sizes
-    blocks, slices, block_rows, block_cols = rows_ref.shape
+    slices, blocks, block_rows, block_cols = rows_ref.shape
     rows = slices * block_rows
     width = blocks * block_cols
     in_group = block_rows // tok_dev
@@ -50,7 +50,7 @@
     heads = local_width // head_dim
     section, own_member, own_slice = position(members)
     group = tick - section
-    parts = [rows_ref[q].reshape(rows, block_cols).astype(jnp.float32) for q in range(blocks)]
+    parts = [rows_ref[:, q].reshape(rows, block_cols).astype(jnp.float32) for q in range(blocks)]
     mean = jnp.sum(sum(parts), axis=-1, keepdims=True) * (1.0 / width)
     parts = [x - mean for x in parts]
     spread = jnp.sum(sum(x * x for x in parts), axis=-1, keepdims=True) * (1.0 / width)
@@ -120,16 +120,16 @@
         at_slice = lax.broadcasted_iota(jnp.int32, (rows, 1), 0) // block_rows
         own = (at_slice == own_slice).astype(jnp.float32)
         projected = projected + own * jnp.concatenate(
-            [rows_ref[q].reshape(rows, block_cols).astype(jnp.float32) for q in range(blocks)],
+            [rows_ref[:, q].reshape(rows, block_cols).astype(jnp.float32) for q in range(blocks)],
             axis=1,
         )
     if closing:
         close_into(partial_ref, projected, rows_ref, section, own_slice, in_group)
     else:
         out_cols = partial_ref.shape[3]
-        for q in range(partial_ref.shape[0]):
+        for q in range(partial_ref.shape[1]):
             piece = projected[:, q * out_cols : (q + 1) * out_cols].astype(jnp.bfloat16)
-            partial_ref[q] = piece.reshape(slices, block_rows, out_cols)
+            partial_ref[:, q] = piece.reshape(slices, block_rows, out_cols)
 
     for kind in range(2):
         rows_of = jnp.concatenate([fresh[kind][head] for head in range(heads)], axis=1)
@@ -139,7 +139,7 @@
 
 def close_into(closing_ref, projected, rows_ref, section, own_slice, in_group):
     branches, patches, slices = closing_ref.shape[:3]
-    blocks, _, block_rows, block_cols = rows_ref.shape
+    _, blocks, block_rows, block_cols = rows_ref.shape
     tok_dev = block_rows // in_group
     per_branch = blocks // branches
 
@@ -153,7 +153,7 @@
                     piece * block_rows : (piece + 1) * block_rows,
                     q * block_cols : (q + 1) * block_cols,
                 ]
-                rows = rows + own * rows_ref[q, piece].astype(jnp.float32)
+                rows = rows + own * rows_ref[piece, q].astype(jnp.float32)
                 by_block.append(rows.reshape(in_group, tok_dev, block_cols))
             for branch in range(branches):
                 for patch in range(patches):
@@ -162,7 +162,7 @@
 
     @pl.when(section < patches)
     def _():
-        finished = [rows_ref[q, own_slice].astype(jnp.float32)[:tok_dev] for q in range(blocks)]
+        finished = [rows_ref[own_slice, q].astype(jnp.float32)[:tok_dev] for q in range(blocks)]
         for branch in range(branches):
             held = jnp.concatenate(finished[branch * per_branch : (branch + 1) * per_branch])
             held = held.astype(jnp.bfloat16)
@@ -178,7 +178,7 @@
 
 
 def added(parts_ref, section, *streams_refs):
-    total = sum(parts_ref[section, piece].astype(jnp.float32) for piece in range(parts_ref.shape[1]))
+    total = sum(parts_ref[piece, section].astype(jnp.float32) for piece in range(parts_ref.shape[0]))
     for ref in streams_refs:
         total = total + ref[section].astype(jnp.float32)
     return total
@@ -193,23 +193,23 @@
         def _():
             at = slice(half * half_cols, (half + 1) * half_cols)
             held = (first + latent_ref[0, :, at].astype(jnp.float32)).astype(jnp.bfloat16)
-            for piece in range(parts_ref.shape[1]):
-                spread_to[0, piece] = latent_ref[1, :, at]
-                spread_to[1, piece] = held
+            for piece in range(parts_ref.shape[0]):
+                spread_to[piece, 0] = latent_ref[1, :, at]
+                spread_to[piece, 1] = held
 
 
 def settle_kernel(parts_ref, *refs):
     *streams_refs, streams_to, spread_to = refs
-    count, slices = parts_ref.shape[:2]
+    slices, count = parts_ref.shape[:2]
     for section in range(count):
         held = added(parts_ref, max(section - 1, 0), *streams_refs).astype(jnp.bfloat16)
         streams_to[section] = held
         for piece in range(slices):
-            spread_to[section, piece] = held
+            spread_to[piece, section] = held
 
 
 def settle_last_kernel(in_group, parts_ref, streams_ref, spread_to):
-    count, slices = parts_ref.shape[:2]
+    slices, count = parts_ref.shape[:2]
     finished = added(parts_ref, count - 1, streams_ref)
     tok_dev = finished.shape[0] // in_group
     last = added(parts_ref, count - 2, streams_ref).astype(jnp.bfloat16)
@@ -219,7 +219,7 @@
             held = finished[section * tok_dev : (section + 1) * tok_dev]
             held = jnp.concatenate([held] * in_group).astype(jnp.bfloat16)
         for piece in range(slices):
-            spread_to[section, piece] = held
+            spread_to[piece, section] = held
 
 
 def guide_kernel(members, closing_ref, table_ref, guided_ref, table_to, sem):
@@ -290,7 +290,7 @@
     half = section_count // 2
     groups_of = range(member_count)
     in_slices = [[a + member_count * b for b in range(slice_count)] for a in groups_of]
-    peers = [[q * seq_count + at for q in range(section_count) for at in g] for g in in_slices]
+    peers = [[q * seq_count + at for at in g for q in range(section_count)] for g in in_slices]
     closing_peers = [
         [
             (c * section_count + q) * seq_count + at
@@ -303,7 +303,7 @@
     ]
 
     pair_peers = [
-        [q * seq_count + at for q in range(first, first + 2) for at in g]
+        [q * seq_count + at for at in g for q in range(first, first + 2)]
         for first in range(0, section_count, 2)
         for g in in_slices
     ]
@@ -319,7 +319,7 @@
     in_vmem = functools.partial(pltpu.with_memory_space_constraint, memory_space=pltpu.VMEM)
     sources = latent.reshape(GROUPS, block_rows, model_width)
     stream_shape = (section_count, block_rows, block_cols)
-    spread_shape = (section_count, slice_count, block_rows, block_cols)
+    spread_shape = (slice_count, section_count, block_rows, block_cols)
     modulation = modulation.reshape(3, 1, model_width)
     norm_gain = norm_gain[0]
     table = own_cache.reshape(2, GROUPS, rows, local_width)
@@ -367,8 +367,8 @@
 
     ticks = GROUPS + section_count - 1
     closing_shape = (2, half, slice_count, block_rows, block_cols)
-    features = lax.all_to_all(spread, "seq", 0, 0, axis_index_groups=in_slices)[None]
-    pair_shape = (2, slice_count, block_rows, model_width // 2)
+    features = lax.all_to_all(spread, "seq", 0, 0, axis_index_groups=in_slices)[:, None]
+    pair_shape = (slice_count, 2, block_rows, model_width // 2)
     partial_out, table = attend(0, features, table, pair_shape)
     parts = exchange(partial_out, pair_peers)
     (spread,) = small(settle_first_kernel, [vmem] * 2, pair_shape)(parts, in_vmem(sources))

time: 140 us -> 143 us (1.021)
  blocking collectives: 125 us -> 128 us
    all_to_all x8, blocking collectives: 97.2 us -> 99.7 us  [exchange(): flat = lax.all_to_all(flat, ('pipe', 'seq'), 0, 0, axis_index_groups=among)]
where the time goes in v21:
time: 143 us
  blocking collectives  128 us (90%)
  Pallas kernels  12.7 us (9%)
    all_to_all x8, blocking collectives, exchange(): flat = lax.all_to_all(flat, ('pipe', 'seq'), 0, 0, axis_index_groups=among)  99.7 us
    all_to_all x1, blocking collectives, local(): lax.all_to_all(spread, 'seq', 0, 0, axis_index_groups=in_slices)[:, None]  15.3 us
    all_to_all x1, blocking collectives, local(): lax.all_to_all(closing.reshape((-1,) + closing_shape[3:]), ('cfg', 'pipe'...  13.1 us
    pallas_call x5, Pallas kernels, attend(): pl.pallas_call(functools.partial(section_kernel, tick, (tok_dev, head_dim...  11.3 us

profile of v21, /device:TPU:0, one launch (start us, length us, event | category | flops | bytes accessed | tf_op | source)
XLA Modules:
  0.0 142.5 jit_solution(8162198530082272803)
XLA Ops:
  0.6 0.0 copy-start.2
  0.6 0.0 copy-start.5
  0.7 0.0 copy-start.1
  0.7 0.0 copy-start
  0.7 0.0 copy-start.3
  0.7 1.0 slice_bitcast_fusion.latent_ref
  1.7 0.0 copy-start.4
  1.7 15.3 %all_to_all.50 = bf16[4,16,2048]{2,1,0:T(8,128)(2,1)S(1)} all-to-all(bf16[4,16,2048]{2,1,0:T(8,128)(2,1)S(1)} %shard_map.77), channel_id=1, replica_groups={{0,1,2,3},{4,5,6,7},{8,9,10,11},{12,13,14,15},{16,17,18,19},{20,21,22,2..., dimensions={0} | all-to-all | bytes 524288 | tf_op jit(solution)/shard_map/all_to_all | solution.py:370
  17.0 0.0 copy-done.2
  17.0 0.0 copy-done.5
  17.0 0.0 copy-done.1
  17.0 0.0 copy-done
  17.0 0.0 copy-done.3
  17.0 2.3 %shard_map.78 = (bf16[4,2,16,1024]{3,2,1,0:T(8,128)(2,1)S(1)}, bf16[2,2,64,512]{3,2,1,0:T(8,128)(2,1)S(1)}) custom-call(bf16[4,1,16,2048]{3,2,1,0:T(8,128)(2,1)S(1)} %bitcast.49, f32[3,1,2048]{2,1,0:T(1,128)S(1)} %bitcast.58, bf16[2048,1536]{1,0:T(8,128)(2,1)S(1)} %bitcast.32, bf16[512,2048]{1,0:T(8,128)(2,1)S(1)} %bitcast.38, f32[2,128]{1,0:T(2,128)S(1)} %bitcast.73, ...), custom_call_target="tpu_custom_call" | custom-call | tf_op jit(solution)/shard_map/pallas_call | solution.py:348
  19.3 12.0 %all_to_all.51 = bf16[8,16,1024]{2,1,0:T(8,128)(2,1)S(1)} all-to-all(bf16[8,16,1024]{2,1,0:T(8,128)(2,1)S(1)} %bitcast.70), channel_id=1, replica_groups={{0,4,1,5,2,6,3,7},{8,12,9,13,10,14,11,15},{16,20,17,21,18,22,19,23},{24..., dimensions={0} | all-to-all | bytes 524288 | tf_op jit(solution)/shard_map/all_to_all | solution.py:313
  31.3 0.0 copy-done.4
  31.3 11.8 %all_to_all.52 = bf16[8,16,1024]{2,1,0:T(8,128)(2,1)S(1)} all-to-all(bf16[8,16,1024]{2,1,0:T(8,128)(2,1)S(1)} %bitcast.56), channel_id=1, replica_groups={{0,4,1,5,2,6,3,7},{8,12,9,13,10,14,11,15},{16,20,17,21,18,22,19,23},{24..., dimensions={0} | all-to-all | bytes 524288 | tf_op jit(solution)/shard_map/all_to_all | solution.py:313
  43.1 2.2 %shard_map.80 = (bf16[4,4,16,512]{3,2,1,0:T(8,128)(2,1)S(1)}, bf16[2,2,64,512]{3,2,1,0:T(8,128)(2,1)S(1)}) custom-call(bf16[4,2,16,1024]{3,2,1,0:T(8,128)(2,1)S(1)} %bitcast.45, f32[3,1,2048]{2,1,0:T(1,128)S(1)} %bitcast.59, bf16[2048,1536]{1,0:T(8,128)(2,1)S(1)} %bitcast.33, bf16[512,2048]{1,0:T(8,128)(2,1)S(1)} %bitcast.39, f32[2,128]{1,0:T(2,128)S(1)} %bitcast.74, ...), custom_call_target="tpu_custom_call" | custom-call | tf_op jit(solution)/shard_map/pallas_call | solution.py:348
  45.4 13.7 %all_to_all.53 = bf16[16,16,512]{2,1,0:T(8,128)(2,1)S(1)} all-to-all(bf16[16,16,512]{2,1,0:T(8,128)(2,1)S(1)} %bitcast.65), channel_id=1, replica_groups={{0,4,8,12,1,5,9,13,2,6,10,14,3,7,11,15},{16,20,24,28,17,21,25,29,18,22,..., dimensions={0} | all-to-all | bytes 524288 | tf_op jit(solution)/shard_map/all_to_all | solution.py:313
  59.1 12.5 %all_to_all.54 = bf16[16,16,512]{2,1,0:T(8,128)(2,1)S(1)} all-to-all(bf16[16,16,512]{2,1,0:T(8,128)(2,1)S(1)} %bitcast.71), channel_id=1, replica_groups={{0,4,8,12,1,5,9,13,2,6,10,14,3,7,11,15},{16,20,24,28,17,21,25,29,18,22,..., dimensions={0} | all-to-all | bytes 524288 | tf_op jit(solution)/shard_map/all_to_all | solution.py:313
  71.7 2.2 %shard_map.82 = (bf16[4,4,16,512]{3,2,1,0:T(8,128)(2,1)S(1)}, bf16[2,2,64,512]{3,2,1,0:T(8,128)(2,1)S(1)}) custom-call(bf16[4,4,16,512]{3,2,1,0:T(8,128)(2,1)S(1)} %bitcast.46, f32[3,1,2048]{2,1,0:T(1,128)S(1)} %bitcast.60, bf16[2048,1536]{1,0:T(8,128)(2,1)S(1)} %bitcast.34, bf16[512,2048]{1,0:T(8,128)(2,1)S(1)} %bitcast.40, f32[2,128]{1,0:T(2,128)S(1)} %bitcast.75, ...), custom_call_target="tpu_custom_call" | custom-call | tf_op jit(solution)/shard_map/pallas_call | solution.py:348
  73.9 12.5 %all_to_all.55 = bf16[16,16,512]{2,1,0:T(8,128)(2,1)S(1)} all-to-all(bf16[16,16,512]{2,1,0:T(8,128)(2,1)S(1)} %bitcast.66), channel_id=1, replica_groups={{0,4,8,12,1,5,9,13,2,6,10,14,3,7,11,15},{16,20,24,28,17,21,25,29,18,22,..., dimensions={0} | all-to-all | bytes 524288 | tf_op jit(solution)/shard_map/all_to_all | solution.py:313
  86.5 12.4 %all_to_all.56 = bf16[16,16,512]{2,1,0:T(8,128)(2,1)S(1)} all-to-all(bf16[16,16,512]{2,1,0:T(8,128)(2,1)S(1)} %bitcast.67), channel_id=1, replica_groups={{0,4,8,12,1,5,9,13,2,6,10,14,3,7,11,15},{16,20,24,28,17,21,25,29,18,22,..., dimensions={0} | all-to-all | bytes 524288 | tf_op jit(solution)/shard_map/all_to_all | solution.py:313
  98.8 2.2 %shard_map.84 = (bf16[4,4,16,512]{3,2,1,0:T(8,128)(2,1)S(1)}, bf16[2,2,64,512]{3,2,1,0:T(8,128)(2,1)S(1)}) custom-call(bf16[4,4,16,512]{3,2,1,0:T(8,128)(2,1)S(1)} %bitcast.47, f32[3,1,2048]{2,1,0:T(1,128)S(1)} %bitcast.61, bf16[2048,1536]{1,0:T(8,128)(2,1)S(1)} %bitcast.35, bf16[512,2048]{1,0:T(8,128)(2,1)S(1)} %bitcast.41, f32[2,128]{1,0:T(2,128)S(1)} %bitcast.76, ...), custom_call_target="tpu_custom_call" | custom-call | tf_op jit(solution)/shard_map/pallas_call | solution.py:348
  101.1 12.4 %all_to_all.57 = bf16[16,16,512]{2,1,0:T(8,128)(2,1)S(1)} all-to-all(bf16[16,16,512]{2,1,0:T(8,128)(2,1)S(1)} %bitcast.68), channel_id=1, replica_groups={{0,4,8,12,1,5,9,13,2,6,10,14,3,7,11,15},{16,20,24,28,17,21,25,29,18,22,..., dimensions={0} | all-to-all | bytes 524288 | tf_op jit(solution)/shard_map/all_to_all | solution.py:313
  113.5 12.4 %all_to_all.58 = bf16[16,16,512]{2,1,0:T(8,128)(2,1)S(1)} all-to-all(bf16[16,16,512]{2,1,0:T(8,128)(2,1)S(1)} %bitcast.54), channel_id=1, replica_groups={{0,4,8,12,1,5,9,13,2,6,10,14,3,7,11,15},{16,20,24,28,17,21,25,29,18,22,..., dimensions={0} | all-to-all | bytes 524288 | tf_op jit(solution)/shard_map/all_to_all | solution.py:313
  125.8 2.3 %shard_map.86 = (bf16[2,2,4,16,512]{4,3,2,1,0:T(8,128)(2,1)S(1)}, bf16[2,2,64,512]{3,2,1,0:T(8,128)(2,1)S(1)}) custom-call(bf16[4,4,16,512]{3,2,1,0:T(8,128)(2,1)S(1)} %bitcast.48, f32[3,1,2048]{2,1,0:T(1,128)S(1)} %bitcast.62, bf16[2048,1536]{1,0:T(8,128)(2,1)S(1)} %bitcast.36, bf16[512,2048]{1,0:T(8,128)(2,1)S(1)} %bitcast.42, f32[2,128]{1,0:T(2,128)S(1)} %bitcast.77, ...), custom_call_target="tpu_custom_call" | custom-call | tf_op jit(solution)/shard_map/pallas_call | solution.py:348
  128.1 13.1 %all_to_all.59 = bf16[16,16,512]{2,1,0:T(8,128)(2,1)S(1)} all-to-all(bf16[16,16,512]{2,1,0:T(8,128)(2,1)S(1)} %bitcast.69), channel_id=1, replica_groups={{0,1,2,3,4,5,6,7,16,17,18,19,20,21,22,23},{8,9,10,11,12,13,14,15,24,25,..., dimensions={0} | all-to-all | bytes 524288 | tf_op jit(solution)/shard_map/all_to_all | solution.py:389
  141.2 1.3 shard_map.87
  (5 shorter events, 0.1 us)
Async XLA Ops:
  0.6 16.4 %copy-start.2 = (bf16[1,1,2,4,1,4,8,512]{7,6,5,4,3,2,1,0:T(8,128)(2,1)S(1)}, bf16[1,1,2,4,1,4,8,512]{7,6,5,4,3,2,1,0:T(8,128)(2,1)}, u32[]{:S(2)}) copy-start(bf16[1,1,2,4,1,4,8,512]{7,6,5,4,3,2,1,0:T(8,128)(2,1)} %param.11) | copy-start | bytes 786436
  0.6 16.3 %copy-start.5 = (f32[1,2,128]{2,1,0:T(2,128)S(1)}, f32[1,2,128]{2,1,0:T(2,128)}, u32[]{:S(2)}) copy-start(f32[1,2,128]{2,1,0:T(2,128)} %param.10) | copy-start | bytes 3076
  0.7 16.3 %copy-start.1 = (bf16[1,512,2048]{2,1,0:T(8,128)(2,1)S(1)}, bf16[1,512,2048]{2,1,0:T(8,128)(2,1)}, u32[]{:S(2)}) copy-start(bf16[1,512,2048]{2,1,0:T(8,128)(2,1)} %param.9) | copy-start | bytes 6291460
  0.7 16.3 %copy-start = (bf16[1,2048,1536]{2,1,0:T(8,128)(2,1)S(1)}, bf16[1,2048,1536]{2,1,0:T(8,128)(2,1)}, u32[]{:S(2)}) copy-start(bf16[1,2048,1536]{2,1,0:T(8,128)(2,1)} %param.8) | copy-start | bytes 18874372
  0.7 16.3 %copy-start.3 = (f32[1,1,3,2048]{3,1,2,0:T(1,128)S(1)}, f32[1,1,3,2048]{3,1,2,0:T(1,128)}, u32[]{:S(2)}) copy-start(f32[1,1,3,2048]{3,1,2,0:T(1,128)} %param.7) | copy-start | bytes 73732
  1.7 29.5 %copy-start.4 = (bf16[4,8,2048]{2,1,0:T(8,128)(2,1)S(1)}, bf16[4,8,2048]{2,1,0:T(8,128)(2,1)}, u32[]{:S(2)}) copy-start(bf16[4,8,2048]{2,1,0:T(8,128)(2,1)} %param.6) | copy-start | bytes 393220

commit v22 on v20

--- a/solution.py
+++ b/solution.py
@@ -137,6 +137,21 @@
             table_ref[kind, at] = jnp.where(group == at, rows_of, old_table_ref[kind, at])
 
 
+def tick_kernel(tick, sizes, *refs):
+    old_table_ref, partial_ref, table_ref = refs[-3:]
+    group = tick - lax.axis_index("pipe")
+    active = jnp.logical_and(group >= 0, group < old_table_ref.shape[1])
+
+    @pl.when(active)
+    def _():
+        section_kernel(tick, sizes, *refs)
+
+    @pl.when(jnp.logical_not(active))
+    def _():
+        partial_ref[...] = jnp.zeros(partial_ref.shape, partial_ref.dtype)
+        table_ref[...] = old_table_ref[...]
+
+
 def close_into(closing_ref, projected, rows_ref, section, own_slice, in_group):
     branches, patches, slices = closing_ref.shape[:3]
     blocks, _, block_rows, block_cols = rows_ref.shape
@@ -335,6 +350,8 @@
     if member_count > 1:
         stale_rows = [group_cache.swapaxes(0, 1).reshape(2, -1, local_width)]
 
+    ticks = GROUPS + section_count - 1
+
     def attend(tick, features, table, partial_shape):
         operands = (
             features,
@@ -346,7 +363,11 @@
             in_vmem(table),
         )
         return pl.pallas_call(
-            functools.partial(section_kernel, tick, (tok_dev, head_dim, member_count)),
+            functools.partial(
+                section_kernel if tick == ticks - 1 else tick_kernel,
+                tick,
+                (tok_dev, head_dim, member_count),
+            ),
             out_shape=(
                 jax.ShapeDtypeStruct(partial_shape, jnp.bfloat16),
                 jax.ShapeDtypeStruct(table.shape, jnp.bfloat16),
@@ -365,7 +386,6 @@
             compiler_params=pltpu.CompilerParams(vmem_limit_bytes=8 * 1024 * 1024),
         )
 
-    ticks = GROUPS + section_count - 1
     closing_shape = (2, half, slice_count, block_rows, block_cols)
     features = lax.all_to_all(spread, "seq", 0, 0, axis_index_groups=in_slices)[None]
     pair_shape = (2, slice_count, block_rows, model_width // 2)

time: 140 us -> 138 us (0.986)
  Pallas kernels: 12.7 us -> 8.33 us
  blocking collectives: 125 us -> 128 us
    pallas_call x5, Pallas kernels: 11.3 us -> 6.87 us  [attend(): pl.pallas_call(functools.partial(section_kernel if tick == ticks - 1 else...]
    all_to_all x8, blocking collectives: 97.2 us -> 100 us  [exchange(): flat = lax.all_to_all(flat, ('pipe', 'seq'), 0, 0, axis_index_groups=among)]
where the time goes in v22:
time: 138 us
  blocking collectives  128 us (93%)
  Pallas kernels  8.33 us (6%)
    all_to_all x8, blocking collectives, exchange(): flat = lax.all_to_all(flat, ('pipe', 'seq'), 0, 0, axis_index_groups=among)  100 us
    all_to_all x1, blocking collectives, local(): lax.all_to_all(spread, 'seq', 0, 0, axis_index_groups=in_slices)[None]  15.3 us
    all_to_all x1, blocking collectives, local(): lax.all_to_all(closing.reshape((-1,) + closing_shape[3:]), ('cfg', 'pipe'...  12.7 us
    pallas_call x5, Pallas kernels, attend(): pl.pallas_call(functools.partial(section_kernel if tick == ticks - 1 else...  6.87 us

profile of v22, /device:TPU:0, one launch (start us, length us, event | category | flops | bytes accessed | tf_op | source)
XLA Modules:
  0.0 138.0 jit_solution(18397527425665638335)
XLA Ops:
  0.6 0.0 copy-start.2
  0.6 0.0 copy-start.5
  0.7 0.0 copy-start.1
  0.7 0.0 copy-start
  0.7 0.0 copy-start.3
  0.7 1.0 slice_bitcast_fusion.latent_ref
  1.7 0.0 copy-start.4
  1.7 15.3 %all_to_all.50 = bf16[4,16,2048]{2,1,0:T(8,128)(2,1)S(1)} all-to-all(bf16[4,16,2048]{2,1,0:T(8,128)(2,1)S(1)} %shard_map.77), channel_id=1, replica_groups={{0,1,2,3},{4,5,6,7},{8,9,10,11},{12,13,14,15},{16,17,18,19},{20,21,22,2..., dimensions={0} | all-to-all | bytes 524288 | tf_op jit(solution)/shard_map/all_to_all | solution.py:390
  17.0 0.0 copy-done.2
  17.0 0.0 copy-done.5
  17.0 0.0 copy-done.1
  17.0 0.0 copy-done
  17.0 0.0 copy-done.3
  17.0 2.3 %shard_map.78 = (bf16[2,4,16,1024]{3,2,1,0:T(8,128)(2,1)S(1)}, bf16[2,2,64,512]{3,2,1,0:T(8,128)(2,1)S(1)}) custom-call(bf16[1,4,16,2048]{3,2,1,0:T(8,128)(2,1)S(1)} %bitcast.49, f32[3,1,2048]{2,1,0:T(1,128)S(1)} %bitcast.58, bf16[2048,1536]{1,0:T(8,128)(2,1)S(1)} %bitcast.32, bf16[512,2048]{1,0:T(8,128)(2,1)S(1)} %bitcast.38, f32[2,128]{1,0:T(2,128)S(1)} %bitcast.73, ...), custom_call_target="tpu_custom_call" | custom-call | tf_op jit(solution)/shard_map/pallas_call | solution.py:365
  19.3 12.0 %all_to_all.51 = bf16[8,16,1024]{2,1,0:T(8,128)(2,1)S(1)} all-to-all(bf16[8,16,1024]{2,1,0:T(8,128)(2,1)S(1)} %bitcast.70), channel_id=1, replica_groups={{0,1,2,3,4,5,6,7},{8,9,10,11,12,13,14,15},{16,17,18,19,20,21,22,23},{24..., dimensions={0} | all-to-all | bytes 524288 | tf_op jit(solution)/shard_map/all_to_all | solution.py:328
  31.3 0.0 copy-done.4
  31.4 11.1 %all_to_all.52 = bf16[8,16,1024]{2,1,0:T(8,128)(2,1)S(1)} all-to-all(bf16[8,16,1024]{2,1,0:T(8,128)(2,1)S(1)} %bitcast.56), channel_id=1, replica_groups={{0,1,2,3,4,5,6,7},{8,9,10,11,12,13,14,15},{16,17,18,19,20,21,22,23},{24..., dimensions={0} | all-to-all | bytes 524288 | tf_op jit(solution)/shard_map/all_to_all | solution.py:328
  42.4 2.2 %shard_map.80 = (bf16[4,4,16,512]{3,2,1,0:T(8,128)(2,1)S(1)}, bf16[2,2,64,512]{3,2,1,0:T(8,128)(2,1)S(1)}) custom-call(bf16[2,4,16,1024]{3,2,1,0:T(8,128)(2,1)S(1)} %bitcast.45, f32[3,1,2048]{2,1,0:T(1,128)S(1)} %bitcast.59, bf16[2048,1536]{1,0:T(8,128)(2,1)S(1)} %bitcast.33, bf16[512,2048]{1,0:T(8,128)(2,1)S(1)} %bitcast.39, f32[2,128]{1,0:T(2,128)S(1)} %bitcast.74, ...), custom_call_target="tpu_custom_call" | custom-call | tf_op jit(solution)/shard_map/pallas_call | solution.py:365
  44.7 11.4 %all_to_all.53 = bf16[16,16,512]{2,1,0:T(8,128)(2,1)S(1)} all-to-all(bf16[16,16,512]{2,1,0:T(8,128)(2,1)S(1)} %bitcast.65), channel_id=1, replica_groups={{0,1,2,3,4,5,6,7,8,9,10,11,12,13,14,15},{16,17,18,19,20,21,22,23,24,25,..., dimensions={0} | all-to-all | bytes 524288 | tf_op jit(solution)/shard_map/all_to_all | solution.py:328
  56.1 11.8 %all_to_all.54 = bf16[16,16,512]{2,1,0:T(8,128)(2,1)S(1)} all-to-all(bf16[16,16,512]{2,1,0:T(8,128)(2,1)S(1)} %bitcast.71), channel_id=1, replica_groups={{0,1,2,3,4,5,6,7,8,9,10,11,12,13,14,15},{16,17,18,19,20,21,22,23,24,25,..., dimensions={0} | all-to-all | bytes 524288 | tf_op jit(solution)/shard_map/all_to_all | solution.py:328
  68.0 13.4 %all_to_all.55 = bf16[16,16,512]{2,1,0:T(8,128)(2,1)S(1)} all-to-all(bf16[16,16,512]{2,1,0:T(8,128)(2,1)S(1)} %bitcast.66), channel_id=1, replica_groups={{0,1,2,3,4,5,6,7,8,9,10,11,12,13,14,15},{16,17,18,19,20,21,22,23,24,25,..., dimensions={0} | all-to-all | bytes 524288 | tf_op jit(solution)/shard_map/all_to_all | solution.py:328
  81.4 11.7 %all_to_all.56 = bf16[16,16,512]{2,1,0:T(8,128)(2,1)S(1)} all-to-all(bf16[16,16,512]{2,1,0:T(8,128)(2,1)S(1)} %bitcast.67), channel_id=1, replica_groups={{0,1,2,3,4,5,6,7,8,9,10,11,12,13,14,15},{16,17,18,19,20,21,22,23,24,25,..., dimensions={0} | all-to-all | bytes 524288 | tf_op jit(solution)/shard_map/all_to_all | solution.py:328
  93.2 16.0 %all_to_all.57 = bf16[16,16,512]{2,1,0:T(8,128)(2,1)S(1)} all-to-all(bf16[16,16,512]{2,1,0:T(8,128)(2,1)S(1)} %bitcast.68), channel_id=1, replica_groups={{0,1,2,3,4,5,6,7,8,9,10,11,12,13,14,15},{16,17,18,19,20,21,22,23,24,25,..., dimensions={0} | all-to-all | bytes 524288 | tf_op jit(solution)/shard_map/all_to_all | solution.py:328
  109.2 12.5 %all_to_all.58 = bf16[16,16,512]{2,1,0:T(8,128)(2,1)S(1)} all-to-all(bf16[16,16,512]{2,1,0:T(8,128)(2,1)S(1)} %bitcast.54), channel_id=1, replica_groups={{0,1,2,3,4,5,6,7,8,9,10,11,12,13,14,15},{16,17,18,19,20,21,22,23,24,25,..., dimensions={0} | all-to-all | bytes 524288 | tf_op jit(solution)/shard_map/all_to_all | solution.py:328
  121.7 2.3 %shard_map.86 = (bf16[2,2,4,16,512]{4,3,2,1,0:T(8,128)(2,1)S(1)}, bf16[2,2,64,512]{3,2,1,0:T(8,128)(2,1)S(1)}) custom-call(bf16[4,4,16,512]{3,2,1,0:T(8,128)(2,1)S(1)} %bitcast.48, f32[3,1,2048]{2,1,0:T(1,128)S(1)} %bitcast.62, bf16[2048,1536]{1,0:T(8,128)(2,1)S(1)} %bitcast.36, bf16[512,2048]{1,0:T(8,128)(2,1)S(1)} %bitcast.42, f32[2,128]{1,0:T(2,128)S(1)} %bitcast.77, ...), custom_call_target="tpu_custom_call" | custom-call | tf_op jit(solution)/shard_map/pallas_call | solution.py:365
  124.0 12.7 %all_to_all.59 = bf16[16,16,512]{2,1,0:T(8,128)(2,1)S(1)} all-to-all(bf16[16,16,512]{2,1,0:T(8,128)(2,1)S(1)} %bitcast.69), channel_id=1, replica_groups={{0,1,2,3,4,5,6,7,16,17,18,19,20,21,22,23},{8,9,10,11,12,13,14,15,24,25,..., dimensions={0} | all-to-all | bytes 524288 | tf_op jit(solution)/shard_map/all_to_all | solution.py:409
  136.7 1.3 shard_map.87
  (7 shorter events, 0.2 us)
Async XLA Ops:
  0.6 16.4 %copy-start.2 = (bf16[1,1,2,4,1,4,8,512]{7,6,5,4,3,2,1,0:T(8,128)(2,1)S(1)}, bf16[1,1,2,4,1,4,8,512]{7,6,5,4,3,2,1,0:T(8,128)(2,1)}, u32[]{:S(2)}) copy-start(bf16[1,1,2,4,1,4,8,512]{7,6,5,4,3,2,1,0:T(8,128)(2,1)} %param.11) | copy-start | bytes 786436
  0.6 16.3 %copy-start.5 = (f32[1,2,128]{2,1,0:T(2,128)S(1)}, f32[1,2,128]{2,1,0:T(2,128)}, u32[]{:S(2)}) copy-start(f32[1,2,128]{2,1,0:T(2,128)} %param.10) | copy-start | bytes 3076
  0.7 16.3 %copy-start.1 = (bf16[1,512,2048]{2,1,0:T(8,128)(2,1)S(1)}, bf16[1,512,2048]{2,1,0:T(8,128)(2,1)}, u32[]{:S(2)}) copy-start(bf16[1,512,2048]{2,1,0:T(8,128)(2,1)} %param.9) | copy-start | bytes 6291460
  0.7 16.3 %copy-start = (bf16[1,2048,1536]{2,1,0:T(8,128)(2,1)S(1)}, bf16[1,2048,1536]{2,1,0:T(8,128)(2,1)}, u32[]{:S(2)}) copy-start(bf16[1,2048,1536]{2,1,0:T(8,128)(2,1)} %param.8) | copy-start | bytes 18874372
  0.7 16.3 %copy-start.3 = (f32[1,1,3,2048]{3,1,2,0:T(1,128)S(1)}, f32[1,1,3,2048]{3,1,2,0:T(1,128)}, u32[]{:S(2)}) copy-start(f32[1,1,3,2048]{3,1,2,0:T(1,128)} %param.7) | copy-start | bytes 73732
  1.7 29.6 %copy-start.4 = (bf16[4,8,2048]{2,1,0:T(8,128)(2,1)S(1)}, bf16[4,8,2048]{2,1,0:T(8,128)(2,1)}, u32[]{:S(2)}) copy-start(bf16[4,8,2048]{2,1,0:T(8,128)(2,1)} %param.6) | copy-start | bytes 393220

commit v23 on v22

--- a/solution.py
+++ b/solution.py
@@ -137,6 +137,19 @@
             table_ref[kind, at] = jnp.where(group == at, rows_of, old_table_ref[kind, at])
 
 
+def close_finished(closing_ref, rows_ref, own_slice, tok_dev):
+    branches, patches, slices = closing_ref.shape[:3]
+    blocks = rows_ref.shape[0]
+    per_branch = blocks // branches
+    finished = [rows_ref[q, own_slice].astype(jnp.float32)[:tok_dev] for q in range(blocks)]
+    for branch in range(branches):
+        held = jnp.concatenate(finished[branch * per_branch : (branch + 1) * per_branch])
+        held = held.astype(jnp.bfloat16)
+        for patch in range(patches):
+            for piece in range(slices):
+                closing_ref[branch, patch, piece] = held
+
+
 def tick_kernel(tick, sizes, *refs):
     old_table_ref, partial_ref, table_ref = refs[-3:]
     group = tick - lax.axis_index("pipe")
@@ -148,7 +161,10 @@
 
     @pl.when(jnp.logical_not(active))
     def _():
-        partial_ref[...] = jnp.zeros(partial_ref.shape, partial_ref.dtype)
+        if len(partial_ref.shape) == 5:
+            close_finished(partial_ref, refs[0], position(sizes[2])[2], sizes[0])
+        else:
+            partial_ref[...] = jnp.zeros(partial_ref.shape, partial_ref.dtype)
         table_ref[...] = old_table_ref[...]
 
 
@@ -177,13 +193,7 @@
 
     @pl.when(section < patches)
     def _():
-        finished = [rows_ref[q, own_slice].astype(jnp.float32)[:tok_dev] for q in range(blocks)]
-        for branch in range(branches):
-            held = jnp.concatenate(finished[branch * per_branch : (branch + 1) * per_branch])
-            held = held.astype(jnp.bfloat16)
-            for patch in range(patches):
-                for piece in range(slices):
-                    closing_ref[branch, patch, piece] = held
+        close_finished(closing_ref, rows_ref, own_slice, tok_dev)
 
 
 def start_kernel(latent_ref, *refs):
@@ -364,7 +374,7 @@
         )
         return pl.pallas_call(
             functools.partial(
-                section_kernel if tick == ticks - 1 else tick_kernel,
+                tick_kernel,
                 tick,
                 (tok_dev, head_dim, member_count),
             ),

time: 138 us -> 137 us (level)
  Pallas kernels: 8.33 us -> 6.07 us
    pallas_call x5, Pallas kernels: 6.87 us -> 4.61 us  [attend(): pl.pallas_call(functools.partial(tick_kernel, tick, (tok_dev, head_dim, m...]
where the time goes in v23:
time: 137 us; the launch traced here: 136 us
  blocking collectives  128 us (93%)
  Pallas kernels  6.07 us (4%)
    all_to_all x8, blocking collectives, exchange(): flat = lax.all_to_all(flat, ('pipe', 'seq'), 0, 0, axis_index_groups=among)  100 us
    all_to_all x1, blocking collectives, local(): lax.all_to_all(spread, 'seq', 0, 0, axis_index_groups=in_slices)[None]  15.3 us
    all_to_all x1, blocking collectives, local(): lax.all_to_all(closing.reshape((-1,) + closing_shape[3:]), ('cfg', 'pipe'...  12.7 us
    pallas_call x5, Pallas kernels, attend(): pl.pallas_call(functools.partial(tick_kernel, tick, (tok_dev, head_dim, m...  4.61 us

profile of v23, /device:TPU:0, one launch (start us, length us, event | category | flops | bytes accessed | tf_op | source)
XLA Modules:
  0.0 135.7 jit_solution(11183110267688667541)
XLA Ops:
  0.6 0.0 copy-start.2
  0.6 0.0 copy-start.5
  0.7 0.0 copy-start.1
  0.7 0.0 copy-start
  0.7 0.0 copy-start.3
  0.7 1.0 slice_bitcast_fusion.latent_ref
  1.7 0.0 copy-start.4
  1.7 15.3 %all_to_all.50 = bf16[4,16,2048]{2,1,0:T(8,128)(2,1)S(1)} all-to-all(bf16[4,16,2048]{2,1,0:T(8,128)(2,1)S(1)} %shard_map.77), channel_id=1, replica_groups={{0,1,2,3},{4,5,6,7},{8,9,10,11},{12,13,14,15},{16,17,18,19},{20,21,22,2..., dimensions={0} | all-to-all | bytes 524288 | tf_op jit(solution)/shard_map/all_to_all | solution.py:400
  17.0 0.0 copy-done.2
  17.0 0.0 copy-done.5
  17.0 0.0 copy-done.1
  17.0 0.0 copy-done
  17.0 0.0 copy-done.3
  17.0 2.3 %shard_map.78 = (bf16[2,4,16,1024]{3,2,1,0:T(8,128)(2,1)S(1)}, bf16[2,2,64,512]{3,2,1,0:T(8,128)(2,1)S(1)}) custom-call(bf16[1,4,16,2048]{3,2,1,0:T(8,128)(2,1)S(1)} %bitcast.49, f32[3,1,2048]{2,1,0:T(1,128)S(1)} %bitcast.58, bf16[2048,1536]{1,0:T(8,128)(2,1)S(1)} %bitcast.32, bf16[512,2048]{1,0:T(8,128)(2,1)S(1)} %bitcast.38, f32[2,128]{1,0:T(2,128)S(1)} %bitcast.73, ...), custom_call_target="tpu_custom_call" | custom-call | tf_op jit(solution)/shard_map/pallas_call | solution.py:375
  19.3 12.0 %all_to_all.51 = bf16[8,16,1024]{2,1,0:T(8,128)(2,1)S(1)} all-to-all(bf16[8,16,1024]{2,1,0:T(8,128)(2,1)S(1)} %bitcast.70), channel_id=1, replica_groups={{0,1,2,3,4,5,6,7},{8,9,10,11,12,13,14,15},{16,17,18,19,20,21,22,23},{24..., dimensions={0} | all-to-all | bytes 524288 | tf_op jit(solution)/shard_map/all_to_all | solution.py:338
  31.3 0.0 copy-done.4
  31.4 11.1 %all_to_all.52 = bf16[8,16,1024]{2,1,0:T(8,128)(2,1)S(1)} all-to-all(bf16[8,16,1024]{2,1,0:T(8,128)(2,1)S(1)} %bitcast.56), channel_id=1, replica_groups={{0,1,2,3,4,5,6,7},{8,9,10,11,12,13,14,15},{16,17,18,19,20,21,22,23},{24..., dimensions={0} | all-to-all | bytes 524288 | tf_op jit(solution)/shard_map/all_to_all | solution.py:338
  42.4 2.2 %shard_map.80 = (bf16[4,4,16,512]{3,2,1,0:T(8,128)(2,1)S(1)}, bf16[2,2,64,512]{3,2,1,0:T(8,128)(2,1)S(1)}) custom-call(bf16[2,4,16,1024]{3,2,1,0:T(8,128)(2,1)S(1)} %bitcast.45, f32[3,1,2048]{2,1,0:T(1,128)S(1)} %bitcast.59, bf16[2048,1536]{1,0:T(8,128)(2,1)S(1)} %bitcast.33, bf16[512,2048]{1,0:T(8,128)(2,1)S(1)} %bitcast.39, f32[2,128]{1,0:T(2,128)S(1)} %bitcast.74, ...), custom_call_target="tpu_custom_call" | custom-call | tf_op jit(solution)/shard_map/pallas_call | solution.py:375
  44.7 11.4 %all_to_all.53 = bf16[16,16,512]{2,1,0:T(8,128)(2,1)S(1)} all-to-all(bf16[16,16,512]{2,1,0:T(8,128)(2,1)S(1)} %bitcast.65), channel_id=1, replica_groups={{0,1,2,3,4,5,6,7,8,9,10,11,12,13,14,15},{16,17,18,19,20,21,22,23,24,25,..., dimensions={0} | all-to-all | bytes 524288 | tf_op jit(solution)/shard_map/all_to_all | solution.py:338
  56.1 11.8 %all_to_all.54 = bf16[16,16,512]{2,1,0:T(8,128)(2,1)S(1)} all-to-all(bf16[16,16,512]{2,1,0:T(8,128)(2,1)S(1)} %bitcast.71), channel_id=1, replica_groups={{0,1,2,3,4,5,6,7,8,9,10,11,12,13,14,15},{16,17,18,19,20,21,22,23,24,25,..., dimensions={0} | all-to-all | bytes 524288 | tf_op jit(solution)/shard_map/all_to_all | solution.py:338
  68.0 13.4 %all_to_all.55 = bf16[16,16,512]{2,1,0:T(8,128)(2,1)S(1)} all-to-all(bf16[16,16,512]{2,1,0:T(8,128)(2,1)S(1)} %bitcast.66), channel_id=1, replica_groups={{0,1,2,3,4,5,6,7,8,9,10,11,12,13,14,15},{16,17,18,19,20,21,22,23,24,25,..., dimensions={0} | all-to-all | bytes 524288 | tf_op jit(solution)/shard_map/all_to_all | solution.py:338
  81.4 11.7 %all_to_all.56 = bf16[16,16,512]{2,1,0:T(8,128)(2,1)S(1)} all-to-all(bf16[16,16,512]{2,1,0:T(8,128)(2,1)S(1)} %bitcast.67), channel_id=1, replica_groups={{0,1,2,3,4,5,6,7,8,9,10,11,12,13,14,15},{16,17,18,19,20,21,22,23,24,25,..., dimensions={0} | all-to-all | bytes 524288 | tf_op jit(solution)/shard_map/all_to_all | solution.py:338
  93.2 16.0 %all_to_all.57 = bf16[16,16,512]{2,1,0:T(8,128)(2,1)S(1)} all-to-all(bf16[16,16,512]{2,1,0:T(8,128)(2,1)S(1)} %bitcast.68), channel_id=1, replica_groups={{0,1,2,3,4,5,6,7,8,9,10,11,12,13,14,15},{16,17,18,19,20,21,22,23,24,25,..., dimensions={0} | all-to-all | bytes 524288 | tf_op jit(solution)/shard_map/all_to_all | solution.py:338
  109.2 12.5 %all_to_all.58 = bf16[16,16,512]{2,1,0:T(8,128)(2,1)S(1)} all-to-all(bf16[16,16,512]{2,1,0:T(8,128)(2,1)S(1)} %bitcast.54), channel_id=1, replica_groups={{0,1,2,3,4,5,6,7,8,9,10,11,12,13,14,15},{16,17,18,19,20,21,22,23,24,25,..., dimensions={0} | all-to-all | bytes 524288 | tf_op jit(solution)/shard_map/all_to_all | solution.py:338
  121.8 12.7 %all_to_all.59 = bf16[16,16,512]{2,1,0:T(8,128)(2,1)S(1)} all-to-all(bf16[16,16,512]{2,1,0:T(8,128)(2,1)S(1)} %bitcast.69), channel_id=1, replica_groups={{0,1,2,3,4,5,6,7,16,17,18,19,20,21,22,23},{8,9,10,11,12,13,14,15,24,25,..., dimensions={0} | all-to-all | bytes 524288 | tf_op jit(solution)/shard_map/all_to_all | solution.py:419
  134.4 1.3 shard_map.87
  (8 shorter events, 0.2 us)
Async XLA Ops:
  0.6 16.4 %copy-start.2 = (bf16[1,1,2,4,1,4,8,512]{7,6,5,4,3,2,1,0:T(8,128)(2,1)S(1)}, bf16[1,1,2,4,1,4,8,512]{7,6,5,4,3,2,1,0:T(8,128)(2,1)}, u32[]{:S(2)}) copy-start(bf16[1,1,2,4,1,4,8,512]{7,6,5,4,3,2,1,0:T(8,128)(2,1)} %param.11) | copy-start | bytes 786436
  0.6 16.3 %copy-start.5 = (f32[1,2,128]{2,1,0:T(2,128)S(1)}, f32[1,2,128]{2,1,0:T(2,128)}, u32[]{:S(2)}) copy-start(f32[1,2,128]{2,1,0:T(2,128)} %param.10) | copy-start | bytes 3076
  0.7 16.3 %copy-start.1 = (bf16[1,512,2048]{2,1,0:T(8,128)(2,1)S(1)}, bf16[1,512,2048]{2,1,0:T(8,128)(2,1)}, u32[]{:S(2)}) copy-start(bf16[1,512,2048]{2,1,0:T(8,128)(2,1)} %param.9) | copy-start | bytes 6291460
  0.7 16.3 %copy-start = (bf16[1,2048,1536]{2,1,0:T(8,128)(2,1)S(1)}, bf16[1,2048,1536]{2,1,0:T(8,128)(2,1)}, u32[]{:S(2)}) copy-start(bf16[1,2048,1536]{2,1,0:T(8,128)(2,1)} %param.8) | copy-start | bytes 18874372
  0.7 16.3 %copy-start.3 = (f32[1,1,3,2048]{3,1,2,0:T(1,128)S(1)}, f32[1,1,3,2048]{3,1,2,0:T(1,128)}, u32[]{:S(2)}) copy-start(f32[1,1,3,2048]{3,1,2,0:T(1,128)} %param.7) | copy-start | bytes 73732
  1.7 29.6 %copy-start.4 = (bf16[4,8,2048]{2,1,0:T(8,128)(2,1)S(1)}, bf16[4,8,2048]{2,1,0:T(8,128)(2,1)}, u32[]{:S(2)}) copy-start(bf16[4,8,2048]{2,1,0:T(8,128)(2,1)} %param.6) | copy-start | bytes 393220

commit v24 on v23

--- a/solution.py
+++ b/solution.py
@@ -197,9 +197,12 @@
 
 
 def start_kernel(latent_ref, *refs):
-    spread_to = refs[-1]
-    for piece in range(spread_to.shape[0]):
-        spread_to[piece] = latent_ref[...]
+    spread_to, sem = refs[-2:]
+    copy = pltpu.make_async_copy(latent_ref.at[0], spread_to.at[0], sem)
+    copy.start()
+    copy.wait()
+    for piece in range(1, spread_to.shape[0]):
+        spread_to[piece] = spread_to[0]
 
 
 def added(parts_ref, section, *streams_refs):
@@ -348,14 +351,15 @@
     modulation = modulation.reshape(3, 1, model_width)
     norm_gain = norm_gain[0]
     table = own_cache.reshape(2, GROUPS, rows, local_width)
-    named = (qkv_slice, out_slice, modulation, norm_gain, table, sources)
+    named = (qkv_slice, out_slice, modulation, norm_gain, table)
     spread = pl.pallas_call(
         start_kernel,
         out_shape=jax.ShapeDtypeStruct((slice_count, block_rows, model_width), jnp.bfloat16),
-        in_specs=[vmem] + [hbm] * len(named),
+        in_specs=[hbm] * (len(named) + 1),
         out_specs=vmem,
+        scratch_shapes=[pltpu.SemaphoreType.DMA],
         compiler_params=pltpu.CompilerParams(vmem_limit_bytes=4 * 1024 * 1024),
-    )(sources[0], *map(in_hbm, named))
+    )(in_hbm(sources), *map(in_hbm, named))
     stale_rows = []
     if member_count > 1:
         stale_rows = [group_cache.swapaxes(0, 1).reshape(2, -1, local_width)]

time: 137 us -> 137 us (level)
  no operation moved by 1% of the time
where the time goes in v24:
time: 137 us; the launch traced here: 136 us
  blocking collectives  128 us (93%)
  Pallas kernels  7.06 us (5%)
    all_to_all x8, blocking collectives, exchange(): flat = lax.all_to_all(flat, ('pipe', 'seq'), 0, 0, axis_index_groups=among)  100 us
    all_to_all x1, blocking collectives, local(): lax.all_to_all(spread, 'seq', 0, 0, axis_index_groups=in_slices)[None]  15.3 us
    all_to_all x1, blocking collectives, local(): lax.all_to_all(closing.reshape((-1,) + closing_shape[3:]), ('cfg', 'pipe'...  12.7 us
    pallas_call x5, Pallas kernels, attend(): pl.pallas_call(functools.partial(tick_kernel, tick, (tok_dev, head_dim, m...  4.61 us

profile of v24, /device:TPU:0, one launch (start us, length us, event | category | flops | bytes accessed | tf_op | source)
XLA Modules:
  0.0 135.7 jit_solution(15063205665297163735)
XLA Ops:
  0.6 0.0 copy-start.2
  0.6 0.0 copy-start.5
  0.7 0.0 copy-start.1
  0.7 0.0 copy-start
  0.7 0.0 copy-start.3
  0.7 1.0 shard_map.77
  1.7 0.0 copy-start.4
  1.7 15.3 %all_to_all.50 = bf16[4,16,2048]{2,1,0:T(8,128)(2,1)S(1)} all-to-all(bf16[4,16,2048]{2,1,0:T(8,128)(2,1)S(1)} %shard_map.77), channel_id=1, replica_groups={{0,1,2,3},{4,5,6,7},{8,9,10,11},{12,13,14,15},{16,17,18,19},{20,21,22,2..., dimensions={0} | all-to-all | bytes 524288 | tf_op jit(solution)/shard_map/all_to_all | solution.py:404
  17.0 0.0 copy-done.2
  17.0 0.0 copy-done.5
  17.0 0.0 copy-done.1
  17.0 0.0 copy-done
  17.0 0.0 copy-done.3
  17.0 2.3 %shard_map.78 = (bf16[2,4,16,1024]{3,2,1,0:T(8,128)(2,1)S(1)}, bf16[2,2,64,512]{3,2,1,0:T(8,128)(2,1)S(1)}) custom-call(bf16[1,4,16,2048]{3,2,1,0:T(8,128)(2,1)S(1)} %bitcast.47, f32[3,1,2048]{2,1,0:T(1,128)S(1)} %bitcast.56, bf16[2048,1536]{1,0:T(8,128)(2,1)S(1)} %bitcast.30, bf16[512,2048]{1,0:T(8,128)(2,1)S(1)} %bitcast.36, f32[2,128]{1,0:T(2,128)S(1)} %bitcast.71, ...), custom_call_target="tpu_custom_call" | custom-call | tf_op jit(solution)/shard_map/pallas_call | solution.py:379
  19.3 12.0 %all_to_all.51 = bf16[8,16,1024]{2,1,0:T(8,128)(2,1)S(1)} all-to-all(bf16[8,16,1024]{2,1,0:T(8,128)(2,1)S(1)} %bitcast.68), channel_id=1, replica_groups={{0,1,2,3,4,5,6,7},{8,9,10,11,12,13,14,15},{16,17,18,19,20,21,22,23},{24..., dimensions={0} | all-to-all | bytes 524288 | tf_op jit(solution)/shard_map/all_to_all | solution.py:341
  31.3 0.0 copy-done.4
  31.4 11.1 %all_to_all.52 = bf16[8,16,1024]{2,1,0:T(8,128)(2,1)S(1)} all-to-all(bf16[8,16,1024]{2,1,0:T(8,128)(2,1)S(1)} %bitcast.54), channel_id=1, replica_groups={{0,1,2,3,4,5,6,7},{8,9,10,11,12,13,14,15},{16,17,18,19,20,21,22,23},{24..., dimensions={0} | all-to-all | bytes 524288 | tf_op jit(solution)/shard_map/all_to_all | solution.py:341
  42.4 2.2 %shard_map.80 = (bf16[4,4,16,512]{3,2,1,0:T(8,128)(2,1)S(1)}, bf16[2,2,64,512]{3,2,1,0:T(8,128)(2,1)S(1)}) custom-call(bf16[2,4,16,1024]{3,2,1,0:T(8,128)(2,1)S(1)} %bitcast.43, f32[3,1,2048]{2,1,0:T(1,128)S(1)} %bitcast.57, bf16[2048,1536]{1,0:T(8,128)(2,1)S(1)} %bitcast.31, bf16[512,2048]{1,0:T(8,128)(2,1)S(1)} %bitcast.37, f32[2,128]{1,0:T(2,128)S(1)} %bitcast.72, ...), custom_call_target="tpu_custom_call" | custom-call | tf_op jit(solution)/shard_map/pallas_call | solution.py:379
  44.6 11.4 %all_to_all.53 = bf16[16,16,512]{2,1,0:T(8,128)(2,1)S(1)} all-to-all(bf16[16,16,512]{2,1,0:T(8,128)(2,1)S(1)} %bitcast.63), channel_id=1, replica_groups={{0,1,2,3,4,5,6,7,8,9,10,11,12,13,14,15},{16,17,18,19,20,21,22,23,24,25,..., dimensions={0} | all-to-all | bytes 524288 | tf_op jit(solution)/shard_map/all_to_all | solution.py:341
  56.1 11.8 %all_to_all.54 = bf16[16,16,512]{2,1,0:T(8,128)(2,1)S(1)} all-to-all(bf16[16,16,512]{2,1,0:T(8,128)(2,1)S(1)} %bitcast.69), channel_id=1, replica_groups={{0,1,2,3,4,5,6,7,8,9,10,11,12,13,14,15},{16,17,18,19,20,21,22,23,24,25,..., dimensions={0} | all-to-all | bytes 524288 | tf_op jit(solution)/shard_map/all_to_all | solution.py:341
  68.0 13.4 %all_to_all.55 = bf16[16,16,512]{2,1,0:T(8,128)(2,1)S(1)} all-to-all(bf16[16,16,512]{2,1,0:T(8,128)(2,1)S(1)} %bitcast.64), channel_id=1, replica_groups={{0,1,2,3,4,5,6,7,8,9,10,11,12,13,14,15},{16,17,18,19,20,21,22,23,24,25,..., dimensions={0} | all-to-all | bytes 524288 | tf_op jit(solution)/shard_map/all_to_all | solution.py:341
  81.4 11.7 %all_to_all.56 = bf16[16,16,512]{2,1,0:T(8,128)(2,1)S(1)} all-to-all(bf16[16,16,512]{2,1,0:T(8,128)(2,1)S(1)} %bitcast.65), channel_id=1, replica_groups={{0,1,2,3,4,5,6,7,8,9,10,11,12,13,14,15},{16,17,18,19,20,21,22,23,24,25,..., dimensions={0} | all-to-all | bytes 524288 | tf_op jit(solution)/shard_map/all_to_all | solution.py:341
  93.2 16.0 %all_to_all.57 = bf16[16,16,512]{2,1,0:T(8,128)(2,1)S(1)} all-to-all(bf16[16,16,512]{2,1,0:T(8,128)(2,1)S(1)} %bitcast.66), channel_id=1, replica_groups={{0,1,2,3,4,5,6,7,8,9,10,11,12,13,14,15},{16,17,18,19,20,21,22,23,24,25,..., dimensions={0} | all-to-all | bytes 524288 | tf_op jit(solution)/shard_map/all_to_all | solution.py:341
  109.2 12.5 %all_to_all.58 = bf16[16,16,512]{2,1,0:T(8,128)(2,1)S(1)} all-to-all(bf16[16,16,512]{2,1,0:T(8,128)(2,1)S(1)} %bitcast.52), channel_id=1, replica_groups={{0,1,2,3,4,5,6,7,8,9,10,11,12,13,14,15},{16,17,18,19,20,21,22,23,24,25,..., dimensions={0} | all-to-all | bytes 524288 | tf_op jit(solution)/shard_map/all_to_all | solution.py:341
  121.7 12.7 %all_to_all.59 = bf16[16,16,512]{2,1,0:T(8,128)(2,1)S(1)} all-to-all(bf16[16,16,512]{2,1,0:T(8,128)(2,1)S(1)} %bitcast.67), channel_id=1, replica_groups={{0,1,2,3,4,5,6,7,16,17,18,19,20,21,22,23},{8,9,10,11,12,13,14,15,24,25,..., dimensions={0} | all-to-all | bytes 524288 | tf_op jit(solution)/shard_map/all_to_all | solution.py:423
  134.4 1.3 shard_map.87
  (7 shorter events, 0.2 us)
Async XLA Ops:
  0.6 16.3 %copy-start.2 = (bf16[1,1,2,4,1,4,8,512]{7,6,5,4,3,2,1,0:T(8,128)(2,1)S(1)}, bf16[1,1,2,4,1,4,8,512]{7,6,5,4,3,2,1,0:T(8,128)(2,1)}, u32[]{:S(2)}) copy-start(bf16[1,1,2,4,1,4,8,512]{7,6,5,4,3,2,1,0:T(8,128)(2,1)} %param.11) | copy-start | bytes 786436
  0.6 16.3 %copy-start.5 = (f32[1,2,128]{2,1,0:T(2,128)S(1)}, f32[1,2,128]{2,1,0:T(2,128)}, u32[]{:S(2)}) copy-start(f32[1,2,128]{2,1,0:T(2,128)} %param.10) | copy-start | bytes 3076
  0.7 16.3 %copy-start.1 = (bf16[1,512,2048]{2,1,0:T(8,128)(2,1)S(1)}, bf16[1,512,2048]{2,1,0:T(8,128)(2,1)}, u32[]{:S(2)}) copy-start(bf16[1,512,2048]{2,1,0:T(8,128)(2,1)} %param.9) | copy-start | bytes 6291460
  0.7 16.3 %copy-start = (bf16[1,2048,1536]{2,1,0:T(8,128)(2,1)S(1)}, bf16[1,2048,1536]{2,1,0:T(8,128)(2,1)}, u32[]{:S(2)}) copy-start(bf16[1,2048,1536]{2,1,0:T(8,128)(2,1)} %param.8) | copy-start | bytes 18874372
  0.7 16.3 %copy-start.3 = (f32[1,1,3,2048]{3,1,2,0:T(1,128)S(1)}, f32[1,1,3,2048]{3,1,2,0:T(1,128)}, u32[]{:S(2)}) copy-start(f32[1,1,3,2048]{3,1,2,0:T(1,128)} %param.7) | copy-start | bytes 73732
  1.7 29.6 %copy-start.4 = (bf16[4,8,2048]{2,1,0:T(8,128)(2,1)S(1)}, bf16[4,8,2048]{2,1,0:T(8,128)(2,1)}, u32[]{:S(2)}) copy-start(bf16[4,8,2048]{2,1,0:T(8,128)(2,1)} %param.6) | copy-start | bytes 393220
